TPU v7x, 32 devices: a whole 2x2x4 slice. The times are simulated.
32 devices in a mesh: dp: 8 (over z, y), seq: 4 (over x, core).
Axes of the slice: x: 2, y: 2, z: 4, core: 2. Of those that a mesh axis runs over, the one named last changes fastest.
Arguments:
- tokens_in: bfloat16 [32, 512, 768], P('dp', 'seq'), may hold values from -6 to 6
- segment_ids: int32 [32, 512], P('dp'), may hold values from 0 to 3, as said below
- pad_mask: int32 [32, 512], P('dp'), may hold values from 0 to 1, as said below
- out_grad: bfloat16 [32, 512, 768], P('dp', 'seq'), may hold values from -6 to 6
- w_query: float32 [768, 768], P(('dp', 'seq')), may hold values from -0.21875 to 0.21875
- w_key: float32 [768, 768], P(('dp', 'seq')), may hold values from -0.21875 to 0.21875
- w_value: float32 [768, 768], P(('dp', 'seq')), may hold values from -0.21875 to 0.21875
- w_out: float32 [768, 768], P(('dp', 'seq')), may hold values from -0.875 to 0.875
- w_up: float32 [768, 3072], P(('dp', 'seq')), may hold values from -0.21875 to 0.21875
- w_down: float32 [3072, 768], P(('dp', 'seq')), may hold values from -0.109375 to 0.109375
- norm_params: float32 [4, 768], P(None, ('dp', 'seq')), may hold values from -0.5 to 3.2, as said below
- first_query: float32 [768, 768], P(('dp', 'seq')), may hold values from -0.0048828125 to 0.0048828125
- first_key: float32 [768, 768], P(('dp', 'seq')), may hold values from -0.0048828125 to 0.0048828125
- first_value: float32 [768, 768], P(('dp', 'seq')), may hold values from -0.001953125 to 0.001953125
- first_out: float32 [768, 768], P(('dp', 'seq')), may hold values from -0.00048828125 to 0.00048828125
- first_up: float32 [768, 3072], P(('dp', 'seq')), may hold values from -0.00048828125 to 0.00048828125
- first_down: float32 [3072, 768], P(('dp', 'seq')), may hold values from -0.0012207031 to 0.0012207031
- first_norm: float32 [4, 768], P(None, ('dp', 'seq')), may hold values from -0.0024414062 to 0.0024414062
- second_query: float32 [768, 768], P(('dp', 'seq')), may hold values from 5.6073225e-07 to 2.2360907e-06
- second_key: float32 [768, 768], P(('dp', 'seq')), may hold values from 5.6073225e-07 to 2.2360907e-06
- second_value: float32 [768, 768], P(('dp', 'seq')), may hold values from 8.77013e-08 to 3.4973567e-07
- second_out: float32 [768, 768], P(('dp', 'seq')), may hold values from 6.673177e-09 to 2.6611328e-08
- second_up: float32 [768, 3072], P(('dp', 'seq')), may hold values from 6.673177e-09 to 2.6611328e-08
- second_down: float32 [3072, 768], P(('dp', 'seq')), may hold values from 3.6378083e-08 to 1.450687e-07
- second_norm: float32 [4, 768], P(None, ('dp', 'seq')), may hold values from 1.15853766e-07 to 4.6200222e-07
Outputs:
- output: bfloat16 [32, 512, 768], P('dp', 'seq')
- input_grad: bfloat16 [32, 512, 768], P('dp', 'seq')
- grad_norm: float32 [], replicated
- w_query_next: float32 [768, 768], P(('dp', 'seq'))
- w_key_next: float32 [768, 768], P(('dp', 'seq'))
- w_value_next: float32 [768, 768], P(('dp', 'seq'))
- w_out_next: float32 [768, 768], P(('dp', 'seq'))
- w_up_next: float32 [768, 3072], P(('dp', 'seq'))
- w_down_next: float32 [3072, 768], P(('dp', 'seq'))
- norm_params_next: float32 [4, 768], P(None, ('dp', 'seq'))
- first_query_next: float32 [768, 768], P(('dp', 'seq'))
- first_key_next: float32 [768, 768], P(('dp', 'seq'))
- first_value_next: float32 [768, 768], P(('dp', 'seq'))
- first_out_next: float32 [768, 768], P(('dp', 'seq'))
- first_up_next: float32 [768, 3072], P(('dp', 'seq'))
- first_down_next: float32 [3072, 768], P(('dp', 'seq'))
- first_norm_next: float32 [4, 768], P(None, ('dp', 'seq'))
- second_query_next: float32 [768, 768], P(('dp', 'seq'))
- second_key_next: float32 [768, 768], P(('dp', 'seq'))
- second_value_next: float32 [768, 768], P(('dp', 'seq'))
- second_out_next: float32 [768, 768], P(('dp', 'seq'))
- second_up_next: float32 [768, 3072], P(('dp', 'seq'))
- second_down_next: float32 [3072, 768], P(('dp', 'seq'))
- second_norm_next: float32 [4, 768], P(None, ('dp', 'seq'))
Inputs may be any that keep to these rules, and one draw needn't show every extreme that they name: `segment_ids`: ids never fall along a row; equal ids form one document. `pad_mask`: in each row the padded positions, at most half of 128 of them, are its last ones. `norm_params`: rows 0 and 2 are gains, rows 1 and 3 shifts.
All inputs are finite; a program needn't handle non-finite values.
Results may differ from a plain program's by a relative error of at most 0.014.
The roundings to bfloat16 on the way count: a program that leaves them out, or rounds other values in their place, can miss the bound.
Values may be sent and summed in bfloat16 or wider, within the bound.
No kernel may reach another device: no remote copies, remote signals or barrier semaphores. Data moves between devices by JAX's collectives and lax.ppermute only.
A program may use at most 128 MiB of HBM per device.

v0:
```python
from functools import partial

import jax
import jax.numpy as jnp
from jax import lax
from jax.experimental import pallas as pl
from jax.experimental.pallas import tpu as pltpu
from jax.sharding import PartitionSpec as P

D = 768
H = 12
HD = 64
FF = 3072
STEP = 7
HALF = D // 2
PAIRS = H // 2
BLOCKS = 4
BF = jnp.bfloat16
F32 = jnp.float32
AXES = ("dp", "seq")
clip_limit = 1.0
MIB = 2**20

VM = pl.BlockSpec(memory_space=pltpu.VMEM)
ANY = pl.BlockSpec(memory_space=pl.ANY)
FAR = pl.BlockSpec(memory_space=pltpu.HBM)


def dot(left, right, left_dim, right_dim):
    return lax.dot_general(
        left, right, (((left_dim,), (right_dim,)), ((), ())), preferred_element_type=F32
    )


def shape(dims, kind):
    return jax.ShapeDtypeStruct(dims, kind)


class Plan:
    def __init__(self, mesh, rows_each):
        self.dp = mesh.shape["dp"]
        self.seq = mesh.shape["seq"]
        self.count = self.dp * self.seq
        self.fast = (
            self.seq == 4
            and self.dp % 2 == 0
            and BLOCKS * 8 == self.count
            and (2 * D // self.count) % 16 == 0
        )
        self.nz = self.dp // 2
        self.rows = D // self.count
        self.far = FF // self.count
        both = range(self.count)
        self.core = [(d, d ^ 1) for d in both]
        self.first = [(d, d ^ (2 if d % 2 == 0 else 4)) for d in both]
        self.second = [(d, d ^ (4 if d % 2 == 0 else 2)) for d in both]
        self.groups = [list(range(low, self.dp, 2)) for low in range(2)]

    def wide(self, rows, columns):
        if self.fast:
            return (2, self.nz, 4, 2 * rows // self.count, columns)
        return (2, BLOCKS, 1, rows // BLOCKS, columns)

    def parts(self):
        return 8 if self.fast else 1

    def grads(self, rows, columns):
        if self.fast:
            half = shape((4 * self.nz, rows // self.count, columns), BF)
            return [half, half]
        return [shape((rows, columns), BF)]

    def outs(self):
        return 2 if self.fast else 1

    def bands(self):
        return self.seq if self.fast else 1

    def band_shapes(self, length):
        return [shape((length // self.bands(), D), BF)] * self.bands()


def place():
    seq = lax.axis_index("seq")
    return seq & 1, seq >> 1, lax.axis_index("dp") & 1


def start_parts(plan, parts, whole, sems, pieces, blocks=None):
    blocks = slice(None) if blocks is None else pl.ds(blocks[0], len(blocks))
    if len(parts) == 1:
        for index, (first, size) in enumerate(pieces):
            columns = pl.ds(first, size)
            pltpu.make_async_copy(
                parts[0].at[:, blocks, :, :, columns], whole.at[..., columns], sems.at[index]
            ).start()
        return
    core, mine_x, mine_y = place()
    for index, (first, size) in enumerate(pieces):
        columns = pl.ds(first, size)
        for number, part in enumerate(parts):
            owner = core if number < 4 else 1 - core
            one, two = (number >> 1) & 1, number & 1
            off_x = jnp.where(owner == 0, one, two)
            off_y = jnp.where(owner == 0, two, one)
            spot = (mine_y ^ off_y) * 2 + (mine_x ^ off_x)
            pltpu.make_async_copy(
                part.at[blocks, :, columns], whole.at[owner, :, spot, :, columns], sems.at[index]
            ).start()


def wait_part(whole, sems, index, piece):
    columns = pl.ds(*piece)
    view = whole.at[..., columns]
    pltpu.make_async_copy(view, view, sems.at[index]).wait()


def band(plan, number, length):
    if plan.bands() == 1:
        return pl.ds(0, length)
    size = length // plan.bands()
    return pl.ds(pl.multiple_of((lax.axis_index("seq") ^ number) * size, size), size)


def load_bands(plan, refs, whole, sems):
    copies = []
    for number, ref in enumerate(refs):
        source = ref.at[lax.axis_index("seq")] if number == 0 and plan.bands() > 1 else ref
        target = whole.at[band(plan, number, whole.shape[0]), :]
        copies.append(pltpu.make_async_copy(source, target, sems.at[number]))
    for copy in copies:
        copy.start()
    return copies


def flat(value):
    return value.reshape(-1, value.shape[-1])


def store_grad(plan, tile, outs, rows, first_row, columns):
    if not plan.fast:
        outs[0][pl.ds(first_row, tile.shape[0]), columns] = tile.astype(BF)
        return
    keep, send = outs
    core, mine_x, mine_y = place()
    step = rows // plan.count

    def spot(pair, owner):
        off_x = (pair & 1) ^ mine_x
        off_y = ((pair >> 1) & 1) ^ mine_y
        one = jnp.where(owner == 0, off_x, off_y)
        return (one * 2 + (off_x + off_y - one)) * plan.nz + (pair >> 2)

    for local in range(tile.shape[0] // (2 * step)):
        pair = first_row // (2 * step) + local
        low = tile[2 * step * local : 2 * step * local + step]
        high = tile[2 * step * local + step : 2 * step * (local + 1)]
        keep[spot(pair, core), :, columns] = jnp.where(core == 0, low, high).astype(BF)
        send[spot(pair, 1 - core), :, columns] = jnp.where(core == 0, high, low).astype(BF)


class Io:
    def __init__(self, ins, outs, held_in, held_out, in_sems, out_sems):
        self.loads = {}
        for number, (index, ref, cut) in enumerate(ins):
            source = ref if cut is None else ref.at[:, pl.ds(*cut)]
            self.loads[index] = pltpu.make_async_copy(source, held_in[number], in_sems.at[number])
            self.loads[index].start()
        self.outs = {
            index: (held_out[number], ref, out_sems.at[number]) for number, (index, ref) in enumerate(outs)
        }
        self.shipped = []

    def need(self, *indices):
        for index in indices:
            self.loads.pop(index).wait()

    def ship(self, index, columns=None):
        held, ref, sem = self.outs[index]
        if columns is None:
            pltpu.make_async_copy(held, ref, sem).start()
        else:
            pltpu.make_async_copy(held.at[..., columns], ref.at[..., columns], sem).start()
        if index not in self.shipped:
            self.shipped.append(index)

    def finish(self):
        self.need(*list(self.loads))
        for index in self.outs:
            if index not in self.shipped:
                self.ship(index)
        for held, ref, sem in self.outs.values():
            pltpu.make_async_copy(held, ref, sem).wait()


def call(name, body, ins, outs, scratch, limit, flops, aliases=None):
    staged_in = [i for i, item in enumerate(ins) if item[1] == "far"]
    staged_out = [i for i, item in enumerate(outs) if item[1] == "far"]
    cuts = {i: (ins[i][2] if len(ins[i]) > 2 else None) for i in staged_in}

    def held_shape(i):
        array = ins[i][0]
        dims = array.shape if cuts[i] is None else (array.shape[0], cuts[i][1])
        return pltpu.VMEM(dims, array.dtype)

    specs = {"near": VM, "far": FAR, "raw": FAR, "any": ANY}
    n_in, n_out, n_scratch = len(ins), len(outs), len(scratch)

    def kernel(*refs):
        in_refs, refs = list(refs[:n_in]), refs[n_in:]
        out_refs, refs = list(refs[:n_out]), refs[n_out:]
        own, refs = refs[:n_scratch], refs[n_scratch:]
        held_in, refs = refs[: len(staged_in)], refs[len(staged_in) :]
        held_out, refs = refs[: len(staged_out)], refs[len(staged_out) :]
        in_sems, out_sems = refs
        io = Io(
            [(i, in_refs[i], cuts[i]) for i in staged_in],
            [(i, out_refs[i]) for i in staged_out],
            held_in, held_out, in_sems, out_sems,
        )
        for number, i in enumerate(staged_in):
            in_refs[i] = held_in[number]
        for number, i in enumerate(staged_out):
            out_refs[i] = held_out[number]
        body(io, in_refs, out_refs, *own)
        io.finish()

    args = [
        pltpu.with_memory_space_constraint(item[0], pltpu.HBM) if item[1] in ("far", "raw") else item[0]
        for item in ins
    ]
    moved = sum(item[0].size * item[0].dtype.itemsize for item in (*ins, *outs))
    return pl.pallas_call(
        kernel,
        out_shape=[pltpu.HBM(o.shape, o.dtype) if kind in ("far", "raw") else o for o, kind in outs],
        in_specs=[specs[item[1]] for item in ins],
        out_specs=[specs[kind] for _, kind in outs],
        scratch_shapes=[
            *scratch,
            *[held_shape(i) for i in staged_in],
            *[pltpu.VMEM(outs[i][0].shape, outs[i][0].dtype) for i in staged_out],
            pltpu.SemaphoreType.DMA((max(1, len(staged_in)),)),
            pltpu.SemaphoreType.DMA((max(1, len(staged_out)),)),
        ],
        input_output_aliases=aliases or {},
        compiler_params=pltpu.CompilerParams(vmem_limit_bytes=limit * MIB),
        cost_estimate=pl.CostEstimate(flops=flops, bytes_accessed=moved, transcendentals=0),
        name=name,
    )(*args)


def far(*arrays):
    return [(array, "far") for array in arrays]


def norm_of(values):
    center = values - jnp.mean(values, axis=-1, keepdims=True)
    inverse = lax.rsqrt(jnp.mean(center * center, axis=-1, keepdims=True) + 1e-05)
    return center * inverse, inverse


def norm_back(upstream, normed, inverse, gain):
    scaled = upstream * gain
    return inverse * (
        scaled
        - jnp.mean(scaled, axis=-1, keepdims=True)
        - normed * jnp.mean(scaled * normed, axis=-1, keepdims=True)
    )


def fill_bias(bias, seg, pad):
    length = bias.shape[0]
    code = (2 * seg + pad).astype(F32)
    wanted = (2 * seg + 1).astype(F32)
    coded = jnp.broadcast_to(code, (length, length)).T
    rows = lax.broadcasted_iota(jnp.int32, (length, length), 0)
    cols = lax.broadcasted_iota(jnp.int32, (length, length), 1)
    bias[...] = jnp.where((coded == wanted) | (rows == cols), 0.0, -1e30)


def halves_of(values):
    lane = lax.broadcasted_iota(jnp.int32, values.shape, 1)
    zero = jnp.zeros_like(values)
    return jnp.where(lane < HD, values, zero), jnp.where(lane < HD, zero, values)


def prepare(plan, matrices, norm_params):
    side = jnp.pad(norm_params.T, ((0, 0), (0, 128 - norm_params.shape[0])))
    matrices = [*matrices[0:3], jnp.concatenate([side, side], axis=1), *matrices[3:]]
    groups = [matrices[0:4], matrices[4:6], matrices[6:7]]

    def body(io, ins, outs):
        core = lax.axis_index("seq") & 1
        first = 0
        for number, group in enumerate(groups):
            at = 0
            for index in range(first, first + len(group)):
                io.need(index)
                size = ins[index].shape[1] // 2
                left, right = ins[index][:, :size], ins[index][:, size:]
                mine = jnp.where(core == 0, left, right).astype(BF)
                other = jnp.where(core == 0, right, left).astype(BF)
                outs[2 * number][:, at : at + size] = mine
                outs[2 * number + 1][:, at : at + size] = other
                at += size
            first += len(group)

    outs = []
    for group in groups:
        outs += [(shape((group[0].shape[0], sum(w.shape[1] for w in group) // 2), BF), "near")] * 2
    flat_outs = call("prepare", body, far(*matrices), outs, [], 8, 10**6)
    return [flat_outs[0:2], flat_outs[2:4], flat_outs[4:6]]


def row_blocks(length):
    for i in range(length // 128):
        yield slice(i * 128, (i + 1) * 128)


def project(plan, tokens, parts):
    length = tokens[0].size // D if len(tokens) == 1 else tokens[1].shape[0] * len(tokens)
    width = 3 * HALF + 128
    pieces = [(0, width)]

    def body(io, ins, outs, whole, rows_in, sems, put_sems):
        h_ref, q_ref, k_ref, v_ref, n_ref, w_ref, x_ref = outs
        start_parts(plan, ins[len(tokens) :], whole, sems, pieces)
        loads = load_bands(plan, ins[: len(tokens)], rows_in, sems.at[pl.ds(1, len(tokens))])
        wait_part(whole, sems, 0, pieces[0])
        puts = [pltpu.make_async_copy(whole, w_ref, put_sems.at[0])]
        puts[0].start()
        norms = flat(whole[0, :, :, :, 3 * HALF :]).astype(F32).T[0:8]
        n_ref[...] = norms
        for load in loads:
            load.wait()
        puts.append(pltpu.make_async_copy(rows_in, x_ref, put_sems.at[1]))
        puts[1].start()
        for rows in row_blocks(length):
            normed, _ = norm_of(rows_in[rows, :].astype(F32))
            h_ref[rows, :] = (normed * norms[0:1, :] + norms[1:2, :]).astype(BF)
        io.ship(0)
        for m, (out, scale) in enumerate(((q_ref, 0.125), (k_ref, 1.0), (v_ref, 1.0))):
            for h in range(2):
                weight = flat(whole[h, :, :, :, m * HALF : (m + 1) * HALF])
                out[:, h * HALF : (h + 1) * HALF] = (dot(h_ref[...], weight, 1, 0) * scale).astype(BF)
            io.ship(1 + m)
        for put in puts:
            put.wait()

    act = shape((length, D), BF)
    wide = plan.wide(D, width)
    return call(
        "project", body, [*[(t, "any") for t in tokens], *[(p, "any") for p in parts]],
        [*[(act, "far")] * 4, (shape((8, D), F32), "near"), (shape(wide, BF), "raw"), (act, "raw")],
        [
            pltpu.VMEM(wide, BF), pltpu.VMEM((length, D), BF),
            pltpu.SemaphoreType.DMA((1 + len(tokens),)), pltpu.SemaphoreType.DMA((2,)),
        ],
        20, 2 * length * 3 * D * D,
    )


def mix(plan, query, key, value, seg, pad):
    length = query.shape[0]

    def body(io, ins, outs, bias):
        q_ref, k_ref, v_ref, seg_ref, pad_ref = ins
        at_ref, a_ref, l_ref = outs
        fill_bias(bias, seg_ref[...], pad_ref[...])
        io.need(0, 1, 2)

        @pl.loop(0, PAIRS)
        def _(p):
            cols = pl.ds(pl.multiple_of(p * 128, 128), 128)
            keys = k_ref[:, cols]
            turned = v_ref[:, cols].T
            for half, query in enumerate(halves_of(q_ref[:, cols])):
                scores = dot(keys, query, 1, 1) + bias[...]
                top = jnp.max(scores, axis=0, keepdims=True)
                lifted = jnp.exp(scores - top)
                total = jnp.sum(lifted, axis=0, keepdims=True)
                soft = (lifted * (1.0 / total)).astype(BF)
                mixed = dot(turned[half * HD : (half + 1) * HD], soft, 1, 0)
                at_ref[pl.ds(pl.multiple_of(p * 128 + half * HD, HD), HD), :] = mixed.astype(BF)
                l_ref[pl.ds(2 * p + half, 1), :] = top + jnp.log(total)
            a_ref[:, cols] = at_ref[pl.ds(pl.multiple_of(p * 128, 128), 128), :].T

    return call(
        "mix", body, [*far(query, key, value), (seg, "near"), (pad, "near")],
        [(shape((D, length), BF), "far"), (shape((length, D), BF), "far"), (shape((H, length), F32), "far")],
        [pltpu.VMEM((length, length), F32)],
        14, 2 * length * (2 * length * D),
    )


def widen(plan, tokens, mixed, cot, norms, parts):
    length = tokens.shape[0]
    pieces = [(0, HALF), (HALF, D), (HALF + D, D)]

    def body(io, ins, outs, whole, g_in, sems, put_sems):
        x_ref, a_ref, n_ref, *rest = ins
        m_ref, h_ref, z_ref, s_ref, *grads = outs[:-2]
        w_ref, g_out = outs[-2:]
        start_parts(plan, rest[len(cot) :], whole, sems, pieces)
        loads = load_bands(plan, rest[: len(cot)], g_in, sems.at[pl.ds(3, len(cot))])
        io.need(0, 1)
        wait_part(whole, sems, 0, pieces[0])
        for h in range(2):
            cols = slice(h * HALF, (h + 1) * HALF)
            weight = flat(whole[h, :, :, :, 0:HALF])
            m_ref[:, cols] = x_ref[:, cols].astype(F32) + dot(a_ref[...], weight, 1, 0)
        io.ship(0)
        for rows in row_blocks(length):
            normed, _ = norm_of(m_ref[rows, :])
            h_ref[rows, :] = (normed * n_ref[2:3, :] + n_ref[3:4, :]).astype(BF)
        io.ship(1)
        wait_part(whole, sems, 1, pieces[1])
        wait_part(whole, sems, 2, pieces[2])
        puts = [pltpu.make_async_copy(whole, w_ref, put_sems.at[0]), pltpu.make_async_copy(g_in, g_out, put_sems.at[1])]
        puts[0].start()
        for load in loads:
            load.wait()
        puts[1].start()
        for part in range(2):
            for h in range(2):
                block = h * 2 + part
                cols = slice(block * D, (block + 1) * D)
                weight = flat(whole[h, :, :, :, HALF + part * D : HALF + (part + 1) * D])
                up = dot(h_ref[...], weight, 1, 0)
                bell = 0.5 + 0.5 * lax.erf(up * 0.7071067811865476)
                z_ref[:, cols] = (up * bell).astype(BF)
                s_ref[:, cols] = (bell + up * (jnp.exp(-0.5 * up * up) * 0.3989422804014327)).astype(BF)
                io.ship(2, pl.ds(block * D, D))
                io.ship(3, pl.ds(block * D, D))
                tile = dot(z_ref[:, cols], g_in[...], 0, 0)
                store_grad(plan, tile, grads, FF, block * D, slice(None))
        for index in range(len(grads)):
            io.ship(4 + index)
        for put in puts:
            put.wait()

    act = shape((length, D), BF)
    wide = plan.wide(D, 5 * HALF)
    outs = [shape((length, D), F32), act, shape((length, FF), BF), shape((length, FF), BF), *plan.grads(FF, D)]
    return call(
        "widen", body,
        [*far(tokens, mixed), (norms, "near"), *[(c, "any") for c in cot], *[(p, "any") for p in parts]],
        [*[(o, "far") for o in outs], (shape(wide, BF), "raw"), (act, "raw")],
        [
            pltpu.VMEM(wide, BF), pltpu.VMEM((length, D), BF),
            pltpu.SemaphoreType.DMA((3 + len(cot),)), pltpu.SemaphoreType.DMA((2,)),
        ],
        40, 2 * length * (D * D + 2 * D * FF),
    )


def narrow(plan, blocks, mid, below, grads, low, hidden, slope, cot, whole_ou, parts_down):
    length = mid.shape[0]
    up_pieces = [(HALF + (block % 2) * D, D) for block in blocks]
    side = blocks[0] // 2
    start, final = blocks[0] == 0, blocks[-1] == BLOCKS - 1
    cut = (blocks[0] * D, len(blocks) * D)
    n_out = plan.outs()

    def body(io, ins, outs, *scratch):
        m_ref, h_ref, z_ref, s_ref, g_ref, up_ref, *rest = ins
        downs = rest[: len(parts_down)]
        b_ref, *grad_refs = outs[: 1 + n_out]
        o_refs = outs[1 + n_out :]
        held, (acc, whole_up, whole_down, sems, put_sems) = scratch[:-5], scratch[-5:]
        copies = []
        start_parts(plan, downs, whole_down, sems.at[pl.ds(0, 1)], [(0, HALF)], blocks)
        ups = []
        for number, (first, size) in enumerate(up_pieces):
            up = pltpu.make_async_copy(
                up_ref.at[side, :, :, :, pl.ds(first, size)], whole_up.at[number], sems.at[1 + number]
            )
            up.start()
            ups.append(up)
        wait_part(whole_down, sems, 0, (0, HALF))
        io.need(4, 3, 1, 2)
        for number, block in enumerate(blocks):
            local = slice(number * D, (number + 1) * D)
            back = dot(g_ref[:, 0:HALF], flat(whole_down[0, number]), 1, 1)
            back += dot(g_ref[:, HALF:D], flat(whole_down[1, number]), 1, 1)
            du = (back * s_ref[:, local]).astype(BF)
            tile = dot(h_ref[...], du, 0, 0)
            store_grad(plan, tile, held, D, 0, local)
            for i in range(n_out):
                copy = pltpu.make_async_copy(
                    held[i].at[..., pl.ds(number * D, D)], grad_refs[i].at[..., pl.ds(block * D, D)], put_sems.at[number, i]
                )
                copy.start()
                copies.append(copy)
            ups[number].wait()
            lower = dot(du, flat(whole_up[number]), 1, 1)
            if number == 0:
                if start:
                    b_ref[...] = lower
                else:
                    io.need(6 + len(parts_down))
                    b_ref[...] = rest[len(parts_down)][...] + lower
                io.need(0)
            else:
                b_ref[...] += lower
            z = z_ref[:, local]
            for h in range(2):
                half = slice(h * HALF, (h + 1) * HALF)
                gain = dot(z, flat(whole_down[h, number]), 1, 0)
                acc[:, half] = gain + (m_ref[:, half] if number == 0 else acc[:, half])
        if final:
            for number, o_ref in enumerate(o_refs):
                o_ref[...] = acc[band(plan, number, length), :].astype(BF)
        else:
            o_refs[0][...] = acc[...]
        for copy in copies:
            copy.wait()

    wide = plan.wide(D, D)
    deep = plan.wide(FF, HALF)
    ins = [
        *far(mid, low), (hidden, "far", cut), (slope, "far", cut), *far(cot), (whole_ou, "raw"),
        *[(p, "any") for p in parts_down],
    ]
    aliases = {}
    if not start:
        ins += far(below)
        aliases = {len(ins) + i: 1 + i for i in range(n_out)}
        ins += [(g, "raw") for g in grads]
    return call(
        "narrow" + str(blocks[0]), body, ins,
        [
            (shape((length, D), F32), "far"), *[(g, "raw") for g in plan.grads(D, FF + D)],
            *[(o, "far") for o in (plan.band_shapes(length) if final else [shape((length, D), F32)])],
        ],
        [pltpu.VMEM(o.shape, BF) for o in plan.grads(D, len(blocks) * D)]
        + [
            pltpu.VMEM((length, D), F32),
            pltpu.VMEM((len(blocks), *wide[1:]), BF),
            pltpu.VMEM((2, len(blocks), *deep[2:]), BF),
            pltpu.SemaphoreType.DMA((1 + len(blocks),)),
            pltpu.SemaphoreType.DMA((len(blocks), n_out)),
        ],
        40, 2 * length * len(blocks) * D * D * 4, aliases,
    )


def turn(plan, mid, back, cot, norms, mixed_t, whole_ou, grads):
    length = mid.shape[0]
    n_out = plan.outs()

    def body(io, ins, outs, *scratch):
        m_ref, b_ref, g_ref, n_ref, at_ref, w_ref, *_ = ins
        x_ref, d_ref, s_ref, *grad_refs = outs
        held, (low, whole, sems, put_sems) = scratch[:-4], scratch[-4:]
        load = pltpu.make_async_copy(w_ref.at[..., pl.ds(0, HALF)], whole, sems.at[0])
        load.start()
        s_ref[...] = jnp.zeros_like(s_ref)
        io.need(0, 1, 2)
        for rows in row_blocks(length):
            normed, inverse = norm_of(m_ref[rows, :])
            upstream = b_ref[rows, :]
            total = g_ref[rows, :].astype(F32) + norm_back(upstream, normed, inverse, n_ref[2:3, :])
            x_ref[rows, :] = total
            low[rows, :] = total.astype(BF)
            s_ref[0:1, :] += jnp.sum(upstream * normed, axis=0, keepdims=True)
            s_ref[1:2, :] += jnp.sum(upstream, axis=0, keepdims=True)
        io.ship(0)
        io.need(4)
        store_grad(plan, dot(at_ref[...], low[...], 1, 0), held, D, 0, slice(None))
        copies = [
            pltpu.make_async_copy(held[i], grad_refs[i].at[..., pl.ds(FF, D)], put_sems.at[i]) for i in range(n_out)
        ]
        for copy in copies:
            copy.start()
        load.wait()
        back_a = dot(low[:, 0:HALF], flat(whole[0]), 1, 1)
        back_a += dot(low[:, HALF:D], flat(whole[1]), 1, 1)
        d_ref[...] = back_a.astype(BF)
        io.ship(1)
        for copy in copies:
            copy.wait()

    ins = [*far(mid, back, cot), (norms, "near"), *far(mixed_t), (whole_ou, "raw"), *[(g, "raw") for g in grads]]
    return call(
        "turn", body, ins,
        [
            (shape((length, D), F32), "far"), (shape((length, D), BF), "far"), (shape((2, D), F32), "near"),
            *[(g, "raw") for g in plan.grads(D, FF + D)],
        ],
        [pltpu.VMEM(o.shape, BF) for o in plan.grads(D, D)]
        + [
            pltpu.VMEM((length, D), BF), pltpu.VMEM(plan.wide(D, HALF), BF),
            pltpu.SemaphoreType.DMA((1,)), pltpu.SemaphoreType.DMA((n_out,)),
        ],
        24, 2 * length * 2 * D * D, {6 + i: 3 + i for i in range(n_out)},
    )


def attend_back(plan, side, low, query, key, value, lse, cot, seg, pad):
    length = low.shape[0]
    cut = (side * HALF, HALF)

    def body(io, ins, outs, bias):
        h_ref, q_ref, k_ref, v_ref, c_ref, l_ref, seg_ref, pad_ref = ins
        d_ref, *grads = outs
        fill_bias(bias, seg_ref[...], pad_ref[...])
        io.need(1, 2, 3, 4, 5)

        @pl.loop(0, PAIRS // 2)
        def _(local):
            p = local + side * (PAIRS // 2)
            first = pl.multiple_of(local * 128, 128)
            cols = pl.ds(first, 128)
            keys, values = k_ref[:, cols], v_ref[:, cols]
            turned = keys.T
            queries, cots = halves_of(q_ref[:, cols]), halves_of(c_ref[:, cols])
            dv = dk = None
            dqs = []
            for half in range(2):
                scores = dot(keys, queries[half], 1, 1) + bias[...]
                soft = jnp.exp(scores - l_ref[pl.ds(2 * p + half, 1), :])
                gain = dot(soft.astype(BF), cots[half], 1, 0)
                dv = gain if dv is None else dv + gain
                dp = dot(values, cots[half], 1, 1)
                share = jnp.sum(soft * dp, axis=0, keepdims=True)
                ds = (soft * (dp - share)).astype(BF)
                gain = dot(ds, queries[half], 1, 0)
                dk = gain if dk is None else dk + gain
                dqs.append(dot(turned[half * HD : (half + 1) * HD], ds, 1, 0) * 0.125)
            d_ref[:, cols] = jnp.concatenate(dqs, axis=0).T.astype(BF)
            d_ref[:, pl.ds(first + HALF, 128)] = dk.astype(BF)
            d_ref[:, pl.ds(first + 2 * HALF, 128)] = dv.astype(BF)

        io.ship(0)
        io.need(0)
        for m in range(3):
            cols = slice(m * HALF, (m + 1) * HALF)
            store_grad(plan, dot(h_ref[...], d_ref[:, cols], 0, 0), grads, D, 0, cols)
            for index in range(len(grads)):
                io.ship(1 + index, pl.ds(m * HALF, HALF))

    return call(
        "attend_back" + str(side), body,
        [
            *far(low), *[(a, "far", cut) for a in (query, key, value, cot)], *far(lse),
            (seg, "near"), (pad, "near"),
        ],
        [(shape((length, 3 * HALF), BF), "far"), *[(g, "far") for g in plan.grads(D, 3 * HALF)]],
        [pltpu.VMEM((length, length), F32)],
        20, length * (3 * D * D + 5 * length * D),
    )


def finish_tokens(plan, tokens, spreads, mid_cot, norms, whole_qkv):
    length = tokens.shape[0]
    pieces = [(0, 3 * HALF)]

    def body(io, ins, outs, back, whole, sems):
        x_ref, d0_ref, d1_ref, c_ref, n_ref, w_ref = ins
        *o_refs, s_ref = outs
        start_parts(plan, [w_ref], whole, sems, pieces)
        s_ref[...] = jnp.zeros_like(s_ref)
        wait_part(whole, sems, 0, pieces[0])
        total = None
        io.need(1, 2)
        for m in range(3):
            for h in range(2):
                cols = slice(m * HALF, (m + 1) * HALF)
                gain = dot((d0_ref, d1_ref)[h][:, cols], flat(whole[h, :, :, :, cols]), 1, 1)
                total = gain if total is None else total + gain
        back[...] = total
        io.need(0, 3)
        for rows in row_blocks(length):
            normed, inverse = norm_of(x_ref[rows, :].astype(F32))
            upstream = back[rows, :]
            c_ref[rows, :] += norm_back(upstream, normed, inverse, n_ref[0:1, :])
            s_ref[0:1, :] += jnp.sum(upstream * normed, axis=0, keepdims=True)
            s_ref[1:2, :] += jnp.sum(upstream, axis=0, keepdims=True)
        for number, o_ref in enumerate(o_refs):
            o_ref[...] = c_ref[band(plan, number, length), :].astype(BF)

    return call(
        "finish_tokens", body, [*far(tokens, *spreads, mid_cot), (norms, "near"), (whole_qkv, "raw")],
        [*[(o, "far") for o in plan.band_shapes(length)], (shape((2, D), F32), "near")],
        [pltpu.VMEM((length, D), F32), pltpu.VMEM(plan.wide(D, 3 * HALF), BF), pltpu.SemaphoreType.DMA((1,))],
        20, 2 * length * 3 * D * D,
    )


def update(plan, grads, squares, masters, firsts, seconds, passed):
    rates = [D**-0.5] * 3 + [4.0 * D**-0.5, D**-0.5, FF**-0.5, 0.2]
    decays = [0.01] * 6 + [0.0]
    count = len(masters)
    given = len(grads)

    def body(io, ins, outs, sems):
        grad_refs, sq_ref = ins[:given], ins[given]
        first = given + 1
        norm = jnp.sqrt(jnp.sum(sq_ref[...], axis=0, keepdims=True))
        outs[0][...] = norm
        factor = jnp.minimum(1.0, clip_limit / (norm + 1e-06))[:, 0:1]
        for i in reversed(range(count)):
            w_ref, m_ref, s_ref = (ins[first + k * count + i] for k in range(3))
            io.need(*(first + k * count + i for k in range(3)))
            if i < 3:
                cols = [
                    (slice(h * HALF, (h + 1) * HALF), grad_refs[0][:, (3 * h + i) * HALF : (3 * h + i + 1) * HALF])
                    for h in range(2)
                ]
            elif i == 3:
                cols = [(slice(None), grad_refs[1][:, FF:])]
            elif i == 4:
                cols = [(slice(None), grad_refs[1][:, :FF])]
            else:
                cols = [(slice(None), grad_refs[i - 3][...])]
            for where, grad in cols:
                clipped = factor * grad
                one = 0.5 * m_ref[:, where] + 0.5 * clipped
                two = 0.55 * s_ref[:, where] + 0.45 * clipped * clipped
                root = jnp.sqrt(two * (1.0 / (1.0 - 0.55**STEP))) + 1e-08
                weight = w_ref[:, where]
                step = (one * (1.0 / (1.0 - 0.5**STEP))) / root + decays[i] * weight
                outs[1 + i][:, where] = weight - rates[i] * step
                outs[1 + count + i][:, where] = one
                outs[1 + 2 * count + i][:, where] = two
            for k in range(3):
                io.ship(1 + k * count + i)
        last = first + 3 * count
        copies = []
        for number in range(len(passed)):
            which, place_in = number // plan.bands(), number % plan.bands()
            io.need(last + number)
            target = outs[1 + 3 * count + which]
            if plan.bands() > 1:
                target = target.at[lax.axis_index("seq") ^ place_in]
            copies.append(pltpu.make_async_copy(ins[last + number], target, sems.at[number]))
            copies[-1].start()
        for copy in copies:
            copy.wait()

    like = [(shape(w.shape, F32), "far") for w in masters] * 3
    pieces = [shape((plan.bands(), *p.shape), BF) if plan.bands() > 1 else p for p in passed[:: plan.bands()]]
    return call(
        "update", body, [*[(g, "near") for g in grads], (squares, "near"), *far(*masters, *firsts, *seconds, *passed)],
        [(shape((1, squares.shape[1]), F32), "near"), *like, *[(o, "raw") for o in pieces]],
        [pltpu.SemaphoreType.DMA((len(passed),))], 20, 10**7,
    )


def after(values, *others):
    return lax.optimization_barrier((values, others))[0]


def send(plan, values, perm):
    return lax.ppermute(values, AXES, perm)


def blocks_of(plan, mine, other):
    core = lax.axis_index("seq") & 1
    got = send(plan, other, plan.core)
    block = jnp.where(core == 0, jnp.concatenate([mine, got]), jnp.concatenate([got, mine]))
    return jnp.broadcast_to(block[None], (plan.nz, *block.shape))


def along_z(plan, values):
    return lax.all_to_all(values, "dp", 0, 0, axis_index_groups=plan.groups, tiled=True)


def gather_whole(matrices):
    split = [w.reshape(w.shape[0], 2, -1) for w in matrices]
    halves = jnp.concatenate(split, axis=2).transpose(1, 0, 2).astype(BF)
    full = lax.all_gather(halves, AXES, axis=1, tiled=True)
    return [full.reshape(2, BLOCKS, 1, -1, full.shape[-1])]


def add(one, two):
    return one.astype(F32) + two.astype(F32)


def fold(keep, got):
    size = keep.shape[0] // 2
    return add(keep[size:], got[size:]).astype(BF), add(keep[:size], got[:size]).astype(BF)


def total(blocks):
    return jnp.sum(blocks.astype(F32), axis=0)


def everywhere(plan, values):
    spread = jnp.broadcast_to(values[None], (plan.count, *values.shape))
    return lax.all_to_all(spread, AXES, 0, 0, tiled=True)


def norm_slices(plan, sums_one, sums_two):
    sums = jnp.concatenate([sums_one, sums_two], axis=0)
    slices = sums.reshape(4, plan.count, -1).transpose(1, 0, 2)
    return jnp.sum(lax.all_to_all(slices, AXES, 0, 0, tiled=True), axis=0)


def finish(plan, grads, masters, firsts, seconds, *passed):
    local = sum(jnp.sum(g * g) for g in grads)
    squares = everywhere(plan, jnp.broadcast_to(local, (1, 128))).reshape(plan.count, 128)
    norm, *updated, output, input_grad = update(plan, grads, squares, masters, firsts, seconds, passed)
    return (output, input_grad, norm[0, 0], *updated)


def on_device(plan, *args):
    tokens_in, segment_ids, pad_mask, out_grad = args[:4]
    masters, firsts, seconds = args[4:11], args[11:18], args[18:25]
    each, piece, _ = tokens_in.shape
    length = each // plan.seq * plan.seq * piece

    plan.fast = plan.fast and each == plan.seq

    def swap(values, number):
        return lax.ppermute(values, "seq", [(i, i ^ number) for i in range(plan.seq)])

    def to_rows(values):
        if not plan.fast:
            return [lax.all_to_all(values, "seq", 0, 0, tiled=True).reshape(length, D)]
        others = [lax.dynamic_index_in_dim(values, row ^ n, 0, keepdims=False) for n in range(1, plan.seq)]
        return [values, *[swap(other, 1 + n) for n, other in enumerate(others)]]

    def to_pieces(bands):
        if not plan.fast:
            return [lax.all_to_all(bands[0].reshape(each, piece, D), "seq", 0, 0, tiled=True)]
        return [bands[0], *[swap(other, 1 + n) for n, other in enumerate(bands[1:])]]

    row = lax.axis_index("seq")
    seg = lax.dynamic_slice_in_dim(segment_ids, row, 1, 0)
    pad = lax.dynamic_slice_in_dim(pad_mask, row, 1, 0)

    if not plan.fast:
        side = jnp.pad(masters[6].T, ((0, 0), (0, 124)))
        side = jnp.concatenate([side, side], axis=1)
        one, two, three = (gather_whole(m) for m in ([*masters[0:3], side], masters[3:5], masters[5:6]))
        low_one, query, key, value, norms, whole_qkv, tokens = project(plan, to_rows(tokens_in), one)
        mixed_t, mixed, lse = mix(plan, query, key, value, seg, pad)
        mid, low_two, hidden, slope, *g_down, whole_ou, cot = widen(plan, tokens, mixed, to_rows(out_grad), norms, two)
        back, *g_up, part = narrow(plan, (0, 1), mid, None, None, low_two, hidden, slope, cot, whole_ou, three)
        back, *g_up, result = narrow(plan, (2, 3), part, back, g_up, low_two, hidden, slope, cot, whole_ou, three)
        mid_cot, mixed_cot, sums_two, *g_up = turn(plan, mid, back, cot, norms, mixed_t, whole_ou, g_up)
        halves = [
            attend_back(plan, side, low_one, query, key, value, lse, mixed_cot, seg, pad) for side in range(2)
        ]
        stream, sums_one = finish_tokens(plan, tokens, [h[0] for h in halves], mid_cot, norms, whole_qkv)
        grads = [
            lax.psum_scatter(g.astype(F32), AXES, scatter_dimension=0, tiled=True)
            for g in (halves[0][1], halves[1][1], *g_up, *g_down)
        ]
        grads = [jnp.concatenate(grads[:2], axis=1), *grads[2:]]
        grads.append(norm_slices(plan, sums_one, sums_two))
        return finish(plan, grads, masters, firsts, seconds, *to_pieces([result]), *to_pieces([stream]))

    first, second, third = prepare(plan, masters[:6], masters[6])
    block_one = blocks_of(plan, *first)
    near_one = along_z(plan, block_one)
    tokens = to_rows(after(tokens_in, first))
    block_two = blocks_of(plan, *second)
    block_three = blocks_of(plan, *third)
    near_one = after(near_one, tokens, block_two, block_three)

    def spread(near):
        return send(plan, near, plan.second), send(plan, near, plan.first)

    def cross(near, beside, across, corner):
        parts = [near, beside, across, corner]
        return parts + [send(plan, part, plan.core) for part in parts]

    beside_one, across_one = spread(near_one)
    near_two = along_z(plan, after(block_two, near_one))
    one = cross(near_one, beside_one, across_one, send(plan, beside_one, plan.first))
    low_one, query, key, value, norms, whole_qkv, tokens = project(plan, tokens, one)
    near_two = after(near_two, query)
    near_three = along_z(plan, after(block_three, near_two))
    beside_two, across_two = spread(near_two)
    query = after(query, near_two)
    cot = to_rows(after(out_grad, query))
    mixed_t, mixed, lse = mix(plan, query, key, value, seg, pad)
    beside_two, across_two = after((beside_two, across_two), lse)
    corner_two = send(plan, beside_two, plan.first)
    near_three = after(near_three, lse)
    beside_three, across_three = spread(near_three)
    two = cross(near_two, beside_two, across_two, corner_two)
    mid, low_two, hidden, slope, *g_down, whole_ou, cot = widen(plan, tokens, after(mixed, near_three), cot, norms, two)
    beside_three, across_three = after((beside_three, across_three), slope)
    corner_three = send(plan, beside_three, plan.first)
    three = cross(near_three, beside_three, across_three, corner_three)

    keep_d, go_d = g_down
    go_d, keep_d = fold(keep_d, send(plan, go_d, plan.core))
    got_d = send(plan, go_d, plan.first)
    back, *g_up, part = narrow(
        plan, (0, 1), after(mid, go_d), None, None, low_two, hidden, slope, cot, whole_ou, three
    )
    got_d = after(got_d, back)
    go_d, keep_d = fold(keep_d, got_d)
    got_d = send(plan, go_d, plan.second)
    back, *g_up_result = narrow(
        plan, (2, 3), after(part, go_d), back, g_up, low_two, hidden, slope, cot, whole_ou, three
    )
    g_up, result = g_up_result[:2], g_up_result[2:]
    output = to_pieces(result)
    block_d = add(keep_d, after(got_d, back)).astype(BF)
    blocks_d = along_z(plan, block_d)
    mid_cot, mixed_cot, sums_two, keep_u, go_u = turn(
        plan, mid, after(back, block_d), cot, norms, mixed_t, whole_ou, g_up
    )
    go_u, keep_u = fold(keep_u, send(plan, go_u, plan.core))
    got_u = send(plan, go_u, plan.first)
    mixed_cot = after(mixed_cot, go_u)
    spread_a, keep_a, go_a = attend_back(plan, 0, low_one, query, key, value, lse, mixed_cot, seg, pad)
    got_u, blocks_d, output = after((got_u, blocks_d, output), spread_a)
    grad_d = total(blocks_d)
    go_u, keep_u = fold(keep_u, got_u)
    got_u = send(plan, go_u, plan.second)
    go_a, keep_a = fold(keep_a, send(plan, go_a, plan.core))
    got_a = send(plan, go_a, plan.first)
    mixed_cot = after(mixed_cot, go_u, go_a)
    spread_b, keep_b, go_b = attend_back(plan, 1, low_one, query, key, value, lse, mixed_cot, seg, pad)
    go_b, keep_b = fold(keep_b, send(plan, go_b, plan.core))
    got_b = send(plan, go_b, plan.first)
    block_u = add(keep_u, after(got_u, spread_b)).astype(BF)
    blocks_u = along_z(plan, block_u)
    go_a, keep_a = fold(keep_a, after(got_a, spread_b))
    got_a = send(plan, go_a, plan.second)
    *stream, sums_one = finish_tokens(
        plan, tokens, [spread_a, spread_b], after(mid_cot, go_b, block_u, go_a), norms, whole_qkv
    )
    got_b, blocks_u = after((got_b, blocks_u), sums_one)
    input_grad = to_pieces(stream)
    go_b, keep_b = fold(keep_b, got_b)
    got_b = send(plan, go_b, plan.second)
    slices = norm_slices(plan, sums_one, sums_two)
    halves = [add(keep_a, after(got_a, sums_one)), add(keep_b, got_b)]
    blocks_ab = along_z(plan, after(jnp.concatenate(halves, axis=2).astype(BF), slices))
    grads = [total(blocks_ab), total(blocks_u), grad_d, slices]
    return finish(plan, grads, masters, firsts, seconds, *output, *input_grad)


def solution(mesh):
    plan = Plan(mesh, None)
    rows = P(AXES, None)
    weights = (*[rows] * 6, P(None, AXES))
    tokens = P("dp", "seq", None)
    return jax.shard_map(
        partial(on_device, plan),
        mesh=mesh,
        in_specs=(tokens, P("dp", None), P("dp", None), tokens, *weights * 3),
        out_specs=(tokens, tokens, P(), *weights * 3),
        check_vma=False,
    )
```

profile of v0, /device:TPU:0, one launch (start us, length us, event | category | flops | bytes accessed | tf_op | source)
XLA Modules:
  0.0 310.9 jit_solution(3503347911099549331)
XLA Ops:
  5.7 6.2 %all-to-all-start = ((bf16[4,48,1280]{2,1,0:T(8,128)(2,1)}), bf16[4,48,1280]{2,1,0:T(8,128)(2,1)S(1)}, u32[]{:S(2)}, u32[]{:S(2)}) async-start(bf16[4,48,1280]{2,1,0:T(8,128)(2,1)} %broadcast_in_dim.6), calls=%async_computation | async-start | bytes 983040 | tf_op jit(solution)/shard_map/all_to_all | solution.py:766
  14.5 5.1 %collective-permute-done.2.refs_3_ = bf16[128,768]{1,0:T(8,128)(2,1)S(1)} collective-permute-done((bf16[128,768]{1,0:T(8,128)(2,1)S(1)}, bf16[128,768]{1,0:T(8,128)(2,1)S(1)}, u32[]{:S(2)}, u32[]{:S(2)}) %collective-permute-start.2) | collective-permute-done | bytes 196640 | tf_op jit(solution)/shard_map/ppermute | solution.py:816
  19.5 4.4 %collective-permute-done.1.refs_2_ = bf16[128,768]{1,0:T(8,128)(2,1)S(1)} collective-permute-done((bf16[128,768]{1,0:T(8,128)(2,1)S(1)}, bf16[128,768]{1,0:T(8,128)(2,1)S(1)}, u32[]{:S(2)}, u32[]{:S(2)}) %collective-permute-start.1) | collective-permute-done | bytes 196640 | tf_op jit(solution)/shard_map/ppermute | solution.py:816
  24.0 2.1 all-to-all-done.refs_4_
  27.9 1.5 collective-permute-start.6
  30.9 11.0 %collective-permute-done.6.refs_5_ = bf16[4,48,1280]{2,1,0:T(8,128)(2,1)S(1)} collective-permute-done((bf16[4,48,1280]{2,1,0:T(8,128)(2,1)S(1)}, bf16[4,48,1280]{2,1,0:T(8,128)(2,1)S(1)}, u32[]{:S(2)}, u32[]{:S(2)}) %collective-permute-start.6) | collective-permute-done | bytes 491552 | tf_op jit(solution)/shard_map/ppermute | solution.py:755
  42.0 3.7 %all-to-all-start.1 = ((bf16[4,48,1920]{2,1,0:T(8,128)(2,1)}), bf16[4,48,1920]{2,1,0:T(8,128)(2,1)S(1)}, u32[]{:S(2)}, u32[]{:S(2)}) async-start(bf16[4,48,1920]{2,1,0:T(8,128)(2,1)} %broadcast_in_dim.7), calls=%async_computation.1 | async-start | bytes 1474560 | tf_op jit(solution)/shard_map/all_to_all | solution.py:766
  46.2 4.6 %collective-permute-done.8.refs_7_ = bf16[4,48,1280]{2,1,0:T(8,128)(2,1)} collective-permute-done((bf16[4,48,1280]{2,1,0:T(8,128)(2,1)S(1)}, bf16[4,48,1280]{2,1,0:T(8,128)(2,1)}, u32[]{:S(2)}, u32[]{:S(2)}) %collective-permute-start.8) | collective-permute-done | bytes 491552 | tf_op jit(solution)/shard_map/ppermute | solution.py:755
  50.9 2.1 collective-permute-done.12.refs_11_
  53.8 5.8 %project.1 = (bf16[512,768]{1,0:T(8,128)(2,1)}, bf16[512,768]{1,0:T(8,128)(2,1)}, bf16[512,768]{1,0:T(8,128)(2,1)}, bf16[512,768]{1,0:T(8,128)(2,1)}, f32[8,768]...) custom-call(bf16[4,128,768]{2,1,0:T(8,128)(2,1)S(1)} %copy-done, ...), custom_call_target="tpu_custom_call" | custom-call | flops 1811939328 | bytes 13197312 | tf_op jit(solution)/shard_map/project/pallas_call | solution.py:232
  59.7 3.3 %all-to-all-done.1.refs_7_ = bf16[4,48,1920]{2,1,0:T(8,128)(2,1)S(1)} async-done(((bf16[4,48,1920]{2,1,0:T(8,128)(2,1)}), bf16[4,48,1920]{2,1,0:T(8,128)(2,1)S(1)}, u32[]{:S(2)}, u32[]{:S(2)}) %all-to-all-start.1) | async-done | bytes 737312 | tf_op jit(solution)/shard_map/all_to_all | solution.py:766
  65.4 11.0 %mix.1 = (bf16[768,512]{1,0:T(8,128)(2,1)}, bf16[512,768]{1,0:T(8,128)(2,1)}, f32[12,512]{1,0:T(8,128)}) custom-call(bf16[512,768]{1,0:T(8,128)(2,1)} %get-tuple-element.144.refs_0_.refs_1_, bf16[512,768]{1,0:T(8,128)(2,1)} %get-tuple-element.145.refs_1_.refs_2_, bf16[512,768]{1,0:T(8,128)(2,1)} %get-tuple-element.146.refs_2_.refs_3_, ...), custom_call_target="tpu_custom_call" | custom-call | flops 805306368 | bytes 3960832 | tf_op jit(solution)/shard_map/mix/pallas_call | solution.py:232
  76.5 3.6 %collective-permute-done.17.refs_9_ = bf16[4,48,1920]{2,1,0:T(8,128)(2,1)S(1)} collective-permute-done((bf16[4,48,1920]{2,1,0:T(8,128)(2,1)S(1)}, bf16[4,48,1920]{2,1,0:T(8,128)(2,1)S(1)}, u32[]{:S(2)}, u32[]{:S(2)}) %collective-permute-start.17) | collective-permute-done | bytes 737312 | tf_op jit(solution)/shard_map/ppermute | solution.py:755
  81.5 3.6 %all-to-all-start.2 = ((bf16[4,192,384]{2,1,0:T(8,128)(2,1)}), bf16[4,192,384]{2,1,0:T(8,128)(2,1)S(1)}, u32[]{:S(2)}, u32[]{:S(2)}) async-start(bf16[4,192,384]{2,1,0:T(8,128)(2,1)} %broadcast_in_dim.8), calls=%async_computation.2 | async-start | bytes 1179648 | tf_op jit(solution)/shard_map/all_to_all | solution.py:766
  85.8 6.2 %collective-permute-done.18.refs_10_ = bf16[4,48,1920]{2,1,0:T(8,128)(2,1)} collective-permute-done((bf16[4,48,1920]{2,1,0:T(8,128)(2,1)}, bf16[4,48,1920]{2,1,0:T(8,128)(2,1)}, u32[]{:S(2)}, u32[]{:S(2)}) %collective-permute-start.18) | collective-permute-done | bytes 737312 | tf_op jit(solution)/shard_map/ppermute | solution.py:755
  94.1 5.1 %collective-permute-done.15.refs_6_ = bf16[128,768]{1,0:T(8,128)(2,1)S(1)} collective-permute-done((bf16[128,768]{1,0:T(8,128)(2,1)S(1)}, bf16[128,768]{1,0:T(8,128)(2,1)S(1)}, u32[]{:S(2)}, u32[]{:S(2)}) %collective-permute-start.15) | collective-permute-done | bytes 196640 | tf_op jit(solution)/shard_map/ppermute | solution.py:816
  100.5 6.3 %collective-permute-done.14.refs_5_ = bf16[128,768]{1,0:T(8,128)(2,1)S(1)} collective-permute-done((bf16[128,768]{1,0:T(8,128)(2,1)S(1)}, bf16[128,768]{1,0:T(8,128)(2,1)S(1)}, u32[]{:S(2)}, u32[]{:S(2)}) %collective-permute-start.14) | collective-permute-done | bytes 196640 | tf_op jit(solution)/shard_map/ppermute | solution.py:816
  106.8 1.6 collective-permute-done.13.refs_4_
  108.5 12.8 %widen.1 = (f32[512,768]{1,0:T(8,128)}, bf16[512,768]{1,0:T(8,128)(2,1)}, bf16[512,3072]{1,0:T(8,128)(2,1)}, bf16[512,3072]{1,0:T(8,128)(2,1)}, bf16[16,96,768]{...) custom-call(bf16[512,768]{1,0:T(8,128)(2,1)} %get-tuple-element.147., ...), custom_call_target="tpu_custom_call" | custom-call | flops 5435817984 | bytes 28925952 | tf_op jit(solution)/shard_map/widen/pallas_call | solution.py:232
  124.1 13.2 %collective-permute-done.25.refs_8_ = bf16[4,192,384]{2,1,0:T(8,128)(2,1)S(1)} collective-permute-done((bf16[4,192,384]{2,1,0:T(8,128)(2,1)S(1)}, bf16[4,192,384]{2,1,0:T(8,128)(2,1)S(1)}, u32[]{:S(2)}, u32[]{:S(2)}) %collective-permute-start.25) | collective-permute-done | bytes 589856 | tf_op jit(solution)/shard_map/ppermute | solution.py:755
  138.6 2.3 add_convert_fusion.2
  142.3 5.0 %collective-permute-done.26.refs_9_ = bf16[4,192,384]{2,1,0:T(8,128)(2,1)S(1)} collective-permute-done((bf16[4,192,384]{2,1,0:T(8,128)(2,1)S(1)}, bf16[4,192,384]{2,1,0:T(8,128)(2,1)S(1)}, u32[]{:S(2)}, u32[]{:S(2)}) %collective-permute-start.26) | collective-permute-done | bytes 589856 | tf_op jit(solution)/shard_map/ppermute | solution.py:755
  147.2 2.0 collective-permute-done.30.refs_13_
  149.2 12.1 %narrow0.1 = (f32[512,768]{1,0:T(8,128)}, bf16[16,24,3840]{2,1,0:T(8,128)(2,1)}, bf16[16,24,3840]{2,1,0:T(8,128)(2,1)}, f32[512,768]{1,0:T(8,128)}) custom-call(f32[512,768]{1,0:T(8,128)} %get-tuple-element.160.refs_0_, bf16[512,768]{1,0:T(8,128)(2,1)} %get-tuple-element.161.refs_1_, bf16[512,3072]{1,0:T(8,128)(2,1)} %get-tuple-element.162.refs_2_, ...), custom_call_target="tpu_custom_call" | custom-call | flops 4831838208 | bytes 29097984 | tf_op jit(solution)/shard_map/narrow0/pallas_call | solution.py:232
  161.5 1.6 collective-permute-start.32
  163.1 12.2 %narrow2.1 = (f32[512,768]{1,0:T(8,128)}, bf16[16,24,3840]{2,1,0:T(8,128)(2,1)}, bf16[16,24,3840]{2,1,0:T(8,128)(2,1)}, bf16[128,768]{1,0:T(8,128)(2,1)}, bf16[1...) custom-call(f32[512,768]{1,0:T(8,128)} %get-tuple-element.171.refs_0, ...), custom_call_target="tpu_custom_call", output_to_operand_aliasing={{1}: (15, {}), {2}: (16, {})} | custom-call | flops 4831838208 | bytes 35782656 | tf_op jit(solution)/shard_map/narrow2/pallas_call | solution.py:232
  176.3 6.5 %turn.1 = (f32[512,768]{1,0:T(8,128)}, bf16[512,768]{1,0:T(8,128)(2,1)}, f32[2,768]{1,0:T(2,128)S(1)}, bf16[16,24,3840]{2,1,0:T(8,128)(2,1)}, bf16[16,24,3840]{2,1,0:T(8,128)(2,1)}) custom-call(f32[512,768]{1,0:T(8,128)} %get-tuple-element.160.refs_0_, f32[512,768]{1,0:T(8,128)} %get-tuple-element.176.refs_1_, ...), custom_call_target="tpu_custom_call", output_to_operand_aliasing={{3}: (6, {}), {4}: (7, {})} | custom-call | flops 1207959552 | bytes 24803328 | tf_op jit(solution)/shard_map/turn/pallas_call | solution.py:232
  182.9 5.6 %collective-permute-done.33 = bf16[16,24,3840]{2,1,0:T(8,128)(2,1)S(1)} collective-permute-done((bf16[16,24,3840]{2,1,0:T(8,128)(2,1)}, bf16[16,24,3840]{2,1,0:T(8,128)(2,1)S(1)}, u32[]{:S(2)}, u32[]{:S(2)}) %collective-permute-start.33) | collective-permute-done | bytes 2949152 | tf_op jit(solution)/shard_map/ppermute | solution.py:755
  188.5 3.7 %add_convert_fusion = (bf16[8,24,3840]{2,1,0:T(8,128)(2,1)S(1)}, bf16[8,24,3840]{2,1,0:T(8,128)(2,1)}) fusion(bf16[16,24,3840]{2,1,0:T(8,128)(2,1)S(1)} %collective-permute-done.33, bf16[16,24,3840]{2,1,0:T(8,128)(2,1)} %get-tuple-element.181), kind=kLoop, calls=%fused_computation | loop fusion | flops 5898240 | bytes 8847360 | tf_op jit(solution)/shard_map/convert_element_type | solution.py:782
  193.5 3.6 %all-to-all-start.3 = ((bf16[4,96,768]{2,1,0:T(8,128)(2,1)}), bf16[4,96,768]{2,1,0:T(8,128)(2,1)S(1)}, u32[]{:S(2)}, u32[]{:S(2)}) async-start(bf16[4,96,768]{2,1,0:T(8,128)(2,1)} %add_convert_fusion.7), calls=%async_computation.3 | async-start | bytes 1179648 | tf_op jit(solution)/shard_map/all_to_all | solution.py:766
  199.1 9.4 %attend_back0.1 = (bf16[512,1152]{1,0:T(8,128)(2,1)}, bf16[16,24,1152]{2,1,0:T(8,128)(2,1)}, bf16[16,24,1152]{2,1,0:T(8,128)(2,1)}) custom-call(bf16[512,768]{1,0:T(8,128)(2,1)} %get-tuple-element.140.refs_0_, bf16[512,768]{1,0:T(8,128)(2,1)} %get-tuple-element.144.refs_0_.refs_1_, bf16[512,768]{1,0:T(8,128)(2,1)} %get-tuple-element.145.refs_1_.refs_2_, ...), custom_call_target="tpu_custom_call" | custom-call | flops 1912602624 | bytes 6909952 | tf_op jit(solution)/shard_map/attend_back0/pallas_call | solution.py:232
  209.0 9.1 %collective-permute-done.38.refs_28_ = bf16[128,768]{1,0:T(8,128)(2,1)S(1)} collective-permute-done((bf16[128,768]{1,0:T(8,128)(2,1)S(1)}, bf16[128,768]{1,0:T(8,128)(2,1)S(1)}, u32[]{:S(2)}, u32[]{:S(2)}) %collective-permute-start.38) | collective-permute-done | bytes 196640 | tf_op jit(solution)/shard_map/ppermute | solution.py:816
  223.5 9.4 %attend_back1.1 = (bf16[512,1152]{1,0:T(8,128)(2,1)}, bf16[16,24,1152]{2,1,0:T(8,128)(2,1)}, bf16[16,24,1152]{2,1,0:T(8,128)(2,1)}) custom-call(bf16[512,768]{1,0:T(8,128)(2,1)} %get-tuple-element.140.refs_0_, bf16[512,768]{1,0:T(8,128)(2,1)} %get-tuple-element.144.refs_0_.refs_1_, bf16[512,768]{1,0:T(8,128)(2,1)} %get-tuple-element.145.refs_1_.refs_2_, ...), custom_call_target="tpu_custom_call" | custom-call | flops 1912602624 | bytes 6909952 | tf_op jit(solution)/shard_map/attend_back1/pallas_call | solution.py:232
  232.9 2.6 collective-permute-done.35
  236.7 2.3 add_convert_fusion.4
  239.0 3.5 %all-to-all-start.4 = ((bf16[4,24,3840]{2,1,0:T(8,128)(2,1)}), bf16[4,24,3840]{2,1,0:T(8,128)(2,1)S(1)}, u32[]{:S(2)}, u32[]{:S(2)}) async-start(bf16[4,24,3840]{2,1,0:T(8,128)(2,1)} %add_convert_fusion.4), calls=%async_computation.4 | async-start | bytes 1474560 | tf_op jit(solution)/shard_map/all_to_all | solution.py:766
  242.5 2.4 add_convert_fusion.11
  246.5 8.2 %finish_tokens.1 = (bf16[128,768]{1,0:T(8,128)(2,1)}, bf16[128,768]{1,0:T(8,128)(2,1)}, bf16[128,768]{1,0:T(8,128)(2,1)}, bf16[128,768]{1,0:T(8,128)(2,1)}, f32[2,768]{1,0:T(2,128)S(1)}) custom-call(bf16[512,768]{1,0:T(8,128)(2,1)} %get-tuple-element.147.refs_0_, bf16[512,1152]{1,0:T(8,128)(2,1)} %get-tuple-element.190.refs_1_, ...), custom_call_target="tpu_custom_call" | custom-call | flops 1811939328 | bytes 9467904 | tf_op jit(solution)/shard_map/finish_tokens/pallas_call | solution.py:232
  255.5 6.6 %all-to-all-done.4 = bf16[4,24,3840]{2,1,0:T(8,128)(2,1)S(1)} async-done(((bf16[4,24,3840]{2,1,0:T(8,128)(2,1)}), bf16[4,24,3840]{2,1,0:T(8,128)(2,1)S(1)}, u32[]{:S(2)}, u32[]{:S(2)}) %all-to-all-start.4) | async-done | bytes 737312 | tf_op jit(solution)/shard_map/all_to_all | solution.py:766
  262.1 2.6 all-to-all-start.5
  265.5 1.7 collective-permute-start.44
  267.2 4.8 %all-to-all-done.5 = f32[32,4,24]{2,1,0:T(4,128)S(1)} async-done(((f32[32,4,24]{2,1,0:T(4,128)}), f32[32,4,24]{2,1,0:T(4,128)S(1)}, u32[]{:S(2)}, u32[]{:S(2)}) %all-to-all-start.5) | async-done | bytes 12320 | tf_op jit(solution)/shard_map/all_to_all | solution.py:797
  274.1 4.5 %all-to-all-start.6 = ((bf16[4,24,2304]{2,1,0:T(8,128)(2,1)}), bf16[4,24,2304]{2,1,0:T(8,128)(2,1)S(1)}, u32[]{:S(2)}, u32[]{:S(2)}) async-start(bf16[4,24,2304]{2,1,0:T(8,128)(2,1)} %pad_maximum_fusion), calls=%async_computation.6 | async-start | bytes 884736 | tf_op jit(solution)/shard_map/all_to_all | solution.py:766
  279.4 1.5 collective-permute-start.46
  282.6 8.2 %all-to-all-done.6 = bf16[4,24,2304]{2,1,0:T(8,128)(2,1)S(1)} async-done(((bf16[4,24,2304]{2,1,0:T(8,128)(2,1)}), bf16[4,24,2304]{2,1,0:T(8,128)(2,1)S(1)}, u32[]{:S(2)}, u32[]{:S(2)}) %all-to-all-start.6) | async-done | bytes 442400 | tf_op jit(solution)/shard_map/all_to_all | solution.py:766
  294.7 3.7 %all-to-all-start.7 = ((f32[32,1,128]{2,1,0:T(1,128)}), f32[32,1,128]{2,1,0:T(1,128)S(1)}, u32[]{:S(2)}, u32[]{:S(2)}) async-start(f32[32,1,128]{2,1,0:T(1,128)} %broadcast_in_dim_broadcast_in_dim_broadcast_in_dim.3), calls=%async_computation.7 | async-start | bytes 32768 | tf_op jit(solution)/shard_map/all_to_all | solution.py:791
  298.5 7.0 %all-to-all-done.7 = f32[32,1,128]{2,1,0:T(1,128)S(1)} async-done(((f32[32,1,128]{2,1,0:T(1,128)}), f32[32,1,128]{2,1,0:T(1,128)S(1)}, u32[]{:S(2)}, u32[]{:S(2)}) %all-to-all-start.7) | async-done | bytes 16416 | tf_op jit(solution)/shard_map/all_to_all | solution.py:791
  305.5 5.2 %update.1 = (f32[1,128]{1,0:T(1,128)}, f32[24,768]{1,0:T(8,128)}, f32[24,768]{1,0:T(8,128)}, f32[24,768]{1,0:T(8,128)}, f32[24,768]{1,0:T(8,128)}, /*index=5*/f3...) custom-call(f32[24,2304]{1,0:T(8,128)S(1)} %convert_reduce_fusion.2., ...), custom_call_target="tpu_custom_call" | custom-call | flops 10000000 | bytes 9358464 | tf_op jit(solution)/shard_map/update/pallas_call | solution.py:232
  (148 shorter events, 46.5 us)
Async XLA Ops:
  5.7 20.3 %all-to-all-start = ((bf16[4,48,1280]{2,1,0:T(8,128)(2,1)}), bf16[4,48,1280]{2,1,0:T(8,128)(2,1)S(1)}, u32[]{:S(2)}, u32[]{:S(2)}) async-start(bf16[4,48,1280]{2,1,0:T(8,128)(2,1)} %broadcast_in_dim.6), calls=%async_computation | async-start | bytes 983040 | tf_op jit(solution)/shard_map/all_to_all | solution.py:766
  12.5 7.1 %collective-permute-start.2 = (bf16[128,768]{1,0:T(8,128)(2,1)S(1)}, bf16[128,768]{1,0:T(8,128)(2,1)S(1)}, u32[]{:S(2)}, u32[]{:S(2)}) collective-permute-start(bf16[128,768]{1,0:T(8,128)(2,1)S(1)} %get-tuple-element.251), channel_id=1, source_target_pairs={{0,3},{1,2},{2,1},{3,0},{4,7},{5,6},{6,5},{7,4},{8,11},{9,10},{10,... | collective-permute-start | bytes 589832 | tf_op jit(solution)/shard_map/ppermute | solution.py:816
  13.6 10.3 %collective-permute-start.1 = (bf16[128,768]{1,0:T(8,128)(2,1)S(1)}, bf16[128,768]{1,0:T(8,128)(2,1)S(1)}, u32[]{:S(2)}, u32[]{:S(2)}) collective-permute-start(bf16[128,768]{1,0:T(8,128)(2,1)S(1)} %get-tuple-element.252), channel_id=1, source_target_pairs={{0,2},{1,3},{2,0},{3,1},{4,6},{5,7},{6,4},{7,5},{8,10},{9,11},{10,... | collective-permute-start | bytes 589832 | tf_op jit(solution)/shard_map/ppermute | solution.py:816
  14.2 9.8 %collective-permute-start = (bf16[128,768]{1,0:T(8,128)(2,1)S(1)}, bf16[128,768]{1,0:T(8,128)(2,1)S(1)}, u32[]{:S(2)}, u32[]{:S(2)}) collective-permute-start(bf16[128,768]{1,0:T(8,128)(2,1)S(1)} %get-tuple-element.253), channel_id=1, source_target_pairs={{0,1},{1,0},{2,3},{3,2},{4,5},{5,4},{6,7},{7,6},{8,9},{9,8},{10,11... | collective-permute-start | bytes 589832 | tf_op jit(solution)/shard_map/ppermute | solution.py:816
  27.9 14.0 %collective-permute-start.6 = (bf16[4,48,1280]{2,1,0:T(8,128)(2,1)S(1)}, bf16[4,48,1280]{2,1,0:T(8,128)(2,1)S(1)}, u32[]{:S(2)}, u32[]{:S(2)}) collective-permute-start(bf16[4,48,1280]{2,1,0:T(8,128)(2,1)S(1)} %all-to-all-done.refs_4_), channel_id=1, source_target_pairs={{0,4},{1,3},{2,6},{3,1},{4,0},{5,7},{6,2},{7,5},{8,12},{9,11},{10,... | collective-permute-start | bytes 1474568 | tf_op jit(solution)/shard_map/ppermute | solution.py:755
  29.4 16.8 %collective-permute-start.7 = (bf16[4,48,1280]{2,1,0:T(8,128)(2,1)S(1)}, bf16[4,48,1280]{2,1,0:T(8,128)(2,1)S(1)}, u32[]{:S(2)}, u32[]{:S(2)}) collective-permute-start(bf16[4,48,1280]{2,1,0:T(8,128)(2,1)S(1)} %all-to-all-done.refs_4_), channel_id=1, source_target_pairs={{0,2},{1,5},{2,0},{3,7},{4,6},{5,1},{6,4},{7,3},{8,10},{9,13},{10,... | collective-permute-start | bytes 1474568 | tf_op jit(solution)/shard_map/ppermute | solution.py:755
  41.9 8.9 %collective-permute-start.8 = (bf16[4,48,1280]{2,1,0:T(8,128)(2,1)S(1)}, bf16[4,48,1280]{2,1,0:T(8,128)(2,1)}, u32[]{:S(2)}, u32[]{:S(2)}) collective-permute-start(bf16[4,48,1280]{2,1,0:T(8,128)(2,1)S(1)} %collective-permute-done.6.refs_5_), channel_id=1, source_target_pairs={{0,2},{1,5},{2,0},{3,7},{4,6},{5,1},{6,4},{7,3},{8,10},{9,13},{10,... | collective-permute-start | bytes 1474568 | tf_op jit(solution)/shard_map/ppermute | solution.py:755
  42.0 20.9 %all-to-all-start.1 = ((bf16[4,48,1920]{2,1,0:T(8,128)(2,1)}), bf16[4,48,1920]{2,1,0:T(8,128)(2,1)S(1)}, u32[]{:S(2)}, u32[]{:S(2)}) async-start(bf16[4,48,1920]{2,1,0:T(8,128)(2,1)} %broadcast_in_dim.7), calls=%async_computation.1 | async-start | bytes 1474560 | tf_op jit(solution)/shard_map/all_to_all | solution.py:766
  45.7 5.1 %collective-permute-start.9 = (bf16[4,48,1280]{2,1,0:T(8,128)(2,1)S(1)}, bf16[4,48,1280]{2,1,0:T(8,128)(2,1)S(1)}, u32[]{:S(2)}, u32[]{:S(2)}) collective-permute-start(bf16[4,48,1280]{2,1,0:T(8,128)(2,1)S(1)} %all-to-all-done.refs_4_), channel_id=1, source_target_pairs={{0,1},{1,0},{2,3},{3,2},{4,5},{5,4},{6,7},{7,6},{8,9},{9,8},{10,11... | collective-permute-start | bytes 1474568 | tf_op jit(solution)/shard_map/ppermute | solution.py:755
  45.7 5.1 %collective-permute-start.10 = (bf16[4,48,1280]{2,1,0:T(8,128)(2,1)S(1)}, bf16[4,48,1280]{2,1,0:T(8,128)(2,1)S(1)}, u32[]{:S(2)}, u32[]{:S(2)}) collective-permute-start(bf16[4,48,1280]{2,1,0:T(8,128)(2,1)S(1)} %collective-permute-done.6.refs_5_), channel_id=1, source_target_pairs={{0,1},{1,0},{2,3},{3,2},{4,5},{5,4},{6,7},{7,6},{8,9},{9,8},{10,11... | collective-permute-start | bytes 1474568 | tf_op jit(solution)/shard_map/ppermute | solution.py:755
  62.9 17.2 %collective-permute-start.17 = (bf16[4,48,1920]{2,1,0:T(8,128)(2,1)S(1)}, bf16[4,48,1920]{2,1,0:T(8,128)(2,1)S(1)}, u32[]{:S(2)}, u32[]{:S(2)}) collective-permute-start(bf16[4,48,1920]{2,1,0:T(8,128)(2,1)S(1)} %all-to-all-done.1.refs_7_), channel_id=1, source_target_pairs={{0,2},{1,5},{2,0},{3,7},{4,6},{5,1},{6,4},{7,3},{8,10},{9,13},{10,... | collective-permute-start | bytes 2211848 | tf_op jit(solution)/shard_map/ppermute | solution.py:755
  64.4 15.8 %collective-permute-start.16 = (bf16[4,48,1920]{2,1,0:T(8,128)(2,1)S(1)}, bf16[4,48,1920]{2,1,0:T(8,128)(2,1)}, u32[]{:S(2)}, u32[]{:S(2)}) collective-permute-start(bf16[4,48,1920]{2,1,0:T(8,128)(2,1)S(1)} %all-to-all-done.1.refs_7_), channel_id=1, source_target_pairs={{0,4},{1,3},{2,6},{3,1},{4,0},{5,7},{6,2},{7,5},{8,12},{9,11},{10,... | collective-permute-start | bytes 2211848 | tf_op jit(solution)/shard_map/ppermute | solution.py:755
  80.2 11.8 %collective-permute-start.18 = (bf16[4,48,1920]{2,1,0:T(8,128)(2,1)}, bf16[4,48,1920]{2,1,0:T(8,128)(2,1)}, u32[]{:S(2)}, u32[]{:S(2)}) collective-permute-start(bf16[4,48,1920]{2,1,0:T(8,128)(2,1)} %collective-permute-done.16.refs_8_), channel_id=1, source_target_pairs={{0,2},{1,5},{2,0},{3,7},{4,6},{5,1},{6,4},{7,3},{8,10},{9,13},{10,... | collective-permute-start | bytes 2211848 | tf_op jit(solution)/shard_map/ppermute | solution.py:755
  81.5 25.3 %all-to-all-start.2 = ((bf16[4,192,384]{2,1,0:T(8,128)(2,1)}), bf16[4,192,384]{2,1,0:T(8,128)(2,1)S(1)}, u32[]{:S(2)}, u32[]{:S(2)}) async-start(bf16[4,192,384]{2,1,0:T(8,128)(2,1)} %broadcast_in_dim.8), calls=%async_computation.2 | async-start | bytes 1179648 | tf_op jit(solution)/shard_map/all_to_all | solution.py:766
  85.1 23.3 %collective-permute-start.19 = (bf16[4,48,1920]{2,1,0:T(8,128)(2,1)S(1)}, bf16[4,48,1920]{2,1,0:T(8,128)(2,1)}, u32[]{:S(2)}, u32[]{:S(2)}) collective-permute-start(bf16[4,48,1920]{2,1,0:T(8,128)(2,1)S(1)} %all-to-all-done.1.refs_7_), channel_id=1, source_target_pairs={{0,1},{1,0},{2,3},{3,2},{4,5},{5,4},{6,7},{7,6},{8,9},{9,8},{10,11... | collective-permute-start | bytes 2211848 | tf_op jit(solution)/shard_map/ppermute | solution.py:755
  85.2 23.3 %collective-permute-start.20 = (bf16[4,48,1920]{2,1,0:T(8,128)(2,1)}, bf16[4,48,1920]{2,1,0:T(8,128)(2,1)}, u32[]{:S(2)}, u32[]{:S(2)}) collective-permute-start(bf16[4,48,1920]{2,1,0:T(8,128)(2,1)} %collective-permute-done.16.refs_8_), channel_id=1, source_target_pairs={{0,1},{1,0},{2,3},{3,2},{4,5},{5,4},{6,7},{7,6},{8,9},{9,8},{10,11... | collective-permute-start | bytes 2211848 | tf_op jit(solution)/shard_map/ppermute | solution.py:755
  85.7 22.8 %collective-permute-start.21 = (bf16[4,48,1920]{2,1,0:T(8,128)(2,1)S(1)}, bf16[4,48,1920]{2,1,0:T(8,128)(2,1)}, u32[]{:S(2)}, u32[]{:S(2)}) collective-permute-start(bf16[4,48,1920]{2,1,0:T(8,128)(2,1)S(1)} %collective-permute-done.17.refs_9_), channel_id=1, source_target_pairs={{0,1},{1,0},{2,3},{3,2},{4,5},{5,4},{6,7},{7,6},{8,9},{9,8},{10,11... | collective-permute-start | bytes 2211848 | tf_op jit(solution)/shard_map/ppermute | solution.py:755
  92.0 16.5 %collective-permute-start.22 = (bf16[4,48,1920]{2,1,0:T(8,128)(2,1)}, bf16[4,48,1920]{2,1,0:T(8,128)(2,1)}, u32[]{:S(2)}, u32[]{:S(2)}) collective-permute-start(bf16[4,48,1920]{2,1,0:T(8,128)(2,1)} %collective-permute-done.18.refs_10_), channel_id=1, source_target_pairs={{0,1},{1,0},{2,3},{3,2},{4,5},{5,4},{6,7},{7,6},{8,9},{9,8},{10,11... | collective-permute-start | bytes 2211848 | tf_op jit(solution)/shard_map/ppermute | solution.py:755
  92.7 6.6 %collective-permute-start.15 = (bf16[128,768]{1,0:T(8,128)(2,1)S(1)}, bf16[128,768]{1,0:T(8,128)(2,1)S(1)}, u32[]{:S(2)}, u32[]{:S(2)}) collective-permute-start(bf16[128,768]{1,0:T(8,128)(2,1)S(1)} %get-tuple-element.248), channel_id=1, source_target_pairs={{0,3},{1,2},{2,1},{3,0},{4,7},{5,6},{6,5},{7,4},{8,11},{9,10},{10,... | collective-permute-start | bytes 589832 | tf_op jit(solution)/shard_map/ppermute | solution.py:816
  99.2 7.6 %collective-permute-start.14 = (bf16[128,768]{1,0:T(8,128)(2,1)S(1)}, bf16[128,768]{1,0:T(8,128)(2,1)S(1)}, u32[]{:S(2)}, u32[]{:S(2)}) collective-permute-start(bf16[128,768]{1,0:T(8,128)(2,1)S(1)} %get-tuple-element.249), channel_id=1, source_target_pairs={{0,2},{1,3},{2,0},{3,1},{4,6},{5,7},{6,4},{7,5},{8,10},{9,11},{10,... | collective-permute-start | bytes 589832 | tf_op jit(solution)/shard_map/ppermute | solution.py:816
  121.3 17.3 %collective-permute-start.23 = (bf16[16,96,768]{2,1,0:T(8,128)(2,1)}, bf16[16,96,768]{2,1,0:T(8,128)(2,1)S(1)}, u32[]{:S(2)}, u32[]{:S(2)}) collective-permute-start(bf16[16,96,768]{2,1,0:T(8,128)(2,1)} %get-tuple-element.159), channel_id=1, source_target_pairs={{0,1},{1,0},{2,3},{3,2},{4,5},{5,4},{6,7},{7,6},{8,9},{9,8},{10,11... | collective-permute-start | bytes 7077896 | tf_op jit(solution)/shard_map/ppermute | solution.py:755
  121.5 15.8 %collective-permute-start.25 = (bf16[4,192,384]{2,1,0:T(8,128)(2,1)S(1)}, bf16[4,192,384]{2,1,0:T(8,128)(2,1)S(1)}, u32[]{:S(2)}, u32[]{:S(2)}) collective-permute-start(bf16[4,192,384]{2,1,0:T(8,128)(2,1)S(1)} %all-to-all-done.2.refs_6_), channel_id=1, source_target_pairs={{0,2},{1,5},{2,0},{3,7},{4,6},{5,1},{6,4},{7,3},{8,10},{9,13},{10,... | collective-permute-start | bytes 1769480 | tf_op jit(solution)/shard_map/ppermute | solution.py:755
  122.8 14.5 %collective-permute-start.24 = (bf16[4,192,384]{2,1,0:T(8,128)(2,1)S(1)}, bf16[4,192,384]{2,1,0:T(8,128)(2,1)S(1)}, u32[]{:S(2)}, u32[]{:S(2)}) collective-permute-start(bf16[4,192,384]{2,1,0:T(8,128)(2,1)S(1)} %all-to-all-done.2.refs_6_), channel_id=1, source_target_pairs={{0,4},{1,3},{2,6},{3,1},{4,0},{5,7},{6,2},{7,5},{8,12},{9,11},{10,... | collective-permute-start | bytes 1769480 | tf_op jit(solution)/shard_map/ppermute | solution.py:755
  137.3 9.9 %collective-permute-start.26 = (bf16[4,192,384]{2,1,0:T(8,128)(2,1)S(1)}, bf16[4,192,384]{2,1,0:T(8,128)(2,1)S(1)}, u32[]{:S(2)}, u32[]{:S(2)}) collective-permute-start(bf16[4,192,384]{2,1,0:T(8,128)(2,1)S(1)} %collective-permute-done.24.refs_7_), channel_id=1, source_target_pairs={{0,2},{1,5},{2,0},{3,7},{4,6},{5,1},{6,4},{7,3},{8,10},{9,13},{10,... | collective-permute-start | bytes 1769480 | tf_op jit(solution)/shard_map/ppermute | solution.py:755
  140.9 20.5 %collective-permute-start.31 = (bf16[8,96,768]{2,1,0:T(8,128)(2,1)S(1)}, bf16[8,96,768]{2,1,0:T(8,128)(2,1)S(1)}, u32[]{:S(2)}, u32[]{:S(2)}) collective-permute-start(bf16[8,96,768]{2,1,0:T(8,128)(2,1)S(1)} %get-tuple-element.243), channel_id=1, source_target_pairs={{0,2},{1,5},{2,0},{3,7},{4,6},{5,1},{6,4},{7,3},{8,10},{9,13},{10,... | collective-permute-start | bytes 3538952 | tf_op jit(solution)/shard_map/ppermute | solution.py:755
  141.7 5.5 %collective-permute-start.27 = (bf16[4,192,384]{2,1,0:T(8,128)(2,1)S(1)}, bf16[4,192,384]{2,1,0:T(8,128)(2,1)S(1)}, u32[]{:S(2)}, u32[]{:S(2)}) collective-permute-start(bf16[4,192,384]{2,1,0:T(8,128)(2,1)S(1)} %all-to-all-done.2.refs_6_), channel_id=1, source_target_pairs={{0,1},{1,0},{2,3},{3,2},{4,5},{5,4},{6,7},{7,6},{8,9},{9,8},{10,11... | collective-permute-start | bytes 1769480 | tf_op jit(solution)/shard_map/ppermute | solution.py:755
  141.7 5.5 %collective-permute-start.28 = (bf16[4,192,384]{2,1,0:T(8,128)(2,1)S(1)}, bf16[4,192,384]{2,1,0:T(8,128)(2,1)S(1)}, u32[]{:S(2)}, u32[]{:S(2)}) collective-permute-start(bf16[4,192,384]{2,1,0:T(8,128)(2,1)S(1)} %collective-permute-done.24.refs_7_), channel_id=1, source_target_pairs={{0,1},{1,0},{2,3},{3,2},{4,5},{5,4},{6,7},{7,6},{8,9},{9,8},{10,11... | collective-permute-start | bytes 1769480 | tf_op jit(solution)/shard_map/ppermute | solution.py:755
  161.5 13.8 %collective-permute-start.32 = (bf16[4,96,768]{2,1,0:T(8,128)(2,1)S(1)}, bf16[4,96,768]{2,1,0:T(8,128)(2,1)S(1)}, u32[]{:S(2)}, u32[]{:S(2)}) collective-permute-start(bf16[4,96,768]{2,1,0:T(8,128)(2,1)S(1)} %add_convert_fusion.9), channel_id=1, source_target_pairs={{0,4},{1,3},{2,6},{3,1},{4,0},{5,7},{6,2},{7,5},{8,12},{9,11},{10,... | collective-permute-start | bytes 1769480 | tf_op jit(solution)/shard_map/ppermute | solution.py:755
  182.9 5.7 %collective-permute-start.33 = (bf16[16,24,3840]{2,1,0:T(8,128)(2,1)}, bf16[16,24,3840]{2,1,0:T(8,128)(2,1)S(1)}, u32[]{:S(2)}, u32[]{:S(2)}) collective-permute-start(bf16[16,24,3840]{2,1,0:T(8,128)(2,1)} %get-tuple-element.182), channel_id=1, source_target_pairs={{0,1},{1,0},{2,3},{3,2},{4,5},{5,4},{6,7},{7,6},{8,9},{9,8},{10,11... | collective-permute-start | bytes 8847368 | tf_op jit(solution)/shard_map/ppermute | solution.py:755
  192.2 26.8 %collective-permute-start.36 = (bf16[8,24,3840]{2,1,0:T(8,128)(2,1)}, bf16[8,24,3840]{2,1,0:T(8,128)(2,1)}, u32[]{:S(2)}, u32[]{:S(2)}) collective-permute-start(bf16[8,24,3840]{2,1,0:T(8,128)(2,1)} %get-tuple-element.241), channel_id=1, source_target_pairs={{0,2},{1,5},{2,0},{3,7},{4,6},{5,1},{6,4},{7,3},{8,10},{9,13},{10,... | collective-permute-start | bytes 4423688 | tf_op jit(solution)/shard_map/ppermute | solution.py:755
  193.5 25.5 %all-to-all-start.3 = ((bf16[4,96,768]{2,1,0:T(8,128)(2,1)}), bf16[4,96,768]{2,1,0:T(8,128)(2,1)S(1)}, u32[]{:S(2)}, u32[]{:S(2)}) async-start(bf16[4,96,768]{2,1,0:T(8,128)(2,1)} %add_convert_fusion.7), calls=%async_computation.3 | async-start | bytes 1179648 | tf_op jit(solution)/shard_map/all_to_all | solution.py:766
  197.2 11.8 %collective-permute-start.37 = (bf16[128,768]{1,0:T(8,128)(2,1)S(1)}, bf16[128,768]{1,0:T(8,128)(2,1)S(1)}, u32[]{:S(2)}, u32[]{:S(2)}) collective-permute-start(bf16[128,768]{1,0:T(8,128)(2,1)S(1)} %copy-done.17), channel_id=1, source_target_pairs={{0,1},{1,0},{2,3},{3,2},{4,5},{5,4},{6,7},{7,6},{8,9},{9,8},{10,11... | collective-permute-start | bytes 589832 | tf_op jit(solution)/shard_map/ppermute | solution.py:816
  197.3 20.8 %collective-permute-start.38 = (bf16[128,768]{1,0:T(8,128)(2,1)S(1)}, bf16[128,768]{1,0:T(8,128)(2,1)S(1)}, u32[]{:S(2)}, u32[]{:S(2)}) collective-permute-start(bf16[128,768]{1,0:T(8,128)(2,1)S(1)} %copy-done.16), channel_id=1, source_target_pairs={{0,2},{1,3},{2,0},{3,1},{4,6},{5,7},{6,4},{7,5},{8,10},{9,11},{10,... | collective-permute-start | bytes 589832 | tf_op jit(solution)/shard_map/ppermute | solution.py:816
  198.1 21.0 %collective-permute-start.39 = (bf16[128,768]{1,0:T(8,128)(2,1)S(1)}, bf16[128,768]{1,0:T(8,128)(2,1)S(1)}, u32[]{:S(2)}, u32[]{:S(2)}) collective-permute-start(bf16[128,768]{1,0:T(8,128)(2,1)S(1)} %copy-done.15), channel_id=1, source_target_pairs={{0,3},{1,2},{2,1},{3,0},{4,7},{5,6},{6,5},{7,4},{8,11},{9,10},{10,... | collective-permute-start | bytes 589832 | tf_op jit(solution)/shard_map/ppermute | solution.py:816
  208.6 12.4 %collective-permute-start.34 = (bf16[16,24,1152]{2,1,0:T(8,128)(2,1)}, bf16[16,24,1152]{2,1,0:T(8,128)(2,1)}, u32[]{:S(2)}, u32[]{:S(2)}) collective-permute-start(bf16[16,24,1152]{2,1,0:T(8,128)(2,1)} %get-tuple-element.185), channel_id=1, source_target_pairs={{0,1},{1,0},{2,3},{3,2},{4,5},{5,4},{6,7},{7,6},{8,9},{9,8},{10,11... | collective-permute-start | bytes 2654216 | tf_op jit(solution)/shard_map/ppermute | solution.py:755
  220.5 16.3 %collective-permute-start.42 = (bf16[4,24,3840]{2,1,0:T(8,128)(2,1)S(1)}, bf16[4,24,3840]{2,1,0:T(8,128)(2,1)S(1)}, u32[]{:S(2)}, u32[]{:S(2)}) collective-permute-start(bf16[4,24,3840]{2,1,0:T(8,128)(2,1)S(1)} %add_convert_fusion.6), channel_id=1, source_target_pairs={{0,4},{1,3},{2,6},{3,1},{4,0},{5,7},{6,2},{7,5},{8,12},{9,11},{10,... | collective-permute-start | bytes 2211848 | tf_op jit(solution)/shard_map/ppermute | solution.py:755
  222.4 13.2 %collective-permute-start.35 = (bf16[8,24,1152]{2,1,0:T(8,128)(2,1)S(1)}, bf16[8,24,1152]{2,1,0:T(8,128)(2,1)S(1)}, u32[]{:S(2)}, u32[]{:S(2)}) collective-permute-start(bf16[8,24,1152]{2,1,0:T(8,128)(2,1)S(1)} %get-tuple-element.245), channel_id=1, source_target_pairs={{0,2},{1,5},{2,0},{3,7},{4,6},{5,1},{6,4},{7,3},{8,10},{9,13},{10,... | collective-permute-start | bytes 1327112 | tf_op jit(solution)/shard_map/ppermute | solution.py:755
  235.5 7.0 %collective-permute-start.41 = (bf16[16,24,1152]{2,1,0:T(8,128)(2,1)}, bf16[16,24,1152]{2,1,0:T(8,128)(2,1)}, u32[]{:S(2)}, u32[]{:S(2)}) collective-permute-start(bf16[16,24,1152]{2,1,0:T(8,128)(2,1)} %get-tuple-element.197), channel_id=1, source_target_pairs={{0,1},{1,0},{2,3},{3,2},{4,5},{5,4},{6,7},{7,6},{8,9},{9,8},{10,11... | collective-permute-start | bytes 2654216 | tf_op jit(solution)/shard_map/ppermute | solution.py:755
  239.0 23.1 %all-to-all-start.4 = ((bf16[4,24,3840]{2,1,0:T(8,128)(2,1)}), bf16[4,24,3840]{2,1,0:T(8,128)(2,1)S(1)}, u32[]{:S(2)}, u32[]{:S(2)}) async-start(bf16[4,24,3840]{2,1,0:T(8,128)(2,1)} %add_convert_fusion.4), calls=%async_computation.4 | async-start | bytes 1474560 | tf_op jit(solution)/shard_map/all_to_all | solution.py:766
  244.9 19.8 %collective-permute-start.43 = (bf16[8,24,1152]{2,1,0:T(8,128)(2,1)}, bf16[8,24,1152]{2,1,0:T(8,128)(2,1)S(1)}, u32[]{:S(2)}, u32[]{:S(2)}) collective-permute-start(bf16[8,24,1152]{2,1,0:T(8,128)(2,1)} %get-tuple-element.246), channel_id=1, source_target_pairs={{0,2},{1,5},{2,0},{3,7},{4,6},{5,1},{6,4},{7,3},{8,10},{9,13},{10,... | collective-permute-start | bytes 1327112 | tf_op jit(solution)/shard_map/ppermute | solution.py:755
  245.7 9.0 %collective-permute-start.40 = (bf16[4,24,1152]{2,1,0:T(8,128)(2,1)S(1)}, bf16[4,24,1152]{2,1,0:T(8,128)(2,1)S(1)}, u32[]{:S(2)}, u32[]{:S(2)}) collective-permute-start(bf16[4,24,1152]{2,1,0:T(8,128)(2,1)S(1)} %add_convert_fusion.18), channel_id=1, source_target_pairs={{0,4},{1,3},{2,6},{3,1},{4,0},{5,7},{6,2},{7,5},{8,12},{9,11},{10,... | collective-permute-start | bytes 663560 | tf_op jit(solution)/shard_map/ppermute | solution.py:755
  262.1 10.0 %all-to-all-start.5 = ((f32[32,4,24]{2,1,0:T(4,128)}), f32[32,4,24]{2,1,0:T(4,128)S(1)}, u32[]{:S(2)}, u32[]{:S(2)}) async-start(f32[32,4,24]{2,1,0:T(4,128)} %copy.56), calls=%async_computation.5 | async-start | bytes 131072 | tf_op jit(solution)/shard_map/all_to_all | solution.py:797
  265.5 6.6 %collective-permute-start.44 = (bf16[4,24,1152]{2,1,0:T(8,128)(2,1)}, bf16[4,24,1152]{2,1,0:T(8,128)(2,1)}, u32[]{:S(2)}, u32[]{:S(2)}) collective-permute-start(bf16[4,24,1152]{2,1,0:T(8,128)(2,1)} %add_convert_fusion.15), channel_id=1, source_target_pairs={{0,4},{1,3},{2,6},{3,1},{4,0},{5,7},{6,2},{7,5},{8,12},{9,11},{10,... | collective-permute-start | bytes 663560 | tf_op jit(solution)/shard_map/ppermute | solution.py:755
  274.1 16.7 %all-to-all-start.6 = ((bf16[4,24,2304]{2,1,0:T(8,128)(2,1)}), bf16[4,24,2304]{2,1,0:T(8,128)(2,1)S(1)}, u32[]{:S(2)}, u32[]{:S(2)}) async-start(bf16[4,24,2304]{2,1,0:T(8,128)(2,1)} %pad_maximum_fusion), calls=%async_computation.6 | async-start | bytes 884736 | tf_op jit(solution)/shard_map/all_to_all | solution.py:766
  279.4 19.0 %collective-permute-start.45 = (bf16[128,768]{1,0:T(8,128)(2,1)S(1)}, bf16[128,768]{1,0:T(8,128)(2,1)S(1)}, u32[]{:S(2)}, u32[]{:S(2)}) collective-permute-start(bf16[128,768]{1,0:T(8,128)(2,1)S(1)} %copy-done.14), channel_id=1, source_target_pairs={{0,1},{1,0},{2,3},{3,2},{4,5},{5,4},{6,7},{7,6},{8,9},{9,8},{10,11... | collective-permute-start | bytes 589832 | tf_op jit(solution)/shard_map/ppermute | solution.py:816
  279.4 19.1 %collective-permute-start.46 = (bf16[128,768]{1,0:T(8,128)(2,1)S(1)}, bf16[128,768]{1,0:T(8,128)(2,1)S(1)}, u32[]{:S(2)}, u32[]{:S(2)}) collective-permute-start(bf16[128,768]{1,0:T(8,128)(2,1)S(1)} %copy-done.13), channel_id=1, source_target_pairs={{0,2},{1,3},{2,0},{3,1},{4,6},{5,7},{6,4},{7,5},{8,10},{9,11},{10,... | collective-permute-start | bytes 589832 | tf_op jit(solution)/shard_map/ppermute | solution.py:816
  280.9 17.5 %collective-permute-start.47 = (bf16[128,768]{1,0:T(8,128)(2,1)S(1)}, bf16[128,768]{1,0:T(8,128)(2,1)S(1)}, u32[]{:S(2)}, u32[]{:S(2)}) collective-permute-start(bf16[128,768]{1,0:T(8,128)(2,1)S(1)} %copy-done.12), channel_id=1, source_target_pairs={{0,3},{1,2},{2,1},{3,0},{4,7},{5,6},{6,5},{7,4},{8,11},{9,10},{10,... | collective-permute-start | bytes 589832 | tf_op jit(solution)/shard_map/ppermute | solution.py:816
  294.7 10.7 %all-to-all-start.7 = ((f32[32,1,128]{2,1,0:T(1,128)}), f32[32,1,128]{2,1,0:T(1,128)S(1)}, u32[]{:S(2)}, u32[]{:S(2)}) async-start(f32[32,1,128]{2,1,0:T(1,128)} %broadcast_in_dim_broadcast_in_dim_broadcast_in_dim.3), calls=%async_computation.7 | async-start | bytes 32768 | tf_op jit(solution)/shard_map/all_to_all | solution.py:791
  (26 other events, 166.5 us)
where the time goes:
time: 317 us; the launch traced here: 311 us
  waiting for transfers between devices  122 us (38%)
  Pallas kernels  93.9 us (30%)
  starting transfers between devices  62.7 us (20%)
  other arithmetic  21.1 us (7%)
  local copies, waits for them, and re-layouts  7.36 us (2%)
  between operations  3.96 us (1%)
    pallas_call x11, Pallas kernels, call(): pl.pallas_call(kernel, out_shape=[pltpu.HBM(o.shape, o.dtype) if kind in...  93.9 us
    ppermute x36, waiting for transfers between devices, send(): return lax.ppermute(values, AXES, perm)  57.3 us
    ppermute x12, waiting for transfers between devices, swap(): lax.ppermute(values, 'seq', [(i, i ^ number) for i in range(plan.seq)])  32.6 us
    all_to_all x6, starting transfers between devices, along_z(): lax.all_to_all(values, 'dp', 0, 0, axis_index_groups=plan.groups, tiled=T...  25.2 us
    ppermute x36, starting transfers between devices, send(): return lax.ppermute(values, AXES, perm)  22.8 us
    all_to_all x6, waiting for transfers between devices, along_z(): lax.all_to_all(values, 'dp', 0, 0, axis_index_groups=plan.groups, tiled=T...  20.1 us
    ppermute x12, starting transfers between devices, swap(): lax.ppermute(values, 'seq', [(i, i ^ number) for i in range(plan.seq)])  8.41 us
    convert_element_type x3, other arithmetic, fold(): add(keep[:size], got[:size]).astype(BF)  7.39 us
  transfers between devices with their start and end apart: 56, of which 26 were waited for; matrix products, arithmetic and copies ran while one was open for 5% of the time, Pallas kernels for 22%

commit v1 on v0

v1 whole, which is shorter than its diff:
```python
from functools import partial

import jax
import jax.numpy as jnp
from jax import lax
from jax.experimental import pallas as pl
from jax.experimental.pallas import tpu as pltpu
from jax.sharding import PartitionSpec as P

D = 768
H = 12
HD = 64
FF = 3072
STEP = 7
HALF = D // 2
PAIRS = H // 2
BLOCKS = 4
BF = jnp.bfloat16
F32 = jnp.float32
AXES = ("dp", "seq")
clip_limit = 1.0
MIB = 2**20

VM = pl.BlockSpec(memory_space=pltpu.VMEM)
ANY = pl.BlockSpec(memory_space=pl.ANY)
FAR = pl.BlockSpec(memory_space=pltpu.HBM)


def dot(left, right, left_dim, right_dim):
    return lax.dot_general(
        left, right, (((left_dim,), (right_dim,)), ((), ())), preferred_element_type=F32
    )


def shape(dims, kind):
    return jax.ShapeDtypeStruct(dims, kind)


class Plan:
    def __init__(self, mesh, rows_each):
        self.dp = mesh.shape["dp"]
        self.seq = mesh.shape["seq"]
        self.count = self.dp * self.seq
        self.fast = (
            self.seq == 4
            and self.dp % 2 == 0
            and BLOCKS * 8 == self.count
            and (2 * D // self.count) % 16 == 0
        )
        self.nz = self.dp // 2
        self.rows = D // self.count
        self.far = FF // self.count
        both = range(self.count)
        self.core = [(d, d ^ 1) for d in both]
        self.first = [(d, d ^ (2 if d % 2 == 0 else 4)) for d in both]
        self.second = [(d, d ^ (4 if d % 2 == 0 else 2)) for d in both]
        self.groups = [list(range(low, self.dp, 2)) for low in range(2)]

    def wide(self, rows, columns):
        if self.fast:
            return (self.nz, 4, 2 * rows // self.count, columns)
        return (BLOCKS, 1, rows // BLOCKS, columns)

    def parts(self):
        return 8 if self.fast else 1

    def grads(self, rows, columns):
        if self.fast:
            half = shape((4, self.nz, rows // self.count, columns), BF)
            return [half, half]
        return [shape((rows, columns), BF)]

    def outs(self):
        return 2 if self.fast else 1

    def bands(self):
        return self.seq if self.fast else 1

    def band_shapes(self, length):
        return [shape((length // self.bands(), D), BF)] * self.bands()


def place():
    seq = lax.axis_index("seq")
    return seq & 1, seq >> 1, lax.axis_index("dp") & 1


def start_parts(plan, parts, whole, sems, pieces, blocks=None):
    blocks = slice(None) if blocks is None else pl.ds(blocks[0], len(blocks))
    for index, (first, size, to) in enumerate(pieces):
        columns = pl.ds(first, size)
        if len(parts) == 1:
            for half in range(2):
                pltpu.make_async_copy(
                    parts[0].at[half, blocks, :, :, columns], whole.at[..., pl.ds(to + half * size, size)], sems.at[index]
                ).start()
            continue
        core, mine_x, mine_y = place()
        for number, part in enumerate(parts):
            owner = core if number < 4 else 1 - core
            one, two = (number >> 1) & 1, number & 1
            off_x = jnp.where(owner == 0, one, two)
            off_y = jnp.where(owner == 0, two, one)
            spot = (mine_y ^ off_y) * 2 + (mine_x ^ off_x)
            target = pl.ds(pl.multiple_of(to + owner * size, 128), size)
            pltpu.make_async_copy(part.at[blocks, :, columns], whole.at[:, spot, :, target], sems.at[index]).start()


def wait_part(whole, sems, index, piece):
    view = whole.at[..., pl.ds(piece[2], 2 * piece[1])]
    pltpu.make_async_copy(view, view, sems.at[index]).wait()


def band(plan, number, length):
    if plan.bands() == 1:
        return pl.ds(0, length)
    size = length // plan.bands()
    return pl.ds(pl.multiple_of((lax.axis_index("seq") ^ number) * size, size), size)


def load_bands(plan, refs, whole, sems):
    copies = []
    for number, ref in enumerate(refs):
        source = ref.at[lax.axis_index("seq")] if number == 0 and plan.bands() > 1 else ref
        target = whole.at[band(plan, number, whole.shape[0]), :]
        copies.append(pltpu.make_async_copy(source, target, sems.at[number]))
    for copy in copies:
        copy.start()
    return copies


def flat(value):
    return value.reshape(-1, value.shape[-1])


def held_grad(plan, rows, columns):
    one = plan.grads(rows, columns)
    return pltpu.VMEM((len(one), *one[0].shape), BF)


def put_grad(held, outs, sems, held_view, out_view):
    copies = [
        pltpu.make_async_copy(held.at[(i, *held_view)], out.at[out_view], sems.at[i]) for i, out in enumerate(outs)
    ]
    for copy in copies:
        copy.start()
    return copies


def store_grad(plan, tile, held, rows, first_row, columns):
    if not plan.fast:
        held[0, pl.ds(first_row, tile.shape[0]), columns] = tile.astype(BF)
        return
    core, mine_x, mine_y = place()
    step = rows // plan.count

    def spot(pair, owner):
        off_x = (pair & 1) ^ mine_x
        off_y = ((pair >> 1) & 1) ^ mine_y
        return (off_x * 2 + off_y if owner == 0 else off_y * 2 + off_x), pair >> 2

    for local in range(tile.shape[0] // (2 * step)):
        pair = first_row // (2 * step) + local
        low = tile[2 * step * local : 2 * step * local + step]
        high = tile[2 * step * local + step : 2 * step * (local + 1)]
        held[core, *spot(pair, 0), :, columns] = low.astype(BF)
        held[1 - core, *spot(pair, 1), :, columns] = high.astype(BF)


class Io:
    def __init__(self, ins, outs, held_in, held_out, in_sems, out_sems):
        self.loads, self.running = {}, []
        for number, (index, ref, cut) in enumerate(ins):
            source = ref if cut is None else ref.at[:, pl.ds(*cut)]
            self.loads[index] = pltpu.make_async_copy(source, held_in[number], in_sems.at[number])
        self.outs = {
            index: (held_out[number], ref, out_sems.at[number]) for number, (index, ref) in enumerate(outs)
        }
        self.shipped = []

    def start(self, *indices):
        for index in indices or [i for i in self.loads if i not in self.running]:
            self.loads[index].start()
            self.running.append(index)

    def need(self, *indices):
        for index in indices:
            self.loads.pop(index).wait()

    def ship(self, index, columns=None):
        held, ref, sem = self.outs[index]
        if columns is None:
            pltpu.make_async_copy(held, ref, sem).start()
        else:
            pltpu.make_async_copy(held.at[..., columns], ref.at[..., columns], sem).start()
        if index not in self.shipped:
            self.shipped.append(index)

    def finish(self):
        self.need(*list(self.loads))
        for index in self.outs:
            if index not in self.shipped:
                self.ship(index)
        for held, ref, sem in self.outs.values():
            pltpu.make_async_copy(held, ref, sem).wait()


def call(name, body, ins, outs, scratch, limit, cost=10**11, aliases=None):
    staged_in = [i for i, item in enumerate(ins) if item[1] == "far"]
    staged_out = [i for i, item in enumerate(outs) if item[1] == "far"]
    cuts = {i: (ins[i][2] if len(ins[i]) > 2 else None) for i in staged_in}

    def held_shape(i):
        array = ins[i][0]
        dims = array.shape if cuts[i] is None else (array.shape[0], cuts[i][1])
        return pltpu.VMEM(dims, array.dtype)

    specs = {"near": VM, "far": FAR, "raw": FAR, "any": ANY}
    n_in, n_out, n_scratch = len(ins), len(outs), len(scratch)

    def kernel(*refs):
        in_refs, refs = list(refs[:n_in]), refs[n_in:]
        out_refs, refs = list(refs[:n_out]), refs[n_out:]
        own, refs = refs[:n_scratch], refs[n_scratch:]
        held_in, refs = refs[: len(staged_in)], refs[len(staged_in) :]
        held_out, refs = refs[: len(staged_out)], refs[len(staged_out) :]
        in_sems, out_sems = refs
        io = Io(
            [(i, in_refs[i], cuts[i]) for i in staged_in],
            [(i, out_refs[i]) for i in staged_out],
            held_in, held_out, in_sems, out_sems,
        )
        for number, i in enumerate(staged_in):
            in_refs[i] = held_in[number]
        for number, i in enumerate(staged_out):
            out_refs[i] = held_out[number]
        body(io, in_refs, out_refs, *own)
        io.finish()

    args = [
        pltpu.with_memory_space_constraint(item[0], pltpu.HBM) if item[1] in ("far", "raw") else item[0]
        for item in ins
    ]
    return pl.pallas_call(
        kernel,
        out_shape=[pltpu.HBM(o.shape, o.dtype) if kind in ("far", "raw") else o for o, kind in outs],
        in_specs=[specs[item[1]] for item in ins],
        out_specs=[specs[kind] for _, kind in outs],
        scratch_shapes=[
            *scratch,
            *[held_shape(i) for i in staged_in],
            *[pltpu.VMEM(outs[i][0].shape, outs[i][0].dtype) for i in staged_out],
            pltpu.SemaphoreType.DMA((max(1, len(staged_in)),)),
            pltpu.SemaphoreType.DMA((max(1, len(staged_out)),)),
        ],
        input_output_aliases=aliases or {},
        compiler_params=pltpu.CompilerParams(vmem_limit_bytes=limit * MIB),
        cost_estimate=pl.CostEstimate(flops=cost, bytes_accessed=1, transcendentals=0),
        name=name,
    )(*args)


def far(*arrays):
    return [(array, "far") for array in arrays]


def norm_of(values):
    center = values - jnp.mean(values, axis=-1, keepdims=True)
    inverse = lax.rsqrt(jnp.mean(center * center, axis=-1, keepdims=True) + 1e-05)
    return center * inverse, inverse


def norm_back(upstream, normed, inverse, gain):
    scaled = upstream * gain
    return inverse * (
        scaled
        - jnp.mean(scaled, axis=-1, keepdims=True)
        - normed * jnp.mean(scaled * normed, axis=-1, keepdims=True)
    )


def fill_bias(plan, bias, seg_ref, pad_ref):
    length = bias.shape[0]
    row = pl.ds(lax.axis_index("seq"), 1)
    seg, pad = seg_ref[row, :], pad_ref[row, :]
    code = (2 * seg + pad).astype(F32)
    wanted = (2 * seg + 1).astype(F32)
    coded = jnp.broadcast_to(code, (length, length)).T
    rows = lax.broadcasted_iota(jnp.int32, (length, length), 0)
    cols = lax.broadcasted_iota(jnp.int32, (length, length), 1)
    bias[...] = jnp.where((coded == wanted) | (rows == cols), 0.0, -1e30)


def halves_of(values):
    lane = lax.broadcasted_iota(jnp.int32, values.shape, 1)
    zero = jnp.zeros_like(values)
    return jnp.where(lane < HD, values, zero), jnp.where(lane < HD, zero, values)


def prepare(plan, matrices, norm_params):
    side = jnp.pad(norm_params.T, ((0, 0), (0, 128 - norm_params.shape[0])))
    matrices = [*matrices[0:3], jnp.concatenate([side, side], axis=1), *matrices[3:]]
    groups = [matrices[0:4], matrices[4:6], matrices[6:7]]

    def body(io, ins, outs):
        io.start()
        core = lax.axis_index("seq") & 1
        first = 0
        for number, group in enumerate(groups):
            at = 0
            for index in range(first, first + len(group)):
                io.need(index)
                size = ins[index].shape[1] // 2
                left, right = ins[index][:, :size], ins[index][:, size:]
                mine = jnp.where(core == 0, left, right).astype(BF)
                other = jnp.where(core == 0, right, left).astype(BF)
                outs[2 * number][:, at : at + size] = mine
                outs[2 * number + 1][:, at : at + size] = other
                at += size
            first += len(group)

    outs = []
    for group in groups:
        outs += [(shape((group[0].shape[0], sum(w.shape[1] for w in group) // 2), BF), "near")] * 2
    flat_outs = call("prepare", body, far(*matrices), outs, [], 8)
    return flat_outs[0:2], flat_outs[2:4], flat_outs[4:6]


def other_rows(plan, arrays):
    others = plan.seq - 1

    def body(io, ins, outs, held, in_sems, out_sems):
        mine = lax.axis_index("seq")
        loads = [
            pltpu.make_async_copy(ins[i // others].at[mine ^ (i % others + 1)], held.at[i], in_sems.at[i])
            for i in range(len(outs))
        ]
        for load in loads:
            load.start()
        puts = [pltpu.make_async_copy(held.at[i], outs[i], out_sems.at[i]) for i in range(len(outs))]
        for load, put in zip(loads, puts):
            load.wait()
            put.start()
        for put in puts:
            put.wait()

    part = arrays[0].shape[1:]
    count = others * len(arrays)
    outs = call(
        "other_rows", body, [(a, "raw") for a in arrays], [(shape(part, BF), "raw")] * count,
        [pltpu.VMEM((count, *part), BF), pltpu.SemaphoreType.DMA((count,)), pltpu.SemaphoreType.DMA((count,))],
        8,
    )
    return [outs[i * others : (i + 1) * others] for i in range(len(arrays))]


def row_blocks(length):
    for i in range(length // 128):
        yield slice(i * 128, (i + 1) * 128)


def project(plan, tokens, parts):
    length = tokens[0].size // D if len(tokens) == 1 else tokens[1].shape[0] * len(tokens)
    width = 3 * D + 256
    pieces = [(3 * HALF, 128, 3 * D), *[(m * HALF, HALF, m * D) for m in range(3)]]

    def body(io, ins, outs, whole, rows_in, sems, put_sems):
        h_ref, q_ref, k_ref, v_ref, n_ref, w_ref, x_ref = outs
        start_parts(plan, ins[len(tokens) :], whole, sems, pieces)
        loads = load_bands(plan, ins[: len(tokens)], rows_in, sems.at[pl.ds(4, len(tokens))])
        wait_part(whole, sems, 0, pieces[0])
        norms = flat(whole[:, :, :, 3 * D : 3 * D + 128]).astype(F32).T[0:8]
        n_ref[...] = norms
        for load in loads:
            load.wait()
        puts = [pltpu.make_async_copy(rows_in, x_ref, put_sems.at[1])]
        puts[0].start()
        for rows in row_blocks(length):
            normed, _ = norm_of(rows_in[rows, :].astype(F32))
            h_ref[rows, :] = (normed * norms[0:1, :] + norms[1:2, :]).astype(BF)
        io.ship(0)
        for m in range(3):
            wait_part(whole, sems, 1 + m, pieces[1 + m])
        puts.append(pltpu.make_async_copy(whole, w_ref, put_sems.at[0]))
        puts[1].start()
        for m, (out, scale) in enumerate(((q_ref, 0.125), (k_ref, 1.0), (v_ref, 1.0))):
            weight = flat(whole[:, :, :, m * D : (m + 1) * D])
            out[...] = (dot(h_ref[...], weight, 1, 0) * scale).astype(BF)
            io.ship(1 + m)
        for put in puts:
            put.wait()

    act = shape((length, D), BF)
    wide = plan.wide(D, width)
    return call(
        "project", body, [*[(t, "any") for t in tokens], *[(p, "any") for p in parts]],
        [*[(act, "far")] * 4, (shape((8, D), F32), "near"), (shape(wide, BF), "raw"), (act, "raw")],
        [
            pltpu.VMEM(wide, BF), pltpu.VMEM((length, D), BF),
            pltpu.SemaphoreType.DMA((4 + len(tokens),)), pltpu.SemaphoreType.DMA((2,)),
        ],
        20, 1,
    )


def mix(plan, query, key, value, seg, pad):
    length = query.shape[0]

    def body(io, ins, outs, bias):
        q_ref, k_ref, v_ref, seg_ref, pad_ref = ins
        at_ref, a_ref, l_ref = outs
        io.start()
        fill_bias(plan, bias, seg_ref, pad_ref)
        io.need(0, 1, 2)

        @pl.loop(0, PAIRS, unroll=True)
        def _(p):
            cols = pl.ds(pl.multiple_of(p * 128, 128), 128)
            keys = k_ref[:, cols]
            turned = v_ref[:, cols].T
            for half, query in enumerate(halves_of(q_ref[:, cols])):
                scores = dot(keys, query, 1, 1) + bias[...]
                top = jnp.max(scores, axis=0, keepdims=True)
                lifted = jnp.exp(scores - top)
                total = jnp.sum(lifted, axis=0, keepdims=True)
                soft = (lifted * (1.0 / total)).astype(BF)
                mixed = dot(turned[half * HD : (half + 1) * HD], soft, 1, 0)
                at_ref[pl.ds(pl.multiple_of(p * 128 + half * HD, HD), HD), :] = mixed.astype(BF)
                l_ref[pl.ds(2 * p + half, 1), :] = top + jnp.log(total)
            a_ref[:, cols] = at_ref[pl.ds(pl.multiple_of(p * 128, 128), 128), :].T

    return call(
        "mix", body, [*far(query, key, value), (seg, "near"), (pad, "near")],
        [(shape((D, length), BF), "far"), (shape((length, D), BF), "far"), (shape((H, length), F32), "far")],
        [pltpu.VMEM((length, length), F32)],
        14,
    )


def widen(plan, tokens, mixed, norms, parts):
    length = tokens.shape[0]
    pieces = [(0, HALF, 0), (HALF, 2 * D, D)]

    def body(io, ins, outs, whole, sems, put_sems):
        x_ref, a_ref, n_ref, *part_refs = ins
        m_ref, h_ref, z_ref, s_ref, w_ref = outs
        io.start(1)
        start_parts(plan, part_refs, whole, sems, pieces[:1])
        io.start(0)
        start_parts(plan, part_refs, whole, sems.at[pl.ds(1, 1)], pieces[1:])
        io.need(0, 1)
        wait_part(whole, sems, 0, pieces[0])
        m_ref[...] = x_ref[...].astype(F32) + dot(a_ref[...], flat(whole[:, :, :, 0:D]), 1, 0)
        io.ship(0)
        for rows in row_blocks(length):
            normed, _ = norm_of(m_ref[rows, :])
            h_ref[rows, :] = (normed * n_ref[2:3, :] + n_ref[3:4, :]).astype(BF)
        io.ship(1)
        wait_part(whole, sems, 1, pieces[1])
        put = pltpu.make_async_copy(whole, w_ref, put_sems.at[0])
        put.start()
        for block in range(BLOCKS):
            cols = slice(block * D, (block + 1) * D)
            up = dot(h_ref[...], flat(whole[:, :, :, (block + 1) * D : (block + 2) * D]), 1, 0)
            bell = 0.5 + 0.5 * lax.erf(up * 0.7071067811865476)
            z_ref[:, cols] = (up * bell).astype(BF)
            s_ref[:, cols] = (bell + up * (jnp.exp(-0.5 * up * up) * 0.3989422804014327)).astype(BF)
            io.ship(2, pl.ds(block * D, D))
            io.ship(3, pl.ds(block * D, D))
        put.wait()

    act = shape((length, D), BF)
    wide = plan.wide(D, D + FF)
    hidden = shape((length, FF), BF)
    outs = [shape((length, D), F32), act, hidden, hidden]
    return call(
        "widen", body, [*far(tokens, mixed), (norms, "near"), *[(p, "any") for p in parts]],
        [*[(o, "far") for o in outs], (shape(wide, BF), "raw")],
        [pltpu.VMEM(wide, BF), pltpu.SemaphoreType.DMA((2,)), pltpu.SemaphoreType.DMA((1,))],
        28,
    )


def grad_of_down(plan, hidden, cot):
    length = hidden.shape[0]

    def body(io, ins, outs, g_in, z_in, sems, z_sems, put_sems, g_sem, held):
        z_ref, *bands = ins
        *grads, g_out = outs
        loads = load_bands(plan, bands, g_in, sems)
        z_loads = [
            pltpu.make_async_copy(z_ref.at[:, pl.ds(i * D, D)], z_in.at[:, pl.ds(i * D, D)], z_sems.at[i])
            for i in range(BLOCKS)
        ]
        for load in z_loads:
            load.start()
        for load in loads:
            load.wait()
        puts = [pltpu.make_async_copy(g_in, g_out, g_sem.at[0])]
        puts[0].start()
        for block in range(BLOCKS):
            z_loads[block].wait()
            tile = dot(z_in[:, block * D : (block + 1) * D], g_in[...], 0, 0)
            store_grad(plan, tile, held, FF, block * D, slice(None))
            view = (slice(None), pl.ds(block, 1)) if plan.fast else (pl.ds(block * D, D),)
            puts += put_grad(held, grads, put_sems.at[block], view, view)
        for put in puts:
            put.wait()

    act = shape((length, D), BF)
    grads = plan.grads(FF, D)
    return call(
        "grad_of_down", body, [(hidden, "raw"), *[(c, "any") for c in cot]],
        [*[(g, "raw") for g in grads], (act, "raw")],
        [
            pltpu.VMEM((length, D), BF), pltpu.VMEM((length, FF), BF),
            pltpu.SemaphoreType.DMA((len(cot),)), pltpu.SemaphoreType.DMA((BLOCKS,)),
            pltpu.SemaphoreType.DMA((BLOCKS, len(grads))), pltpu.SemaphoreType.DMA((1,)),
            held_grad(plan, FF, D),
        ],
        28,
    )


def narrow(plan, blocks, mid, below, grads, low, hidden, slope, cot, whole_ou, parts_down):
    length = mid.shape[0]
    count = len(blocks)
    start, final = blocks[0] == 0, blocks[-1] == BLOCKS - 1
    cut = (blocks[0] * D, count * D)
    n_out = plan.outs()

    def body(io, ins, outs, *scratch):
        m_ref, h_ref, z_ref, s_ref, g_ref, up_ref, *rest = ins
        downs = rest[: len(parts_down)]
        b_ref, *grad_refs = outs[: 1 + n_out]
        o_refs = outs[1 + n_out :]
        held, du_ref, acc, whole_up, whole_down, sems, put_sems = scratch
        copies = []
        down = (0, HALF, 0)
        io.start(4)
        start_parts(plan, downs, whole_down, sems.at[pl.ds(0, 1)], [down], blocks)
        io.start(3, 1)
        up = pltpu.make_async_copy(up_ref.at[..., pl.ds(D + cut[0], cut[1])], whole_up, sems.at[1])
        up.start()
        io.start()
        io.need(4)
        wait_part(whole_down, sems, 0, down)
        io.need(3, 1)
        for number, block in enumerate(blocks):
            local = slice(number * D, (number + 1) * D)
            back = dot(g_ref[...], flat(whole_down[number]), 1, 1)
            du_ref[:, local] = (back * s_ref[:, local]).astype(BF)
            tile = dot(h_ref[...], du_ref[:, local], 0, 0)
            store_grad(plan, tile, held, D, 0, local)
            views = [(*[slice(None)] * (plan.grads(D, D)[0].ndim - 1), pl.ds(at * D, D)) for at in (number, block)]
            copies += put_grad(held, grad_refs, put_sems.at[number], *views)
        up.wait()
        lower = dot(du_ref[...], flat(whole_up[...]), 1, 1)
        if start:
            b_ref[...] = lower
        else:
            io.need(6 + len(parts_down))
            b_ref[...] = rest[len(parts_down)][...] + lower
        io.ship(0)
        io.need(0, 2)
        gain = m_ref[...] + dot(z_ref[...], whole_down[...].reshape(count * D, D), 1, 0)
        if final:
            acc[...] = gain
            for number, o_ref in enumerate(o_refs):
                o_ref[...] = acc[band(plan, number, length), :].astype(BF)
        else:
            o_refs[0][...] = gain
        for copy in copies:
            copy.wait()

    deep = plan.wide(FF, D)
    ins = [
        *far(mid, low), (hidden, "far", cut), (slope, "far", cut), *far(cot), (whole_ou, "raw"),
        *[(p, "any") for p in parts_down],
    ]
    aliases = {}
    if not start:
        ins += far(below)
        aliases = {len(ins) + i: 1 + i for i in range(n_out)}
        ins += [(g, "raw") for g in grads]
    return call(
        "narrow" + str(blocks[0]), body, ins,
        [
            (shape((length, D), F32), "far"), *[(g, "raw") for g in plan.grads(D, FF)],
            *[(o, "far") for o in (plan.band_shapes(length) if final else [shape((length, D), F32)])],
        ],
        [
            held_grad(plan, D, count * D),
            pltpu.VMEM((length, count * D), BF),
            pltpu.VMEM((length, D), F32),
            pltpu.VMEM(plan.wide(D, count * D), BF),
            pltpu.VMEM((count, *deep[1:]), BF),
            pltpu.SemaphoreType.DMA((2,)),
            pltpu.SemaphoreType.DMA((count, n_out)),
        ],
        40, aliases=aliases,
    )


def turn(plan, mid, back, cot, norms, whole_ou):
    length = mid.shape[0]

    def body(io, ins, outs, whole, sems):
        m_ref, b_ref, g_ref, n_ref, w_ref = ins
        x_ref, low, d_ref, s_ref = outs
        io.start()
        load = pltpu.make_async_copy(w_ref.at[..., pl.ds(0, D)], whole, sems.at[0])
        load.start()
        s_ref[...] = jnp.zeros_like(s_ref)
        io.need(0, 1, 2)
        for rows in row_blocks(length):
            normed, inverse = norm_of(m_ref[rows, :])
            upstream = b_ref[rows, :]
            total = g_ref[rows, :].astype(F32) + norm_back(upstream, normed, inverse, n_ref[2:3, :])
            x_ref[rows, :] = total
            low[rows, :] = total.astype(BF)
            s_ref[0:1, :] += jnp.sum(upstream * normed, axis=0, keepdims=True)
            s_ref[1:2, :] += jnp.sum(upstream, axis=0, keepdims=True)
        io.ship(0)
        io.ship(1)
        load.wait()
        d_ref[...] = dot(low[...], flat(whole[...]), 1, 1).astype(BF)

    act = shape((length, D), BF)
    return call(
        "turn", body, [*far(mid, back, cot), (norms, "near"), (whole_ou, "raw")],
        [(shape((length, D), F32), "far"), (act, "far"), (act, "far"), (shape((2, D), F32), "near")],
        [pltpu.VMEM(plan.wide(D, D), BF), pltpu.SemaphoreType.DMA((1,))],
        24,
    )


def attend_back(plan, side, low, query, key, value, lse, cot, seg, pad, extra=()):
    length = low.shape[0]
    width = 3 * HALF + (D if extra else 0)
    cut = (side * HALF, HALF)

    def body(io, ins, outs, bias, held, put_sems):
        h_ref, q_ref, k_ref, v_ref, c_ref, l_ref, seg_ref, pad_ref, *more = ins
        d_ref, *grads = outs
        io.start(1, 2, 3, 4, 5)
        io.start()
        fill_bias(plan, bias, seg_ref, pad_ref)
        io.need(1, 2, 3, 4, 5)

        @pl.loop(0, PAIRS // 2)
        def _(local):
            p = local + side * (PAIRS // 2)
            first = pl.multiple_of(local * 128, 128)
            cols = pl.ds(first, 128)
            keys, values = k_ref[:, cols], v_ref[:, cols]
            turned = keys.T
            queries, cots = halves_of(q_ref[:, cols]), halves_of(c_ref[:, cols])
            dv = dk = None
            dqs = []
            for half in range(2):
                scores = dot(keys, queries[half], 1, 1) + bias[...]
                soft = jnp.exp(scores - l_ref[pl.ds(2 * p + half, 1), :])
                gain = dot(soft.astype(BF), cots[half], 1, 0)
                dv = gain if dv is None else dv + gain
                dp = dot(values, cots[half], 1, 1)
                share = jnp.sum(soft * dp, axis=0, keepdims=True)
                ds = (soft * (dp - share)).astype(BF)
                gain = dot(ds, queries[half], 1, 0)
                dk = gain if dk is None else dk + gain
                dqs.append(dot(turned[half * HD : (half + 1) * HD], ds, 1, 0) * 0.125)
            d_ref[:, cols] = jnp.concatenate(dqs, axis=0).T.astype(BF)
            d_ref[:, pl.ds(first + HALF, 128)] = dk.astype(BF)
            d_ref[:, pl.ds(first + 2 * HALF, 128)] = dv.astype(BF)

        io.ship(0)
        io.need(0)
        lead, copies = [slice(None)] * (len(grads[0].shape) - 1), []
        if extra:
            io.need(8, 9)
            tile = dot(more[0][...], more[1][...], 1, 0)
            store_grad(plan, tile, held, D, 0, slice(3 * HALF, width))
            view = (*lead, pl.ds(3 * HALF, D))
            copies += put_grad(held, grads, put_sems.at[3], view, view)
        for m in range(3):
            cols = slice(m * HALF, (m + 1) * HALF)
            store_grad(plan, dot(h_ref[...], d_ref[:, cols], 0, 0), held, D, 0, cols)
            view = (*lead, pl.ds(m * HALF, HALF))
            copies += put_grad(held, grads, put_sems.at[m], view, view)
        for copy in copies:
            copy.wait()

    return call(
        "attend_back" + str(side), body,
        [
            *far(low), *[(a, "far", cut) for a in (query, key, value, cot)], *far(lse),
            (seg, "near"), (pad, "near"), *far(*extra),
        ],
        [(shape((length, 3 * HALF), BF), "far"), *[(g, "raw") for g in plan.grads(D, width)]],
        [
            pltpu.VMEM((length, length), F32), held_grad(plan, D, width),
            pltpu.SemaphoreType.DMA((4, plan.outs())),
        ],
        26,
    )


def finish_tokens(plan, tokens, spreads, mid_cot, norms, whole_qkv):
    length = tokens.shape[0]

    def body(io, ins, outs, back, whole, sems):
        x_ref, d0_ref, d1_ref, c_ref, n_ref, w_ref = ins
        *o_refs, s_ref = outs
        io.start(1, 2)
        load = pltpu.make_async_copy(w_ref.at[..., pl.ds(0, 3 * D)], whole, sems.at[0])
        load.start()
        io.start()
        s_ref[...] = jnp.zeros_like(s_ref)
        io.need(1, 2)
        load.wait()
        back[...] = sum(
            dot(
                jnp.concatenate([d[:, m * HALF : (m + 1) * HALF] for d in (d0_ref, d1_ref)], axis=1),
                flat(whole[:, :, :, m * D : (m + 1) * D]), 1, 1,
            )
            for m in range(3)
        )
        io.need(0, 3)
        for rows in row_blocks(length):
            normed, inverse = norm_of(x_ref[rows, :].astype(F32))
            upstream = back[rows, :]
            c_ref[rows, :] += norm_back(upstream, normed, inverse, n_ref[0:1, :])
            s_ref[0:1, :] += jnp.sum(upstream * normed, axis=0, keepdims=True)
            s_ref[1:2, :] += jnp.sum(upstream, axis=0, keepdims=True)
        for number, o_ref in enumerate(o_refs):
            o_ref[...] = c_ref[band(plan, number, length), :].astype(BF)

    return call(
        "finish_tokens", body, [*far(tokens, *spreads, mid_cot), (norms, "near"), (whole_qkv, "raw")],
        [*[(o, "far") for o in plan.band_shapes(length)], (shape((2, D), F32), "near")],
        [pltpu.VMEM((length, D), F32), pltpu.VMEM(plan.wide(D, 3 * D), BF), pltpu.SemaphoreType.DMA((1,))],
        20, 1,
    )


def sum_up(plan, blocks, others, slices):
    nz, rows, columns = blocks.shape
    wide = 4 * D // plan.count

    def body(io, ins, outs, held, sems):
        blocks_ref, others_ref, slice_ref = ins
        g_ref, card_ref = outs
        loads = [pltpu.make_async_copy(blocks_ref.at[i], held.at[i], sems.at[i]) for i in range(nz)]
        for load in loads:
            load.start()
        for load in loads:
            load.wait()
        value = jnp.sum(held[...].astype(F32), axis=0)
        g_ref[...] = value
        left = jnp.sum(jnp.sum(value * value, axis=0, keepdims=True), axis=1, keepdims=True) + others_ref[0:1, 0:1]
        lane = lax.broadcasted_iota(jnp.int32, slice_ref.shape, 1)
        card = slice_ref[...]
        for i in range(3):
            piece = left.astype(BF).astype(F32)
            card = jnp.where(lane == wide + i, piece, card)
            left = left - piece
        card = card.astype(BF)
        for i in range(plan.count):
            card_ref[i] = card

    return call(
        "sum_up", body, [(blocks, "any"), (others, "near"), (slices, "near")],
        [(shape((rows, columns), F32), "near"), (shape((plan.count, *slices.shape), BF), "near")],
        [pltpu.VMEM(blocks.shape, BF), pltpu.SemaphoreType.DMA((nz,))], 8,
    )


def update(plan, grads, cards, masters, firsts, seconds, passed):
    rates = [D**-0.5] * 3 + [4.0 * D**-0.5, D**-0.5, FF**-0.5, 0.2]
    decays = [0.01] * 6 + [0.0]
    count = len(masters)
    given = len(grads)

    def body(io, ins, outs, total, sems):
        grad_refs, card_ref = ins[:given], ins[given]
        first = given + 1
        io.start(*(first + k * count + i for i in reversed(range(count)) for k in range(3)))
        io.start()
        total[...] = jnp.sum(card_ref[...].astype(F32), axis=0)
        rows, wide = total.shape[0], 4 * D // plan.count
        all_norms = total[...]
        lane = lax.broadcasted_iota(jnp.int32, all_norms.shape, 1)
        own = jnp.where(lane < wide, all_norms * all_norms, all_norms * (1.0 / rows))
        square = jnp.sum(jnp.sum(own, axis=0, keepdims=True), axis=1, keepdims=True)
        norm = jnp.sqrt(square)
        outs[0][...] = jnp.broadcast_to(norm, outs[0].shape)
        factor = jnp.minimum(1.0, clip_limit / (norm + 1e-06))
        mine = total[pl.ds(lax.axis_index("dp") * plan.seq + lax.axis_index("seq"), 1), :]
        each = wide // 4
        grad_norms = jnp.concatenate([mine[:, p * each : (p + 1) * each] for p in range(4)], axis=0)
        for i in reversed(range(count)):
            w_ref, m_ref, s_ref = (ins[first + k * count + i] for k in range(3))
            io.need(*(first + k * count + i for k in range(3)))
            if i < 3:
                cols = [
                    (slice(h * HALF, (h + 1) * HALF), grad_refs[0][:, (5 * h + i) * HALF : (5 * h + i + 1) * HALF])
                    for h in range(2)
                ]
            elif i == 3:
                cols = [(slice(None), grad_refs[0][:, 3 * HALF : 5 * HALF])]
            elif i < 6:
                cols = [(slice(None), grad_refs[i - 3][...])]
            else:
                cols = [(slice(None), grad_norms)]
            for where, grad in cols:
                clipped = factor * grad
                one = 0.5 * m_ref[:, where] + 0.5 * clipped
                two = 0.55 * s_ref[:, where] + 0.45 * clipped * clipped
                root = jnp.sqrt(two * (1.0 / (1.0 - 0.55**STEP))) + 1e-08
                weight = w_ref[:, where]
                step = (one * (1.0 / (1.0 - 0.5**STEP))) / root + decays[i] * weight
                outs[1 + i][:, where] = weight - rates[i] * step
                outs[1 + count + i][:, where] = one
                outs[1 + 2 * count + i][:, where] = two
            for k in range(3):
                io.ship(1 + k * count + i)
        last = first + 3 * count
        copies = []
        for number in range(len(passed)):
            which, place_in = number // plan.bands(), number % plan.bands()
            io.need(last + number)
            target = outs[1 + 3 * count + which]
            if plan.bands() > 1:
                target = target.at[lax.axis_index("seq") ^ place_in]
            copies.append(pltpu.make_async_copy(ins[last + number], target, sems.at[number]))
            copies[-1].start()
        for copy in copies:
            copy.wait()

    like = [(shape(w.shape, F32), "far") for w in masters] * 3
    pieces = [shape((plan.bands(), *p.shape), BF) if plan.bands() > 1 else p for p in passed[:: plan.bands()]]
    return call(
        "update", body, [*[(g, "near") for g in grads], (cards, "near"), *far(*masters, *firsts, *seconds, *passed)],
        [(shape((1, 128), F32), "near"), *like, *[(o, "raw") for o in pieces]],
        [pltpu.VMEM(cards.shape[1:], F32), pltpu.SemaphoreType.DMA((len(passed),))], 20,
    )


def after(values, *others):
    return lax.optimization_barrier((values, others))[0]


def meet(*values):
    return lax.optimization_barrier(values)


def send(plan, values, perm):
    return lax.ppermute(values, AXES, perm)


def block_of(plan, mine, other):
    core = lax.axis_index("seq") & 1
    got = send(plan, other, plan.core)
    return jnp.where(core == 0, jnp.concatenate([mine, got]), jnp.concatenate([got, mine]))


def copies_of(plan, block):
    return jnp.broadcast_to(block[None], (plan.nz, *block.shape))


def along_z(plan, values):
    return lax.all_to_all(values, "dp", 0, 0, axis_index_groups=plan.groups, tiled=True)


def gather_whole(matrices):
    split = [w.reshape(w.shape[0], 2, -1) for w in matrices]
    halves = jnp.concatenate(split, axis=2).transpose(1, 0, 2).astype(BF)
    full = lax.all_gather(halves, AXES, axis=1, tiled=True)
    return [full.reshape(2, BLOCKS, 1, -1, full.shape[-1])]


def add(one, two):
    return one.astype(F32) + two.astype(F32)


def fold(keep, got):
    if keep.ndim == 4:
        keep, got = (v.reshape(-1, *v.shape[2:]) for v in (keep, got))
    size = keep.shape[0] // 2
    return add(keep[size:], got[size:]).astype(BF), add(keep[:size], got[:size]).astype(BF)


def total(blocks):
    return jnp.sum(blocks.astype(F32), axis=0)


def finish(plan, grads, sums, masters, firsts, seconds, *passed):
    wide = sums.shape[0] * D // plan.count
    slices = sums.reshape(sums.shape[0], plan.count, -1).transpose(1, 0, 2).reshape(plan.count, wide)
    slices = jnp.pad(slices, ((0, 0), (0, 128 - wide)))
    if plan.fast:
        blocks, *others = grads
        left = jnp.broadcast_to(sum(jnp.sum(g * g) for g in others), (1, 128))
        left, slices, blocks, early = meet(left, slices, blocks, passed[:-1])
        passed = [*early, passed[-1]]
        last, cards = sum_up(plan, blocks, left, slices)
        grads = [last, *others]
        cards = lax.all_to_all(cards, AXES, 0, 0, tiled=True)
    else:
        left = jnp.broadcast_to(sum(jnp.sum(g * g) for g in grads), (plan.count, 1))
        cards = lax.psum(slices + jnp.pad(left, ((0, 0), (wide, 127 - wide))), AXES)[None]
    norm, *updated, output, input_grad = update(plan, grads, cards, masters, firsts, seconds, passed)
    return (output, input_grad, norm[0, 0], *updated)


def on_device(plan, *args):
    tokens_in, segment_ids, pad_mask, out_grad = args[:4]
    masters, firsts, seconds = args[4:11], args[11:18], args[18:25]
    each, piece, _ = tokens_in.shape
    length = each // plan.seq * plan.seq * piece

    plan.fast = plan.fast and each == plan.seq

    def swap(values, number):
        return lax.ppermute(values, "seq", [(i, i ^ number) for i in range(plan.seq)])

    def to_rows(values, others=None):
        if not plan.fast:
            return [lax.all_to_all(values, "seq", 0, 0, tiled=True).reshape(length, D)]
        return [values, *[swap(other, 1 + n) for n, other in enumerate(others)]]

    def to_pieces(bands):
        if not plan.fast:
            return [lax.all_to_all(bands[0].reshape(each, piece, D), "seq", 0, 0, tiled=True)]
        return [bands[0], *[swap(other, 1 + n) for n, other in enumerate(bands[1:])]]

    seg, pad = segment_ids, pad_mask

    if not plan.fast:
        side = jnp.pad(masters[6].T, ((0, 0), (0, 124)))
        side = jnp.concatenate([side, side], axis=1)
        one, two, three = (gather_whole(m) for m in ([*masters[0:3], side], masters[3:5], masters[5:6]))
        low_one, query, key, value, norms, whole_qkv, tokens = project(plan, to_rows(tokens_in), one)
        mixed_t, mixed, lse = mix(plan, query, key, value, seg, pad)
        mid, low_two, hidden, slope, whole_ou = widen(plan, tokens, mixed, norms, two)
        *g_down, cot = grad_of_down(plan, hidden, to_rows(out_grad))
        back, *g_up, part = narrow(plan, (0, 1), mid, None, None, low_two, hidden, slope, cot, whole_ou, three)
        back, *g_up, result = narrow(plan, (2, 3), part, back, g_up, low_two, hidden, slope, cot, whole_ou, three)
        mid_cot, low_cot, mixed_cot, sums_two = turn(plan, mid, back, cot, norms, whole_ou)
        halves = [
            attend_back(plan, side, low_one, query, key, value, lse, mixed_cot, seg, pad, extra)
            for side, extra in enumerate(((mixed_t, low_cot), ()))
        ]
        stream, sums_one = finish_tokens(plan, tokens, [h[0] for h in halves], mid_cot, norms, whole_qkv)
        grads = [
            lax.psum_scatter(g.astype(F32), AXES, scatter_dimension=0, tiled=True)
            for g in (halves[0][1], halves[1][1], *g_up, *g_down)
        ]
        grads = [jnp.concatenate(grads[:2], axis=1), *grads[2:]]
        sums = jnp.concatenate([sums_one, sums_two], axis=0)
        return finish(plan, grads, sums, masters, firsts, seconds, *to_pieces([result]), *to_pieces([stream]))

    first, second, third = prepare(plan, masters[:6], masters[6])
    block = block_of(plan, *first)
    near_one = along_z(plan, copies_of(plan, block))
    others, others_cot = other_rows(plan, [after(tokens_in, block), out_grad])
    tokens = to_rows(tokens_in, others)
    block_two = block_of(plan, *second)
    spread_two = copies_of(plan, block_two)
    spread_three = copies_of(plan, block_of(plan, *third))
    near_one, tokens, spread_two, spread_three = meet(near_one, tokens, spread_two, spread_three)

    def spread(near):
        return send(plan, near, plan.second), send(plan, near, plan.first)

    def to_core(*parts):
        return [send(plan, part, plan.core) for part in parts]

    beside_one, across_one = spread(near_one)
    near_two = along_z(plan, spread_two)
    beside_one, across_one = meet(beside_one, across_one)
    corner_one = send(plan, beside_one, plan.first)
    one = [near_one, beside_one, across_one]
    one_core = to_core(*one)
    corner_one, one_core = meet(corner_one, one_core)
    one = [*one, corner_one, *one_core, *to_core(corner_one)]
    low_one, query, key, value, norms, whole_qkv, tokens = project(plan, tokens, one)
    cot = to_rows(out_grad, after(others_cot, corner_one))
    near_two, query, cot = meet(near_two, query, cot)
    beside_two, across_two = spread(near_two)
    near_three = along_z(plan, after(spread_three, near_two))
    mixed_t, mixed, lse = mix(plan, query, key, value, seg, pad)
    beside_two, across_two, near_three, mixed, lse, mixed_t = meet(
        beside_two, across_two, near_three, mixed, lse, mixed_t
    )
    corner_two = send(plan, beside_two, plan.first)
    beside_three, across_three = spread(near_three)
    two = [near_two, beside_two, across_two]
    two_core = to_core(*two)
    corner_two, two_core = meet(corner_two, two_core)
    two = [*two, corner_two, *two_core, *to_core(corner_two)]
    mid, low_two, hidden, slope, whole_ou = widen(plan, tokens, mixed, norms, two)
    beside_three, across_three, hidden = meet(beside_three, across_three, hidden)
    corner_three = send(plan, beside_three, plan.first)
    three = [near_three, beside_three, across_three]
    three_core = to_core(*three)
    keep_d, go_d, cot = grad_of_down(plan, hidden, cot)
    corner_three, three_core, keep_d, go_d, cot = meet(corner_three, three_core, keep_d, go_d, cot)
    three = [*three, corner_three, *three_core, *to_core(corner_three)]

    got_d = send(plan, go_d, plan.core)
    back, *g_up, part = narrow(plan, (0, 1), mid, None, None, low_two, hidden, slope, cot, whole_ou, three)
    got_d, back, part = meet(got_d, back, part)
    go_d, keep_d = fold(keep_d, got_d)
    got_d = send(plan, go_d, plan.first)
    part = after(part, go_d)
    back, *rest = narrow(plan, (2, 3), part, back, g_up, low_two, hidden, slope, cot, whole_ou, three)
    got_d, back, rest = meet(got_d, back, rest)
    (keep_u, go_u), result = rest[:2], rest[2:]
    got_u = send(plan, go_u, plan.core)
    go_d, keep_d = fold(keep_d, got_d)
    got_d = send(plan, go_d, plan.second)
    back = after(back, go_d)
    mid_cot, low_cot, mixed_cot, sums_two = turn(plan, mid, back, cot, norms, whole_ou)
    got_u, mixed_cot, low_cot, mid_cot, result = meet(got_u, mixed_cot, low_cot, mid_cot, result)
    go_u, keep_u = fold(keep_u, got_u)
    got_d, go_u = meet(got_d, go_u)
    got_u = send(plan, go_u, plan.first)
    mixed_cot = after(mixed_cot, go_u)
    spread_a, keep_a, go_a = attend_back(
        plan, 0, low_one, query, key, value, lse, mixed_cot, seg, pad, (mixed_t, low_cot)
    )
    got_u, keep_a, spread_a = meet(got_u, keep_a, spread_a)
    got_a = send(plan, go_a, plan.core)
    block_d = add(keep_d, got_d).astype(BF)
    blocks_d = along_z(plan, block_d)
    go_u, keep_u = fold(keep_u, got_u)
    got_u = send(plan, go_u, plan.second)
    go_a, keep_a = fold(keep_a, got_a)
    got_a = send(plan, go_a, plan.first)
    mixed_cot = after(mixed_cot, go_u, go_a, block_d)
    spread_b, keep_b, go_b = attend_back(plan, 1, low_one, query, key, value, lse, mixed_cot, seg, pad)
    blocks_d, got_u, got_a, go_b, keep_b, spread_b = meet(blocks_d, got_u, got_a, go_b, keep_b, spread_b)
    got_b = send(plan, go_b, plan.core)
    block_u = add(keep_u, got_u).astype(BF)
    blocks_u = along_z(plan, block_u)
    go_b, keep_b = fold(keep_b, after(got_b, block_u))
    got_b = send(plan, go_b, plan.first)
    go_a, keep_a = fold(keep_a, after(got_a, go_b))
    got_a = send(plan, go_a, plan.second)
    mid_cot = after(mid_cot, go_a, go_b)
    *stream, sums_one = finish_tokens(plan, tokens, [spread_a, spread_b], mid_cot, norms, whole_qkv)
    got_b, sums_one, stream = meet(got_b, sums_one, stream)
    go_b, keep_b = fold(keep_b, got_b)
    got_b = send(plan, go_b, plan.second)
    got_a = after(got_a, go_b)
    output = to_pieces(after(result, go_b))
    input_grad = to_pieces(after(stream, go_b))
    halves = [add(keep_a, got_a), add(keep_b, got_b)]
    blocks_ab = along_z(plan, jnp.concatenate(halves, axis=2).astype(BF))
    grads = [blocks_ab, total(blocks_u), total(blocks_d)]
    sums = jnp.concatenate([sums_one, sums_two], axis=0)
    return finish(plan, grads, sums, masters, firsts, seconds, *output, *input_grad)


def solution(mesh):
    plan = Plan(mesh, None)
    rows = P(AXES, None)
    weights = (*[rows] * 6, P(None, AXES))
    tokens = P("dp", "seq", None)
    return jax.shard_map(
        partial(on_device, plan),
        mesh=mesh,
        in_specs=(tokens, P("dp", None), P("dp", None), tokens, *weights * 3),
        out_specs=(tokens, tokens, P(), *weights * 3),
        check_vma=False,
    )
```

time: 317 us -> 280 us (0.88)
  waiting for transfers between devices: 122 us -> 87.3 us
  other arithmetic: 21.1 us -> 16.1 us
  starting transfers between devices: 62.7 us -> 67.4 us
    all_to_all x6, waiting for transfers between devices: 20.1 us -> 4.99 us  [along_z(): lax.all_to_all(values, 'dp', 0, 0, axis_index_groups=plan.groups, tiled=T...]
    all_to_all x2 -> x1, waiting for transfers between devices: 11.8 us -> 1.29 us  [finish(): cards = lax.all_to_all(cards, AXES, 0, 0, tiled=True)]
    ppermute x36, waiting for transfers between devices: 57.3 us -> 51.9 us  [send(): return lax.ppermute(values, AXES, perm)]
    unnamed x37 -> x61, local copies, waits for them, and re-layouts: 1.84 us -> 6.13 us
    all_to_all x6, starting transfers between devices: 25.2 us -> 29.1 us  [along_z(): lax.all_to_all(values, 'dp', 0, 0, axis_index_groups=plan.groups, tiled=T...]
    ppermute x12, waiting for transfers between devices: 32.6 us -> 29.2 us  [swap(): lax.ppermute(values, 'seq', [(i, i ^ number) for i in range(plan.seq)])]
    pallas_call x11 -> x14, Pallas kernels: 93.9 us -> 92 us  [call(): pl.pallas_call(kernel, out_shape=[pltpu.HBM(o.shape, o.dtype) if kind in...]
  transfers between devices with their start and end apart: 56 -> 55, of which waited for: 26 -> 32; matrix products, arithmetic and copies ran while one was open for 5% -> 6% of each run, Pallas kernels for 22% -> 31%
where the time goes in v1:
time: 280 us; the launch traced here: 275 us
  Pallas kernels  92 us (33%)
  waiting for transfers between devices  87.3 us (31%)
  starting transfers between devices  67.4 us (24%)
  other arithmetic  16.1 us (6%)
  local copies, waits for them, and re-layouts  9.01 us (3%)
    pallas_call x14, Pallas kernels, call(): pl.pallas_call(kernel, out_shape=[pltpu.HBM(o.shape, o.dtype) if kind in...  92 us
    ppermute x36, waiting for transfers between devices, send(): return lax.ppermute(values, AXES, perm)  51.9 us
    ppermute x12, waiting for transfers between devices, swap(): lax.ppermute(values, 'seq', [(i, i ^ number) for i in range(plan.seq)])  29.2 us
    all_to_all x6, starting transfers between devices, along_z(): lax.all_to_all(values, 'dp', 0, 0, axis_index_groups=plan.groups, tiled=T...  29.1 us
    ppermute x36, starting transfers between devices, send(): return lax.ppermute(values, AXES, perm)  23.6 us
    ppermute x12, starting transfers between devices, swap(): lax.ppermute(values, 'seq', [(i, i ^ number) for i in range(plan.seq)])  9.18 us
    convert_element_type x3, other arithmetic, fold(): add(keep[:size], got[:size]).astype(BF)  6.33 us
    unnamed x61, local copies, waits for them, and re-layouts  6.13 us
  transfers between devices with their start and end apart: 55, of which 32 were waited for; matrix products, arithmetic and copies ran while one was open for 6% of the time, Pallas kernels for 31%

profile of v1, /device:TPU:0, one launch (start us, length us, event | category | flops | bytes accessed | tf_op | source)
XLA Modules:
  0.0 274.5 jit_solution(8354723381809741617)
XLA Ops:
  5.6 6.2 %all-to-all-start = ((bf16[4,48,1280]{2,1,0:T(8,128)(2,1)}), bf16[4,48,1280]{2,1,0:T(8,128)(2,1)S(1)}, u32[]{:S(2)}, u32[]{:S(2)}) async-start(bf16[4,48,1280]{2,1,0:T(8,128)(2,1)} %broadcast_in_dim.8), calls=%async_computation | async-start | bytes 983040 | tf_op jit(solution)/shard_map/all_to_all | solution.py:872
  11.8 2.1 other_rows.1
  14.1 1.6 collective-permute-start.2
  16.0 6.0 %collective-permute-done.2.refs_2_ = bf16[128,768]{1,0:T(8,128)(2,1)S(1)} collective-permute-done((bf16[128,768]{1,0:T(8,128)(2,1)}, bf16[128,768]{1,0:T(8,128)(2,1)S(1)}, u32[]{:S(2)}, u32[]{:S(2)}) %collective-permute-start.2) | collective-permute-done | bytes 196640 | tf_op jit(solution)/shard_map/ppermute | solution.py:925
  22.0 3.3 %collective-permute-done.3.refs_3_ = bf16[128,768]{1,0:T(8,128)(2,1)S(1)} collective-permute-done((bf16[128,768]{1,0:T(8,128)(2,1)}, bf16[128,768]{1,0:T(8,128)(2,1)S(1)}, u32[]{:S(2)}, u32[]{:S(2)}) %collective-permute-start.3) | collective-permute-done | bytes 196640 | tf_op jit(solution)/shard_map/ppermute | solution.py:925
  27.8 1.5 collective-permute-start.7
  29.3 1.5 collective-permute-start.6
  30.9 5.1 %all-to-all-start.1 = ((bf16[4,48,1920]{2,1,0:T(8,128)(2,1)}), bf16[4,48,1920]{2,1,0:T(8,128)(2,1)S(1)}, u32[]{:S(2)}, u32[]{:S(2)}) async-start(bf16[4,48,1920]{2,1,0:T(8,128)(2,1)} %broadcast_in_dim.9), calls=%async_computation.1 | async-start | bytes 1474560 | tf_op jit(solution)/shard_map/all_to_all | solution.py:872
  35.9 5.2 %collective-permute-done.7.refs_6_ = bf16[4,48,1280]{2,1,0:T(8,128)(2,1)S(1)} collective-permute-done((bf16[4,48,1280]{2,1,0:T(8,128)(2,1)S(1)}, bf16[4,48,1280]{2,1,0:T(8,128)(2,1)S(1)}, u32[]{:S(2)}, u32[]{:S(2)}) %collective-permute-start.7) | collective-permute-done | bytes 491552 | tf_op jit(solution)/shard_map/ppermute | solution.py:858
  44.2 6.6 %collective-permute-done.8.refs_7_ = bf16[4,48,1280]{2,1,0:T(8,128)(2,1)S(1)} collective-permute-done((bf16[4,48,1280]{2,1,0:T(8,128)(2,1)S(1)}, bf16[4,48,1280]{2,1,0:T(8,128)(2,1)S(1)}, u32[]{:S(2)}, u32[]{:S(2)}) %collective-permute-start.8) | collective-permute-done | bytes 491552 | tf_op jit(solution)/shard_map/ppermute | solution.py:858
  54.0 5.4 %project.1 = (bf16[512,768]{1,0:T(8,128)(2,1)}, bf16[512,768]{1,0:T(8,128)(2,1)}, bf16[512,768]{1,0:T(8,128)(2,1)}, bf16[512,768]{1,0:T(8,128)(2,1)}, f32[8,768]...) custom-call(bf16[4,128,768]{2,1,0:T(8,128)(2,1)S(1)} %copy-done, ...), custom_call_target="tpu_custom_call" | custom-call | flops 1 | bytes 1 | tf_op jit(solution)/shard_map/project/pallas_call | solution.py:244
  59.5 2.3 collective-permute-done.15.refs_4_
  64.1 1.7 collective-permute-start.16
  65.8 5.0 %all-to-all-start.2 = ((bf16[4,192,384]{2,1,0:T(8,128)(2,1)}), bf16[4,192,384]{2,1,0:T(8,128)(2,1)}, u32[]{:S(2)}, u32[]{:S(2)}) async-start(bf16[4,192,384]{2,1,0:T(8,128)(2,1)} %broadcast_in_dim.10), calls=%async_computation.2 | async-start | bytes 1179648 | tf_op jit(solution)/shard_map/all_to_all | solution.py:872
  70.8 9.8 %mix.1 = (bf16[768,512]{1,0:T(8,128)(2,1)}, bf16[512,768]{1,0:T(8,128)(2,1)}, f32[12,512]{1,0:T(8,128)}) custom-call(bf16[512,768]{1,0:T(8,128)(2,1)} %get-tuple-element.242.refs_0_.refs_1_, bf16[512,768]{1,0:T(8,128)(2,1)} %get-tuple-element.243.refs_1_.refs_2_, bf16[512,768]{1,0:T(8,128)(2,1)} %get-tuple-element.244.refs_2_.refs_3_, ...), custom_call_target="tpu_custom_call" | custom-call | flops 99999997952 | bytes 1 | tf_op jit(solution)/shard_map/mix/pallas_call | solution.py:244
  81.5 4.9 %all-to-all-done.2.refs_6_ = bf16[4,192,384]{2,1,0:T(8,128)(2,1)} async-done(((bf16[4,192,384]{2,1,0:T(8,128)(2,1)}), bf16[4,192,384]{2,1,0:T(8,128)(2,1)}, u32[]{:S(2)}, u32[]{:S(2)}) %all-to-all-start.2) | async-done | bytes 589856 | tf_op jit(solution)/shard_map/all_to_all | solution.py:872
  89.9 9.6 %collective-permute-done.20.refs_6_ = bf16[4,48,1920]{2,1,0:T(8,128)(2,1)S(1)} collective-permute-done((bf16[4,48,1920]{2,1,0:T(8,128)(2,1)}, bf16[4,48,1920]{2,1,0:T(8,128)(2,1)S(1)}, u32[]{:S(2)}, u32[]{:S(2)}) %collective-permute-start.20) | collective-permute-done | bytes 737312 | tf_op jit(solution)/shard_map/ppermute | solution.py:858
  103.7 8.8 %widen.1 = (f32[512,768]{1,0:T(8,128)}, bf16[512,768]{1,0:T(8,128)(2,1)}, bf16[512,3072]{1,0:T(8,128)(2,1)}, bf16[512,3072]{1,0:T(8,128)(2,1)}, bf16[4,4,48,3840]{3,2,1,0:T(8,128)(2,1)}) custom-call(bf16[512,768]{1,0:T(8,128)(2,1)} %get-tuple-element.249.refs_0_, bf16[512,768]{1,0:T(8,128)(2,1)} %get-tuple-element.250.refs_1_, ...), custom_call_target="tpu_custom_call" | custom-call | flops 99999997952 | bytes 1 | tf_op jit(solution)/shard_map/widen/pallas_call | solution.py:244
  112.5 3.2 %collective-permute-done.19.refs_8_ = bf16[4,192,384]{2,1,0:T(8,128)(2,1)S(1)} collective-permute-done((bf16[4,192,384]{2,1,0:T(8,128)(2,1)}, bf16[4,192,384]{2,1,0:T(8,128)(2,1)S(1)}, u32[]{:S(2)}, u32[]{:S(2)}) %collective-permute-start.19) | collective-permute-done | bytes 589856 | tf_op jit(solution)/shard_map/ppermute | solution.py:858
  117.0 7.3 %grad_of_down.1 = (bf16[4,4,96,768]{3,2,1,0:T(8,128)(2,1)}, bf16[4,4,96,768]{3,2,1,0:T(8,128)(2,1)}, bf16[512,768]{1,0:T(8,128)(2,1)}) custom-call(bf16[512,3072]{1,0:T(8,128)(2,1)} %get-tuple-element.261.refs_0_.refs_2_, bf16[4,128,768]{2,1,0:T(8,128)(2,1)S(1)} %copy-done.3, bf16[128,768]{1,0:T(8,128)(2,1)} %collective-permute-done.13.refs_2_, ...), custom_call_target="tpu_custom_call" | custom-call | flops 99999997952 | bytes 1 | tf_op jit(solution)/shard_map/grad_of_down/pallas_call | solution.py:244
  126.2 2.3 collective-permute-done.30.refs_13_
  128.5 9.7 %narrow0.1 = (f32[512,768]{1,0:T(8,128)}, bf16[4,4,24,3072]{3,2,1,0:T(8,128)(2,1)}, bf16[4,4,24,3072]{3,2,1,0:T(8,128)(2,1)}, f32[512,768]{1,0:T(8,128)}) custom-call(f32[512,768]{1,0:T(8,128)} %get-tuple-element.271.refs_0_, bf16[512,768]{1,0:T(8,128)(2,1)} %get-tuple-element.272.refs_1_, bf16[512,3072]{1,0:T(8,128)(2,1)} %get-tuple-element.261.refs_0_.refs_2_, ...), custom_call_target="tpu_custom_call" | custom-call | flops 99999997952 | bytes 1 | tf_op jit(solution)/shard_map/narrow0/pallas_call | solution.py:244
  139.6 9.7 %narrow2.1 = (f32[512,768]{1,0:T(8,128)}, bf16[4,4,24,3072]{3,2,1,0:T(8,128)(2,1)}, bf16[4,4,24,3072]{3,2,1,0:T(8,128)(2,1)}, bf16[128,768]{1,0:T(8,128)(2,1)}, ...) custom-call(f32[512,768]{1,0:T(8,128)} %get-tuple-element.284.refs_0, ...), custom_call_target="tpu_custom_call", output_to_operand_aliasing={{1}: (15, {}), {2}: (16, {})} | custom-call | flops 99999997952 | bytes 1 | tf_op jit(solution)/shard_map/narrow2/pallas_call | solution.py:244
  149.3 5.9 %collective-permute-done.31 = bf16[8,96,768]{2,1,0:T(8,128)(2,1)S(1)} collective-permute-done((bf16[8,96,768]{2,1,0:T(8,128)(2,1)S(1)}, bf16[8,96,768]{2,1,0:T(8,128)(2,1)S(1)}, u32[]{:S(2)}, u32[]{:S(2)}) %collective-permute-start.31) | collective-permute-done | bytes 1179680 | tf_op jit(solution)/shard_map/ppermute | solution.py:858
  156.6 5.1 %turn.1 = (f32[512,768]{1,0:T(8,128)}, bf16[512,768]{1,0:T(8,128)(2,1)}, bf16[512,768]{1,0:T(8,128)(2,1)}, f32[2,768]{1,0:T(2,128)S(1)}) custom-call(f32[512,768]{1,0:T(8,128)} %get-tuple-element.271.refs_0_, f32[512,768]{1,0:T(8,128)} %get-tuple-element.299.refs_1_, bf16[512,768]{1,0:T(8,128)(2,1)} %get-tuple-element.274.refs_4_.refs_2_, ...), custom_call_target="tpu_custom_call" | custom-call | flops 99999997952 | bytes 1 | tf_op jit(solution)/shard_map/turn/pallas_call | solution.py:244
  161.8 2.3 add_convert_fusion.1
  165.9 10.0 %attend_back0.1 = (bf16[512,1152]{1,0:T(8,128)(2,1)}, bf16[4,4,24,1920]{3,2,1,0:T(8,128)(2,1)}, bf16[4,4,24,1920]{3,2,1,0:T(8,128)(2,1)}) custom-call(bf16[512,768]{1,0:T(8,128)(2,1)} %get-tuple-element.309.refs_0_, bf16[512,768]{1,0:T(8,128)(2,1)} %get-tuple-element.242.refs_0_.refs_1_, bf16[512,768]{1,0:T(8,128)(2,1)} %get-tuple-element.243.refs_1_.refs_2_, ...), custom_call_target="tpu_custom_call" | custom-call | flops 99999997952 | bytes 1 | tf_op jit(solution)/shard_map/attend_back0/pallas_call | solution.py:244
  177.0 3.8 %all-to-all-start.3 = ((bf16[4,96,768]{2,1,0:T(8,128)(2,1)}), bf16[4,96,768]{2,1,0:T(8,128)(2,1)S(1)}, u32[]{:S(2)}, u32[]{:S(2)}) async-start(bf16[4,96,768]{2,1,0:T(8,128)(2,1)} %add_convert_fusion.7), calls=%async_computation.3 | async-start | bytes 1179648 | tf_op jit(solution)/shard_map/all_to_all | solution.py:872
  181.9 2.0 fusion
  185.1 2.6 add_convert_fusion.4
  188.3 9.3 %attend_back1.1 = (bf16[512,1152]{1,0:T(8,128)(2,1)}, bf16[4,4,24,1152]{3,2,1,0:T(8,128)(2,1)}, bf16[4,4,24,1152]{3,2,1,0:T(8,128)(2,1)}) custom-call(bf16[512,768]{1,0:T(8,128)(2,1)} %get-tuple-element.309.refs_0_, bf16[512,768]{1,0:T(8,128)(2,1)} %get-tuple-element.242.refs_0_.refs_1_, bf16[512,768]{1,0:T(8,128)(2,1)} %get-tuple-element.243.refs_1_.refs_2_, ...), custom_call_target="tpu_custom_call" | custom-call | flops 99999997952 | bytes 1 | tf_op jit(solution)/shard_map/attend_back1/pallas_call | solution.py:244
  198.0 2.6 collective-permute-done.37
  202.6 2.3 add_convert_fusion.6
  204.9 4.2 %all-to-all-start.4 = ((bf16[4,24,3072]{2,1,0:T(8,128)(2,1)}), bf16[4,24,3072]{2,1,0:T(8,128)(2,1)S(1)}, u32[]{:S(2)}, u32[]{:S(2)}) async-start(bf16[4,24,3072]{2,1,0:T(8,128)(2,1)} %add_convert_fusion.6), calls=%async_computation.4 | async-start | bytes 1179648 | tf_op jit(solution)/shard_map/all_to_all | solution.py:872
  210.5 1.6 collective-permute-start.39
  213.4 7.1 %finish_tokens.1 = (bf16[128,768]{1,0:T(8,128)(2,1)}, bf16[128,768]{1,0:T(8,128)(2,1)}, bf16[128,768]{1,0:T(8,128)(2,1)}, bf16[128,768]{1,0:T(8,128)(2,1)}, f32[2,768]{1,0:T(2,128)S(1)}) custom-call(bf16[512,768]{1,0:T(8,128)(2,1)} %get-tuple-element.249.refs_0_, bf16[512,1152]{1,0:T(8,128)(2,1)} %get-tuple-element.330.refs_1_, ...), custom_call_target="tpu_custom_call" | custom-call | flops 1 | bytes 1 | tf_op jit(solution)/shard_map/finish_tokens/pallas_call | solution.py:244
  220.5 2.2 collective-permute-done.39
  223.8 4.9 %collective-permute-done.41 = bf16[4,24,1152]{2,1,0:T(8,128)(2,1)S(1)} collective-permute-done((bf16[4,24,1152]{2,1,0:T(8,128)(2,1)S(1)}, bf16[4,24,1152]{2,1,0:T(8,128)(2,1)S(1)}, u32[]{:S(2)}, u32[]{:S(2)}) %collective-permute-start.41) | collective-permute-done | bytes 221216 | tf_op jit(solution)/shard_map/ppermute | solution.py:858
  229.7 4.8 %all-to-all-start.5 = ((bf16[4,24,3072]{2,1,0:T(8,128)(2,1)}), bf16[4,24,3072]{2,1,0:T(8,128)(2,1)S(1)}, u32[]{:S(2)}, u32[]{:S(2)}) async-start(bf16[4,24,3072]{2,1,0:T(8,128)(2,1)} %pad_maximum_fusion), calls=%async_computation.5 | async-start | bytes 1179648 | tf_op jit(solution)/shard_map/all_to_all | solution.py:872
  235.5 1.5 collective-permute-start.43
  241.5 1.8 collective-permute-done.43.refs_27_
  243.3 3.3 %collective-permute-done.44.refs_28_ = bf16[128,768]{1,0:T(8,128)(2,1)S(1)} collective-permute-done((bf16[128,768]{1,0:T(8,128)(2,1)S(1)}, bf16[128,768]{1,0:T(8,128)(2,1)S(1)}, u32[]{:S(2)}, u32[]{:S(2)}) %collective-permute-start.44) | collective-permute-done | bytes 196640 | tf_op jit(solution)/shard_map/ppermute | solution.py:925
  246.5 4.7 %collective-permute-done.46.refs_31_ = bf16[128,768]{1,0:T(8,128)(2,1)S(1)} collective-permute-done((bf16[128,768]{1,0:T(8,128)(2,1)S(1)}, bf16[128,768]{1,0:T(8,128)(2,1)S(1)}, u32[]{:S(2)}, u32[]{:S(2)}) %collective-permute-start.46) | collective-permute-done | bytes 196640 | tf_op jit(solution)/shard_map/ppermute | solution.py:925
  251.9 1.8 sum_up.1
  253.7 5.4 %all-to-all-start.6 = ((bf16[32,32,128]{2,1,0:T(8,128)(2,1)}), bf16[32,32,128]{2,1,0:T(8,128)(2,1)S(1)}, u32[]{:S(2)}, u32[]{:S(2)}) async-start(bf16[32,32,128]{2,1,0:T(8,128)(2,1)} %get-tuple-element.365), calls=%async_computation.6 | async-start | bytes 524288 | tf_op jit(solution)/shard_map/all_to_all | solution.py:908
  259.2 1.6 collective-permute-start.47
  260.8 7.7 %collective-permute-done.47.refs_32_ = bf16[128,768]{1,0:T(8,128)(2,1)S(1)} collective-permute-done((bf16[128,768]{1,0:T(8,128)(2,1)S(1)}, bf16[128,768]{1,0:T(8,128)(2,1)S(1)}, u32[]{:S(2)}, u32[]{:S(2)}) %collective-permute-start.47) | collective-permute-done | bytes 196640 | tf_op jit(solution)/shard_map/ppermute | solution.py:925
  269.8 4.5 %update.1 = (f32[1,128]{1,0:T(1,128)}, f32[24,768]{1,0:T(8,128)}, f32[24,768]{1,0:T(8,128)}, f32[24,768]{1,0:T(8,128)}, f32[24,768]{1,0:T(8,128)}, /*index=5*/f3...) custom-call(f32[24,3072]{1,0:T(8,128)S(1)} %get-tuple-element.364.re, ...), custom_call_target="tpu_custom_call" | custom-call | flops 99999997952 | bytes 1 | tf_op jit(solution)/shard_map/update/pallas_call | solution.py:244
  (168 shorter events, 49.8 us)
Async XLA Ops:
  3.9 12.0 %collective-permute-start.5 = (bf16[96,384]{1,0:T(8,128)(2,1)S(1)}, bf16[96,384]{1,0:T(8,128)(2,1)S(1)}, u32[]{:S(2)}, u32[]{:S(2)}) collective-permute-start(bf16[96,384]{1,0:T(8,128)(2,1)S(1)} %get-tuple-element.219), channel_id=1, source_target_pairs={{0,1},{1,0},{2,3},{3,2},{4,5},{5,4},{6,7},{7,6},{8,9},{9,8},{10,11... | collective-permute-start | bytes 221192 | tf_op jit(solution)/shard_map/ppermute | solution.py:858
  4.0 12.0 %collective-permute-start.4 = (bf16[24,1920]{1,0:T(8,128)(2,1)S(1)}, bf16[24,1920]{1,0:T(8,128)(2,1)S(1)}, u32[]{:S(2)}, u32[]{:S(2)}) collective-permute-start(bf16[24,1920]{1,0:T(8,128)(2,1)S(1)} %get-tuple-element.217), channel_id=1, source_target_pairs={{0,1},{1,0},{2,3},{3,2},{4,5},{5,4},{6,7},{7,6},{8,9},{9,8},{10,11... | collective-permute-start | bytes 276488 | tf_op jit(solution)/shard_map/ppermute | solution.py:858
  5.6 20.4 %all-to-all-start = ((bf16[4,48,1280]{2,1,0:T(8,128)(2,1)}), bf16[4,48,1280]{2,1,0:T(8,128)(2,1)S(1)}, u32[]{:S(2)}, u32[]{:S(2)}) async-start(bf16[4,48,1280]{2,1,0:T(8,128)(2,1)} %broadcast_in_dim.8), calls=%async_computation | async-start | bytes 983040 | tf_op jit(solution)/shard_map/all_to_all | solution.py:872
  14.1 8.0 %collective-permute-start.2 = (bf16[128,768]{1,0:T(8,128)(2,1)}, bf16[128,768]{1,0:T(8,128)(2,1)S(1)}, u32[]{:S(2)}, u32[]{:S(2)}) collective-permute-start(bf16[128,768]{1,0:T(8,128)(2,1)} %get-tuple-element.214), channel_id=1, source_target_pairs={{0,2},{1,3},{2,0},{3,1},{4,6},{5,7},{6,4},{7,5},{8,10},{9,11},{10,... | collective-permute-start | bytes 589832 | tf_op jit(solution)/shard_map/ppermute | solution.py:925
  15.6 9.7 %collective-permute-start.3 = (bf16[128,768]{1,0:T(8,128)(2,1)}, bf16[128,768]{1,0:T(8,128)(2,1)S(1)}, u32[]{:S(2)}, u32[]{:S(2)}) collective-permute-start(bf16[128,768]{1,0:T(8,128)(2,1)} %get-tuple-element.215), channel_id=1, source_target_pairs={{0,3},{1,2},{2,1},{3,0},{4,7},{5,6},{6,5},{7,4},{8,11},{9,10},{10,... | collective-permute-start | bytes 589832 | tf_op jit(solution)/shard_map/ppermute | solution.py:925
  27.8 13.3 %collective-permute-start.7 = (bf16[4,48,1280]{2,1,0:T(8,128)(2,1)S(1)}, bf16[4,48,1280]{2,1,0:T(8,128)(2,1)S(1)}, u32[]{:S(2)}, u32[]{:S(2)}) collective-permute-start(bf16[4,48,1280]{2,1,0:T(8,128)(2,1)S(1)} %all-to-all-done.refs_4_), channel_id=1, source_target_pairs={{0,2},{1,5},{2,0},{3,7},{4,6},{5,1},{6,4},{7,3},{8,10},{9,13},{10,... | collective-permute-start | bytes 1474568 | tf_op jit(solution)/shard_map/ppermute | solution.py:858
  29.3 12.2 %collective-permute-start.6 = (bf16[4,48,1280]{2,1,0:T(8,128)(2,1)S(1)}, bf16[4,48,1280]{2,1,0:T(8,128)(2,1)S(1)}, u32[]{:S(2)}, u32[]{:S(2)}) collective-permute-start(bf16[4,48,1280]{2,1,0:T(8,128)(2,1)S(1)} %all-to-all-done.refs_4_), channel_id=1, source_target_pairs={{0,4},{1,3},{2,6},{3,1},{4,0},{5,7},{6,2},{7,5},{8,12},{9,11},{10,... | collective-permute-start | bytes 1474568 | tf_op jit(solution)/shard_map/ppermute | solution.py:858
  30.9 28.5 %all-to-all-start.1 = ((bf16[4,48,1920]{2,1,0:T(8,128)(2,1)}), bf16[4,48,1920]{2,1,0:T(8,128)(2,1)S(1)}, u32[]{:S(2)}, u32[]{:S(2)}) async-start(bf16[4,48,1920]{2,1,0:T(8,128)(2,1)} %broadcast_in_dim.9), calls=%async_computation.1 | async-start | bytes 1474560 | tf_op jit(solution)/shard_map/all_to_all | solution.py:872
  35.9 7.6 %collective-permute-start.9 = (bf16[4,48,1280]{2,1,0:T(8,128)(2,1)S(1)}, bf16[4,48,1280]{2,1,0:T(8,128)(2,1)S(1)}, u32[]{:S(2)}, u32[]{:S(2)}) collective-permute-start(bf16[4,48,1280]{2,1,0:T(8,128)(2,1)S(1)} %all-to-all-done.refs_4_), channel_id=1, source_target_pairs={{0,1},{1,0},{2,3},{3,2},{4,5},{5,4},{6,7},{7,6},{8,9},{9,8},{10,11... | collective-permute-start | bytes 1474568 | tf_op jit(solution)/shard_map/ppermute | solution.py:858
  42.1 8.8 %collective-permute-start.8 = (bf16[4,48,1280]{2,1,0:T(8,128)(2,1)S(1)}, bf16[4,48,1280]{2,1,0:T(8,128)(2,1)S(1)}, u32[]{:S(2)}, u32[]{:S(2)}) collective-permute-start(bf16[4,48,1280]{2,1,0:T(8,128)(2,1)S(1)} %collective-permute-done.6.refs_5_), channel_id=1, source_target_pairs={{0,2},{1,5},{2,0},{3,7},{4,6},{5,1},{6,4},{7,3},{8,10},{9,13},{10,... | collective-permute-start | bytes 1474568 | tf_op jit(solution)/shard_map/ppermute | solution.py:858
  50.9 8.5 %collective-permute-start.13 = (bf16[128,768]{1,0:T(8,128)(2,1)}, bf16[128,768]{1,0:T(8,128)(2,1)}, u32[]{:S(2)}, u32[]{:S(2)}) collective-permute-start(bf16[128,768]{1,0:T(8,128)(2,1)} %get-tuple-element.236), channel_id=1, source_target_pairs={{0,1},{1,0},{2,3},{3,2},{4,5},{5,4},{6,7},{7,6},{8,9},{9,8},{10,11... | collective-permute-start | bytes 589832 | tf_op jit(solution)/shard_map/ppermute | solution.py:925
  51.4 8.1 %collective-permute-start.14 = (bf16[128,768]{1,0:T(8,128)(2,1)}, bf16[128,768]{1,0:T(8,128)(2,1)}, u32[]{:S(2)}, u32[]{:S(2)}) collective-permute-start(bf16[128,768]{1,0:T(8,128)(2,1)} %get-tuple-element.237), channel_id=1, source_target_pairs={{0,2},{1,3},{2,0},{3,1},{4,6},{5,7},{6,4},{7,5},{8,10},{9,11},{10,... | collective-permute-start | bytes 589832 | tf_op jit(solution)/shard_map/ppermute | solution.py:925
  52.9 8.9 %collective-permute-start.15 = (bf16[128,768]{1,0:T(8,128)(2,1)}, bf16[128,768]{1,0:T(8,128)(2,1)}, u32[]{:S(2)}, u32[]{:S(2)}) collective-permute-start(bf16[128,768]{1,0:T(8,128)(2,1)} %get-tuple-element.238), channel_id=1, source_target_pairs={{0,3},{1,2},{2,1},{3,0},{4,7},{5,6},{6,5},{7,4},{8,11},{9,10},{10,... | collective-permute-start | bytes 589832 | tf_op jit(solution)/shard_map/ppermute | solution.py:925
  61.8 26.6 %collective-permute-start.21 = (bf16[4,48,1920]{2,1,0:T(8,128)(2,1)S(1)}, bf16[4,48,1920]{2,1,0:T(8,128)(2,1)S(1)}, u32[]{:S(2)}, u32[]{:S(2)}) collective-permute-start(bf16[4,48,1920]{2,1,0:T(8,128)(2,1)S(1)} %all-to-all-done.1.refs_3_), channel_id=1, source_target_pairs={{0,1},{1,0},{2,3},{3,2},{4,5},{5,4},{6,7},{7,6},{8,9},{9,8},{10,11... | collective-permute-start | bytes 2211848 | tf_op jit(solution)/shard_map/ppermute | solution.py:858
  62.6 18.9 %collective-permute-start.17 = (bf16[4,48,1920]{2,1,0:T(8,128)(2,1)S(1)}, bf16[4,48,1920]{2,1,0:T(8,128)(2,1)S(1)}, u32[]{:S(2)}, u32[]{:S(2)}) collective-permute-start(bf16[4,48,1920]{2,1,0:T(8,128)(2,1)S(1)} %all-to-all-done.1.refs_3_), channel_id=1, source_target_pairs={{0,2},{1,5},{2,0},{3,7},{4,6},{5,1},{6,4},{7,3},{8,10},{9,13},{10,... | collective-permute-start | bytes 2211848 | tf_op jit(solution)/shard_map/ppermute | solution.py:858
  64.1 17.4 %collective-permute-start.16 = (bf16[4,48,1920]{2,1,0:T(8,128)(2,1)S(1)}, bf16[4,48,1920]{2,1,0:T(8,128)(2,1)}, u32[]{:S(2)}, u32[]{:S(2)}) collective-permute-start(bf16[4,48,1920]{2,1,0:T(8,128)(2,1)S(1)} %all-to-all-done.1.refs_3_), channel_id=1, source_target_pairs={{0,4},{1,3},{2,6},{3,1},{4,0},{5,7},{6,2},{7,5},{8,12},{9,11},{10,... | collective-permute-start | bytes 2211848 | tf_op jit(solution)/shard_map/ppermute | solution.py:858
  65.8 20.6 %all-to-all-start.2 = ((bf16[4,192,384]{2,1,0:T(8,128)(2,1)}), bf16[4,192,384]{2,1,0:T(8,128)(2,1)}, u32[]{:S(2)}, u32[]{:S(2)}) async-start(bf16[4,192,384]{2,1,0:T(8,128)(2,1)} %broadcast_in_dim.10), calls=%async_computation.2 | async-start | bytes 1179648 | tf_op jit(solution)/shard_map/all_to_all | solution.py:872
  87.8 11.7 %collective-permute-start.20 = (bf16[4,48,1920]{2,1,0:T(8,128)(2,1)}, bf16[4,48,1920]{2,1,0:T(8,128)(2,1)S(1)}, u32[]{:S(2)}, u32[]{:S(2)}) collective-permute-start(bf16[4,48,1920]{2,1,0:T(8,128)(2,1)} %collective-permute-done.16.refs_4_), channel_id=1, source_target_pairs={{0,2},{1,5},{2,0},{3,7},{4,6},{5,1},{6,4},{7,3},{8,10},{9,13},{10,... | collective-permute-start | bytes 2211848 | tf_op jit(solution)/shard_map/ppermute | solution.py:858
  99.5 3.1 %collective-permute-start.24 = (bf16[4,48,1920]{2,1,0:T(8,128)(2,1)S(1)}, bf16[4,48,1920]{2,1,0:T(8,128)(2,1)S(1)}, u32[]{:S(2)}, u32[]{:S(2)}) collective-permute-start(bf16[4,48,1920]{2,1,0:T(8,128)(2,1)S(1)} %collective-permute-done.20.refs_6_), channel_id=1, source_target_pairs={{0,1},{1,0},{2,3},{3,2},{4,5},{5,4},{6,7},{7,6},{8,9},{9,8},{10,11... | collective-permute-start | bytes 2211848 | tf_op jit(solution)/shard_map/ppermute | solution.py:858
  99.5 24.9 %collective-permute-start.26 = (bf16[4,192,384]{2,1,0:T(8,128)(2,1)}, bf16[4,192,384]{2,1,0:T(8,128)(2,1)}, u32[]{:S(2)}, u32[]{:S(2)}) collective-permute-start(bf16[4,192,384]{2,1,0:T(8,128)(2,1)} %all-to-all-done.2.refs_6_), channel_id=1, source_target_pairs={{0,1},{1,0},{2,3},{3,2},{4,5},{5,4},{6,7},{7,6},{8,9},{9,8},{10,11... | collective-permute-start | bytes 1769480 | tf_op jit(solution)/shard_map/ppermute | solution.py:858
  100.0 15.7 %collective-permute-start.19 = (bf16[4,192,384]{2,1,0:T(8,128)(2,1)}, bf16[4,192,384]{2,1,0:T(8,128)(2,1)S(1)}, u32[]{:S(2)}, u32[]{:S(2)}) collective-permute-start(bf16[4,192,384]{2,1,0:T(8,128)(2,1)} %all-to-all-done.2.refs_6_), channel_id=1, source_target_pairs={{0,2},{1,5},{2,0},{3,7},{4,6},{5,1},{6,4},{7,3},{8,10},{9,13},{10,... | collective-permute-start | bytes 1769480 | tf_op jit(solution)/shard_map/ppermute | solution.py:858
  100.5 15.2 %collective-permute-start.18 = (bf16[4,192,384]{2,1,0:T(8,128)(2,1)}, bf16[4,192,384]{2,1,0:T(8,128)(2,1)S(1)}, u32[]{:S(2)}, u32[]{:S(2)}) collective-permute-start(bf16[4,192,384]{2,1,0:T(8,128)(2,1)} %all-to-all-done.2.refs_6_), channel_id=1, source_target_pairs={{0,4},{1,3},{2,6},{3,1},{4,0},{5,7},{6,2},{7,5},{8,12},{9,11},{10,... | collective-permute-start | bytes 1769480 | tf_op jit(solution)/shard_map/ppermute | solution.py:858
  115.8 8.6 %collective-permute-start.27 = (bf16[4,192,384]{2,1,0:T(8,128)(2,1)S(1)}, bf16[4,192,384]{2,1,0:T(8,128)(2,1)S(1)}, u32[]{:S(2)}, u32[]{:S(2)}) collective-permute-start(bf16[4,192,384]{2,1,0:T(8,128)(2,1)S(1)} %collective-permute-done.18.refs_7_), channel_id=1, source_target_pairs={{0,1},{1,0},{2,3},{3,2},{4,5},{5,4},{6,7},{7,6},{8,9},{9,8},{10,11... | collective-permute-start | bytes 1769480 | tf_op jit(solution)/shard_map/ppermute | solution.py:858
  115.8 9.9 %collective-permute-start.25 = (bf16[4,192,384]{2,1,0:T(8,128)(2,1)S(1)}, bf16[4,192,384]{2,1,0:T(8,128)(2,1)S(1)}, u32[]{:S(2)}, u32[]{:S(2)}) collective-permute-start(bf16[4,192,384]{2,1,0:T(8,128)(2,1)S(1)} %collective-permute-done.18.refs_7_), channel_id=1, source_target_pairs={{0,2},{1,5},{2,0},{3,7},{4,6},{5,1},{6,4},{7,3},{8,10},{9,13},{10,... | collective-permute-start | bytes 1769480 | tf_op jit(solution)/shard_map/ppermute | solution.py:858
  116.3 8.1 %collective-permute-start.28 = (bf16[4,192,384]{2,1,0:T(8,128)(2,1)S(1)}, bf16[4,192,384]{2,1,0:T(8,128)(2,1)S(1)}, u32[]{:S(2)}, u32[]{:S(2)}) collective-permute-start(bf16[4,192,384]{2,1,0:T(8,128)(2,1)S(1)} %collective-permute-done.19.refs_8_), channel_id=1, source_target_pairs={{0,1},{1,0},{2,3},{3,2},{4,5},{5,4},{6,7},{7,6},{8,9},{9,8},{10,11... | collective-permute-start | bytes 1769480 | tf_op jit(solution)/shard_map/ppermute | solution.py:858
  125.6 2.8 %collective-permute-start.30 = (bf16[4,192,384]{2,1,0:T(8,128)(2,1)S(1)}, bf16[4,192,384]{2,1,0:T(8,128)(2,1)S(1)}, u32[]{:S(2)}, u32[]{:S(2)}) collective-permute-start(bf16[4,192,384]{2,1,0:T(8,128)(2,1)S(1)} %collective-permute-done.25.refs_9_), channel_id=1, source_target_pairs={{0,1},{1,0},{2,3},{3,2},{4,5},{5,4},{6,7},{7,6},{8,9},{9,8},{10,11... | collective-permute-start | bytes 1769480 | tf_op jit(solution)/shard_map/ppermute | solution.py:858
  125.7 12.6 %collective-permute-start.29 = (bf16[4,4,96,768]{3,2,1,0:T(8,128)(2,1)}, bf16[4,4,96,768]{3,2,1,0:T(8,128)(2,1)S(1)}, u32[]{:S(2)}, u32[]{:S(2)}) collective-permute-start(bf16[4,4,96,768]{3,2,1,0:T(8,128)(2,1)} %get-tuple-element.270), channel_id=1, source_target_pairs={{0,1},{1,0},{2,3},{3,2},{4,5},{5,4},{6,7},{7,6},{8,9},{9,8},{10,11... | collective-permute-start | bytes 7077896 | tf_op jit(solution)/shard_map/ppermute | solution.py:858
  139.0 16.3 %collective-permute-start.31 = (bf16[8,96,768]{2,1,0:T(8,128)(2,1)S(1)}, bf16[8,96,768]{2,1,0:T(8,128)(2,1)S(1)}, u32[]{:S(2)}, u32[]{:S(2)}) collective-permute-start(bf16[8,96,768]{2,1,0:T(8,128)(2,1)S(1)} %bitcast.48), channel_id=1, source_target_pairs={{0,2},{1,5},{2,0},{3,7},{4,6},{5,1},{6,4},{7,3},{8,10},{9,13},{10,... | collective-permute-start | bytes 3538952 | tf_op jit(solution)/shard_map/ppermute | solution.py:858
  155.4 9.9 %collective-permute-start.33 = (bf16[4,96,768]{2,1,0:T(8,128)(2,1)S(1)}, bf16[4,96,768]{2,1,0:T(8,128)(2,1)S(1)}, u32[]{:S(2)}, u32[]{:S(2)}) collective-permute-start(bf16[4,96,768]{2,1,0:T(8,128)(2,1)S(1)} %fusion.3), channel_id=1, source_target_pairs={{0,4},{1,3},{2,6},{3,1},{4,0},{5,7},{6,2},{7,5},{8,12},{9,11},{10,... | collective-permute-start | bytes 1769480 | tf_op jit(solution)/shard_map/ppermute | solution.py:858
  156.6 5.2 %collective-permute-start.32 = (bf16[4,4,24,3072]{3,2,1,0:T(8,128)(2,1)}, bf16[4,4,24,3072]{3,2,1,0:T(8,128)(2,1)S(1)}, u32[]{:S(2)}, u32[]{:S(2)}) collective-permute-start(bf16[4,4,24,3072]{3,2,1,0:T(8,128)(2,1)} %get-tuple-element.296), channel_id=1, source_target_pairs={{0,1},{1,0},{2,3},{3,2},{4,5},{5,4},{6,7},{7,6},{8,9},{9,8},{10,11... | collective-permute-start | bytes 7077896 | tf_op jit(solution)/shard_map/ppermute | solution.py:858
  165.4 16.5 %collective-permute-start.34 = (bf16[8,24,3072]{2,1,0:T(8,128)(2,1)}, bf16[8,24,3072]{2,1,0:T(8,128)(2,1)}, u32[]{:S(2)}, u32[]{:S(2)}) collective-permute-start(bf16[8,24,3072]{2,1,0:T(8,128)(2,1)} %bitcast.4), channel_id=1, source_target_pairs={{0,2},{1,5},{2,0},{3,7},{4,6},{5,1},{6,4},{7,3},{8,10},{9,13},{10,... | collective-permute-start | bytes 3538952 | tf_op jit(solution)/shard_map/ppermute | solution.py:858
  175.9 9.2 %collective-permute-start.36 = (bf16[4,4,24,1920]{3,2,1,0:T(8,128)(2,1)}, bf16[4,4,24,1920]{3,2,1,0:T(8,128)(2,1)}, u32[]{:S(2)}, u32[]{:S(2)}) collective-permute-start(bf16[4,4,24,1920]{3,2,1,0:T(8,128)(2,1)} %get-tuple-element.320), channel_id=1, source_target_pairs={{0,1},{1,0},{2,3},{3,2},{4,5},{5,4},{6,7},{7,6},{8,9},{9,8},{10,11... | collective-permute-start | bytes 4423688 | tf_op jit(solution)/shard_map/ppermute | solution.py:858
  177.0 20.6 %all-to-all-start.3 = ((bf16[4,96,768]{2,1,0:T(8,128)(2,1)}), bf16[4,96,768]{2,1,0:T(8,128)(2,1)S(1)}, u32[]{:S(2)}, u32[]{:S(2)}) async-start(bf16[4,96,768]{2,1,0:T(8,128)(2,1)} %add_convert_fusion.7), calls=%async_computation.3 | async-start | bytes 1179648 | tf_op jit(solution)/shard_map/all_to_all | solution.py:872
  183.9 14.0 %collective-permute-start.35 = (bf16[4,24,3072]{2,1,0:T(8,128)(2,1)}, bf16[4,24,3072]{2,1,0:T(8,128)(2,1)}, u32[]{:S(2)}, u32[]{:S(2)}) collective-permute-start(bf16[4,24,3072]{2,1,0:T(8,128)(2,1)} %fusion), channel_id=1, source_target_pairs={{0,4},{1,3},{2,6},{3,1},{4,0},{5,7},{6,2},{7,5},{8,12},{9,11},{10,... | collective-permute-start | bytes 1769480 | tf_op jit(solution)/shard_map/ppermute | solution.py:858
  187.7 12.9 %collective-permute-start.37 = (bf16[8,24,1920]{2,1,0:T(8,128)(2,1)}, bf16[8,24,1920]{2,1,0:T(8,128)(2,1)S(1)}, u32[]{:S(2)}, u32[]{:S(2)}) collective-permute-start(bf16[8,24,1920]{2,1,0:T(8,128)(2,1)} %bitcast.7), channel_id=1, source_target_pairs={{0,2},{1,5},{2,0},{3,7},{4,6},{5,1},{6,4},{7,3},{8,10},{9,13},{10,... | collective-permute-start | bytes 2211848 | tf_op jit(solution)/shard_map/ppermute | solution.py:858
  201.4 7.6 %collective-permute-start.38 = (bf16[4,4,24,1152]{3,2,1,0:T(8,128)(2,1)}, bf16[4,4,24,1152]{3,2,1,0:T(8,128)(2,1)}, u32[]{:S(2)}, u32[]{:S(2)}) collective-permute-start(bf16[4,4,24,1152]{3,2,1,0:T(8,128)(2,1)} %get-tuple-element.328), channel_id=1, source_target_pairs={{0,1},{1,0},{2,3},{3,2},{4,5},{5,4},{6,7},{7,6},{8,9},{9,8},{10,11... | collective-permute-start | bytes 2654216 | tf_op jit(solution)/shard_map/ppermute | solution.py:858
  204.9 24.8 %all-to-all-start.4 = ((bf16[4,24,3072]{2,1,0:T(8,128)(2,1)}), bf16[4,24,3072]{2,1,0:T(8,128)(2,1)S(1)}, u32[]{:S(2)}, u32[]{:S(2)}) async-start(bf16[4,24,3072]{2,1,0:T(8,128)(2,1)} %add_convert_fusion.6), calls=%async_computation.4 | async-start | bytes 1179648 | tf_op jit(solution)/shard_map/all_to_all | solution.py:872
  210.5 12.2 %collective-permute-start.39 = (bf16[8,24,1152]{2,1,0:T(8,128)(2,1)S(1)}, bf16[8,24,1152]{2,1,0:T(8,128)(2,1)S(1)}, u32[]{:S(2)}, u32[]{:S(2)}) collective-permute-start(bf16[8,24,1152]{2,1,0:T(8,128)(2,1)S(1)} %bitcast.49), channel_id=1, source_target_pairs={{0,2},{1,5},{2,0},{3,7},{4,6},{5,1},{6,4},{7,3},{8,10},{9,13},{10,... | collective-permute-start | bytes 1327112 | tf_op jit(solution)/shard_map/ppermute | solution.py:858
  212.2 11.5 %collective-permute-start.40 = (bf16[4,24,1920]{2,1,0:T(8,128)(2,1)S(1)}, bf16[4,24,1920]{2,1,0:T(8,128)(2,1)S(1)}, u32[]{:S(2)}, u32[]{:S(2)}) collective-permute-start(bf16[4,24,1920]{2,1,0:T(8,128)(2,1)S(1)} %fusion.5), channel_id=1, source_target_pairs={{0,4},{1,3},{2,6},{3,1},{4,0},{5,7},{6,2},{7,5},{8,12},{9,11},{10,... | collective-permute-start | bytes 1105928 | tf_op jit(solution)/shard_map/ppermute | solution.py:858
  222.7 6.0 %collective-permute-start.41 = (bf16[4,24,1152]{2,1,0:T(8,128)(2,1)S(1)}, bf16[4,24,1152]{2,1,0:T(8,128)(2,1)S(1)}, u32[]{:S(2)}, u32[]{:S(2)}) collective-permute-start(bf16[4,24,1152]{2,1,0:T(8,128)(2,1)S(1)} %fusion.7), channel_id=1, source_target_pairs={{0,4},{1,3},{2,6},{3,1},{4,0},{5,7},{6,2},{7,5},{8,12},{9,11},{10,... | collective-permute-start | bytes 663560 | tf_op jit(solution)/shard_map/ppermute | solution.py:858
  229.7 21.5 %all-to-all-start.5 = ((bf16[4,24,3072]{2,1,0:T(8,128)(2,1)}), bf16[4,24,3072]{2,1,0:T(8,128)(2,1)S(1)}, u32[]{:S(2)}, u32[]{:S(2)}) async-start(bf16[4,24,3072]{2,1,0:T(8,128)(2,1)} %pad_maximum_fusion), calls=%async_computation.5 | async-start | bytes 1179648 | tf_op jit(solution)/shard_map/all_to_all | solution.py:872
  235.4 6.0 %collective-permute-start.42 = (bf16[128,768]{1,0:T(8,128)(2,1)S(1)}, bf16[128,768]{1,0:T(8,128)(2,1)S(1)}, u32[]{:S(2)}, u32[]{:S(2)}) collective-permute-start(bf16[128,768]{1,0:T(8,128)(2,1)S(1)} %copy-done.21), channel_id=1, source_target_pairs={{0,1},{1,0},{2,3},{3,2},{4,5},{5,4},{6,7},{7,6},{8,9},{9,8},{10,11... | collective-permute-start | bytes 589832 | tf_op jit(solution)/shard_map/ppermute | solution.py:925
  235.5 7.7 %collective-permute-start.43 = (bf16[128,768]{1,0:T(8,128)(2,1)S(1)}, bf16[128,768]{1,0:T(8,128)(2,1)S(1)}, u32[]{:S(2)}, u32[]{:S(2)}) collective-permute-start(bf16[128,768]{1,0:T(8,128)(2,1)S(1)} %copy-done.20), channel_id=1, source_target_pairs={{0,2},{1,3},{2,0},{3,1},{4,6},{5,7},{6,4},{7,5},{8,10},{9,11},{10,... | collective-permute-start | bytes 589832 | tf_op jit(solution)/shard_map/ppermute | solution.py:925
  237.0 9.5 %collective-permute-start.44 = (bf16[128,768]{1,0:T(8,128)(2,1)S(1)}, bf16[128,768]{1,0:T(8,128)(2,1)S(1)}, u32[]{:S(2)}, u32[]{:S(2)}) collective-permute-start(bf16[128,768]{1,0:T(8,128)(2,1)S(1)} %copy-done.19), channel_id=1, source_target_pairs={{0,3},{1,2},{2,1},{3,0},{4,7},{5,6},{6,5},{7,4},{8,11},{9,10},{10,... | collective-permute-start | bytes 589832 | tf_op jit(solution)/shard_map/ppermute | solution.py:925
  237.3 9.2 %collective-permute-start.45 = (bf16[128,768]{1,0:T(8,128)(2,1)}, bf16[128,768]{1,0:T(8,128)(2,1)S(1)}, u32[]{:S(2)}, u32[]{:S(2)}) collective-permute-start(bf16[128,768]{1,0:T(8,128)(2,1)} %get-tuple-element.359), channel_id=1, source_target_pairs={{0,1},{1,0},{2,3},{3,2},{4,5},{5,4},{6,7},{7,6},{8,9},{9,8},{10,11... | collective-permute-start | bytes 589832 | tf_op jit(solution)/shard_map/ppermute | solution.py:925
  237.7 13.5 %collective-permute-start.46 = (bf16[128,768]{1,0:T(8,128)(2,1)S(1)}, bf16[128,768]{1,0:T(8,128)(2,1)S(1)}, u32[]{:S(2)}, u32[]{:S(2)}) collective-permute-start(bf16[128,768]{1,0:T(8,128)(2,1)S(1)} %copy-done.26), channel_id=1, source_target_pairs={{0,2},{1,3},{2,0},{3,1},{4,6},{5,7},{6,4},{7,5},{8,10},{9,11},{10,... | collective-permute-start | bytes 589832 | tf_op jit(solution)/shard_map/ppermute | solution.py:925
  253.7 16.0 %all-to-all-start.6 = ((bf16[32,32,128]{2,1,0:T(8,128)(2,1)}), bf16[32,32,128]{2,1,0:T(8,128)(2,1)S(1)}, u32[]{:S(2)}, u32[]{:S(2)}) async-start(bf16[32,32,128]{2,1,0:T(8,128)(2,1)} %get-tuple-element.365), calls=%async_computation.6 | async-start | bytes 524288 | tf_op jit(solution)/shard_map/all_to_all | solution.py:908
  259.2 9.3 %collective-permute-start.47 = (bf16[128,768]{1,0:T(8,128)(2,1)S(1)}, bf16[128,768]{1,0:T(8,128)(2,1)S(1)}, u32[]{:S(2)}, u32[]{:S(2)}) collective-permute-start(bf16[128,768]{1,0:T(8,128)(2,1)S(1)} %copy-done.22), channel_id=1, source_target_pairs={{0,3},{1,2},{2,1},{3,0},{4,7},{5,6},{6,5},{7,4},{8,11},{9,10},{10,... | collective-permute-start | bytes 589832 | tf_op jit(solution)/shard_map/ppermute | solution.py:925
  (37 other events, 210.6 us)

commit v2 on v1

--- a/solution.py
+++ b/solution.py
@@ -298,14 +298,22 @@
 
 
 def prepare(plan, matrices, norm_params):
-    side = jnp.pad(norm_params.T, ((0, 0), (0, 128 - norm_params.shape[0])))
-    matrices = [*matrices[0:3], jnp.concatenate([side, side], axis=1), *matrices[3:]]
-    groups = [matrices[0:4], matrices[4:6], matrices[6:7]]
+    groups = [matrices[0:3], matrices[3:5], matrices[5:6]]
 
     def body(io, ins, outs):
         io.start()
         core = lax.axis_index("seq") & 1
         first = 0
+        rows = norm_params.shape[1]
+        same = lax.broadcasted_iota(jnp.int32, (rows, rows), 0) == lax.broadcasted_iota(jnp.int32, (rows, rows), 1)
+        lane = lax.broadcasted_iota(jnp.int32, (rows, 128), 1)
+        side = jnp.zeros((rows, 128), F32)
+        for p in range(norm_params.shape[0]):
+            row = jnp.broadcast_to(ins[-1][p : p + 1, :], (rows, rows))
+            column = jnp.sum(jnp.where(same, row, 0.0), axis=1, keepdims=True)
+            side = jnp.where(lane == p, column, side)
+        for out in outs[:2]:
+            out[:, 3 * HALF :] = side.astype(BF)
         for number, group in enumerate(groups):
             at = 0
             for index in range(first, first + len(group)):
@@ -321,8 +329,9 @@
 
     outs = []
     for group in groups:
-        outs += [(shape((group[0].shape[0], sum(w.shape[1] for w in group) // 2), BF), "near")] * 2
-    flat_outs = call("prepare", body, far(*matrices), outs, [], 8)
+        width = sum(w.shape[1] for w in group) // 2 + (128 if group is groups[0] else 0)
+        outs += [(shape((group[0].shape[0], width), BF), "near")] * 2
+    flat_outs = call("prepare", body, [*far(*matrices), (norm_params, "near")], outs, [], 8)
     return flat_outs[0:2], flat_outs[2:4], flat_outs[4:6]
 
 
@@ -786,8 +795,12 @@
         first = given + 1
         io.start(*(first + k * count + i for i in reversed(range(count)) for k in range(3)))
         io.start()
-        total[...] = jnp.sum(card_ref[...].astype(F32), axis=0)
-        rows, wide = total.shape[0], 4 * D // plan.count
+        sources, rows, _ = card_ref.shape
+        split = min(2, sources)
+        for c in range(split):
+            cards_c = [card_ref[i].astype(F32) for i in range(c, sources, split)]
+            total[c * rows : (c + 1) * rows, :] = sum(cards_c[1:], cards_c[0])
+        wide = 4 * D // plan.count
         all_norms = total[...]
         lane = lax.broadcasted_iota(jnp.int32, all_norms.shape, 1)
         own = jnp.where(lane < wide, all_norms * all_norms, all_norms * (1.0 / rows))
@@ -795,7 +808,10 @@
         norm = jnp.sqrt(square)
         outs[0][...] = jnp.broadcast_to(norm, outs[0].shape)
         factor = jnp.minimum(1.0, clip_limit / (norm + 1e-06))
-        mine = total[pl.ds(lax.axis_index("dp") * plan.seq + lax.axis_index("seq"), 1), :]
+        place_of = lax.axis_index("dp") * plan.seq + lax.axis_index("seq")
+        if split == 2:
+            place_of = (place_of & 1) * rows + (place_of >> 1)
+        mine = total[pl.ds(place_of, 1), :]
         each = wide // 4
         grad_norms = jnp.concatenate([mine[:, p * each : (p + 1) * each] for p in range(4)], axis=0)
         for i in reversed(range(count)):
@@ -842,7 +858,7 @@
     return call(
         "update", body, [*[(g, "near") for g in grads], (cards, "near"), *far(*masters, *firsts, *seconds, *passed)],
         [(shape((1, 128), F32), "near"), *like, *[(o, "raw") for o in pieces]],
-        [pltpu.VMEM(cards.shape[1:], F32), pltpu.SemaphoreType.DMA((len(passed),))], 20,
+        [pltpu.VMEM((min(2, cards.shape[0]) * cards.shape[1], 128), F32), pltpu.SemaphoreType.DMA((len(passed),))], 20,
     )
 
 
@@ -899,6 +915,10 @@
     slices = sums.reshape(sums.shape[0], plan.count, -1).transpose(1, 0, 2).reshape(plan.count, wide)
     slices = jnp.pad(slices, ((0, 0), (0, 128 - wide)))
     if plan.fast:
+        core = lax.axis_index("seq") & 1
+        pairs = slices.reshape(-1, 2, 128)
+        mine, other = (lax.dynamic_index_in_dim(pairs, c, 1, keepdims=False) for c in (core, 1 - core))
+        slices = mine + send(plan, other, plan.core)
         blocks, *others = grads
         left = jnp.broadcast_to(sum(jnp.sum(g * g) for g in others), (1, 128))
         left, slices, blocks, early = meet(left, slices, blocks, passed[:-1])
@@ -1040,7 +1060,7 @@
     got_a = send(plan, go_a, plan.first)
     mixed_cot = after(mixed_cot, go_u, go_a, block_d)
     spread_b, keep_b, go_b = attend_back(plan, 1, low_one, query, key, value, lse, mixed_cot, seg, pad)
-    blocks_d, got_u, got_a, go_b, keep_b, spread_b = meet(blocks_d, got_u, got_a, go_b, keep_b, spread_b)
+    blocks_d, got_u, got_a, keep_b, spread_b = meet(blocks_d, got_u, got_a, keep_b, spread_b)
     got_b = send(plan, go_b, plan.core)
     block_u = add(keep_u, got_u).astype(BF)
     blocks_u = along_z(plan, block_u)

time: 280 us -> 272 us (0.971)
  starting transfers between devices: 67.4 us -> 63.5 us
    ppermute x36 -> x37, starting transfers between devices: 23.6 us -> 17.8 us  [send(): return lax.ppermute(values, AXES, perm)]
    unnamed x61 -> x54, local copies, waits for them, and re-layouts: 6.13 us -> 4.81 us
    ppermute x36 -> x37, waiting for transfers between devices: 51.9 us -> 51.2 us  [send(): return lax.ppermute(values, AXES, perm)]
  transfers between devices with their start and end apart: 55 -> 56, of which waited for: 32 -> 28; matrix products, arithmetic and copies ran while one was open for 6% -> 6% of each run, Pallas kernels for 31% -> 32%
where the time goes in v2:
time: 272 us; the launch traced here: 267 us
  Pallas kernels  91.8 us (34%)
  waiting for transfers between devices  85 us (31%)
  starting transfers between devices  63.5 us (23%)
  other arithmetic  16 us (6%)
  local copies, waits for them, and re-layouts  7.69 us (3%)
  between operations  2.8 us (1%)
    pallas_call x14, Pallas kernels, call(): pl.pallas_call(kernel, out_shape=[pltpu.HBM(o.shape, o.dtype) if kind in...  91.8 us
    ppermute x37, waiting for transfers between devices, send(): return lax.ppermute(values, AXES, perm)  51.2 us
    all_to_all x6, starting transfers between devices, along_z(): lax.all_to_all(values, 'dp', 0, 0, axis_index_groups=plan.groups, tiled=T...  30.2 us
    ppermute x12, waiting for transfers between devices, swap(): lax.ppermute(values, 'seq', [(i, i ^ number) for i in range(plan.seq)])  26.4 us
    ppermute x37, starting transfers between devices, send(): return lax.ppermute(values, AXES, perm)  17.8 us
    ppermute x12, starting transfers between devices, swap(): lax.ppermute(values, 'seq', [(i, i ^ number) for i in range(plan.seq)])  10.1 us
    all_to_all x6, waiting for transfers between devices, along_z(): lax.all_to_all(values, 'dp', 0, 0, axis_index_groups=plan.groups, tiled=T...  7.09 us
    convert_element_type x3, other arithmetic, fold(): add(keep[:size], got[:size]).astype(BF)  5.87 us
  transfers between devices with their start and end apart: 56, of which 28 were waited for; matrix products, arithmetic and copies ran while one was open for 6% of the time, Pallas kernels for 32%

profile of v2, /device:TPU:0, one launch (start us, length us, event | category | flops | bytes accessed | tf_op | source)
XLA Modules:
  0.0 266.9 jit_solution(16889245129647696475)
XLA Ops:
  4.9 6.2 %all-to-all-start = ((bf16[4,48,1280]{2,1,0:T(8,128)(2,1)}), bf16[4,48,1280]{2,1,0:T(8,128)(2,1)S(1)}, u32[]{:S(2)}, u32[]{:S(2)}) async-start(bf16[4,48,1280]{2,1,0:T(8,128)(2,1)} %broadcast_in_dim.8), calls=%async_computation | async-start | bytes 983040 | tf_op jit(solution)/shard_map/all_to_all | solution.py:888
  11.1 2.1 other_rows.1
  16.5 4.8 %collective-permute-done.2.refs_2_ = bf16[128,768]{1,0:T(8,128)(2,1)S(1)} collective-permute-done((bf16[128,768]{1,0:T(8,128)(2,1)}, bf16[128,768]{1,0:T(8,128)(2,1)S(1)}, u32[]{:S(2)}, u32[]{:S(2)}) %collective-permute-start.2) | collective-permute-done | bytes 196640 | tf_op jit(solution)/shard_map/ppermute | solution.py:945
  21.3 3.3 %collective-permute-done.3.refs_3_ = bf16[128,768]{1,0:T(8,128)(2,1)S(1)} collective-permute-done((bf16[128,768]{1,0:T(8,128)(2,1)}, bf16[128,768]{1,0:T(8,128)(2,1)S(1)}, u32[]{:S(2)}, u32[]{:S(2)}) %collective-permute-start.3) | collective-permute-done | bytes 196640 | tf_op jit(solution)/shard_map/ppermute | solution.py:945
  30.1 5.1 %all-to-all-start.1 = ((bf16[4,48,1920]{2,1,0:T(8,128)(2,1)}), bf16[4,48,1920]{2,1,0:T(8,128)(2,1)S(1)}, u32[]{:S(2)}, u32[]{:S(2)}) async-start(bf16[4,48,1920]{2,1,0:T(8,128)(2,1)} %broadcast_in_dim.9), calls=%async_computation.1 | async-start | bytes 1474560 | tf_op jit(solution)/shard_map/all_to_all | solution.py:888
  35.2 5.2 %collective-permute-done.6.refs_5_ = bf16[4,48,1280]{2,1,0:T(8,128)(2,1)S(1)} collective-permute-done((bf16[4,48,1280]{2,1,0:T(8,128)(2,1)S(1)}, bf16[4,48,1280]{2,1,0:T(8,128)(2,1)S(1)}, u32[]{:S(2)}, u32[]{:S(2)}) %collective-permute-start.6) | collective-permute-done | bytes 491552 | tf_op jit(solution)/shard_map/ppermute | solution.py:874
  40.8 1.8 collective-permute-start.8
  43.1 6.6 %collective-permute-done.8.refs_7_ = bf16[4,48,1280]{2,1,0:T(8,128)(2,1)S(1)} collective-permute-done((bf16[4,48,1280]{2,1,0:T(8,128)(2,1)S(1)}, bf16[4,48,1280]{2,1,0:T(8,128)(2,1)S(1)}, u32[]{:S(2)}, u32[]{:S(2)}) %collective-permute-start.8) | collective-permute-done | bytes 491552 | tf_op jit(solution)/shard_map/ppermute | solution.py:874
  50.2 1.8 collective-permute-start.14
  52.9 5.4 %project.1 = (bf16[512,768]{1,0:T(8,128)(2,1)}, bf16[512,768]{1,0:T(8,128)(2,1)}, bf16[512,768]{1,0:T(8,128)(2,1)}, bf16[512,768]{1,0:T(8,128)(2,1)}, f32[8,768]...) custom-call(bf16[4,128,768]{2,1,0:T(8,128)(2,1)S(1)} %copy-done, ...), custom_call_target="tpu_custom_call" | custom-call | flops 1 | bytes 1 | tf_op jit(solution)/shard_map/project/pallas_call | solution.py:244
  58.3 2.5 collective-permute-done.15.refs_4_
  62.4 1.6 collective-permute-start.17
  64.1 5.0 %all-to-all-start.2 = ((bf16[4,192,384]{2,1,0:T(8,128)(2,1)}), bf16[4,192,384]{2,1,0:T(8,128)(2,1)}, u32[]{:S(2)}, u32[]{:S(2)}) async-start(bf16[4,192,384]{2,1,0:T(8,128)(2,1)} %broadcast_in_dim.10), calls=%async_computation.2 | async-start | bytes 1179648 | tf_op jit(solution)/shard_map/all_to_all | solution.py:888
  69.2 9.8 %mix.1 = (bf16[768,512]{1,0:T(8,128)(2,1)}, bf16[512,768]{1,0:T(8,128)(2,1)}, f32[12,512]{1,0:T(8,128)}) custom-call(bf16[512,768]{1,0:T(8,128)(2,1)} %get-tuple-element.241.refs_0_.refs_1_, bf16[512,768]{1,0:T(8,128)(2,1)} %get-tuple-element.242.refs_1_.refs_2_, bf16[512,768]{1,0:T(8,128)(2,1)} %get-tuple-element.243.refs_2_.refs_3_, ...), custom_call_target="tpu_custom_call" | custom-call | flops 99999997952 | bytes 1 | tf_op jit(solution)/shard_map/mix/pallas_call | solution.py:244
  79.8 5.8 %all-to-all-done.2.refs_6_ = bf16[4,192,384]{2,1,0:T(8,128)(2,1)} async-done(((bf16[4,192,384]{2,1,0:T(8,128)(2,1)}), bf16[4,192,384]{2,1,0:T(8,128)(2,1)}, u32[]{:S(2)}, u32[]{:S(2)}) %all-to-all-start.2) | async-done | bytes 589856 | tf_op jit(solution)/shard_map/all_to_all | solution.py:888
  87.6 9.5 %collective-permute-done.20.refs_6_ = bf16[4,48,1920]{2,1,0:T(8,128)(2,1)S(1)} collective-permute-done((bf16[4,48,1920]{2,1,0:T(8,128)(2,1)S(1)}, bf16[4,48,1920]{2,1,0:T(8,128)(2,1)S(1)}, u32[]{:S(2)}, u32[]{:S(2)}) %collective-permute-start.20) | collective-permute-done | bytes 737312 | tf_op jit(solution)/shard_map/ppermute | solution.py:874
  100.4 8.8 %widen.1 = (f32[512,768]{1,0:T(8,128)}, bf16[512,768]{1,0:T(8,128)(2,1)}, bf16[512,3072]{1,0:T(8,128)(2,1)}, bf16[512,3072]{1,0:T(8,128)(2,1)}, bf16[4,4,48,3840]{3,2,1,0:T(8,128)(2,1)}) custom-call(bf16[512,768]{1,0:T(8,128)(2,1)} %get-tuple-element.248.refs_0_, bf16[512,768]{1,0:T(8,128)(2,1)} %get-tuple-element.249.refs_1_, ...), custom_call_target="tpu_custom_call" | custom-call | flops 99999997952 | bytes 1 | tf_op jit(solution)/shard_map/widen/pallas_call | solution.py:244
  109.3 4.0 %collective-permute-done.18.refs_7_ = bf16[4,192,384]{2,1,0:T(8,128)(2,1)S(1)} collective-permute-done((bf16[4,192,384]{2,1,0:T(8,128)(2,1)}, bf16[4,192,384]{2,1,0:T(8,128)(2,1)S(1)}, u32[]{:S(2)}, u32[]{:S(2)}) %collective-permute-start.18) | collective-permute-done | bytes 589856 | tf_op jit(solution)/shard_map/ppermute | solution.py:874
  114.1 7.3 %grad_of_down.1 = (bf16[4,4,96,768]{3,2,1,0:T(8,128)(2,1)}, bf16[4,4,96,768]{3,2,1,0:T(8,128)(2,1)}, bf16[512,768]{1,0:T(8,128)(2,1)}) custom-call(bf16[512,3072]{1,0:T(8,128)(2,1)} %get-tuple-element.260.refs_0_.refs_2_, bf16[4,128,768]{2,1,0:T(8,128)(2,1)S(1)} %copy-done.3, bf16[128,768]{1,0:T(8,128)(2,1)} %collective-permute-done.13.refs_2_, ...), custom_call_target="tpu_custom_call" | custom-call | flops 99999997952 | bytes 1 | tf_op jit(solution)/shard_map/grad_of_down/pallas_call | solution.py:244
  121.4 1.8 collective-permute-done.25.refs_9_
  123.7 1.6 collective-permute-done.30.refs_13_
  125.3 9.7 %narrow0.1 = (f32[512,768]{1,0:T(8,128)}, bf16[4,4,24,3072]{3,2,1,0:T(8,128)(2,1)}, bf16[4,4,24,3072]{3,2,1,0:T(8,128)(2,1)}, f32[512,768]{1,0:T(8,128)}) custom-call(f32[512,768]{1,0:T(8,128)} %get-tuple-element.270.refs_0_, bf16[512,768]{1,0:T(8,128)(2,1)} %get-tuple-element.271.refs_1_, bf16[512,3072]{1,0:T(8,128)(2,1)} %get-tuple-element.260.refs_0_.refs_2_, ...), custom_call_target="tpu_custom_call" | custom-call | flops 99999997952 | bytes 1 | tf_op jit(solution)/shard_map/narrow0/pallas_call | solution.py:244
  136.1 9.8 %narrow2.1 = (f32[512,768]{1,0:T(8,128)}, bf16[4,4,24,3072]{3,2,1,0:T(8,128)(2,1)}, bf16[4,4,24,3072]{3,2,1,0:T(8,128)(2,1)}, bf16[128,768]{1,0:T(8,128)(2,1)}, ...) custom-call(f32[512,768]{1,0:T(8,128)} %get-tuple-element.283.refs_0, ...), custom_call_target="tpu_custom_call", output_to_operand_aliasing={{1}: (15, {}), {2}: (16, {})} | custom-call | flops 99999997952 | bytes 1 | tf_op jit(solution)/shard_map/narrow2/pallas_call | solution.py:244
  145.9 6.1 %collective-permute-done.31 = bf16[8,96,768]{2,1,0:T(8,128)(2,1)S(1)} collective-permute-done((bf16[8,96,768]{2,1,0:T(8,128)(2,1)S(1)}, bf16[8,96,768]{2,1,0:T(8,128)(2,1)S(1)}, u32[]{:S(2)}, u32[]{:S(2)}) %collective-permute-start.31) | collective-permute-done | bytes 1179680 | tf_op jit(solution)/shard_map/ppermute | solution.py:874
  152.8 5.1 %turn.1 = (f32[512,768]{1,0:T(8,128)}, bf16[512,768]{1,0:T(8,128)(2,1)}, bf16[512,768]{1,0:T(8,128)(2,1)}, f32[2,768]{1,0:T(2,128)S(1)}) custom-call(f32[512,768]{1,0:T(8,128)} %get-tuple-element.270.refs_0_, f32[512,768]{1,0:T(8,128)} %get-tuple-element.298.refs_1_, bf16[512,768]{1,0:T(8,128)(2,1)} %get-tuple-element.273.refs_4_.refs_2_, ...), custom_call_target="tpu_custom_call" | custom-call | flops 99999997952 | bytes 1 | tf_op jit(solution)/shard_map/turn/pallas_call | solution.py:244
  158.0 1.9 add_convert_fusion.1
  159.9 2.3 collective-permute-done.33
  162.4 10.0 %attend_back0.1 = (bf16[512,1152]{1,0:T(8,128)(2,1)}, bf16[4,4,24,1920]{3,2,1,0:T(8,128)(2,1)}, bf16[4,4,24,1920]{3,2,1,0:T(8,128)(2,1)}) custom-call(bf16[512,768]{1,0:T(8,128)(2,1)} %get-tuple-element.308.refs_0_, bf16[512,768]{1,0:T(8,128)(2,1)} %get-tuple-element.241.refs_0_.refs_1_, bf16[512,768]{1,0:T(8,128)(2,1)} %get-tuple-element.242.refs_1_.refs_2_, ...), custom_call_target="tpu_custom_call" | custom-call | flops 99999997952 | bytes 1 | tf_op jit(solution)/shard_map/attend_back0/pallas_call | solution.py:244
  173.6 3.7 %all-to-all-start.3 = ((bf16[4,96,768]{2,1,0:T(8,128)(2,1)}), bf16[4,96,768]{2,1,0:T(8,128)(2,1)S(1)}, u32[]{:S(2)}, u32[]{:S(2)}) async-start(bf16[4,96,768]{2,1,0:T(8,128)(2,1)} %add_convert_fusion.7), calls=%async_computation.3 | async-start | bytes 1179648 | tf_op jit(solution)/shard_map/all_to_all | solution.py:888
  180.5 2.6 add_convert_fusion.4
  183.5 9.2 %attend_back1.1 = (bf16[512,1152]{1,0:T(8,128)(2,1)}, bf16[4,4,24,1152]{3,2,1,0:T(8,128)(2,1)}, bf16[4,4,24,1152]{3,2,1,0:T(8,128)(2,1)}) custom-call(bf16[512,768]{1,0:T(8,128)(2,1)} %get-tuple-element.308.refs_0_, bf16[512,768]{1,0:T(8,128)(2,1)} %get-tuple-element.241.refs_0_.refs_1_, bf16[512,768]{1,0:T(8,128)(2,1)} %get-tuple-element.242.refs_1_.refs_2_, ...), custom_call_target="tpu_custom_call" | custom-call | flops 99999997952 | bytes 1 | tf_op jit(solution)/shard_map/attend_back1/pallas_call | solution.py:244
  194.1 2.0 collective-permute-done.37
  196.1 2.3 add_convert_fusion.6
  198.4 4.9 %all-to-all-start.4 = ((bf16[4,24,3072]{2,1,0:T(8,128)(2,1)}), bf16[4,24,3072]{2,1,0:T(8,128)(2,1)S(1)}, u32[]{:S(2)}, u32[]{:S(2)}) async-start(bf16[4,24,3072]{2,1,0:T(8,128)(2,1)} %add_convert_fusion.6), calls=%async_computation.4 | async-start | bytes 1179648 | tf_op jit(solution)/shard_map/all_to_all | solution.py:888
  204.7 1.8 collective-permute-start.39
  208.1 7.1 %finish_tokens.1 = (bf16[128,768]{1,0:T(8,128)(2,1)}, bf16[128,768]{1,0:T(8,128)(2,1)}, bf16[128,768]{1,0:T(8,128)(2,1)}, bf16[128,768]{1,0:T(8,128)(2,1)}, f32[2,768]{1,0:T(2,128)S(1)}) custom-call(bf16[512,768]{1,0:T(8,128)(2,1)} %get-tuple-element.248.refs_0_, bf16[512,1152]{1,0:T(8,128)(2,1)} %get-tuple-element.328.refs_1_, ...), custom_call_target="tpu_custom_call" | custom-call | flops 1 | bytes 1 | tf_op jit(solution)/shard_map/finish_tokens/pallas_call | solution.py:244
  215.2 1.7 collective-permute-done.39
  218.2 4.8 %collective-permute-done.42 = bf16[4,24,1152]{2,1,0:T(8,128)(2,1)S(1)} collective-permute-done((bf16[4,24,1152]{2,1,0:T(8,128)(2,1)S(1)}, bf16[4,24,1152]{2,1,0:T(8,128)(2,1)S(1)}, u32[]{:S(2)}, u32[]{:S(2)}) %collective-permute-start.42) | collective-permute-done | bytes 221216 | tf_op jit(solution)/shard_map/ppermute | solution.py:874
  224.0 5.2 %all-to-all-start.5 = ((bf16[4,24,3072]{2,1,0:T(8,128)(2,1)}), bf16[4,24,3072]{2,1,0:T(8,128)(2,1)S(1)}, u32[]{:S(2)}, u32[]{:S(2)}) async-start(bf16[4,24,3072]{2,1,0:T(8,128)(2,1)} %pad_maximum_fusion), calls=%async_computation.5 | async-start | bytes 1179648 | tf_op jit(solution)/shard_map/all_to_all | solution.py:888
  230.9 1.7 collective-permute-start.44
  233.0 1.7 collective-permute-start.47
  236.9 1.8 collective-permute-done.44.refs_27_
  238.7 3.5 %collective-permute-done.45.refs_28_ = bf16[128,768]{1,0:T(8,128)(2,1)S(1)} collective-permute-done((bf16[128,768]{1,0:T(8,128)(2,1)S(1)}, bf16[128,768]{1,0:T(8,128)(2,1)S(1)}, u32[]{:S(2)}, u32[]{:S(2)}) %collective-permute-start.45) | collective-permute-done | bytes 196640 | tf_op jit(solution)/shard_map/ppermute | solution.py:945
  242.1 4.2 %collective-permute-done.47.refs_31_ = bf16[128,768]{1,0:T(8,128)(2,1)} collective-permute-done((bf16[128,768]{1,0:T(8,128)(2,1)S(1)}, bf16[128,768]{1,0:T(8,128)(2,1)}, u32[]{:S(2)}, u32[]{:S(2)}) %collective-permute-start.47) | collective-permute-done | bytes 196640 | tf_op jit(solution)/shard_map/ppermute | solution.py:945
  246.3 1.8 sum_up.1
  248.1 5.4 %all-to-all-start.6 = ((bf16[32,16,128]{2,1,0:T(8,128)(2,1)}), bf16[32,16,128]{2,1,0:T(8,128)(2,1)S(1)}, u32[]{:S(2)}, u32[]{:S(2)}) async-start(bf16[32,16,128]{2,1,0:T(8,128)(2,1)} %get-tuple-element.363), calls=%async_computation.6 | async-start | bytes 262144 | tf_op jit(solution)/shard_map/all_to_all | solution.py:928
  255.1 6.4 %collective-permute-done.48.refs_32_ = bf16[128,768]{1,0:T(8,128)(2,1)S(1)} collective-permute-done((bf16[128,768]{1,0:T(8,128)(2,1)S(1)}, bf16[128,768]{1,0:T(8,128)(2,1)S(1)}, u32[]{:S(2)}, u32[]{:S(2)}) %collective-permute-start.48) | collective-permute-done | bytes 196640 | tf_op jit(solution)/shard_map/ppermute | solution.py:945
  262.1 4.5 %update.1 = (f32[1,128]{1,0:T(1,128)}, f32[24,768]{1,0:T(8,128)}, f32[24,768]{1,0:T(8,128)}, f32[24,768]{1,0:T(8,128)}, f32[24,768]{1,0:T(8,128)}, /*index=5*/f3...) custom-call(f32[24,3072]{1,0:T(8,128)S(1)} %get-tuple-element.362.re, ...), custom_call_target="tpu_custom_call" | custom-call | flops 99999997952 | bytes 1 | tf_op jit(solution)/shard_map/update/pallas_call | solution.py:244
  (163 shorter events, 42.8 us)
Async XLA Ops:
  3.1 12.4 %collective-permute-start.5 = (bf16[96,384]{1,0:T(8,128)(2,1)S(1)}, bf16[96,384]{1,0:T(8,128)(2,1)S(1)}, u32[]{:S(2)}, u32[]{:S(2)}) collective-permute-start(bf16[96,384]{1,0:T(8,128)(2,1)S(1)} %get-tuple-element.218), channel_id=1, source_target_pairs={{0,1},{1,0},{2,3},{3,2},{4,5},{5,4},{6,7},{7,6},{8,9},{9,8},{10,11... | collective-permute-start | bytes 221192 | tf_op jit(solution)/shard_map/ppermute | solution.py:874
  4.9 20.4 %all-to-all-start = ((bf16[4,48,1280]{2,1,0:T(8,128)(2,1)}), bf16[4,48,1280]{2,1,0:T(8,128)(2,1)S(1)}, u32[]{:S(2)}, u32[]{:S(2)}) async-start(bf16[4,48,1280]{2,1,0:T(8,128)(2,1)} %broadcast_in_dim.8), calls=%async_computation | async-start | bytes 983040 | tf_op jit(solution)/shard_map/all_to_all | solution.py:888
  13.3 8.0 %collective-permute-start.2 = (bf16[128,768]{1,0:T(8,128)(2,1)}, bf16[128,768]{1,0:T(8,128)(2,1)S(1)}, u32[]{:S(2)}, u32[]{:S(2)}) collective-permute-start(bf16[128,768]{1,0:T(8,128)(2,1)} %get-tuple-element.213), channel_id=1, source_target_pairs={{0,2},{1,3},{2,0},{3,1},{4,6},{5,7},{6,4},{7,5},{8,10},{9,11},{10,... | collective-permute-start | bytes 589832 | tf_op jit(solution)/shard_map/ppermute | solution.py:945
  14.9 9.7 %collective-permute-start.3 = (bf16[128,768]{1,0:T(8,128)(2,1)}, bf16[128,768]{1,0:T(8,128)(2,1)S(1)}, u32[]{:S(2)}, u32[]{:S(2)}) collective-permute-start(bf16[128,768]{1,0:T(8,128)(2,1)} %get-tuple-element.214), channel_id=1, source_target_pairs={{0,3},{1,2},{2,1},{3,0},{4,7},{5,6},{6,5},{7,4},{8,11},{9,10},{10,... | collective-permute-start | bytes 589832 | tf_op jit(solution)/shard_map/ppermute | solution.py:945
  27.1 13.3 %collective-permute-start.6 = (bf16[4,48,1280]{2,1,0:T(8,128)(2,1)S(1)}, bf16[4,48,1280]{2,1,0:T(8,128)(2,1)S(1)}, u32[]{:S(2)}, u32[]{:S(2)}) collective-permute-start(bf16[4,48,1280]{2,1,0:T(8,128)(2,1)S(1)} %all-to-all-done.refs_4_), channel_id=1, source_target_pairs={{0,4},{1,3},{2,6},{3,1},{4,0},{5,7},{6,2},{7,5},{8,12},{9,11},{10,... | collective-permute-start | bytes 1474568 | tf_op jit(solution)/shard_map/ppermute | solution.py:874
  28.6 12.2 %collective-permute-start.7 = (bf16[4,48,1280]{2,1,0:T(8,128)(2,1)S(1)}, bf16[4,48,1280]{2,1,0:T(8,128)(2,1)S(1)}, u32[]{:S(2)}, u32[]{:S(2)}) collective-permute-start(bf16[4,48,1280]{2,1,0:T(8,128)(2,1)S(1)} %all-to-all-done.refs_4_), channel_id=1, source_target_pairs={{0,2},{1,5},{2,0},{3,7},{4,6},{5,1},{6,4},{7,3},{8,10},{9,13},{10,... | collective-permute-start | bytes 1474568 | tf_op jit(solution)/shard_map/ppermute | solution.py:874
  30.1 28.1 %all-to-all-start.1 = ((bf16[4,48,1920]{2,1,0:T(8,128)(2,1)}), bf16[4,48,1920]{2,1,0:T(8,128)(2,1)S(1)}, u32[]{:S(2)}, u32[]{:S(2)}) async-start(bf16[4,48,1920]{2,1,0:T(8,128)(2,1)} %broadcast_in_dim.9), calls=%async_computation.1 | async-start | bytes 1474560 | tf_op jit(solution)/shard_map/all_to_all | solution.py:888
  35.2 7.9 %collective-permute-start.9 = (bf16[4,48,1280]{2,1,0:T(8,128)(2,1)S(1)}, bf16[4,48,1280]{2,1,0:T(8,128)(2,1)S(1)}, u32[]{:S(2)}, u32[]{:S(2)}) collective-permute-start(bf16[4,48,1280]{2,1,0:T(8,128)(2,1)S(1)} %all-to-all-done.refs_4_), channel_id=1, source_target_pairs={{0,1},{1,0},{2,3},{3,2},{4,5},{5,4},{6,7},{7,6},{8,9},{9,8},{10,11... | collective-permute-start | bytes 1474568 | tf_op jit(solution)/shard_map/ppermute | solution.py:874
  40.8 8.8 %collective-permute-start.8 = (bf16[4,48,1280]{2,1,0:T(8,128)(2,1)S(1)}, bf16[4,48,1280]{2,1,0:T(8,128)(2,1)S(1)}, u32[]{:S(2)}, u32[]{:S(2)}) collective-permute-start(bf16[4,48,1280]{2,1,0:T(8,128)(2,1)S(1)} %collective-permute-done.6.refs_5_), channel_id=1, source_target_pairs={{0,2},{1,5},{2,0},{3,7},{4,6},{5,1},{6,4},{7,3},{8,10},{9,13},{10,... | collective-permute-start | bytes 1474568 | tf_op jit(solution)/shard_map/ppermute | solution.py:874
  42.6 7.1 %collective-permute-start.10 = (bf16[4,48,1280]{2,1,0:T(8,128)(2,1)S(1)}, bf16[4,48,1280]{2,1,0:T(8,128)(2,1)S(1)}, u32[]{:S(2)}, u32[]{:S(2)}) collective-permute-start(bf16[4,48,1280]{2,1,0:T(8,128)(2,1)S(1)} %collective-permute-done.6.refs_5_), channel_id=1, source_target_pairs={{0,1},{1,0},{2,3},{3,2},{4,5},{5,4},{6,7},{7,6},{8,9},{9,8},{10,11... | collective-permute-start | bytes 1474568 | tf_op jit(solution)/shard_map/ppermute | solution.py:874
  42.6 7.1 %collective-permute-start.11 = (bf16[4,48,1280]{2,1,0:T(8,128)(2,1)S(1)}, bf16[4,48,1280]{2,1,0:T(8,128)(2,1)S(1)}, u32[]{:S(2)}, u32[]{:S(2)}) collective-permute-start(bf16[4,48,1280]{2,1,0:T(8,128)(2,1)S(1)} %collective-permute-done.7.refs_6_), channel_id=1, source_target_pairs={{0,1},{1,0},{2,3},{3,2},{4,5},{5,4},{6,7},{7,6},{8,9},{9,8},{10,11... | collective-permute-start | bytes 1474568 | tf_op jit(solution)/shard_map/ppermute | solution.py:874
  49.7 8.6 %collective-permute-start.13 = (bf16[128,768]{1,0:T(8,128)(2,1)}, bf16[128,768]{1,0:T(8,128)(2,1)}, u32[]{:S(2)}, u32[]{:S(2)}) collective-permute-start(bf16[128,768]{1,0:T(8,128)(2,1)} %get-tuple-element.235), channel_id=1, source_target_pairs={{0,1},{1,0},{2,3},{3,2},{4,5},{5,4},{6,7},{7,6},{8,9},{9,8},{10,11... | collective-permute-start | bytes 589832 | tf_op jit(solution)/shard_map/ppermute | solution.py:945
  50.2 8.1 %collective-permute-start.14 = (bf16[128,768]{1,0:T(8,128)(2,1)}, bf16[128,768]{1,0:T(8,128)(2,1)}, u32[]{:S(2)}, u32[]{:S(2)}) collective-permute-start(bf16[128,768]{1,0:T(8,128)(2,1)} %get-tuple-element.236), channel_id=1, source_target_pairs={{0,2},{1,3},{2,0},{3,1},{4,6},{5,7},{6,4},{7,5},{8,10},{9,11},{10,... | collective-permute-start | bytes 589832 | tf_op jit(solution)/shard_map/ppermute | solution.py:945
  51.9 8.9 %collective-permute-start.15 = (bf16[128,768]{1,0:T(8,128)(2,1)}, bf16[128,768]{1,0:T(8,128)(2,1)}, u32[]{:S(2)}, u32[]{:S(2)}) collective-permute-start(bf16[128,768]{1,0:T(8,128)(2,1)} %get-tuple-element.237), channel_id=1, source_target_pairs={{0,3},{1,2},{2,1},{3,0},{4,7},{5,6},{6,5},{7,4},{8,11},{9,10},{10,... | collective-permute-start | bytes 589832 | tf_op jit(solution)/shard_map/ppermute | solution.py:945
  60.8 18.3 %collective-permute-start.16 = (bf16[4,48,1920]{2,1,0:T(8,128)(2,1)S(1)}, bf16[4,48,1920]{2,1,0:T(8,128)(2,1)S(1)}, u32[]{:S(2)}, u32[]{:S(2)}) collective-permute-start(bf16[4,48,1920]{2,1,0:T(8,128)(2,1)S(1)} %all-to-all-done.1.refs_3_), channel_id=1, source_target_pairs={{0,4},{1,3},{2,6},{3,1},{4,0},{5,7},{6,2},{7,5},{8,12},{9,11},{10,... | collective-permute-start | bytes 2211848 | tf_op jit(solution)/shard_map/ppermute | solution.py:874
  62.4 17.4 %collective-permute-start.17 = (bf16[4,48,1920]{2,1,0:T(8,128)(2,1)S(1)}, bf16[4,48,1920]{2,1,0:T(8,128)(2,1)S(1)}, u32[]{:S(2)}, u32[]{:S(2)}) collective-permute-start(bf16[4,48,1920]{2,1,0:T(8,128)(2,1)S(1)} %all-to-all-done.1.refs_3_), channel_id=1, source_target_pairs={{0,2},{1,5},{2,0},{3,7},{4,6},{5,1},{6,4},{7,3},{8,10},{9,13},{10,... | collective-permute-start | bytes 2211848 | tf_op jit(solution)/shard_map/ppermute | solution.py:874
  64.0 23.6 %collective-permute-start.21 = (bf16[4,48,1920]{2,1,0:T(8,128)(2,1)S(1)}, bf16[4,48,1920]{2,1,0:T(8,128)(2,1)}, u32[]{:S(2)}, u32[]{:S(2)}) collective-permute-start(bf16[4,48,1920]{2,1,0:T(8,128)(2,1)S(1)} %all-to-all-done.1.refs_3_), channel_id=1, source_target_pairs={{0,1},{1,0},{2,3},{3,2},{4,5},{5,4},{6,7},{7,6},{8,9},{9,8},{10,11... | collective-permute-start | bytes 2211848 | tf_op jit(solution)/shard_map/ppermute | solution.py:874
  64.1 21.5 %all-to-all-start.2 = ((bf16[4,192,384]{2,1,0:T(8,128)(2,1)}), bf16[4,192,384]{2,1,0:T(8,128)(2,1)}, u32[]{:S(2)}, u32[]{:S(2)}) async-start(bf16[4,192,384]{2,1,0:T(8,128)(2,1)} %broadcast_in_dim.10), calls=%async_computation.2 | async-start | bytes 1179648 | tf_op jit(solution)/shard_map/all_to_all | solution.py:888
  85.6 11.5 %collective-permute-start.20 = (bf16[4,48,1920]{2,1,0:T(8,128)(2,1)S(1)}, bf16[4,48,1920]{2,1,0:T(8,128)(2,1)S(1)}, u32[]{:S(2)}, u32[]{:S(2)}) collective-permute-start(bf16[4,48,1920]{2,1,0:T(8,128)(2,1)S(1)} %collective-permute-done.16.refs_4_), channel_id=1, source_target_pairs={{0,2},{1,5},{2,0},{3,7},{4,6},{5,1},{6,4},{7,3},{8,10},{9,13},{10,... | collective-permute-start | bytes 2211848 | tf_op jit(solution)/shard_map/ppermute | solution.py:874
  86.2 10.9 %collective-permute-start.22 = (bf16[4,48,1920]{2,1,0:T(8,128)(2,1)S(1)}, bf16[4,48,1920]{2,1,0:T(8,128)(2,1)S(1)}, u32[]{:S(2)}, u32[]{:S(2)}) collective-permute-start(bf16[4,48,1920]{2,1,0:T(8,128)(2,1)S(1)} %collective-permute-done.16.refs_4_), channel_id=1, source_target_pairs={{0,1},{1,0},{2,3},{3,2},{4,5},{5,4},{6,7},{7,6},{8,9},{9,8},{10,11... | collective-permute-start | bytes 2211848 | tf_op jit(solution)/shard_map/ppermute | solution.py:874
  86.2 10.9 %collective-permute-start.23 = (bf16[4,48,1920]{2,1,0:T(8,128)(2,1)S(1)}, bf16[4,48,1920]{2,1,0:T(8,128)(2,1)S(1)}, u32[]{:S(2)}, u32[]{:S(2)}) collective-permute-start(bf16[4,48,1920]{2,1,0:T(8,128)(2,1)S(1)} %collective-permute-done.17.refs_5_), channel_id=1, source_target_pairs={{0,1},{1,0},{2,3},{3,2},{4,5},{5,4},{6,7},{7,6},{8,9},{9,8},{10,11... | collective-permute-start | bytes 2211848 | tf_op jit(solution)/shard_map/ppermute | solution.py:874
  97.1 16.2 %collective-permute-start.18 = (bf16[4,192,384]{2,1,0:T(8,128)(2,1)}, bf16[4,192,384]{2,1,0:T(8,128)(2,1)S(1)}, u32[]{:S(2)}, u32[]{:S(2)}) collective-permute-start(bf16[4,192,384]{2,1,0:T(8,128)(2,1)} %all-to-all-done.2.refs_6_), channel_id=1, source_target_pairs={{0,4},{1,3},{2,6},{3,1},{4,0},{5,7},{6,2},{7,5},{8,12},{9,11},{10,... | collective-permute-start | bytes 1769480 | tf_op jit(solution)/shard_map/ppermute | solution.py:874
  97.7 15.6 %collective-permute-start.19 = (bf16[4,192,384]{2,1,0:T(8,128)(2,1)}, bf16[4,192,384]{2,1,0:T(8,128)(2,1)S(1)}, u32[]{:S(2)}, u32[]{:S(2)}) collective-permute-start(bf16[4,192,384]{2,1,0:T(8,128)(2,1)} %all-to-all-done.2.refs_6_), channel_id=1, source_target_pairs={{0,2},{1,5},{2,0},{3,7},{4,6},{5,1},{6,4},{7,3},{8,10},{9,13},{10,... | collective-permute-start | bytes 1769480 | tf_op jit(solution)/shard_map/ppermute | solution.py:874
  98.2 23.2 %collective-permute-start.26 = (bf16[4,192,384]{2,1,0:T(8,128)(2,1)}, bf16[4,192,384]{2,1,0:T(8,128)(2,1)}, u32[]{:S(2)}, u32[]{:S(2)}) collective-permute-start(bf16[4,192,384]{2,1,0:T(8,128)(2,1)} %all-to-all-done.2.refs_6_), channel_id=1, source_target_pairs={{0,1},{1,0},{2,3},{3,2},{4,5},{5,4},{6,7},{7,6},{8,9},{9,8},{10,11... | collective-permute-start | bytes 1769480 | tf_op jit(solution)/shard_map/ppermute | solution.py:874
  113.3 9.9 %collective-permute-start.25 = (bf16[4,192,384]{2,1,0:T(8,128)(2,1)S(1)}, bf16[4,192,384]{2,1,0:T(8,128)(2,1)S(1)}, u32[]{:S(2)}, u32[]{:S(2)}) collective-permute-start(bf16[4,192,384]{2,1,0:T(8,128)(2,1)S(1)} %collective-permute-done.18.refs_7_), channel_id=1, source_target_pairs={{0,2},{1,5},{2,0},{3,7},{4,6},{5,1},{6,4},{7,3},{8,10},{9,13},{10,... | collective-permute-start | bytes 1769480 | tf_op jit(solution)/shard_map/ppermute | solution.py:874
  113.6 9.6 %collective-permute-start.27 = (bf16[4,192,384]{2,1,0:T(8,128)(2,1)S(1)}, bf16[4,192,384]{2,1,0:T(8,128)(2,1)S(1)}, u32[]{:S(2)}, u32[]{:S(2)}) collective-permute-start(bf16[4,192,384]{2,1,0:T(8,128)(2,1)S(1)} %collective-permute-done.18.refs_7_), channel_id=1, source_target_pairs={{0,1},{1,0},{2,3},{3,2},{4,5},{5,4},{6,7},{7,6},{8,9},{9,8},{10,11... | collective-permute-start | bytes 1769480 | tf_op jit(solution)/shard_map/ppermute | solution.py:874
  113.6 9.6 %collective-permute-start.28 = (bf16[4,192,384]{2,1,0:T(8,128)(2,1)S(1)}, bf16[4,192,384]{2,1,0:T(8,128)(2,1)S(1)}, u32[]{:S(2)}, u32[]{:S(2)}) collective-permute-start(bf16[4,192,384]{2,1,0:T(8,128)(2,1)S(1)} %collective-permute-done.19.refs_8_), channel_id=1, source_target_pairs={{0,1},{1,0},{2,3},{3,2},{4,5},{5,4},{6,7},{7,6},{8,9},{9,8},{10,11... | collective-permute-start | bytes 1769480 | tf_op jit(solution)/shard_map/ppermute | solution.py:874
  123.2 11.9 %collective-permute-start.29 = (bf16[4,4,96,768]{3,2,1,0:T(8,128)(2,1)}, bf16[4,4,96,768]{3,2,1,0:T(8,128)(2,1)S(1)}, u32[]{:S(2)}, u32[]{:S(2)}) collective-permute-start(bf16[4,4,96,768]{3,2,1,0:T(8,128)(2,1)} %get-tuple-element.269), channel_id=1, source_target_pairs={{0,1},{1,0},{2,3},{3,2},{4,5},{5,4},{6,7},{7,6},{8,9},{9,8},{10,11... | collective-permute-start | bytes 7077896 | tf_op jit(solution)/shard_map/ppermute | solution.py:874
  135.8 16.3 %collective-permute-start.31 = (bf16[8,96,768]{2,1,0:T(8,128)(2,1)S(1)}, bf16[8,96,768]{2,1,0:T(8,128)(2,1)S(1)}, u32[]{:S(2)}, u32[]{:S(2)}) collective-permute-start(bf16[8,96,768]{2,1,0:T(8,128)(2,1)S(1)} %bitcast.50), channel_id=1, source_target_pairs={{0,2},{1,5},{2,0},{3,7},{4,6},{5,1},{6,4},{7,3},{8,10},{9,13},{10,... | collective-permute-start | bytes 3538952 | tf_op jit(solution)/shard_map/ppermute | solution.py:874
  152.2 9.9 %collective-permute-start.33 = (bf16[4,96,768]{2,1,0:T(8,128)(2,1)S(1)}, bf16[4,96,768]{2,1,0:T(8,128)(2,1)S(1)}, u32[]{:S(2)}, u32[]{:S(2)}) collective-permute-start(bf16[4,96,768]{2,1,0:T(8,128)(2,1)S(1)} %fusion.3), channel_id=1, source_target_pairs={{0,4},{1,3},{2,6},{3,1},{4,0},{5,7},{6,2},{7,5},{8,12},{9,11},{10,... | collective-permute-start | bytes 1769480 | tf_op jit(solution)/shard_map/ppermute | solution.py:874
  162.2 16.5 %collective-permute-start.34 = (bf16[8,24,3072]{2,1,0:T(8,128)(2,1)}, bf16[8,24,3072]{2,1,0:T(8,128)(2,1)}, u32[]{:S(2)}, u32[]{:S(2)}) collective-permute-start(bf16[8,24,3072]{2,1,0:T(8,128)(2,1)} %bitcast.3), channel_id=1, source_target_pairs={{0,2},{1,5},{2,0},{3,7},{4,6},{5,1},{6,4},{7,3},{8,10},{9,13},{10,... | collective-permute-start | bytes 3538952 | tf_op jit(solution)/shard_map/ppermute | solution.py:874
  172.4 8.0 %collective-permute-start.36 = (bf16[4,4,24,1920]{3,2,1,0:T(8,128)(2,1)}, bf16[4,4,24,1920]{3,2,1,0:T(8,128)(2,1)}, u32[]{:S(2)}, u32[]{:S(2)}) collective-permute-start(bf16[4,4,24,1920]{3,2,1,0:T(8,128)(2,1)} %get-tuple-element.319), channel_id=1, source_target_pairs={{0,1},{1,0},{2,3},{3,2},{4,5},{5,4},{6,7},{7,6},{8,9},{9,8},{10,11... | collective-permute-start | bytes 4423688 | tf_op jit(solution)/shard_map/ppermute | solution.py:874
  173.6 20.5 %all-to-all-start.3 = ((bf16[4,96,768]{2,1,0:T(8,128)(2,1)}), bf16[4,96,768]{2,1,0:T(8,128)(2,1)S(1)}, u32[]{:S(2)}, u32[]{:S(2)}) async-start(bf16[4,96,768]{2,1,0:T(8,128)(2,1)} %add_convert_fusion.7), calls=%async_computation.3 | async-start | bytes 1179648 | tf_op jit(solution)/shard_map/all_to_all | solution.py:888
  179.9 14.2 %collective-permute-start.35 = (bf16[4,24,3072]{2,1,0:T(8,128)(2,1)S(1)}, bf16[4,24,3072]{2,1,0:T(8,128)(2,1)}, u32[]{:S(2)}, u32[]{:S(2)}) collective-permute-start(bf16[4,24,3072]{2,1,0:T(8,128)(2,1)S(1)} %fusion), channel_id=1, source_target_pairs={{0,4},{1,3},{2,6},{3,1},{4,0},{5,7},{6,2},{7,5},{8,12},{9,11},{10,... | collective-permute-start | bytes 1769480 | tf_op jit(solution)/shard_map/ppermute | solution.py:874
  183.0 13.1 %collective-permute-start.37 = (bf16[8,24,1920]{2,1,0:T(8,128)(2,1)}, bf16[8,24,1920]{2,1,0:T(8,128)(2,1)}, u32[]{:S(2)}, u32[]{:S(2)}) collective-permute-start(bf16[8,24,1920]{2,1,0:T(8,128)(2,1)} %bitcast.6), channel_id=1, source_target_pairs={{0,2},{1,5},{2,0},{3,7},{4,6},{5,1},{6,4},{7,3},{8,10},{9,13},{10,... | collective-permute-start | bytes 2211848 | tf_op jit(solution)/shard_map/ppermute | solution.py:874
  192.7 10.6 %collective-permute-start.38 = (bf16[4,4,24,1152]{3,2,1,0:T(8,128)(2,1)}, bf16[4,4,24,1152]{3,2,1,0:T(8,128)(2,1)}, u32[]{:S(2)}, u32[]{:S(2)}) collective-permute-start(bf16[4,4,24,1152]{3,2,1,0:T(8,128)(2,1)} %get-tuple-element.326), channel_id=1, source_target_pairs={{0,1},{1,0},{2,3},{3,2},{4,5},{5,4},{6,7},{7,6},{8,9},{9,8},{10,11... | collective-permute-start | bytes 2654216 | tf_op jit(solution)/shard_map/ppermute | solution.py:874
  198.4 25.6 %all-to-all-start.4 = ((bf16[4,24,3072]{2,1,0:T(8,128)(2,1)}), bf16[4,24,3072]{2,1,0:T(8,128)(2,1)S(1)}, u32[]{:S(2)}, u32[]{:S(2)}) async-start(bf16[4,24,3072]{2,1,0:T(8,128)(2,1)} %add_convert_fusion.6), calls=%async_computation.4 | async-start | bytes 1179648 | tf_op jit(solution)/shard_map/all_to_all | solution.py:888
  204.7 12.3 %collective-permute-start.39 = (bf16[8,24,1152]{2,1,0:T(8,128)(2,1)S(1)}, bf16[8,24,1152]{2,1,0:T(8,128)(2,1)S(1)}, u32[]{:S(2)}, u32[]{:S(2)}) collective-permute-start(bf16[8,24,1152]{2,1,0:T(8,128)(2,1)S(1)} %bitcast.51), channel_id=1, source_target_pairs={{0,2},{1,5},{2,0},{3,7},{4,6},{5,1},{6,4},{7,3},{8,10},{9,13},{10,... | collective-permute-start | bytes 1327112 | tf_op jit(solution)/shard_map/ppermute | solution.py:874
  207.5 9.6 %collective-permute-start.41 = (bf16[4,24,1920]{2,1,0:T(8,128)(2,1)S(1)}, bf16[4,24,1920]{2,1,0:T(8,128)(2,1)S(1)}, u32[]{:S(2)}, u32[]{:S(2)}) collective-permute-start(bf16[4,24,1920]{2,1,0:T(8,128)(2,1)S(1)} %fusion.5), channel_id=1, source_target_pairs={{0,4},{1,3},{2,6},{3,1},{4,0},{5,7},{6,2},{7,5},{8,12},{9,11},{10,... | collective-permute-start | bytes 1105928 | tf_op jit(solution)/shard_map/ppermute | solution.py:874
  217.0 6.0 %collective-permute-start.42 = (bf16[4,24,1152]{2,1,0:T(8,128)(2,1)S(1)}, bf16[4,24,1152]{2,1,0:T(8,128)(2,1)S(1)}, u32[]{:S(2)}, u32[]{:S(2)}) collective-permute-start(bf16[4,24,1152]{2,1,0:T(8,128)(2,1)S(1)} %fusion.7), channel_id=1, source_target_pairs={{0,4},{1,3},{2,6},{3,1},{4,0},{5,7},{6,2},{7,5},{8,12},{9,11},{10,... | collective-permute-start | bytes 663560 | tf_op jit(solution)/shard_map/ppermute | solution.py:874
  224.0 22.3 %all-to-all-start.5 = ((bf16[4,24,3072]{2,1,0:T(8,128)(2,1)}), bf16[4,24,3072]{2,1,0:T(8,128)(2,1)S(1)}, u32[]{:S(2)}, u32[]{:S(2)}) async-start(bf16[4,24,3072]{2,1,0:T(8,128)(2,1)} %pad_maximum_fusion), calls=%async_computation.5 | async-start | bytes 1179648 | tf_op jit(solution)/shard_map/all_to_all | solution.py:888
  230.4 6.5 %collective-permute-start.43 = (bf16[128,768]{1,0:T(8,128)(2,1)S(1)}, bf16[128,768]{1,0:T(8,128)(2,1)S(1)}, u32[]{:S(2)}, u32[]{:S(2)}) collective-permute-start(bf16[128,768]{1,0:T(8,128)(2,1)S(1)} %copy-done.19), channel_id=1, source_target_pairs={{0,1},{1,0},{2,3},{3,2},{4,5},{5,4},{6,7},{7,6},{8,9},{9,8},{10,11... | collective-permute-start | bytes 589832 | tf_op jit(solution)/shard_map/ppermute | solution.py:945
  230.9 7.8 %collective-permute-start.44 = (bf16[128,768]{1,0:T(8,128)(2,1)S(1)}, bf16[128,768]{1,0:T(8,128)(2,1)S(1)}, u32[]{:S(2)}, u32[]{:S(2)}) collective-permute-start(bf16[128,768]{1,0:T(8,128)(2,1)S(1)} %copy-done.18), channel_id=1, source_target_pairs={{0,2},{1,3},{2,0},{3,1},{4,6},{5,7},{6,4},{7,5},{8,10},{9,11},{10,... | collective-permute-start | bytes 589832 | tf_op jit(solution)/shard_map/ppermute | solution.py:945
  232.6 9.5 %collective-permute-start.45 = (bf16[128,768]{1,0:T(8,128)(2,1)S(1)}, bf16[128,768]{1,0:T(8,128)(2,1)S(1)}, u32[]{:S(2)}, u32[]{:S(2)}) collective-permute-start(bf16[128,768]{1,0:T(8,128)(2,1)S(1)} %copy-done.17), channel_id=1, source_target_pairs={{0,3},{1,2},{2,1},{3,0},{4,7},{5,6},{6,5},{7,4},{8,11},{9,10},{10,... | collective-permute-start | bytes 589832 | tf_op jit(solution)/shard_map/ppermute | solution.py:945
  232.6 9.5 %collective-permute-start.46 = (bf16[128,768]{1,0:T(8,128)(2,1)S(1)}, bf16[128,768]{1,0:T(8,128)(2,1)}, u32[]{:S(2)}, u32[]{:S(2)}) collective-permute-start(bf16[128,768]{1,0:T(8,128)(2,1)S(1)} %copy-done.22), channel_id=1, source_target_pairs={{0,1},{1,0},{2,3},{3,2},{4,5},{5,4},{6,7},{7,6},{8,9},{9,8},{10,11... | collective-permute-start | bytes 589832 | tf_op jit(solution)/shard_map/ppermute | solution.py:945
  233.0 13.2 %collective-permute-start.47 = (bf16[128,768]{1,0:T(8,128)(2,1)S(1)}, bf16[128,768]{1,0:T(8,128)(2,1)}, u32[]{:S(2)}, u32[]{:S(2)}) collective-permute-start(bf16[128,768]{1,0:T(8,128)(2,1)S(1)} %copy-done.21), channel_id=1, source_target_pairs={{0,2},{1,3},{2,0},{3,1},{4,6},{5,7},{6,4},{7,5},{8,10},{9,11},{10,... | collective-permute-start | bytes 589832 | tf_op jit(solution)/shard_map/ppermute | solution.py:945
  248.1 13.6 %all-to-all-start.6 = ((bf16[32,16,128]{2,1,0:T(8,128)(2,1)}), bf16[32,16,128]{2,1,0:T(8,128)(2,1)S(1)}, u32[]{:S(2)}, u32[]{:S(2)}) async-start(bf16[32,16,128]{2,1,0:T(8,128)(2,1)} %get-tuple-element.363), calls=%async_computation.6 | async-start | bytes 262144 | tf_op jit(solution)/shard_map/all_to_all | solution.py:928
  253.5 8.0 %collective-permute-start.48 = (bf16[128,768]{1,0:T(8,128)(2,1)S(1)}, bf16[128,768]{1,0:T(8,128)(2,1)S(1)}, u32[]{:S(2)}, u32[]{:S(2)}) collective-permute-start(bf16[128,768]{1,0:T(8,128)(2,1)S(1)} %copy-done.20), channel_id=1, source_target_pairs={{0,3},{1,2},{2,1},{3,0},{4,7},{5,6},{6,5},{7,4},{8,11},{9,10},{10,... | collective-permute-start | bytes 589832 | tf_op jit(solution)/shard_map/ppermute | solution.py:945
  (35 other events, 224.3 us)

commit v3 on v2

--- a/solution.py
+++ b/solution.py
@@ -1006,18 +1006,17 @@
     one = [*one, corner_one, *one_core, *to_core(corner_one)]
     low_one, query, key, value, norms, whole_qkv, tokens = project(plan, tokens, one)
     cot = to_rows(out_grad, after(others_cot, corner_one))
-    near_two, query, cot = meet(near_two, query, cot)
+    near_two, query = meet(near_two, query)
     beside_two, across_two = spread(near_two)
-    near_three = along_z(plan, after(spread_three, near_two))
+    spread_three, cot = meet(after(spread_three, near_two), cot)
+    near_three = along_z(plan, spread_three)
     mixed_t, mixed, lse = mix(plan, query, key, value, seg, pad)
-    beside_two, across_two, near_three, mixed, lse, mixed_t = meet(
-        beside_two, across_two, near_three, mixed, lse, mixed_t
-    )
+    beside_two, across_two, mixed, lse, mixed_t = meet(beside_two, across_two, mixed, lse, mixed_t)
     corner_two = send(plan, beside_two, plan.first)
-    beside_three, across_three = spread(near_three)
     two = [near_two, beside_two, across_two]
     two_core = to_core(*two)
-    corner_two, two_core = meet(corner_two, two_core)
+    corner_two, two_core, near_three = meet(corner_two, two_core, near_three)
+    beside_three, across_three = spread(near_three)
     two = [*two, corner_two, *two_core, *to_core(corner_two)]
     mid, low_two, hidden, slope, whole_ou = widen(plan, tokens, mixed, norms, two)
     beside_three, across_three, hidden = meet(beside_three, across_three, hidden)

time: 272 us -> 266 us (0.978)
  waiting for transfers between devices: 85 us -> 66.6 us
  starting transfers between devices: 63.5 us -> 75.8 us
    ppermute x37, waiting for transfers between devices: 51.2 us -> 36.9 us  [send(): return lax.ppermute(values, AXES, perm)]
    ppermute x37, starting transfers between devices: 17.8 us -> 29.6 us  [send(): return lax.ppermute(values, AXES, perm)]
    all_to_all x6, waiting for transfers between devices: 7.09 us -> 4.03 us  [along_z(): lax.all_to_all(values, 'dp', 0, 0, axis_index_groups=plan.groups, tiled=T...]
  transfers between devices with their start and end apart: 56 -> 56, of which waited for: 28 -> 26; matrix products, arithmetic and copies ran while one was open for 6% -> 6% of each run, Pallas kernels for 32% -> 32%
where the time goes in v3:
time: 266 us; the launch traced here: 261 us
  Pallas kernels  91.9 us (35%)
  starting transfers between devices  75.8 us (28%)
  waiting for transfers between devices  66.6 us (25%)
  other arithmetic  16.2 us (6%)
  local copies, waits for them, and re-layouts  7.64 us (3%)
  between operations  2.77 us (1%)
    pallas_call x14, Pallas kernels, call(): pl.pallas_call(kernel, out_shape=[pltpu.HBM(o.shape, o.dtype) if kind in...  91.9 us
    ppermute x37, waiting for transfers between devices, send(): return lax.ppermute(values, AXES, perm)  36.9 us
    all_to_all x6, starting transfers between devices, along_z(): lax.all_to_all(values, 'dp', 0, 0, axis_index_groups=plan.groups, tiled=T...  31.9 us
    ppermute x37, starting transfers between devices, send(): return lax.ppermute(values, AXES, perm)  29.6 us
    ppermute x12, waiting for transfers between devices, swap(): lax.ppermute(values, 'seq', [(i, i ^ number) for i in range(plan.seq)])  25.4 us
    ppermute x12, starting transfers between devices, swap(): lax.ppermute(values, 'seq', [(i, i ^ number) for i in range(plan.seq)])  8.7 us
    convert_element_type x3, other arithmetic, fold(): add(keep[:size], got[:size]).astype(BF)  5.87 us
    all_to_all x1, starting transfers between devices, finish(): cards = lax.all_to_all(cards, AXES, 0, 0, tiled=True)  5.65 us
  transfers between devices with their start and end apart: 56, of which 26 were waited for; matrix products, arithmetic and copies ran while one was open for 6% of the time, Pallas kernels for 32%

profile of v3, /device:TPU:0, one launch (start us, length us, event | category | flops | bytes accessed | tf_op | source)
XLA Modules:
  0.0 260.9 jit_solution(11598700085571462679)
XLA Ops:
  4.9 6.2 %all-to-all-start = ((bf16[4,48,1280]{2,1,0:T(8,128)(2,1)}), bf16[4,48,1280]{2,1,0:T(8,128)(2,1)S(1)}, u32[]{:S(2)}, u32[]{:S(2)}) async-start(bf16[4,48,1280]{2,1,0:T(8,128)(2,1)} %broadcast_in_dim.8), calls=%async_computation | async-start | bytes 983040 | tf_op jit(solution)/shard_map/all_to_all | solution.py:888
  11.1 2.1 other_rows.1
  16.5 4.8 %collective-permute-done.2.refs_2_ = bf16[128,768]{1,0:T(8,128)(2,1)S(1)} collective-permute-done((bf16[128,768]{1,0:T(8,128)(2,1)}, bf16[128,768]{1,0:T(8,128)(2,1)S(1)}, u32[]{:S(2)}, u32[]{:S(2)}) %collective-permute-start.2) | collective-permute-done | bytes 196640 | tf_op jit(solution)/shard_map/ppermute | solution.py:945
  21.3 3.3 %collective-permute-done.3.refs_3_ = bf16[128,768]{1,0:T(8,128)(2,1)S(1)} collective-permute-done((bf16[128,768]{1,0:T(8,128)(2,1)}, bf16[128,768]{1,0:T(8,128)(2,1)S(1)}, u32[]{:S(2)}, u32[]{:S(2)}) %collective-permute-start.3) | collective-permute-done | bytes 196640 | tf_op jit(solution)/shard_map/ppermute | solution.py:945
  30.1 5.1 %all-to-all-start.1 = ((bf16[4,48,1920]{2,1,0:T(8,128)(2,1)}), bf16[4,48,1920]{2,1,0:T(8,128)(2,1)S(1)}, u32[]{:S(2)}, u32[]{:S(2)}) async-start(bf16[4,48,1920]{2,1,0:T(8,128)(2,1)} %broadcast_in_dim.9), calls=%async_computation.1 | async-start | bytes 1474560 | tf_op jit(solution)/shard_map/all_to_all | solution.py:888
  35.2 5.2 %collective-permute-done.6.refs_5_ = bf16[4,48,1280]{2,1,0:T(8,128)(2,1)S(1)} collective-permute-done((bf16[4,48,1280]{2,1,0:T(8,128)(2,1)S(1)}, bf16[4,48,1280]{2,1,0:T(8,128)(2,1)S(1)}, u32[]{:S(2)}, u32[]{:S(2)}) %collective-permute-start.6) | collective-permute-done | bytes 491552 | tf_op jit(solution)/shard_map/ppermute | solution.py:874
  40.8 1.8 collective-permute-start.8
  43.1 6.6 %collective-permute-done.8.refs_7_ = bf16[4,48,1280]{2,1,0:T(8,128)(2,1)S(1)} collective-permute-done((bf16[4,48,1280]{2,1,0:T(8,128)(2,1)S(1)}, bf16[4,48,1280]{2,1,0:T(8,128)(2,1)S(1)}, u32[]{:S(2)}, u32[]{:S(2)}) %collective-permute-start.8) | collective-permute-done | bytes 491552 | tf_op jit(solution)/shard_map/ppermute | solution.py:874
  50.2 1.8 collective-permute-start.20
  52.9 5.4 %project.1 = (bf16[512,768]{1,0:T(8,128)(2,1)}, bf16[512,768]{1,0:T(8,128)(2,1)}, bf16[512,768]{1,0:T(8,128)(2,1)}, bf16[512,768]{1,0:T(8,128)(2,1)}, f32[8,768]...) custom-call(bf16[4,128,768]{2,1,0:T(8,128)(2,1)S(1)} %copy-done, ...), custom_call_target="tpu_custom_call" | custom-call | flops 1 | bytes 1 | tf_op jit(solution)/shard_map/project/pallas_call | solution.py:244
  58.3 1.6 collective-permute-start.13
  61.4 5.0 %all-to-all-start.2 = ((bf16[4,192,384]{2,1,0:T(8,128)(2,1)}), bf16[4,192,384]{2,1,0:T(8,128)(2,1)}, u32[]{:S(2)}, u32[]{:S(2)}) async-start(bf16[4,192,384]{2,1,0:T(8,128)(2,1)} %broadcast_in_dim.10), calls=%async_computation.2 | async-start | bytes 1179648 | tf_op jit(solution)/shard_map/all_to_all | solution.py:888
  66.5 9.8 %mix.1 = (bf16[768,512]{1,0:T(8,128)(2,1)}, bf16[512,768]{1,0:T(8,128)(2,1)}, f32[12,512]{1,0:T(8,128)}) custom-call(bf16[512,768]{1,0:T(8,128)(2,1)} %get-tuple-element.234.refs_0_.refs_1_, bf16[512,768]{1,0:T(8,128)(2,1)} %get-tuple-element.235.refs_1_.refs_2_, bf16[512,768]{1,0:T(8,128)(2,1)} %get-tuple-element.236.refs_2_.refs_3_, ...), custom_call_target="tpu_custom_call" | custom-call | flops 99999997952 | bytes 1 | tf_op jit(solution)/shard_map/mix/pallas_call | solution.py:244
  77.3 1.7 collective-permute-start.15
  80.4 2.6 all-to-all-done.2.refs_6_
  83.0 5.9 %collective-permute-done.15.refs_6_ = bf16[4,48,1920]{2,1,0:T(8,128)(2,1)} collective-permute-done((bf16[4,48,1920]{2,1,0:T(8,128)(2,1)S(1)}, bf16[4,48,1920]{2,1,0:T(8,128)(2,1)}, u32[]{:S(2)}, u32[]{:S(2)}) %collective-permute-start.15) | collective-permute-done | bytes 737312 | tf_op jit(solution)/shard_map/ppermute | solution.py:874
  90.4 1.7 collective-permute-start.23
  93.3 8.9 %widen.1 = (f32[512,768]{1,0:T(8,128)}, bf16[512,768]{1,0:T(8,128)(2,1)}, bf16[512,3072]{1,0:T(8,128)(2,1)}, bf16[512,3072]{1,0:T(8,128)(2,1)}, bf16[4,4,48,3840]{3,2,1,0:T(8,128)(2,1)}) custom-call(bf16[512,768]{1,0:T(8,128)(2,1)} %get-tuple-element.252.refs_0_, bf16[512,768]{1,0:T(8,128)(2,1)} %get-tuple-element.253.refs_1_, ...), custom_call_target="tpu_custom_call" | custom-call | flops 99999997952 | bytes 1 | tf_op jit(solution)/shard_map/widen/pallas_call | solution.py:244
  102.3 2.2 collective-permute-done.22.refs_7_
  104.8 1.8 collective-permute-start.25
  107.1 7.3 %grad_of_down.1 = (bf16[4,4,96,768]{3,2,1,0:T(8,128)(2,1)}, bf16[4,4,96,768]{3,2,1,0:T(8,128)(2,1)}, bf16[512,768]{1,0:T(8,128)(2,1)}) custom-call(bf16[512,3072]{1,0:T(8,128)(2,1)} %get-tuple-element.262.refs_0_.refs_2_, bf16[4,128,768]{2,1,0:T(8,128)(2,1)S(1)} %copy-done.3, bf16[128,768]{1,0:T(8,128)(2,1)} %collective-permute-done.19.refs_2_, ...), custom_call_target="tpu_custom_call" | custom-call | flops 99999997952 | bytes 1 | tf_op jit(solution)/shard_map/grad_of_down/pallas_call | solution.py:244
  115.2 1.6 collective-permute-done.30.refs_13_
  116.8 9.7 %narrow0.1 = (f32[512,768]{1,0:T(8,128)}, bf16[4,4,24,3072]{3,2,1,0:T(8,128)(2,1)}, bf16[4,4,24,3072]{3,2,1,0:T(8,128)(2,1)}, f32[512,768]{1,0:T(8,128)}) custom-call(f32[512,768]{1,0:T(8,128)} %get-tuple-element.272.refs_0_, bf16[512,768]{1,0:T(8,128)(2,1)} %get-tuple-element.273.refs_1_, bf16[512,3072]{1,0:T(8,128)(2,1)} %get-tuple-element.262.refs_0_.refs_2_, ...), custom_call_target="tpu_custom_call" | custom-call | flops 99999997952 | bytes 1 | tf_op jit(solution)/shard_map/narrow0/pallas_call | solution.py:244
  127.3 1.8 collective-permute-start.31
  129.1 9.7 %narrow2.1 = (f32[512,768]{1,0:T(8,128)}, bf16[4,4,24,3072]{3,2,1,0:T(8,128)(2,1)}, bf16[4,4,24,3072]{3,2,1,0:T(8,128)(2,1)}, bf16[128,768]{1,0:T(8,128)(2,1)}, ...) custom-call(f32[512,768]{1,0:T(8,128)} %get-tuple-element.285.refs_0, ...), custom_call_target="tpu_custom_call", output_to_operand_aliasing={{1}: (15, {}), {2}: (16, {})} | custom-call | flops 99999997952 | bytes 1 | tf_op jit(solution)/shard_map/narrow2/pallas_call | solution.py:244
  138.8 4.7 %collective-permute-done.31 = bf16[8,96,768]{2,1,0:T(8,128)(2,1)S(1)} collective-permute-done((bf16[8,96,768]{2,1,0:T(8,128)(2,1)S(1)}, bf16[8,96,768]{2,1,0:T(8,128)(2,1)S(1)}, u32[]{:S(2)}, u32[]{:S(2)}) %collective-permute-start.31) | collective-permute-done | bytes 1179680 | tf_op jit(solution)/shard_map/ppermute | solution.py:874
  145.3 5.1 %turn.1 = (f32[512,768]{1,0:T(8,128)}, bf16[512,768]{1,0:T(8,128)(2,1)}, bf16[512,768]{1,0:T(8,128)(2,1)}, f32[2,768]{1,0:T(2,128)S(1)}) custom-call(f32[512,768]{1,0:T(8,128)} %get-tuple-element.272.refs_0_, f32[512,768]{1,0:T(8,128)} %get-tuple-element.300.refs_1_, bf16[512,768]{1,0:T(8,128)(2,1)} %get-tuple-element.275.refs_4_.refs_2_, ...), custom_call_target="tpu_custom_call" | custom-call | flops 99999997952 | bytes 1 | tf_op jit(solution)/shard_map/turn/pallas_call | solution.py:244
  150.5 1.9 add_convert_fusion.1
  153.7 1.8 collective-permute-start.34
  155.4 10.0 %attend_back0.1 = (bf16[512,1152]{1,0:T(8,128)(2,1)}, bf16[4,4,24,1920]{3,2,1,0:T(8,128)(2,1)}, bf16[4,4,24,1920]{3,2,1,0:T(8,128)(2,1)}) custom-call(bf16[512,768]{1,0:T(8,128)(2,1)} %get-tuple-element.310.refs_0_, bf16[512,768]{1,0:T(8,128)(2,1)} %get-tuple-element.234.refs_0_.refs_1_, bf16[512,768]{1,0:T(8,128)(2,1)} %get-tuple-element.235.refs_1_.refs_2_, ...), custom_call_target="tpu_custom_call" | custom-call | flops 99999997952 | bytes 1 | tf_op jit(solution)/shard_map/attend_back0/pallas_call | solution.py:244
  166.5 5.2 %all-to-all-start.3 = ((bf16[4,96,768]{2,1,0:T(8,128)(2,1)}), bf16[4,96,768]{2,1,0:T(8,128)(2,1)S(1)}, u32[]{:S(2)}, u32[]{:S(2)}) async-start(bf16[4,96,768]{2,1,0:T(8,128)(2,1)} %add_convert_fusion.7), calls=%async_computation.3 | async-start | bytes 1179648 | tf_op jit(solution)/shard_map/all_to_all | solution.py:888
  174.7 2.6 add_convert_fusion.4
  177.6 9.2 %attend_back1.1 = (bf16[512,1152]{1,0:T(8,128)(2,1)}, bf16[4,4,24,1152]{3,2,1,0:T(8,128)(2,1)}, bf16[4,4,24,1152]{3,2,1,0:T(8,128)(2,1)}) custom-call(bf16[512,768]{1,0:T(8,128)(2,1)} %get-tuple-element.310.refs_0_, bf16[512,768]{1,0:T(8,128)(2,1)} %get-tuple-element.234.refs_0_.refs_1_, bf16[512,768]{1,0:T(8,128)(2,1)} %get-tuple-element.235.refs_1_.refs_2_, ...), custom_call_target="tpu_custom_call" | custom-call | flops 99999997952 | bytes 1 | tf_op jit(solution)/shard_map/attend_back1/pallas_call | solution.py:244
  188.3 2.0 collective-permute-done.37
  190.3 2.3 add_convert_fusion.6
  192.6 4.9 %all-to-all-start.4 = ((bf16[4,24,3072]{2,1,0:T(8,128)(2,1)}), bf16[4,24,3072]{2,1,0:T(8,128)(2,1)S(1)}, u32[]{:S(2)}, u32[]{:S(2)}) async-start(bf16[4,24,3072]{2,1,0:T(8,128)(2,1)} %add_convert_fusion.6), calls=%async_computation.4 | async-start | bytes 1179648 | tf_op jit(solution)/shard_map/all_to_all | solution.py:888
  201.9 7.1 %finish_tokens.1 = (bf16[128,768]{1,0:T(8,128)(2,1)}, bf16[128,768]{1,0:T(8,128)(2,1)}, bf16[128,768]{1,0:T(8,128)(2,1)}, bf16[128,768]{1,0:T(8,128)(2,1)}, f32[2,768]{1,0:T(2,128)S(1)}) custom-call(bf16[512,768]{1,0:T(8,128)(2,1)} %get-tuple-element.252.refs_0_, bf16[512,1152]{1,0:T(8,128)(2,1)} %get-tuple-element.330.refs_1_, ...), custom_call_target="tpu_custom_call" | custom-call | flops 1 | bytes 1 | tf_op jit(solution)/shard_map/finish_tokens/pallas_call | solution.py:244
  210.0 2.7 %collective-permute-start.42 = (bf16[4,24,1152]{2,1,0:T(8,128)(2,1)S(1)}, bf16[4,24,1152]{2,1,0:T(8,128)(2,1)S(1)}, u32[]{:S(2)}, u32[]{:S(2)}) collective-permute-start(bf16[4,24,1152]{2,1,0:T(8,128)(2,1)S(1)} %fusion.7), channel_id=1, source_target_pairs={{0,4},{1,3},{2,6},{3,1},{4,0},{5,7},{6,2},{7,5},{8,12},{9,11},{10,... | collective-permute-start | bytes 663560 | tf_op jit(solution)/shard_map/ppermute | solution.py:874
  213.8 2.8 %collective-permute-done.42 = bf16[4,24,1152]{2,1,0:T(8,128)(2,1)S(1)} collective-permute-done((bf16[4,24,1152]{2,1,0:T(8,128)(2,1)S(1)}, bf16[4,24,1152]{2,1,0:T(8,128)(2,1)S(1)}, u32[]{:S(2)}, u32[]{:S(2)}) %collective-permute-start.42) | collective-permute-done | bytes 221216 | tf_op jit(solution)/shard_map/ppermute | solution.py:874
  217.6 5.4 %all-to-all-start.5 = ((bf16[4,24,3072]{2,1,0:T(8,128)(2,1)}), bf16[4,24,3072]{2,1,0:T(8,128)(2,1)S(1)}, u32[]{:S(2)}, u32[]{:S(2)}) async-start(bf16[4,24,3072]{2,1,0:T(8,128)(2,1)} %pad_maximum_fusion), calls=%async_computation.5 | async-start | bytes 1179648 | tf_op jit(solution)/shard_map/all_to_all | solution.py:888
  229.2 3.2 %collective-permute-done.44.refs_27_ = bf16[128,768]{1,0:T(8,128)(2,1)S(1)} collective-permute-done((bf16[128,768]{1,0:T(8,128)(2,1)S(1)}, bf16[128,768]{1,0:T(8,128)(2,1)S(1)}, u32[]{:S(2)}, u32[]{:S(2)}) %collective-permute-start.44) | collective-permute-done | bytes 196640 | tf_op jit(solution)/shard_map/ppermute | solution.py:945
  232.4 2.4 collective-permute-done.45.refs_28_
  234.8 5.2 %collective-permute-done.47.refs_31_ = bf16[128,768]{1,0:T(8,128)(2,1)} collective-permute-done((bf16[128,768]{1,0:T(8,128)(2,1)S(1)}, bf16[128,768]{1,0:T(8,128)(2,1)}, u32[]{:S(2)}, u32[]{:S(2)}) %collective-permute-start.47) | collective-permute-done | bytes 196640 | tf_op jit(solution)/shard_map/ppermute | solution.py:945
  240.1 1.8 sum_up.1
  241.9 5.6 %all-to-all-start.6 = ((bf16[32,16,128]{2,1,0:T(8,128)(2,1)}), bf16[32,16,128]{2,1,0:T(8,128)(2,1)S(1)}, u32[]{:S(2)}, u32[]{:S(2)}) async-start(bf16[32,16,128]{2,1,0:T(8,128)(2,1)} %get-tuple-element.365), calls=%async_computation.6 | async-start | bytes 262144 | tf_op jit(solution)/shard_map/all_to_all | solution.py:928
  247.5 1.6 collective-permute-start.48
  249.1 6.4 %collective-permute-done.48.refs_32_ = bf16[128,768]{1,0:T(8,128)(2,1)S(1)} collective-permute-done((bf16[128,768]{1,0:T(8,128)(2,1)S(1)}, bf16[128,768]{1,0:T(8,128)(2,1)S(1)}, u32[]{:S(2)}, u32[]{:S(2)}) %collective-permute-start.48) | collective-permute-done | bytes 196640 | tf_op jit(solution)/shard_map/ppermute | solution.py:945
  256.2 4.5 %update.1 = (f32[1,128]{1,0:T(1,128)}, f32[24,768]{1,0:T(8,128)}, f32[24,768]{1,0:T(8,128)}, f32[24,768]{1,0:T(8,128)}, f32[24,768]{1,0:T(8,128)}, /*index=5*/f3...) custom-call(f32[24,3072]{1,0:T(8,128)S(1)} %get-tuple-element.364.re, ...), custom_call_target="tpu_custom_call" | custom-call | flops 99999997952 | bytes 1 | tf_op jit(solution)/shard_map/update/pallas_call | solution.py:244
  (163 shorter events, 46.2 us)
Async XLA Ops:
  3.1 12.4 %collective-permute-start.5 = (bf16[96,384]{1,0:T(8,128)(2,1)S(1)}, bf16[96,384]{1,0:T(8,128)(2,1)S(1)}, u32[]{:S(2)}, u32[]{:S(2)}) collective-permute-start(bf16[96,384]{1,0:T(8,128)(2,1)S(1)} %get-tuple-element.219), channel_id=1, source_target_pairs={{0,1},{1,0},{2,3},{3,2},{4,5},{5,4},{6,7},{7,6},{8,9},{9,8},{10,11... | collective-permute-start | bytes 221192 | tf_op jit(solution)/shard_map/ppermute | solution.py:874
  4.9 20.4 %all-to-all-start = ((bf16[4,48,1280]{2,1,0:T(8,128)(2,1)}), bf16[4,48,1280]{2,1,0:T(8,128)(2,1)S(1)}, u32[]{:S(2)}, u32[]{:S(2)}) async-start(bf16[4,48,1280]{2,1,0:T(8,128)(2,1)} %broadcast_in_dim.8), calls=%async_computation | async-start | bytes 983040 | tf_op jit(solution)/shard_map/all_to_all | solution.py:888
  13.3 8.0 %collective-permute-start.2 = (bf16[128,768]{1,0:T(8,128)(2,1)}, bf16[128,768]{1,0:T(8,128)(2,1)S(1)}, u32[]{:S(2)}, u32[]{:S(2)}) collective-permute-start(bf16[128,768]{1,0:T(8,128)(2,1)} %get-tuple-element.214), channel_id=1, source_target_pairs={{0,2},{1,3},{2,0},{3,1},{4,6},{5,7},{6,4},{7,5},{8,10},{9,11},{10,... | collective-permute-start | bytes 589832 | tf_op jit(solution)/shard_map/ppermute | solution.py:945
  14.9 9.7 %collective-permute-start.3 = (bf16[128,768]{1,0:T(8,128)(2,1)}, bf16[128,768]{1,0:T(8,128)(2,1)S(1)}, u32[]{:S(2)}, u32[]{:S(2)}) collective-permute-start(bf16[128,768]{1,0:T(8,128)(2,1)} %get-tuple-element.215), channel_id=1, source_target_pairs={{0,3},{1,2},{2,1},{3,0},{4,7},{5,6},{6,5},{7,4},{8,11},{9,10},{10,... | collective-permute-start | bytes 589832 | tf_op jit(solution)/shard_map/ppermute | solution.py:945
  27.1 13.3 %collective-permute-start.6 = (bf16[4,48,1280]{2,1,0:T(8,128)(2,1)S(1)}, bf16[4,48,1280]{2,1,0:T(8,128)(2,1)S(1)}, u32[]{:S(2)}, u32[]{:S(2)}) collective-permute-start(bf16[4,48,1280]{2,1,0:T(8,128)(2,1)S(1)} %all-to-all-done.refs_4_), channel_id=1, source_target_pairs={{0,4},{1,3},{2,6},{3,1},{4,0},{5,7},{6,2},{7,5},{8,12},{9,11},{10,... | collective-permute-start | bytes 1474568 | tf_op jit(solution)/shard_map/ppermute | solution.py:874
  28.6 12.2 %collective-permute-start.7 = (bf16[4,48,1280]{2,1,0:T(8,128)(2,1)S(1)}, bf16[4,48,1280]{2,1,0:T(8,128)(2,1)S(1)}, u32[]{:S(2)}, u32[]{:S(2)}) collective-permute-start(bf16[4,48,1280]{2,1,0:T(8,128)(2,1)S(1)} %all-to-all-done.refs_4_), channel_id=1, source_target_pairs={{0,2},{1,5},{2,0},{3,7},{4,6},{5,1},{6,4},{7,3},{8,10},{9,13},{10,... | collective-permute-start | bytes 1474568 | tf_op jit(solution)/shard_map/ppermute | solution.py:874
  30.1 28.1 %all-to-all-start.1 = ((bf16[4,48,1920]{2,1,0:T(8,128)(2,1)}), bf16[4,48,1920]{2,1,0:T(8,128)(2,1)S(1)}, u32[]{:S(2)}, u32[]{:S(2)}) async-start(bf16[4,48,1920]{2,1,0:T(8,128)(2,1)} %broadcast_in_dim.9), calls=%async_computation.1 | async-start | bytes 1474560 | tf_op jit(solution)/shard_map/all_to_all | solution.py:888
  35.2 7.9 %collective-permute-start.9 = (bf16[4,48,1280]{2,1,0:T(8,128)(2,1)S(1)}, bf16[4,48,1280]{2,1,0:T(8,128)(2,1)S(1)}, u32[]{:S(2)}, u32[]{:S(2)}) collective-permute-start(bf16[4,48,1280]{2,1,0:T(8,128)(2,1)S(1)} %all-to-all-done.refs_4_), channel_id=1, source_target_pairs={{0,1},{1,0},{2,3},{3,2},{4,5},{5,4},{6,7},{7,6},{8,9},{9,8},{10,11... | collective-permute-start | bytes 1474568 | tf_op jit(solution)/shard_map/ppermute | solution.py:874
  40.8 8.8 %collective-permute-start.8 = (bf16[4,48,1280]{2,1,0:T(8,128)(2,1)S(1)}, bf16[4,48,1280]{2,1,0:T(8,128)(2,1)S(1)}, u32[]{:S(2)}, u32[]{:S(2)}) collective-permute-start(bf16[4,48,1280]{2,1,0:T(8,128)(2,1)S(1)} %collective-permute-done.6.refs_5_), channel_id=1, source_target_pairs={{0,2},{1,5},{2,0},{3,7},{4,6},{5,1},{6,4},{7,3},{8,10},{9,13},{10,... | collective-permute-start | bytes 1474568 | tf_op jit(solution)/shard_map/ppermute | solution.py:874
  42.6 7.1 %collective-permute-start.10 = (bf16[4,48,1280]{2,1,0:T(8,128)(2,1)S(1)}, bf16[4,48,1280]{2,1,0:T(8,128)(2,1)S(1)}, u32[]{:S(2)}, u32[]{:S(2)}) collective-permute-start(bf16[4,48,1280]{2,1,0:T(8,128)(2,1)S(1)} %collective-permute-done.6.refs_5_), channel_id=1, source_target_pairs={{0,1},{1,0},{2,3},{3,2},{4,5},{5,4},{6,7},{7,6},{8,9},{9,8},{10,11... | collective-permute-start | bytes 1474568 | tf_op jit(solution)/shard_map/ppermute | solution.py:874
  42.6 7.1 %collective-permute-start.11 = (bf16[4,48,1280]{2,1,0:T(8,128)(2,1)S(1)}, bf16[4,48,1280]{2,1,0:T(8,128)(2,1)S(1)}, u32[]{:S(2)}, u32[]{:S(2)}) collective-permute-start(bf16[4,48,1280]{2,1,0:T(8,128)(2,1)S(1)} %collective-permute-done.7.refs_6_), channel_id=1, source_target_pairs={{0,1},{1,0},{2,3},{3,2},{4,5},{5,4},{6,7},{7,6},{8,9},{9,8},{10,11... | collective-permute-start | bytes 1474568 | tf_op jit(solution)/shard_map/ppermute | solution.py:874
  49.7 11.6 %collective-permute-start.19 = (bf16[128,768]{1,0:T(8,128)(2,1)}, bf16[128,768]{1,0:T(8,128)(2,1)}, u32[]{:S(2)}, u32[]{:S(2)}) collective-permute-start(bf16[128,768]{1,0:T(8,128)(2,1)} %get-tuple-element.247), channel_id=1, source_target_pairs={{0,1},{1,0},{2,3},{3,2},{4,5},{5,4},{6,7},{7,6},{8,9},{9,8},{10,11... | collective-permute-start | bytes 589832 | tf_op jit(solution)/shard_map/ppermute | solution.py:945
  50.2 11.3 %collective-permute-start.20 = (bf16[128,768]{1,0:T(8,128)(2,1)}, bf16[128,768]{1,0:T(8,128)(2,1)}, u32[]{:S(2)}, u32[]{:S(2)}) collective-permute-start(bf16[128,768]{1,0:T(8,128)(2,1)} %get-tuple-element.248), channel_id=1, source_target_pairs={{0,2},{1,3},{2,0},{3,1},{4,6},{5,7},{6,4},{7,5},{8,10},{9,11},{10,... | collective-permute-start | bytes 589832 | tf_op jit(solution)/shard_map/ppermute | solution.py:945
  51.9 9.5 %collective-permute-start.21 = (bf16[128,768]{1,0:T(8,128)(2,1)}, bf16[128,768]{1,0:T(8,128)(2,1)}, u32[]{:S(2)}, u32[]{:S(2)}) collective-permute-start(bf16[128,768]{1,0:T(8,128)(2,1)} %get-tuple-element.249), channel_id=1, source_target_pairs={{0,3},{1,2},{2,1},{3,0},{4,7},{5,6},{6,5},{7,4},{8,11},{9,10},{10,... | collective-permute-start | bytes 589832 | tf_op jit(solution)/shard_map/ppermute | solution.py:945
  58.3 18.6 %collective-permute-start.13 = (bf16[4,48,1920]{2,1,0:T(8,128)(2,1)S(1)}, bf16[4,48,1920]{2,1,0:T(8,128)(2,1)S(1)}, u32[]{:S(2)}, u32[]{:S(2)}) collective-permute-start(bf16[4,48,1920]{2,1,0:T(8,128)(2,1)S(1)} %all-to-all-done.1.refs_3_), channel_id=1, source_target_pairs={{0,4},{1,3},{2,6},{3,1},{4,0},{5,7},{6,2},{7,5},{8,12},{9,11},{10,... | collective-permute-start | bytes 2211848 | tf_op jit(solution)/shard_map/ppermute | solution.py:874
  59.9 17.4 %collective-permute-start.14 = (bf16[4,48,1920]{2,1,0:T(8,128)(2,1)S(1)}, bf16[4,48,1920]{2,1,0:T(8,128)(2,1)S(1)}, u32[]{:S(2)}, u32[]{:S(2)}) collective-permute-start(bf16[4,48,1920]{2,1,0:T(8,128)(2,1)S(1)} %all-to-all-done.1.refs_3_), channel_id=1, source_target_pairs={{0,2},{1,5},{2,0},{3,7},{4,6},{5,1},{6,4},{7,3},{8,10},{9,13},{10,... | collective-permute-start | bytes 2211848 | tf_op jit(solution)/shard_map/ppermute | solution.py:874
  61.3 19.1 %collective-permute-start.16 = (bf16[4,48,1920]{2,1,0:T(8,128)(2,1)S(1)}, bf16[4,48,1920]{2,1,0:T(8,128)(2,1)}, u32[]{:S(2)}, u32[]{:S(2)}) collective-permute-start(bf16[4,48,1920]{2,1,0:T(8,128)(2,1)S(1)} %all-to-all-done.1.refs_3_), channel_id=1, source_target_pairs={{0,1},{1,0},{2,3},{3,2},{4,5},{5,4},{6,7},{7,6},{8,9},{9,8},{10,11... | collective-permute-start | bytes 2211848 | tf_op jit(solution)/shard_map/ppermute | solution.py:874
  61.4 21.5 %all-to-all-start.2 = ((bf16[4,192,384]{2,1,0:T(8,128)(2,1)}), bf16[4,192,384]{2,1,0:T(8,128)(2,1)}, u32[]{:S(2)}, u32[]{:S(2)}) async-start(bf16[4,192,384]{2,1,0:T(8,128)(2,1)} %broadcast_in_dim.10), calls=%async_computation.2 | async-start | bytes 1179648 | tf_op jit(solution)/shard_map/all_to_all | solution.py:888
  77.3 11.6 %collective-permute-start.15 = (bf16[4,48,1920]{2,1,0:T(8,128)(2,1)S(1)}, bf16[4,48,1920]{2,1,0:T(8,128)(2,1)}, u32[]{:S(2)}, u32[]{:S(2)}) collective-permute-start(bf16[4,48,1920]{2,1,0:T(8,128)(2,1)S(1)} %collective-permute-done.13.refs_4_), channel_id=1, source_target_pairs={{0,2},{1,5},{2,0},{3,7},{4,6},{5,1},{6,4},{7,3},{8,10},{9,13},{10,... | collective-permute-start | bytes 2211848 | tf_op jit(solution)/shard_map/ppermute | solution.py:874
  79.0 9.8 %collective-permute-start.17 = (bf16[4,48,1920]{2,1,0:T(8,128)(2,1)S(1)}, bf16[4,48,1920]{2,1,0:T(8,128)(2,1)}, u32[]{:S(2)}, u32[]{:S(2)}) collective-permute-start(bf16[4,48,1920]{2,1,0:T(8,128)(2,1)S(1)} %collective-permute-done.13.refs_4_), channel_id=1, source_target_pairs={{0,1},{1,0},{2,3},{3,2},{4,5},{5,4},{6,7},{7,6},{8,9},{9,8},{10,11... | collective-permute-start | bytes 2211848 | tf_op jit(solution)/shard_map/ppermute | solution.py:874
  79.2 9.7 %collective-permute-start.18 = (bf16[4,48,1920]{2,1,0:T(8,128)(2,1)S(1)}, bf16[4,48,1920]{2,1,0:T(8,128)(2,1)}, u32[]{:S(2)}, u32[]{:S(2)}) collective-permute-start(bf16[4,48,1920]{2,1,0:T(8,128)(2,1)S(1)} %collective-permute-done.14.refs_5_), channel_id=1, source_target_pairs={{0,1},{1,0},{2,3},{3,2},{4,5},{5,4},{6,7},{7,6},{8,9},{9,8},{10,11... | collective-permute-start | bytes 2211848 | tf_op jit(solution)/shard_map/ppermute | solution.py:874
  88.9 15.6 %collective-permute-start.22 = (bf16[4,192,384]{2,1,0:T(8,128)(2,1)}, bf16[4,192,384]{2,1,0:T(8,128)(2,1)S(1)}, u32[]{:S(2)}, u32[]{:S(2)}) collective-permute-start(bf16[4,192,384]{2,1,0:T(8,128)(2,1)} %all-to-all-done.2.refs_6_), channel_id=1, source_target_pairs={{0,4},{1,3},{2,6},{3,1},{4,0},{5,7},{6,2},{7,5},{8,12},{9,11},{10,... | collective-permute-start | bytes 1769480 | tf_op jit(solution)/shard_map/ppermute | solution.py:874
  90.4 14.4 %collective-permute-start.23 = (bf16[4,192,384]{2,1,0:T(8,128)(2,1)}, bf16[4,192,384]{2,1,0:T(8,128)(2,1)S(1)}, u32[]{:S(2)}, u32[]{:S(2)}) collective-permute-start(bf16[4,192,384]{2,1,0:T(8,128)(2,1)} %all-to-all-done.2.refs_6_), channel_id=1, source_target_pairs={{0,2},{1,5},{2,0},{3,7},{4,6},{5,1},{6,4},{7,3},{8,10},{9,13},{10,... | collective-permute-start | bytes 1769480 | tf_op jit(solution)/shard_map/ppermute | solution.py:874
  92.2 22.2 %collective-permute-start.26 = (bf16[4,192,384]{2,1,0:T(8,128)(2,1)}, bf16[4,192,384]{2,1,0:T(8,128)(2,1)}, u32[]{:S(2)}, u32[]{:S(2)}) collective-permute-start(bf16[4,192,384]{2,1,0:T(8,128)(2,1)} %all-to-all-done.2.refs_6_), channel_id=1, source_target_pairs={{0,1},{1,0},{2,3},{3,2},{4,5},{5,4},{6,7},{7,6},{8,9},{9,8},{10,11... | collective-permute-start | bytes 1769480 | tf_op jit(solution)/shard_map/ppermute | solution.py:874
  104.8 9.9 %collective-permute-start.25 = (bf16[4,192,384]{2,1,0:T(8,128)(2,1)S(1)}, bf16[4,192,384]{2,1,0:T(8,128)(2,1)S(1)}, u32[]{:S(2)}, u32[]{:S(2)}) collective-permute-start(bf16[4,192,384]{2,1,0:T(8,128)(2,1)S(1)} %collective-permute-done.22.refs_7_), channel_id=1, source_target_pairs={{0,2},{1,5},{2,0},{3,7},{4,6},{5,1},{6,4},{7,3},{8,10},{9,13},{10,... | collective-permute-start | bytes 1769480 | tf_op jit(solution)/shard_map/ppermute | solution.py:874
  106.5 8.1 %collective-permute-start.27 = (bf16[4,192,384]{2,1,0:T(8,128)(2,1)S(1)}, bf16[4,192,384]{2,1,0:T(8,128)(2,1)S(1)}, u32[]{:S(2)}, u32[]{:S(2)}) collective-permute-start(bf16[4,192,384]{2,1,0:T(8,128)(2,1)S(1)} %collective-permute-done.22.refs_7_), channel_id=1, source_target_pairs={{0,1},{1,0},{2,3},{3,2},{4,5},{5,4},{6,7},{7,6},{8,9},{9,8},{10,11... | collective-permute-start | bytes 1769480 | tf_op jit(solution)/shard_map/ppermute | solution.py:874
  106.6 8.1 %collective-permute-start.28 = (bf16[4,192,384]{2,1,0:T(8,128)(2,1)S(1)}, bf16[4,192,384]{2,1,0:T(8,128)(2,1)S(1)}, u32[]{:S(2)}, u32[]{:S(2)}) collective-permute-start(bf16[4,192,384]{2,1,0:T(8,128)(2,1)S(1)} %collective-permute-done.23.refs_8_), channel_id=1, source_target_pairs={{0,1},{1,0},{2,3},{3,2},{4,5},{5,4},{6,7},{7,6},{8,9},{9,8},{10,11... | collective-permute-start | bytes 1769480 | tf_op jit(solution)/shard_map/ppermute | solution.py:874
  114.7 11.9 %collective-permute-start.29 = (bf16[4,4,96,768]{3,2,1,0:T(8,128)(2,1)}, bf16[4,4,96,768]{3,2,1,0:T(8,128)(2,1)S(1)}, u32[]{:S(2)}, u32[]{:S(2)}) collective-permute-start(bf16[4,4,96,768]{3,2,1,0:T(8,128)(2,1)} %get-tuple-element.271), channel_id=1, source_target_pairs={{0,1},{1,0},{2,3},{3,2},{4,5},{5,4},{6,7},{7,6},{8,9},{9,8},{10,11... | collective-permute-start | bytes 7077896 | tf_op jit(solution)/shard_map/ppermute | solution.py:874
  127.3 16.3 %collective-permute-start.31 = (bf16[8,96,768]{2,1,0:T(8,128)(2,1)S(1)}, bf16[8,96,768]{2,1,0:T(8,128)(2,1)S(1)}, u32[]{:S(2)}, u32[]{:S(2)}) collective-permute-start(bf16[8,96,768]{2,1,0:T(8,128)(2,1)S(1)} %bitcast.50), channel_id=1, source_target_pairs={{0,2},{1,5},{2,0},{3,7},{4,6},{5,1},{6,4},{7,3},{8,10},{9,13},{10,... | collective-permute-start | bytes 3538952 | tf_op jit(solution)/shard_map/ppermute | solution.py:874
  143.7 9.9 %collective-permute-start.33 = (bf16[4,96,768]{2,1,0:T(8,128)(2,1)S(1)}, bf16[4,96,768]{2,1,0:T(8,128)(2,1)S(1)}, u32[]{:S(2)}, u32[]{:S(2)}) collective-permute-start(bf16[4,96,768]{2,1,0:T(8,128)(2,1)S(1)} %fusion.3), channel_id=1, source_target_pairs={{0,4},{1,3},{2,6},{3,1},{4,0},{5,7},{6,2},{7,5},{8,12},{9,11},{10,... | collective-permute-start | bytes 1769480 | tf_op jit(solution)/shard_map/ppermute | solution.py:874
  145.3 5.2 %collective-permute-start.32 = (bf16[4,4,24,3072]{3,2,1,0:T(8,128)(2,1)}, bf16[4,4,24,3072]{3,2,1,0:T(8,128)(2,1)S(1)}, u32[]{:S(2)}, u32[]{:S(2)}) collective-permute-start(bf16[4,4,24,3072]{3,2,1,0:T(8,128)(2,1)} %get-tuple-element.297), channel_id=1, source_target_pairs={{0,1},{1,0},{2,3},{3,2},{4,5},{5,4},{6,7},{7,6},{8,9},{9,8},{10,11... | collective-permute-start | bytes 7077896 | tf_op jit(solution)/shard_map/ppermute | solution.py:874
  153.7 18.2 %collective-permute-start.34 = (bf16[8,24,3072]{2,1,0:T(8,128)(2,1)}, bf16[8,24,3072]{2,1,0:T(8,128)(2,1)}, u32[]{:S(2)}, u32[]{:S(2)}) collective-permute-start(bf16[8,24,3072]{2,1,0:T(8,128)(2,1)} %bitcast.3), channel_id=1, source_target_pairs={{0,2},{1,5},{2,0},{3,7},{4,6},{5,1},{6,4},{7,3},{8,10},{9,13},{10,... | collective-permute-start | bytes 3538952 | tf_op jit(solution)/shard_map/ppermute | solution.py:874
  165.4 9.3 %collective-permute-start.36 = (bf16[4,4,24,1920]{3,2,1,0:T(8,128)(2,1)}, bf16[4,4,24,1920]{3,2,1,0:T(8,128)(2,1)}, u32[]{:S(2)}, u32[]{:S(2)}) collective-permute-start(bf16[4,4,24,1920]{3,2,1,0:T(8,128)(2,1)} %get-tuple-element.321), channel_id=1, source_target_pairs={{0,1},{1,0},{2,3},{3,2},{4,5},{5,4},{6,7},{7,6},{8,9},{9,8},{10,11... | collective-permute-start | bytes 4423688 | tf_op jit(solution)/shard_map/ppermute | solution.py:874
  166.5 21.8 %all-to-all-start.3 = ((bf16[4,96,768]{2,1,0:T(8,128)(2,1)}), bf16[4,96,768]{2,1,0:T(8,128)(2,1)S(1)}, u32[]{:S(2)}, u32[]{:S(2)}) async-start(bf16[4,96,768]{2,1,0:T(8,128)(2,1)} %add_convert_fusion.7), calls=%async_computation.3 | async-start | bytes 1179648 | tf_op jit(solution)/shard_map/all_to_all | solution.py:888
  173.1 15.2 %collective-permute-start.35 = (bf16[4,24,3072]{2,1,0:T(8,128)(2,1)S(1)}, bf16[4,24,3072]{2,1,0:T(8,128)(2,1)}, u32[]{:S(2)}, u32[]{:S(2)}) collective-permute-start(bf16[4,24,3072]{2,1,0:T(8,128)(2,1)S(1)} %fusion), channel_id=1, source_target_pairs={{0,4},{1,3},{2,6},{3,1},{4,0},{5,7},{6,2},{7,5},{8,12},{9,11},{10,... | collective-permute-start | bytes 1769480 | tf_op jit(solution)/shard_map/ppermute | solution.py:874
  177.3 13.0 %collective-permute-start.37 = (bf16[8,24,1920]{2,1,0:T(8,128)(2,1)}, bf16[8,24,1920]{2,1,0:T(8,128)(2,1)}, u32[]{:S(2)}, u32[]{:S(2)}) collective-permute-start(bf16[8,24,1920]{2,1,0:T(8,128)(2,1)} %bitcast.6), channel_id=1, source_target_pairs={{0,2},{1,5},{2,0},{3,7},{4,6},{5,1},{6,4},{7,3},{8,10},{9,13},{10,... | collective-permute-start | bytes 2211848 | tf_op jit(solution)/shard_map/ppermute | solution.py:874
  186.8 10.8 %collective-permute-start.38 = (bf16[4,4,24,1152]{3,2,1,0:T(8,128)(2,1)}, bf16[4,4,24,1152]{3,2,1,0:T(8,128)(2,1)}, u32[]{:S(2)}, u32[]{:S(2)}) collective-permute-start(bf16[4,4,24,1152]{3,2,1,0:T(8,128)(2,1)} %get-tuple-element.328), channel_id=1, source_target_pairs={{0,1},{1,0},{2,3},{3,2},{4,5},{5,4},{6,7},{7,6},{8,9},{9,8},{10,11... | collective-permute-start | bytes 2654216 | tf_op jit(solution)/shard_map/ppermute | solution.py:874
  192.6 25.0 %all-to-all-start.4 = ((bf16[4,24,3072]{2,1,0:T(8,128)(2,1)}), bf16[4,24,3072]{2,1,0:T(8,128)(2,1)S(1)}, u32[]{:S(2)}, u32[]{:S(2)}) async-start(bf16[4,24,3072]{2,1,0:T(8,128)(2,1)} %add_convert_fusion.6), calls=%async_computation.4 | async-start | bytes 1179648 | tf_op jit(solution)/shard_map/all_to_all | solution.py:888
  198.9 11.0 %collective-permute-start.39 = (bf16[8,24,1152]{2,1,0:T(8,128)(2,1)S(1)}, bf16[8,24,1152]{2,1,0:T(8,128)(2,1)S(1)}, u32[]{:S(2)}, u32[]{:S(2)}) collective-permute-start(bf16[8,24,1152]{2,1,0:T(8,128)(2,1)S(1)} %bitcast.51), channel_id=1, source_target_pairs={{0,2},{1,5},{2,0},{3,7},{4,6},{5,1},{6,4},{7,3},{8,10},{9,13},{10,... | collective-permute-start | bytes 1327112 | tf_op jit(solution)/shard_map/ppermute | solution.py:874
  200.3 12.3 %collective-permute-start.41 = (bf16[4,24,1920]{2,1,0:T(8,128)(2,1)S(1)}, bf16[4,24,1920]{2,1,0:T(8,128)(2,1)S(1)}, u32[]{:S(2)}, u32[]{:S(2)}) collective-permute-start(bf16[4,24,1920]{2,1,0:T(8,128)(2,1)S(1)} %fusion.5), channel_id=1, source_target_pairs={{0,4},{1,3},{2,6},{3,1},{4,0},{5,7},{6,2},{7,5},{8,12},{9,11},{10,... | collective-permute-start | bytes 1105928 | tf_op jit(solution)/shard_map/ppermute | solution.py:874
  210.0 6.6 %collective-permute-start.42 = (bf16[4,24,1152]{2,1,0:T(8,128)(2,1)S(1)}, bf16[4,24,1152]{2,1,0:T(8,128)(2,1)S(1)}, u32[]{:S(2)}, u32[]{:S(2)}) collective-permute-start(bf16[4,24,1152]{2,1,0:T(8,128)(2,1)S(1)} %fusion.7), channel_id=1, source_target_pairs={{0,4},{1,3},{2,6},{3,1},{4,0},{5,7},{6,2},{7,5},{8,12},{9,11},{10,... | collective-permute-start | bytes 663560 | tf_op jit(solution)/shard_map/ppermute | solution.py:874
  217.6 22.5 %all-to-all-start.5 = ((bf16[4,24,3072]{2,1,0:T(8,128)(2,1)}), bf16[4,24,3072]{2,1,0:T(8,128)(2,1)S(1)}, u32[]{:S(2)}, u32[]{:S(2)}) async-start(bf16[4,24,3072]{2,1,0:T(8,128)(2,1)} %pad_maximum_fusion), calls=%async_computation.5 | async-start | bytes 1179648 | tf_op jit(solution)/shard_map/all_to_all | solution.py:888
  224.7 7.8 %collective-permute-start.44 = (bf16[128,768]{1,0:T(8,128)(2,1)S(1)}, bf16[128,768]{1,0:T(8,128)(2,1)S(1)}, u32[]{:S(2)}, u32[]{:S(2)}) collective-permute-start(bf16[128,768]{1,0:T(8,128)(2,1)S(1)} %copy-done.18), channel_id=1, source_target_pairs={{0,2},{1,3},{2,0},{3,1},{4,6},{5,7},{6,4},{7,5},{8,10},{9,11},{10,... | collective-permute-start | bytes 589832 | tf_op jit(solution)/shard_map/ppermute | solution.py:945
  224.9 9.9 %collective-permute-start.45 = (bf16[128,768]{1,0:T(8,128)(2,1)S(1)}, bf16[128,768]{1,0:T(8,128)(2,1)S(1)}, u32[]{:S(2)}, u32[]{:S(2)}) collective-permute-start(bf16[128,768]{1,0:T(8,128)(2,1)S(1)} %copy-done.17), channel_id=1, source_target_pairs={{0,3},{1,2},{2,1},{3,0},{4,7},{5,6},{6,5},{7,4},{8,11},{9,10},{10,... | collective-permute-start | bytes 589832 | tf_op jit(solution)/shard_map/ppermute | solution.py:945
  226.1 8.8 %collective-permute-start.46 = (bf16[128,768]{1,0:T(8,128)(2,1)S(1)}, bf16[128,768]{1,0:T(8,128)(2,1)}, u32[]{:S(2)}, u32[]{:S(2)}) collective-permute-start(bf16[128,768]{1,0:T(8,128)(2,1)S(1)} %copy-done.22), channel_id=1, source_target_pairs={{0,1},{1,0},{2,3},{3,2},{4,5},{5,4},{6,7},{7,6},{8,9},{9,8},{10,11... | collective-permute-start | bytes 589832 | tf_op jit(solution)/shard_map/ppermute | solution.py:945
  226.8 13.2 %collective-permute-start.47 = (bf16[128,768]{1,0:T(8,128)(2,1)S(1)}, bf16[128,768]{1,0:T(8,128)(2,1)}, u32[]{:S(2)}, u32[]{:S(2)}) collective-permute-start(bf16[128,768]{1,0:T(8,128)(2,1)S(1)} %copy-done.21), channel_id=1, source_target_pairs={{0,2},{1,3},{2,0},{3,1},{4,6},{5,7},{6,4},{7,5},{8,10},{9,11},{10,... | collective-permute-start | bytes 589832 | tf_op jit(solution)/shard_map/ppermute | solution.py:945
  241.9 13.9 %all-to-all-start.6 = ((bf16[32,16,128]{2,1,0:T(8,128)(2,1)}), bf16[32,16,128]{2,1,0:T(8,128)(2,1)S(1)}, u32[]{:S(2)}, u32[]{:S(2)}) async-start(bf16[32,16,128]{2,1,0:T(8,128)(2,1)} %get-tuple-element.365), calls=%async_computation.6 | async-start | bytes 262144 | tf_op jit(solution)/shard_map/all_to_all | solution.py:928
  247.5 8.0 %collective-permute-start.48 = (bf16[128,768]{1,0:T(8,128)(2,1)S(1)}, bf16[128,768]{1,0:T(8,128)(2,1)S(1)}, u32[]{:S(2)}, u32[]{:S(2)}) collective-permute-start(bf16[128,768]{1,0:T(8,128)(2,1)S(1)} %copy-done.20), channel_id=1, source_target_pairs={{0,3},{1,2},{2,1},{3,0},{4,7},{5,6},{6,5},{7,4},{8,11},{9,10},{10,... | collective-permute-start | bytes 589832 | tf_op jit(solution)/shard_map/ppermute | solution.py:945
  (35 other events, 222.8 us)

commit v4 on v3

--- a/solution.py
+++ b/solution.py
@@ -921,8 +921,7 @@
         slices = mine + send(plan, other, plan.core)
         blocks, *others = grads
         left = jnp.broadcast_to(sum(jnp.sum(g * g) for g in others), (1, 128))
-        left, slices, blocks, early = meet(left, slices, blocks, passed[:-1])
-        passed = [*early, passed[-1]]
+        left, slices, blocks, passed = meet(left, slices, blocks, passed)
         last, cards = sum_up(plan, blocks, left, slices)
         grads = [last, *others]
         cards = lax.all_to_all(cards, AXES, 0, 0, tiled=True)
@@ -1063,7 +1062,8 @@
     got_b = send(plan, go_b, plan.core)
     block_u = add(keep_u, got_u).astype(BF)
     blocks_u = along_z(plan, block_u)
-    go_b, keep_b = fold(keep_b, after(got_b, block_u))
+    output = to_pieces(after(result, spread_b))
+    go_b, keep_b = fold(keep_b, after(got_b, block_u, output))
     got_b = send(plan, go_b, plan.first)
     go_a, keep_a = fold(keep_a, after(got_a, go_b))
     got_a = send(plan, go_a, plan.second)
@@ -1073,7 +1073,6 @@
     go_b, keep_b = fold(keep_b, got_b)
     got_b = send(plan, go_b, plan.second)
     got_a = after(got_a, go_b)
-    output = to_pieces(after(result, go_b))
     input_grad = to_pieces(after(stream, go_b))
     halves = [add(keep_a, got_a), add(keep_b, got_b)]
     blocks_ab = along_z(plan, jnp.concatenate(halves, axis=2).astype(BF))

time: 266 us -> 264 us (level)
  blocking collectives: 0 us -> 10.8 us
  starting transfers between devices: 75.8 us -> 69.5 us
  waiting for transfers between devices: 66.6 us -> 60.5 us
    all_to_all x0 -> x1, blocking collectives: none -> 10.8 us  [finish(): cards = lax.all_to_all(cards, AXES, 0, 0, tiled=True)]
    ppermute x12, waiting for transfers between devices: 25.4 us -> 16.4 us  [swap(): lax.ppermute(values, 'seq', [(i, i ^ number) for i in range(plan.seq)])]
    all_to_all x1 -> x0, starting transfers between devices: 5.65 us -> none  [finish(): cards = lax.all_to_all(cards, AXES, 0, 0, tiled=True)]
    all_to_all x6, waiting for transfers between devices: 4.03 us -> 7.69 us  [along_z(): lax.all_to_all(values, 'dp', 0, 0, axis_index_groups=plan.groups, tiled=T...]
  transfers between devices with their start and end apart: 56 -> 55, of which waited for: 26 -> 25; matrix products, arithmetic and copies ran while one was open for 6% -> 6% of each run, Pallas kernels for 32% -> 33%
where the time goes in v4:
time: 264 us; the launch traced here: 259 us
  Pallas kernels  91.4 us (35%)
  starting transfers between devices  69.5 us (26%)
  waiting for transfers between devices  60.5 us (23%)
  other arithmetic  16.4 us (6%)
  blocking collectives  10.8 us (4%)
  local copies, waits for them, and re-layouts  7.21 us (3%)
  between operations  2.78 us (1%)
    pallas_call x14, Pallas kernels, call(): pl.pallas_call(kernel, out_shape=[pltpu.HBM(o.shape, o.dtype) if kind in...  91.4 us
    ppermute x37, waiting for transfers between devices, send(): return lax.ppermute(values, AXES, perm)  36.4 us
    all_to_all x6, starting transfers between devices, along_z(): lax.all_to_all(values, 'dp', 0, 0, axis_index_groups=plan.groups, tiled=T...  31.7 us
    ppermute x37, starting transfers between devices, send(): return lax.ppermute(values, AXES, perm)  29.8 us
    ppermute x12, waiting for transfers between devices, swap(): lax.ppermute(values, 'seq', [(i, i ^ number) for i in range(plan.seq)])  16.4 us
    all_to_all x1, blocking collectives, finish(): cards = lax.all_to_all(cards, AXES, 0, 0, tiled=True)  10.8 us
    ppermute x12, starting transfers between devices, swap(): lax.ppermute(values, 'seq', [(i, i ^ number) for i in range(plan.seq)])  8.04 us
    all_to_all x6, waiting for transfers between devices, along_z(): lax.all_to_all(values, 'dp', 0, 0, axis_index_groups=plan.groups, tiled=T...  7.69 us
  transfers between devices with their start and end apart: 55, of which 25 were waited for; matrix products, arithmetic and copies ran while one was open for 6% of the time, Pallas kernels for 33%

profile of v4, /device:TPU:0, one launch (start us, length us, event | category | flops | bytes accessed | tf_op | source)
XLA Modules:
  0.0 258.6 jit_solution(15204430222502325345)
XLA Ops:
  4.9 6.2 %all-to-all-start = ((bf16[4,48,1280]{2,1,0:T(8,128)(2,1)}), bf16[4,48,1280]{2,1,0:T(8,128)(2,1)S(1)}, u32[]{:S(2)}, u32[]{:S(2)}) async-start(bf16[4,48,1280]{2,1,0:T(8,128)(2,1)} %broadcast_in_dim.8), calls=%async_computation | async-start | bytes 983040 | tf_op jit(solution)/shard_map/all_to_all | solution.py:888
  11.1 2.1 other_rows.1
  16.5 4.8 %collective-permute-done.2.refs_2_ = bf16[128,768]{1,0:T(8,128)(2,1)S(1)} collective-permute-done((bf16[128,768]{1,0:T(8,128)(2,1)}, bf16[128,768]{1,0:T(8,128)(2,1)S(1)}, u32[]{:S(2)}, u32[]{:S(2)}) %collective-permute-start.2) | collective-permute-done | bytes 196640 | tf_op jit(solution)/shard_map/ppermute | solution.py:944
  21.3 3.3 %collective-permute-done.3.refs_3_ = bf16[128,768]{1,0:T(8,128)(2,1)S(1)} collective-permute-done((bf16[128,768]{1,0:T(8,128)(2,1)}, bf16[128,768]{1,0:T(8,128)(2,1)S(1)}, u32[]{:S(2)}, u32[]{:S(2)}) %collective-permute-start.3) | collective-permute-done | bytes 196640 | tf_op jit(solution)/shard_map/ppermute | solution.py:944
  30.1 5.1 %all-to-all-start.1 = ((bf16[4,48,1920]{2,1,0:T(8,128)(2,1)}), bf16[4,48,1920]{2,1,0:T(8,128)(2,1)S(1)}, u32[]{:S(2)}, u32[]{:S(2)}) async-start(bf16[4,48,1920]{2,1,0:T(8,128)(2,1)} %broadcast_in_dim.9), calls=%async_computation.1 | async-start | bytes 1474560 | tf_op jit(solution)/shard_map/all_to_all | solution.py:888
  35.2 5.2 %collective-permute-done.6.refs_5_ = bf16[4,48,1280]{2,1,0:T(8,128)(2,1)S(1)} collective-permute-done((bf16[4,48,1280]{2,1,0:T(8,128)(2,1)S(1)}, bf16[4,48,1280]{2,1,0:T(8,128)(2,1)S(1)}, u32[]{:S(2)}, u32[]{:S(2)}) %collective-permute-start.6) | collective-permute-done | bytes 491552 | tf_op jit(solution)/shard_map/ppermute | solution.py:874
  40.8 1.8 collective-permute-start.8
  43.1 6.6 %collective-permute-done.8.refs_7_ = bf16[4,48,1280]{2,1,0:T(8,128)(2,1)S(1)} collective-permute-done((bf16[4,48,1280]{2,1,0:T(8,128)(2,1)S(1)}, bf16[4,48,1280]{2,1,0:T(8,128)(2,1)S(1)}, u32[]{:S(2)}, u32[]{:S(2)}) %collective-permute-start.8) | collective-permute-done | bytes 491552 | tf_op jit(solution)/shard_map/ppermute | solution.py:874
  50.2 1.8 collective-permute-start.20
  52.9 5.4 %project.1 = (bf16[512,768]{1,0:T(8,128)(2,1)}, bf16[512,768]{1,0:T(8,128)(2,1)}, bf16[512,768]{1,0:T(8,128)(2,1)}, bf16[512,768]{1,0:T(8,128)(2,1)}, f32[8,768]...) custom-call(bf16[4,128,768]{2,1,0:T(8,128)(2,1)S(1)} %copy-done, ...), custom_call_target="tpu_custom_call" | custom-call | flops 1 | bytes 1 | tf_op jit(solution)/shard_map/project/pallas_call | solution.py:244
  61.5 5.0 %all-to-all-start.2 = ((bf16[4,192,384]{2,1,0:T(8,128)(2,1)}), bf16[4,192,384]{2,1,0:T(8,128)(2,1)}, u32[]{:S(2)}, u32[]{:S(2)}) async-start(bf16[4,192,384]{2,1,0:T(8,128)(2,1)} %broadcast_in_dim.10), calls=%async_computation.2 | async-start | bytes 1179648 | tf_op jit(solution)/shard_map/all_to_all | solution.py:888
  66.5 9.8 %mix.1 = (bf16[768,512]{1,0:T(8,128)(2,1)}, bf16[512,768]{1,0:T(8,128)(2,1)}, f32[12,512]{1,0:T(8,128)}) custom-call(bf16[512,768]{1,0:T(8,128)(2,1)} %get-tuple-element.235.refs_0_.refs_1_, bf16[512,768]{1,0:T(8,128)(2,1)} %get-tuple-element.236.refs_1_.refs_2_, bf16[512,768]{1,0:T(8,128)(2,1)} %get-tuple-element.237.refs_2_.refs_3_, ...), custom_call_target="tpu_custom_call" | custom-call | flops 99999997952 | bytes 1 | tf_op jit(solution)/shard_map/mix/pallas_call | solution.py:244
  77.3 1.7 collective-permute-start.15
  80.4 2.6 %all-to-all-done.2.refs_6_ = bf16[4,192,384]{2,1,0:T(8,128)(2,1)} async-done(((bf16[4,192,384]{2,1,0:T(8,128)(2,1)}), bf16[4,192,384]{2,1,0:T(8,128)(2,1)}, u32[]{:S(2)}, u32[]{:S(2)}) %all-to-all-start.2) | async-done | bytes 589856 | tf_op jit(solution)/shard_map/all_to_all | solution.py:888
  83.0 5.8 %collective-permute-done.15.refs_6_ = bf16[4,48,1920]{2,1,0:T(8,128)(2,1)} collective-permute-done((bf16[4,48,1920]{2,1,0:T(8,128)(2,1)S(1)}, bf16[4,48,1920]{2,1,0:T(8,128)(2,1)}, u32[]{:S(2)}, u32[]{:S(2)}) %collective-permute-start.15) | collective-permute-done | bytes 737312 | tf_op jit(solution)/shard_map/ppermute | solution.py:874
  90.4 1.7 collective-permute-start.23
  93.3 8.9 %widen.1 = (f32[512,768]{1,0:T(8,128)}, bf16[512,768]{1,0:T(8,128)(2,1)}, bf16[512,3072]{1,0:T(8,128)(2,1)}, bf16[512,3072]{1,0:T(8,128)(2,1)}, bf16[4,4,48,3840]{3,2,1,0:T(8,128)(2,1)}) custom-call(bf16[512,768]{1,0:T(8,128)(2,1)} %get-tuple-element.253.refs_0_, bf16[512,768]{1,0:T(8,128)(2,1)} %get-tuple-element.254.refs_1_, ...), custom_call_target="tpu_custom_call" | custom-call | flops 99999997952 | bytes 1 | tf_op jit(solution)/shard_map/widen/pallas_call | solution.py:244
  102.3 2.2 collective-permute-done.22.refs_7_
  104.8 1.8 collective-permute-start.25
  107.1 7.3 %grad_of_down.1 = (bf16[4,4,96,768]{3,2,1,0:T(8,128)(2,1)}, bf16[4,4,96,768]{3,2,1,0:T(8,128)(2,1)}, bf16[512,768]{1,0:T(8,128)(2,1)}) custom-call(bf16[512,3072]{1,0:T(8,128)(2,1)} %get-tuple-element.263.refs_0_.refs_2_, bf16[4,128,768]{2,1,0:T(8,128)(2,1)S(1)} %copy-done.3, bf16[128,768]{1,0:T(8,128)(2,1)} %collective-permute-done.19.refs_2_, ...), custom_call_target="tpu_custom_call" | custom-call | flops 99999997952 | bytes 1 | tf_op jit(solution)/shard_map/grad_of_down/pallas_call | solution.py:244
  115.2 1.6 collective-permute-done.30.refs_13_
  116.8 9.7 %narrow0.1 = (f32[512,768]{1,0:T(8,128)}, bf16[4,4,24,3072]{3,2,1,0:T(8,128)(2,1)}, bf16[4,4,24,3072]{3,2,1,0:T(8,128)(2,1)}, f32[512,768]{1,0:T(8,128)}) custom-call(f32[512,768]{1,0:T(8,128)} %get-tuple-element.273.refs_0_, bf16[512,768]{1,0:T(8,128)(2,1)} %get-tuple-element.274.refs_1_, bf16[512,3072]{1,0:T(8,128)(2,1)} %get-tuple-element.263.refs_0_.refs_2_, ...), custom_call_target="tpu_custom_call" | custom-call | flops 99999997952 | bytes 1 | tf_op jit(solution)/shard_map/narrow0/pallas_call | solution.py:244
  127.3 1.8 collective-permute-start.31
  129.1 9.7 %narrow2.1 = (f32[512,768]{1,0:T(8,128)}, bf16[4,4,24,3072]{3,2,1,0:T(8,128)(2,1)}, bf16[4,4,24,3072]{3,2,1,0:T(8,128)(2,1)}, bf16[128,768]{1,0:T(8,128)(2,1)}, ...) custom-call(f32[512,768]{1,0:T(8,128)} %get-tuple-element.286.refs_0, ...), custom_call_target="tpu_custom_call", output_to_operand_aliasing={{1}: (15, {}), {2}: (16, {})} | custom-call | flops 99999997952 | bytes 1 | tf_op jit(solution)/shard_map/narrow2/pallas_call | solution.py:244
  138.8 4.7 %collective-permute-done.31 = bf16[8,96,768]{2,1,0:T(8,128)(2,1)S(1)} collective-permute-done((bf16[8,96,768]{2,1,0:T(8,128)(2,1)S(1)}, bf16[8,96,768]{2,1,0:T(8,128)(2,1)S(1)}, u32[]{:S(2)}, u32[]{:S(2)}) %collective-permute-start.31) | collective-permute-done | bytes 1179680 | tf_op jit(solution)/shard_map/ppermute | solution.py:874
  145.3 5.2 %turn.1 = (f32[512,768]{1,0:T(8,128)}, bf16[512,768]{1,0:T(8,128)(2,1)}, bf16[512,768]{1,0:T(8,128)(2,1)}, f32[2,768]{1,0:T(2,128)S(1)}) custom-call(f32[512,768]{1,0:T(8,128)} %get-tuple-element.273.refs_0_, f32[512,768]{1,0:T(8,128)} %get-tuple-element.301.refs_1_, bf16[512,768]{1,0:T(8,128)(2,1)} %get-tuple-element.276.refs_4_.refs_2_, ...), custom_call_target="tpu_custom_call" | custom-call | flops 99999997952 | bytes 1 | tf_op jit(solution)/shard_map/turn/pallas_call | solution.py:244
  150.5 1.9 add_convert_fusion.1
  153.7 1.8 collective-permute-start.34
  155.4 10.0 %attend_back0.1 = (bf16[512,1152]{1,0:T(8,128)(2,1)}, bf16[4,4,24,1920]{3,2,1,0:T(8,128)(2,1)}, bf16[4,4,24,1920]{3,2,1,0:T(8,128)(2,1)}) custom-call(bf16[512,768]{1,0:T(8,128)(2,1)} %get-tuple-element.311.refs_0_, bf16[512,768]{1,0:T(8,128)(2,1)} %get-tuple-element.235.refs_0_.refs_1_, bf16[512,768]{1,0:T(8,128)(2,1)} %get-tuple-element.236.refs_1_.refs_2_, ...), custom_call_target="tpu_custom_call" | custom-call | flops 99999997952 | bytes 1 | tf_op jit(solution)/shard_map/attend_back0/pallas_call | solution.py:244
  166.5 5.3 %all-to-all-start.3 = ((bf16[4,96,768]{2,1,0:T(8,128)(2,1)}), bf16[4,96,768]{2,1,0:T(8,128)(2,1)S(1)}, u32[]{:S(2)}, u32[]{:S(2)}) async-start(bf16[4,96,768]{2,1,0:T(8,128)(2,1)} %add_convert_fusion.7), calls=%async_computation.3 | async-start | bytes 1179648 | tf_op jit(solution)/shard_map/all_to_all | solution.py:888
  173.1 1.6 collective-permute-start.35
  174.7 2.6 %add_convert_fusion.4 = (bf16[2,4,24,1920]{3,2,1,0:T(8,128)(2,1)S(1)}, bf16[2,4,24,1920]{3,2,1,0:T(8,128)(2,1)}) fusion(bf16[4,4,24,1920]{3,2,1,0:T(8,128)(2,1)} %collective-permute-done.36, bf16[4,4,24,1920]{3,2,1,0:T(8,128)(2,1)S(1)} %copy-done.13), kind=kLoop, calls=%fused_computation.4 | loop fusion | flops 2949120 | bytes 4423680 | tf_op jit(solution)/shard_map/convert_element_type | solution.py:906
  177.6 9.2 %attend_back1.1 = (bf16[512,1152]{1,0:T(8,128)(2,1)}, bf16[4,4,24,1152]{3,2,1,0:T(8,128)(2,1)}, bf16[4,4,24,1152]{3,2,1,0:T(8,128)(2,1)}) custom-call(bf16[512,768]{1,0:T(8,128)(2,1)} %get-tuple-element.311.refs_0_, bf16[512,768]{1,0:T(8,128)(2,1)} %get-tuple-element.235.refs_0_.refs_1_, bf16[512,768]{1,0:T(8,128)(2,1)} %get-tuple-element.236.refs_1_.refs_2_, ...), custom_call_target="tpu_custom_call" | custom-call | flops 99999997952 | bytes 1 | tf_op jit(solution)/shard_map/attend_back1/pallas_call | solution.py:244
  188.3 2.0 collective-permute-done.37
  192.3 2.3 add_convert_fusion.6
  194.5 5.1 %all-to-all-start.4 = ((bf16[4,24,3072]{2,1,0:T(8,128)(2,1)}), bf16[4,24,3072]{2,1,0:T(8,128)(2,1)S(1)}, u32[]{:S(2)}, u32[]{:S(2)}) async-start(bf16[4,24,3072]{2,1,0:T(8,128)(2,1)} %add_convert_fusion.6), calls=%async_computation.4 | async-start | bytes 1179648 | tf_op jit(solution)/shard_map/all_to_all | solution.py:888
  199.7 1.6 collective-permute-done.41.refs_28_
  201.3 1.6 add_convert_fusion.8
  204.6 1.6 collective-permute-start.44
  206.2 7.1 %finish_tokens.1 = (bf16[128,768]{1,0:T(8,128)(2,1)}, bf16[128,768]{1,0:T(8,128)(2,1)}, bf16[128,768]{1,0:T(8,128)(2,1)}, bf16[128,768]{1,0:T(8,128)(2,1)}, f32[2,768]{1,0:T(2,128)S(1)}) custom-call(bf16[512,768]{1,0:T(8,128)(2,1)} %get-tuple-element.253.refs_0_, bf16[512,1152]{1,0:T(8,128)(2,1)} %get-tuple-element.340.refs_1_, ...), custom_call_target="tpu_custom_call" | custom-call | flops 1 | bytes 1 | tf_op jit(solution)/shard_map/finish_tokens/pallas_call | solution.py:244
  213.8 2.7 %collective-permute-start.45 = (bf16[4,24,1152]{2,1,0:T(8,128)(2,1)S(1)}, bf16[4,24,1152]{2,1,0:T(8,128)(2,1)S(1)}, u32[]{:S(2)}, u32[]{:S(2)}) collective-permute-start(bf16[4,24,1152]{2,1,0:T(8,128)(2,1)S(1)} %fusion.7), channel_id=1, source_target_pairs={{0,4},{1,3},{2,6},{3,1},{4,0},{5,7},{6,2},{7,5},{8,12},{9,11},{10,... | collective-permute-start | bytes 663560 | tf_op jit(solution)/shard_map/ppermute | solution.py:874
  217.6 2.8 %collective-permute-done.45 = bf16[4,24,1152]{2,1,0:T(8,128)(2,1)S(1)} collective-permute-done((bf16[4,24,1152]{2,1,0:T(8,128)(2,1)S(1)}, bf16[4,24,1152]{2,1,0:T(8,128)(2,1)S(1)}, u32[]{:S(2)}, u32[]{:S(2)}) %collective-permute-start.45) | collective-permute-done | bytes 221216 | tf_op jit(solution)/shard_map/ppermute | solution.py:874
  221.4 5.0 %all-to-all-start.5 = ((bf16[4,24,3072]{2,1,0:T(8,128)(2,1)}), bf16[4,24,3072]{2,1,0:T(8,128)(2,1)S(1)}, u32[]{:S(2)}, u32[]{:S(2)}) async-start(bf16[4,24,3072]{2,1,0:T(8,128)(2,1)} %pad_maximum_fusion), calls=%async_computation.5 | async-start | bytes 1179648 | tf_op jit(solution)/shard_map/all_to_all | solution.py:888
  231.5 4.2 %collective-permute-done.47.refs_31_ = bf16[128,768]{1,0:T(8,128)(2,1)S(1)} collective-permute-done((bf16[128,768]{1,0:T(8,128)(2,1)S(1)}, bf16[128,768]{1,0:T(8,128)(2,1)S(1)}, u32[]{:S(2)}, u32[]{:S(2)}) %collective-permute-start.47) | collective-permute-done | bytes 196640 | tf_op jit(solution)/shard_map/ppermute | solution.py:944
  235.8 2.4 collective-permute-done.48.refs_32_
  238.2 3.7 %all-to-all-done.5.refs_0_ = bf16[4,24,3072]{2,1,0:T(8,128)(2,1)S(1)} async-done(((bf16[4,24,3072]{2,1,0:T(8,128)(2,1)}), bf16[4,24,3072]{2,1,0:T(8,128)(2,1)S(1)}, u32[]{:S(2)}, u32[]{:S(2)}) %all-to-all-start.5) | async-done | bytes 589856 | tf_op jit(solution)/shard_map/all_to_all | solution.py:888
  243.0 10.8 %all_to_all.35.refs_3_ = bf16[32,16,128]{2,1,0:T(8,128)(2,1)S(1)} all-to-all(bf16[32,16,128]{2,1,0:T(8,128)(2,1)S(1)} %get-tuple-element.367), channel_id=1, replica_groups=mesh['dp'=8,'seq'=4] {'dp','seq'}, dimensions={0} | all-to-all | bytes 262144 | tf_op jit(solution)/shard_map/all_to_all | solution.py:927
  253.9 4.5 %update.1 = (f32[1,128]{1,0:T(1,128)}, f32[24,768]{1,0:T(8,128)}, f32[24,768]{1,0:T(8,128)}, f32[24,768]{1,0:T(8,128)}, f32[24,768]{1,0:T(8,128)}, /*index=5*/f3...) custom-call(f32[24,3072]{1,0:T(8,128)S(1)} %get-tuple-element.366.re, ...), custom_call_target="tpu_custom_call" | custom-call | flops 99999997952 | bytes 1 | tf_op jit(solution)/shard_map/update/pallas_call | solution.py:244
  (156 shorter events, 44.2 us)
Async XLA Ops:
  3.1 12.4 %collective-permute-start.5 = (bf16[96,384]{1,0:T(8,128)(2,1)S(1)}, bf16[96,384]{1,0:T(8,128)(2,1)S(1)}, u32[]{:S(2)}, u32[]{:S(2)}) collective-permute-start(bf16[96,384]{1,0:T(8,128)(2,1)S(1)} %get-tuple-element.220), channel_id=1, source_target_pairs={{0,1},{1,0},{2,3},{3,2},{4,5},{5,4},{6,7},{7,6},{8,9},{9,8},{10,11... | collective-permute-start | bytes 221192 | tf_op jit(solution)/shard_map/ppermute | solution.py:874
  4.9 20.4 %all-to-all-start = ((bf16[4,48,1280]{2,1,0:T(8,128)(2,1)}), bf16[4,48,1280]{2,1,0:T(8,128)(2,1)S(1)}, u32[]{:S(2)}, u32[]{:S(2)}) async-start(bf16[4,48,1280]{2,1,0:T(8,128)(2,1)} %broadcast_in_dim.8), calls=%async_computation | async-start | bytes 983040 | tf_op jit(solution)/shard_map/all_to_all | solution.py:888
  13.3 8.0 %collective-permute-start.2 = (bf16[128,768]{1,0:T(8,128)(2,1)}, bf16[128,768]{1,0:T(8,128)(2,1)S(1)}, u32[]{:S(2)}, u32[]{:S(2)}) collective-permute-start(bf16[128,768]{1,0:T(8,128)(2,1)} %get-tuple-element.215), channel_id=1, source_target_pairs={{0,2},{1,3},{2,0},{3,1},{4,6},{5,7},{6,4},{7,5},{8,10},{9,11},{10,... | collective-permute-start | bytes 589832 | tf_op jit(solution)/shard_map/ppermute | solution.py:944
  14.9 9.7 %collective-permute-start.3 = (bf16[128,768]{1,0:T(8,128)(2,1)}, bf16[128,768]{1,0:T(8,128)(2,1)S(1)}, u32[]{:S(2)}, u32[]{:S(2)}) collective-permute-start(bf16[128,768]{1,0:T(8,128)(2,1)} %get-tuple-element.216), channel_id=1, source_target_pairs={{0,3},{1,2},{2,1},{3,0},{4,7},{5,6},{6,5},{7,4},{8,11},{9,10},{10,... | collective-permute-start | bytes 589832 | tf_op jit(solution)/shard_map/ppermute | solution.py:944
  27.1 13.3 %collective-permute-start.6 = (bf16[4,48,1280]{2,1,0:T(8,128)(2,1)S(1)}, bf16[4,48,1280]{2,1,0:T(8,128)(2,1)S(1)}, u32[]{:S(2)}, u32[]{:S(2)}) collective-permute-start(bf16[4,48,1280]{2,1,0:T(8,128)(2,1)S(1)} %all-to-all-done.refs_4_), channel_id=1, source_target_pairs={{0,4},{1,3},{2,6},{3,1},{4,0},{5,7},{6,2},{7,5},{8,12},{9,11},{10,... | collective-permute-start | bytes 1474568 | tf_op jit(solution)/shard_map/ppermute | solution.py:874
  28.6 12.2 %collective-permute-start.7 = (bf16[4,48,1280]{2,1,0:T(8,128)(2,1)S(1)}, bf16[4,48,1280]{2,1,0:T(8,128)(2,1)S(1)}, u32[]{:S(2)}, u32[]{:S(2)}) collective-permute-start(bf16[4,48,1280]{2,1,0:T(8,128)(2,1)S(1)} %all-to-all-done.refs_4_), channel_id=1, source_target_pairs={{0,2},{1,5},{2,0},{3,7},{4,6},{5,1},{6,4},{7,3},{8,10},{9,13},{10,... | collective-permute-start | bytes 1474568 | tf_op jit(solution)/shard_map/ppermute | solution.py:874
  30.1 28.2 %all-to-all-start.1 = ((bf16[4,48,1920]{2,1,0:T(8,128)(2,1)}), bf16[4,48,1920]{2,1,0:T(8,128)(2,1)S(1)}, u32[]{:S(2)}, u32[]{:S(2)}) async-start(bf16[4,48,1920]{2,1,0:T(8,128)(2,1)} %broadcast_in_dim.9), calls=%async_computation.1 | async-start | bytes 1474560 | tf_op jit(solution)/shard_map/all_to_all | solution.py:888
  35.2 7.9 %collective-permute-start.9 = (bf16[4,48,1280]{2,1,0:T(8,128)(2,1)S(1)}, bf16[4,48,1280]{2,1,0:T(8,128)(2,1)S(1)}, u32[]{:S(2)}, u32[]{:S(2)}) collective-permute-start(bf16[4,48,1280]{2,1,0:T(8,128)(2,1)S(1)} %all-to-all-done.refs_4_), channel_id=1, source_target_pairs={{0,1},{1,0},{2,3},{3,2},{4,5},{5,4},{6,7},{7,6},{8,9},{9,8},{10,11... | collective-permute-start | bytes 1474568 | tf_op jit(solution)/shard_map/ppermute | solution.py:874
  40.8 8.8 %collective-permute-start.8 = (bf16[4,48,1280]{2,1,0:T(8,128)(2,1)S(1)}, bf16[4,48,1280]{2,1,0:T(8,128)(2,1)S(1)}, u32[]{:S(2)}, u32[]{:S(2)}) collective-permute-start(bf16[4,48,1280]{2,1,0:T(8,128)(2,1)S(1)} %collective-permute-done.6.refs_5_), channel_id=1, source_target_pairs={{0,2},{1,5},{2,0},{3,7},{4,6},{5,1},{6,4},{7,3},{8,10},{9,13},{10,... | collective-permute-start | bytes 1474568 | tf_op jit(solution)/shard_map/ppermute | solution.py:874
  42.6 7.1 %collective-permute-start.10 = (bf16[4,48,1280]{2,1,0:T(8,128)(2,1)S(1)}, bf16[4,48,1280]{2,1,0:T(8,128)(2,1)S(1)}, u32[]{:S(2)}, u32[]{:S(2)}) collective-permute-start(bf16[4,48,1280]{2,1,0:T(8,128)(2,1)S(1)} %collective-permute-done.6.refs_5_), channel_id=1, source_target_pairs={{0,1},{1,0},{2,3},{3,2},{4,5},{5,4},{6,7},{7,6},{8,9},{9,8},{10,11... | collective-permute-start | bytes 1474568 | tf_op jit(solution)/shard_map/ppermute | solution.py:874
  42.6 7.1 %collective-permute-start.11 = (bf16[4,48,1280]{2,1,0:T(8,128)(2,1)S(1)}, bf16[4,48,1280]{2,1,0:T(8,128)(2,1)S(1)}, u32[]{:S(2)}, u32[]{:S(2)}) collective-permute-start(bf16[4,48,1280]{2,1,0:T(8,128)(2,1)S(1)} %collective-permute-done.7.refs_6_), channel_id=1, source_target_pairs={{0,1},{1,0},{2,3},{3,2},{4,5},{5,4},{6,7},{7,6},{8,9},{9,8},{10,11... | collective-permute-start | bytes 1474568 | tf_op jit(solution)/shard_map/ppermute | solution.py:874
  49.7 11.6 %collective-permute-start.19 = (bf16[128,768]{1,0:T(8,128)(2,1)}, bf16[128,768]{1,0:T(8,128)(2,1)}, u32[]{:S(2)}, u32[]{:S(2)}) collective-permute-start(bf16[128,768]{1,0:T(8,128)(2,1)} %get-tuple-element.248), channel_id=1, source_target_pairs={{0,1},{1,0},{2,3},{3,2},{4,5},{5,4},{6,7},{7,6},{8,9},{9,8},{10,11... | collective-permute-start | bytes 589832 | tf_op jit(solution)/shard_map/ppermute | solution.py:944
  50.2 11.3 %collective-permute-start.20 = (bf16[128,768]{1,0:T(8,128)(2,1)}, bf16[128,768]{1,0:T(8,128)(2,1)}, u32[]{:S(2)}, u32[]{:S(2)}) collective-permute-start(bf16[128,768]{1,0:T(8,128)(2,1)} %get-tuple-element.249), channel_id=1, source_target_pairs={{0,2},{1,3},{2,0},{3,1},{4,6},{5,7},{6,4},{7,5},{8,10},{9,11},{10,... | collective-permute-start | bytes 589832 | tf_op jit(solution)/shard_map/ppermute | solution.py:944
  51.9 9.6 %collective-permute-start.21 = (bf16[128,768]{1,0:T(8,128)(2,1)}, bf16[128,768]{1,0:T(8,128)(2,1)}, u32[]{:S(2)}, u32[]{:S(2)}) collective-permute-start(bf16[128,768]{1,0:T(8,128)(2,1)} %get-tuple-element.250), channel_id=1, source_target_pairs={{0,3},{1,2},{2,1},{3,0},{4,7},{5,6},{6,5},{7,4},{8,11},{9,10},{10,... | collective-permute-start | bytes 589832 | tf_op jit(solution)/shard_map/ppermute | solution.py:944
  58.3 18.6 %collective-permute-start.13 = (bf16[4,48,1920]{2,1,0:T(8,128)(2,1)S(1)}, bf16[4,48,1920]{2,1,0:T(8,128)(2,1)S(1)}, u32[]{:S(2)}, u32[]{:S(2)}) collective-permute-start(bf16[4,48,1920]{2,1,0:T(8,128)(2,1)S(1)} %all-to-all-done.1.refs_3_), channel_id=1, source_target_pairs={{0,4},{1,3},{2,6},{3,1},{4,0},{5,7},{6,2},{7,5},{8,12},{9,11},{10,... | collective-permute-start | bytes 2211848 | tf_op jit(solution)/shard_map/ppermute | solution.py:874
  59.9 17.4 %collective-permute-start.14 = (bf16[4,48,1920]{2,1,0:T(8,128)(2,1)S(1)}, bf16[4,48,1920]{2,1,0:T(8,128)(2,1)S(1)}, u32[]{:S(2)}, u32[]{:S(2)}) collective-permute-start(bf16[4,48,1920]{2,1,0:T(8,128)(2,1)S(1)} %all-to-all-done.1.refs_3_), channel_id=1, source_target_pairs={{0,2},{1,5},{2,0},{3,7},{4,6},{5,1},{6,4},{7,3},{8,10},{9,13},{10,... | collective-permute-start | bytes 2211848 | tf_op jit(solution)/shard_map/ppermute | solution.py:874
  61.3 19.1 %collective-permute-start.16 = (bf16[4,48,1920]{2,1,0:T(8,128)(2,1)S(1)}, bf16[4,48,1920]{2,1,0:T(8,128)(2,1)}, u32[]{:S(2)}, u32[]{:S(2)}) collective-permute-start(bf16[4,48,1920]{2,1,0:T(8,128)(2,1)S(1)} %all-to-all-done.1.refs_3_), channel_id=1, source_target_pairs={{0,1},{1,0},{2,3},{3,2},{4,5},{5,4},{6,7},{7,6},{8,9},{9,8},{10,11... | collective-permute-start | bytes 2211848 | tf_op jit(solution)/shard_map/ppermute | solution.py:874
  61.5 21.5 %all-to-all-start.2 = ((bf16[4,192,384]{2,1,0:T(8,128)(2,1)}), bf16[4,192,384]{2,1,0:T(8,128)(2,1)}, u32[]{:S(2)}, u32[]{:S(2)}) async-start(bf16[4,192,384]{2,1,0:T(8,128)(2,1)} %broadcast_in_dim.10), calls=%async_computation.2 | async-start | bytes 1179648 | tf_op jit(solution)/shard_map/all_to_all | solution.py:888
  77.3 11.6 %collective-permute-start.15 = (bf16[4,48,1920]{2,1,0:T(8,128)(2,1)S(1)}, bf16[4,48,1920]{2,1,0:T(8,128)(2,1)}, u32[]{:S(2)}, u32[]{:S(2)}) collective-permute-start(bf16[4,48,1920]{2,1,0:T(8,128)(2,1)S(1)} %collective-permute-done.13.refs_4_), channel_id=1, source_target_pairs={{0,2},{1,5},{2,0},{3,7},{4,6},{5,1},{6,4},{7,3},{8,10},{9,13},{10,... | collective-permute-start | bytes 2211848 | tf_op jit(solution)/shard_map/ppermute | solution.py:874
  79.0 9.8 %collective-permute-start.17 = (bf16[4,48,1920]{2,1,0:T(8,128)(2,1)S(1)}, bf16[4,48,1920]{2,1,0:T(8,128)(2,1)}, u32[]{:S(2)}, u32[]{:S(2)}) collective-permute-start(bf16[4,48,1920]{2,1,0:T(8,128)(2,1)S(1)} %collective-permute-done.13.refs_4_), channel_id=1, source_target_pairs={{0,1},{1,0},{2,3},{3,2},{4,5},{5,4},{6,7},{7,6},{8,9},{9,8},{10,11... | collective-permute-start | bytes 2211848 | tf_op jit(solution)/shard_map/ppermute | solution.py:874
  79.2 9.7 %collective-permute-start.18 = (bf16[4,48,1920]{2,1,0:T(8,128)(2,1)S(1)}, bf16[4,48,1920]{2,1,0:T(8,128)(2,1)}, u32[]{:S(2)}, u32[]{:S(2)}) collective-permute-start(bf16[4,48,1920]{2,1,0:T(8,128)(2,1)S(1)} %collective-permute-done.14.refs_5_), channel_id=1, source_target_pairs={{0,1},{1,0},{2,3},{3,2},{4,5},{5,4},{6,7},{7,6},{8,9},{9,8},{10,11... | collective-permute-start | bytes 2211848 | tf_op jit(solution)/shard_map/ppermute | solution.py:874
  88.9 15.6 %collective-permute-start.22 = (bf16[4,192,384]{2,1,0:T(8,128)(2,1)}, bf16[4,192,384]{2,1,0:T(8,128)(2,1)S(1)}, u32[]{:S(2)}, u32[]{:S(2)}) collective-permute-start(bf16[4,192,384]{2,1,0:T(8,128)(2,1)} %all-to-all-done.2.refs_6_), channel_id=1, source_target_pairs={{0,4},{1,3},{2,6},{3,1},{4,0},{5,7},{6,2},{7,5},{8,12},{9,11},{10,... | collective-permute-start | bytes 1769480 | tf_op jit(solution)/shard_map/ppermute | solution.py:874
  90.4 14.4 %collective-permute-start.23 = (bf16[4,192,384]{2,1,0:T(8,128)(2,1)}, bf16[4,192,384]{2,1,0:T(8,128)(2,1)S(1)}, u32[]{:S(2)}, u32[]{:S(2)}) collective-permute-start(bf16[4,192,384]{2,1,0:T(8,128)(2,1)} %all-to-all-done.2.refs_6_), channel_id=1, source_target_pairs={{0,2},{1,5},{2,0},{3,7},{4,6},{5,1},{6,4},{7,3},{8,10},{9,13},{10,... | collective-permute-start | bytes 1769480 | tf_op jit(solution)/shard_map/ppermute | solution.py:874
  92.2 22.2 %collective-permute-start.26 = (bf16[4,192,384]{2,1,0:T(8,128)(2,1)}, bf16[4,192,384]{2,1,0:T(8,128)(2,1)}, u32[]{:S(2)}, u32[]{:S(2)}) collective-permute-start(bf16[4,192,384]{2,1,0:T(8,128)(2,1)} %all-to-all-done.2.refs_6_), channel_id=1, source_target_pairs={{0,1},{1,0},{2,3},{3,2},{4,5},{5,4},{6,7},{7,6},{8,9},{9,8},{10,11... | collective-permute-start | bytes 1769480 | tf_op jit(solution)/shard_map/ppermute | solution.py:874
  104.8 9.9 %collective-permute-start.25 = (bf16[4,192,384]{2,1,0:T(8,128)(2,1)S(1)}, bf16[4,192,384]{2,1,0:T(8,128)(2,1)S(1)}, u32[]{:S(2)}, u32[]{:S(2)}) collective-permute-start(bf16[4,192,384]{2,1,0:T(8,128)(2,1)S(1)} %collective-permute-done.22.refs_7_), channel_id=1, source_target_pairs={{0,2},{1,5},{2,0},{3,7},{4,6},{5,1},{6,4},{7,3},{8,10},{9,13},{10,... | collective-permute-start | bytes 1769480 | tf_op jit(solution)/shard_map/ppermute | solution.py:874
  106.6 8.1 %collective-permute-start.27 = (bf16[4,192,384]{2,1,0:T(8,128)(2,1)S(1)}, bf16[4,192,384]{2,1,0:T(8,128)(2,1)S(1)}, u32[]{:S(2)}, u32[]{:S(2)}) collective-permute-start(bf16[4,192,384]{2,1,0:T(8,128)(2,1)S(1)} %collective-permute-done.22.refs_7_), channel_id=1, source_target_pairs={{0,1},{1,0},{2,3},{3,2},{4,5},{5,4},{6,7},{7,6},{8,9},{9,8},{10,11... | collective-permute-start | bytes 1769480 | tf_op jit(solution)/shard_map/ppermute | solution.py:874
  106.6 8.1 %collective-permute-start.28 = (bf16[4,192,384]{2,1,0:T(8,128)(2,1)S(1)}, bf16[4,192,384]{2,1,0:T(8,128)(2,1)S(1)}, u32[]{:S(2)}, u32[]{:S(2)}) collective-permute-start(bf16[4,192,384]{2,1,0:T(8,128)(2,1)S(1)} %collective-permute-done.23.refs_8_), channel_id=1, source_target_pairs={{0,1},{1,0},{2,3},{3,2},{4,5},{5,4},{6,7},{7,6},{8,9},{9,8},{10,11... | collective-permute-start | bytes 1769480 | tf_op jit(solution)/shard_map/ppermute | solution.py:874
  114.7 11.9 %collective-permute-start.29 = (bf16[4,4,96,768]{3,2,1,0:T(8,128)(2,1)}, bf16[4,4,96,768]{3,2,1,0:T(8,128)(2,1)S(1)}, u32[]{:S(2)}, u32[]{:S(2)}) collective-permute-start(bf16[4,4,96,768]{3,2,1,0:T(8,128)(2,1)} %get-tuple-element.272), channel_id=1, source_target_pairs={{0,1},{1,0},{2,3},{3,2},{4,5},{5,4},{6,7},{7,6},{8,9},{9,8},{10,11... | collective-permute-start | bytes 7077896 | tf_op jit(solution)/shard_map/ppermute | solution.py:874
  127.3 16.3 %collective-permute-start.31 = (bf16[8,96,768]{2,1,0:T(8,128)(2,1)S(1)}, bf16[8,96,768]{2,1,0:T(8,128)(2,1)S(1)}, u32[]{:S(2)}, u32[]{:S(2)}) collective-permute-start(bf16[8,96,768]{2,1,0:T(8,128)(2,1)S(1)} %bitcast.50), channel_id=1, source_target_pairs={{0,2},{1,5},{2,0},{3,7},{4,6},{5,1},{6,4},{7,3},{8,10},{9,13},{10,... | collective-permute-start | bytes 3538952 | tf_op jit(solution)/shard_map/ppermute | solution.py:874
  143.7 9.9 %collective-permute-start.33 = (bf16[4,96,768]{2,1,0:T(8,128)(2,1)S(1)}, bf16[4,96,768]{2,1,0:T(8,128)(2,1)S(1)}, u32[]{:S(2)}, u32[]{:S(2)}) collective-permute-start(bf16[4,96,768]{2,1,0:T(8,128)(2,1)S(1)} %fusion.3), channel_id=1, source_target_pairs={{0,4},{1,3},{2,6},{3,1},{4,0},{5,7},{6,2},{7,5},{8,12},{9,11},{10,... | collective-permute-start | bytes 1769480 | tf_op jit(solution)/shard_map/ppermute | solution.py:874
  145.3 5.2 %collective-permute-start.32 = (bf16[4,4,24,3072]{3,2,1,0:T(8,128)(2,1)}, bf16[4,4,24,3072]{3,2,1,0:T(8,128)(2,1)S(1)}, u32[]{:S(2)}, u32[]{:S(2)}) collective-permute-start(bf16[4,4,24,3072]{3,2,1,0:T(8,128)(2,1)} %get-tuple-element.298), channel_id=1, source_target_pairs={{0,1},{1,0},{2,3},{3,2},{4,5},{5,4},{6,7},{7,6},{8,9},{9,8},{10,11... | collective-permute-start | bytes 7077896 | tf_op jit(solution)/shard_map/ppermute | solution.py:874
  153.7 18.2 %collective-permute-start.34 = (bf16[8,24,3072]{2,1,0:T(8,128)(2,1)}, bf16[8,24,3072]{2,1,0:T(8,128)(2,1)}, u32[]{:S(2)}, u32[]{:S(2)}) collective-permute-start(bf16[8,24,3072]{2,1,0:T(8,128)(2,1)} %bitcast.3), channel_id=1, source_target_pairs={{0,2},{1,5},{2,0},{3,7},{4,6},{5,1},{6,4},{7,3},{8,10},{9,13},{10,... | collective-permute-start | bytes 3538952 | tf_op jit(solution)/shard_map/ppermute | solution.py:874
  165.4 9.4 %collective-permute-start.36 = (bf16[4,4,24,1920]{3,2,1,0:T(8,128)(2,1)}, bf16[4,4,24,1920]{3,2,1,0:T(8,128)(2,1)}, u32[]{:S(2)}, u32[]{:S(2)}) collective-permute-start(bf16[4,4,24,1920]{3,2,1,0:T(8,128)(2,1)} %get-tuple-element.322), channel_id=1, source_target_pairs={{0,1},{1,0},{2,3},{3,2},{4,5},{5,4},{6,7},{7,6},{8,9},{9,8},{10,11... | collective-permute-start | bytes 4423688 | tf_op jit(solution)/shard_map/ppermute | solution.py:874
  166.5 21.8 %all-to-all-start.3 = ((bf16[4,96,768]{2,1,0:T(8,128)(2,1)}), bf16[4,96,768]{2,1,0:T(8,128)(2,1)S(1)}, u32[]{:S(2)}, u32[]{:S(2)}) async-start(bf16[4,96,768]{2,1,0:T(8,128)(2,1)} %add_convert_fusion.7), calls=%async_computation.3 | async-start | bytes 1179648 | tf_op jit(solution)/shard_map/all_to_all | solution.py:888
  173.1 15.2 %collective-permute-start.35 = (bf16[4,24,3072]{2,1,0:T(8,128)(2,1)S(1)}, bf16[4,24,3072]{2,1,0:T(8,128)(2,1)}, u32[]{:S(2)}, u32[]{:S(2)}) collective-permute-start(bf16[4,24,3072]{2,1,0:T(8,128)(2,1)S(1)} %fusion), channel_id=1, source_target_pairs={{0,4},{1,3},{2,6},{3,1},{4,0},{5,7},{6,2},{7,5},{8,12},{9,11},{10,... | collective-permute-start | bytes 1769480 | tf_op jit(solution)/shard_map/ppermute | solution.py:874
  177.3 13.0 %collective-permute-start.37 = (bf16[8,24,1920]{2,1,0:T(8,128)(2,1)}, bf16[8,24,1920]{2,1,0:T(8,128)(2,1)}, u32[]{:S(2)}, u32[]{:S(2)}) collective-permute-start(bf16[8,24,1920]{2,1,0:T(8,128)(2,1)} %bitcast.6), channel_id=1, source_target_pairs={{0,2},{1,5},{2,0},{3,7},{4,6},{5,1},{6,4},{7,3},{8,10},{9,13},{10,... | collective-permute-start | bytes 2211848 | tf_op jit(solution)/shard_map/ppermute | solution.py:874
  186.9 12.8 %collective-permute-start.38 = (bf16[4,4,24,1152]{3,2,1,0:T(8,128)(2,1)}, bf16[4,4,24,1152]{3,2,1,0:T(8,128)(2,1)}, u32[]{:S(2)}, u32[]{:S(2)}) collective-permute-start(bf16[4,4,24,1152]{3,2,1,0:T(8,128)(2,1)} %get-tuple-element.329), channel_id=1, source_target_pairs={{0,1},{1,0},{2,3},{3,2},{4,5},{5,4},{6,7},{7,6},{8,9},{9,8},{10,11... | collective-permute-start | bytes 2654216 | tf_op jit(solution)/shard_map/ppermute | solution.py:874
  190.3 9.3 %collective-permute-start.39 = (bf16[128,768]{1,0:T(8,128)(2,1)}, bf16[128,768]{1,0:T(8,128)(2,1)S(1)}, u32[]{:S(2)}, u32[]{:S(2)}) collective-permute-start(bf16[128,768]{1,0:T(8,128)(2,1)} %get-tuple-element.336), channel_id=1, source_target_pairs={{0,1},{1,0},{2,3},{3,2},{4,5},{5,4},{6,7},{7,6},{8,9},{9,8},{10,11... | collective-permute-start | bytes 589832 | tf_op jit(solution)/shard_map/ppermute | solution.py:944
  190.9 8.7 %collective-permute-start.40 = (bf16[128,768]{1,0:T(8,128)(2,1)}, bf16[128,768]{1,0:T(8,128)(2,1)S(1)}, u32[]{:S(2)}, u32[]{:S(2)}) collective-permute-start(bf16[128,768]{1,0:T(8,128)(2,1)} %get-tuple-element.337), channel_id=1, source_target_pairs={{0,2},{1,3},{2,0},{3,1},{4,6},{5,7},{6,4},{7,5},{8,10},{9,11},{10,... | collective-permute-start | bytes 589832 | tf_op jit(solution)/shard_map/ppermute | solution.py:944
  191.2 10.1 %collective-permute-start.41 = (bf16[128,768]{1,0:T(8,128)(2,1)}, bf16[128,768]{1,0:T(8,128)(2,1)}, u32[]{:S(2)}, u32[]{:S(2)}) collective-permute-start(bf16[128,768]{1,0:T(8,128)(2,1)} %get-tuple-element.338), channel_id=1, source_target_pairs={{0,3},{1,2},{2,1},{3,0},{4,7},{5,6},{6,5},{7,4},{8,11},{9,10},{10,... | collective-permute-start | bytes 589832 | tf_op jit(solution)/shard_map/ppermute | solution.py:944
  194.5 26.8 %all-to-all-start.4 = ((bf16[4,24,3072]{2,1,0:T(8,128)(2,1)}), bf16[4,24,3072]{2,1,0:T(8,128)(2,1)S(1)}, u32[]{:S(2)}, u32[]{:S(2)}) async-start(bf16[4,24,3072]{2,1,0:T(8,128)(2,1)} %add_convert_fusion.6), calls=%async_computation.4 | async-start | bytes 1179648 | tf_op jit(solution)/shard_map/all_to_all | solution.py:888
  202.9 10.8 %collective-permute-start.42 = (bf16[8,24,1152]{2,1,0:T(8,128)(2,1)S(1)}, bf16[8,24,1152]{2,1,0:T(8,128)(2,1)S(1)}, u32[]{:S(2)}, u32[]{:S(2)}) collective-permute-start(bf16[8,24,1152]{2,1,0:T(8,128)(2,1)S(1)} %bitcast.51), channel_id=1, source_target_pairs={{0,2},{1,5},{2,0},{3,7},{4,6},{5,1},{6,4},{7,3},{8,10},{9,13},{10,... | collective-permute-start | bytes 1327112 | tf_op jit(solution)/shard_map/ppermute | solution.py:874
  204.6 11.9 %collective-permute-start.44 = (bf16[4,24,1920]{2,1,0:T(8,128)(2,1)S(1)}, bf16[4,24,1920]{2,1,0:T(8,128)(2,1)S(1)}, u32[]{:S(2)}, u32[]{:S(2)}) collective-permute-start(bf16[4,24,1920]{2,1,0:T(8,128)(2,1)S(1)} %fusion.5), channel_id=1, source_target_pairs={{0,4},{1,3},{2,6},{3,1},{4,0},{5,7},{6,2},{7,5},{8,12},{9,11},{10,... | collective-permute-start | bytes 1105928 | tf_op jit(solution)/shard_map/ppermute | solution.py:874
  213.8 6.6 %collective-permute-start.45 = (bf16[4,24,1152]{2,1,0:T(8,128)(2,1)S(1)}, bf16[4,24,1152]{2,1,0:T(8,128)(2,1)S(1)}, u32[]{:S(2)}, u32[]{:S(2)}) collective-permute-start(bf16[4,24,1152]{2,1,0:T(8,128)(2,1)S(1)} %fusion.7), channel_id=1, source_target_pairs={{0,4},{1,3},{2,6},{3,1},{4,0},{5,7},{6,2},{7,5},{8,12},{9,11},{10,... | collective-permute-start | bytes 663560 | tf_op jit(solution)/shard_map/ppermute | solution.py:874
  221.4 20.5 %all-to-all-start.5 = ((bf16[4,24,3072]{2,1,0:T(8,128)(2,1)}), bf16[4,24,3072]{2,1,0:T(8,128)(2,1)S(1)}, u32[]{:S(2)}, u32[]{:S(2)}) async-start(bf16[4,24,3072]{2,1,0:T(8,128)(2,1)} %pad_maximum_fusion), calls=%async_computation.5 | async-start | bytes 1179648 | tf_op jit(solution)/shard_map/all_to_all | solution.py:888
  227.5 4.0 %collective-permute-start.46 = (bf16[128,768]{1,0:T(8,128)(2,1)S(1)}, bf16[128,768]{1,0:T(8,128)(2,1)S(1)}, u32[]{:S(2)}, u32[]{:S(2)}) collective-permute-start(bf16[128,768]{1,0:T(8,128)(2,1)S(1)} %copy-done.20), channel_id=1, source_target_pairs={{0,1},{1,0},{2,3},{3,2},{4,5},{5,4},{6,7},{7,6},{8,9},{9,8},{10,11... | collective-permute-start | bytes 589832 | tf_op jit(solution)/shard_map/ppermute | solution.py:944
  228.0 7.8 %collective-permute-start.47 = (bf16[128,768]{1,0:T(8,128)(2,1)S(1)}, bf16[128,768]{1,0:T(8,128)(2,1)S(1)}, u32[]{:S(2)}, u32[]{:S(2)}) collective-permute-start(bf16[128,768]{1,0:T(8,128)(2,1)S(1)} %copy-done.19), channel_id=1, source_target_pairs={{0,2},{1,3},{2,0},{3,1},{4,6},{5,7},{6,4},{7,5},{8,10},{9,11},{10,... | collective-permute-start | bytes 589832 | tf_op jit(solution)/shard_map/ppermute | solution.py:944
  228.8 9.4 %collective-permute-start.48 = (bf16[128,768]{1,0:T(8,128)(2,1)S(1)}, bf16[128,768]{1,0:T(8,128)(2,1)S(1)}, u32[]{:S(2)}, u32[]{:S(2)}) collective-permute-start(bf16[128,768]{1,0:T(8,128)(2,1)S(1)} %copy-done.18), channel_id=1, source_target_pairs={{0,3},{1,2},{2,1},{3,0},{4,7},{5,6},{6,5},{7,4},{8,11},{9,10},{10,... | collective-permute-start | bytes 589832 | tf_op jit(solution)/shard_map/ppermute | solution.py:944
  (31 other events, 188.1 us)

commit v5 on v4

--- a/solution.py
+++ b/solution.py
@@ -691,11 +691,10 @@
             store_grad(plan, tile, held, D, 0, slice(3 * HALF, width))
             view = (*lead, pl.ds(3 * HALF, D))
             copies += put_grad(held, grads, put_sems.at[3], view, view)
-        for m in range(3):
-            cols = slice(m * HALF, (m + 1) * HALF)
-            store_grad(plan, dot(h_ref[...], d_ref[:, cols], 0, 0), held, D, 0, cols)
-            view = (*lead, pl.ds(m * HALF, HALF))
-            copies += put_grad(held, grads, put_sems.at[m], view, view)
+        cols = slice(0, 3 * HALF)
+        store_grad(plan, dot(h_ref[...], d_ref[...], 0, 0), held, D, 0, cols)
+        view = (*lead, pl.ds(0, 3 * HALF))
+        copies += put_grad(held, grads, put_sems.at[0], view, view)
         for copy in copies:
             copy.wait()
 

time: 264 us -> 264 us (level)
  no operation moved by 1% of the time
where the time goes in v5:
time: 264 us; the launch traced here: 259 us
  Pallas kernels  91.7 us (35%)
  starting transfers between devices  69.6 us (26%)
  waiting for transfers between devices  60.3 us (23%)
  other arithmetic  16.4 us (6%)
  blocking collectives  10.8 us (4%)
  local copies, waits for them, and re-layouts  7.21 us (3%)
  between operations  2.78 us (1%)
    pallas_call x14, Pallas kernels, call(): pl.pallas_call(kernel, out_shape=[pltpu.HBM(o.shape, o.dtype) if kind in...  91.7 us
    ppermute x37, waiting for transfers between devices, send(): return lax.ppermute(values, AXES, perm)  36.4 us
    all_to_all x6, starting transfers between devices, along_z(): lax.all_to_all(values, 'dp', 0, 0, axis_index_groups=plan.groups, tiled=T...  31.7 us
    ppermute x37, starting transfers between devices, send(): return lax.ppermute(values, AXES, perm)  29.8 us
    ppermute x12, waiting for transfers between devices, swap(): lax.ppermute(values, 'seq', [(i, i ^ number) for i in range(plan.seq)])  16.4 us
    all_to_all x1, blocking collectives, finish(): cards = lax.all_to_all(cards, AXES, 0, 0, tiled=True)  10.8 us
    ppermute x12, starting transfers between devices, swap(): lax.ppermute(values, 'seq', [(i, i ^ number) for i in range(plan.seq)])  8.04 us
    all_to_all x6, waiting for transfers between devices, along_z(): lax.all_to_all(values, 'dp', 0, 0, axis_index_groups=plan.groups, tiled=T...  7.51 us
  transfers between devices with their start and end apart: 55, of which 25 were waited for; matrix products, arithmetic and copies ran while one was open for 6% of the time, Pallas kernels for 33%

profile of v5, /device:TPU:0, one launch (start us, length us, event | category | flops | bytes accessed | tf_op | source)
XLA Modules:
  0.0 258.8 jit_solution(3456930094499204788)
XLA Ops:
  4.9 6.2 %all-to-all-start = ((bf16[4,48,1280]{2,1,0:T(8,128)(2,1)}), bf16[4,48,1280]{2,1,0:T(8,128)(2,1)S(1)}, u32[]{:S(2)}, u32[]{:S(2)}) async-start(bf16[4,48,1280]{2,1,0:T(8,128)(2,1)} %broadcast_in_dim.8), calls=%async_computation | async-start | bytes 983040 | tf_op jit(solution)/shard_map/all_to_all | solution.py:887
  11.1 2.1 other_rows.1
  16.5 4.8 %collective-permute-done.2.refs_2_ = bf16[128,768]{1,0:T(8,128)(2,1)S(1)} collective-permute-done((bf16[128,768]{1,0:T(8,128)(2,1)}, bf16[128,768]{1,0:T(8,128)(2,1)S(1)}, u32[]{:S(2)}, u32[]{:S(2)}) %collective-permute-start.2) | collective-permute-done | bytes 196640 | tf_op jit(solution)/shard_map/ppermute | solution.py:943
  21.3 3.3 %collective-permute-done.3.refs_3_ = bf16[128,768]{1,0:T(8,128)(2,1)S(1)} collective-permute-done((bf16[128,768]{1,0:T(8,128)(2,1)}, bf16[128,768]{1,0:T(8,128)(2,1)S(1)}, u32[]{:S(2)}, u32[]{:S(2)}) %collective-permute-start.3) | collective-permute-done | bytes 196640 | tf_op jit(solution)/shard_map/ppermute | solution.py:943
  30.1 5.1 %all-to-all-start.1 = ((bf16[4,48,1920]{2,1,0:T(8,128)(2,1)}), bf16[4,48,1920]{2,1,0:T(8,128)(2,1)S(1)}, u32[]{:S(2)}, u32[]{:S(2)}) async-start(bf16[4,48,1920]{2,1,0:T(8,128)(2,1)} %broadcast_in_dim.9), calls=%async_computation.1 | async-start | bytes 1474560 | tf_op jit(solution)/shard_map/all_to_all | solution.py:887
  35.2 5.2 %collective-permute-done.6.refs_5_ = bf16[4,48,1280]{2,1,0:T(8,128)(2,1)S(1)} collective-permute-done((bf16[4,48,1280]{2,1,0:T(8,128)(2,1)S(1)}, bf16[4,48,1280]{2,1,0:T(8,128)(2,1)S(1)}, u32[]{:S(2)}, u32[]{:S(2)}) %collective-permute-start.6) | collective-permute-done | bytes 491552 | tf_op jit(solution)/shard_map/ppermute | solution.py:873
  40.8 1.8 collective-permute-start.8
  43.1 6.6 %collective-permute-done.8.refs_7_ = bf16[4,48,1280]{2,1,0:T(8,128)(2,1)S(1)} collective-permute-done((bf16[4,48,1280]{2,1,0:T(8,128)(2,1)S(1)}, bf16[4,48,1280]{2,1,0:T(8,128)(2,1)S(1)}, u32[]{:S(2)}, u32[]{:S(2)}) %collective-permute-start.8) | collective-permute-done | bytes 491552 | tf_op jit(solution)/shard_map/ppermute | solution.py:873
  50.2 1.8 collective-permute-start.20
  52.9 5.4 %project.1 = (bf16[512,768]{1,0:T(8,128)(2,1)}, bf16[512,768]{1,0:T(8,128)(2,1)}, bf16[512,768]{1,0:T(8,128)(2,1)}, bf16[512,768]{1,0:T(8,128)(2,1)}, f32[8,768]...) custom-call(bf16[4,128,768]{2,1,0:T(8,128)(2,1)S(1)} %copy-done, ...), custom_call_target="tpu_custom_call" | custom-call | flops 1 | bytes 1 | tf_op jit(solution)/shard_map/project/pallas_call | solution.py:244
  61.5 5.0 %all-to-all-start.2 = ((bf16[4,192,384]{2,1,0:T(8,128)(2,1)}), bf16[4,192,384]{2,1,0:T(8,128)(2,1)}, u32[]{:S(2)}, u32[]{:S(2)}) async-start(bf16[4,192,384]{2,1,0:T(8,128)(2,1)} %broadcast_in_dim.10), calls=%async_computation.2 | async-start | bytes 1179648 | tf_op jit(solution)/shard_map/all_to_all | solution.py:887
  66.5 9.8 %mix.1 = (bf16[768,512]{1,0:T(8,128)(2,1)}, bf16[512,768]{1,0:T(8,128)(2,1)}, f32[12,512]{1,0:T(8,128)}) custom-call(bf16[512,768]{1,0:T(8,128)(2,1)} %get-tuple-element.235.refs_0_.refs_1_, bf16[512,768]{1,0:T(8,128)(2,1)} %get-tuple-element.236.refs_1_.refs_2_, bf16[512,768]{1,0:T(8,128)(2,1)} %get-tuple-element.237.refs_2_.refs_3_, ...), custom_call_target="tpu_custom_call" | custom-call | flops 99999997952 | bytes 1 | tf_op jit(solution)/shard_map/mix/pallas_call | solution.py:244
  77.3 1.7 collective-permute-start.15
  80.4 2.6 %all-to-all-done.2.refs_6_ = bf16[4,192,384]{2,1,0:T(8,128)(2,1)} async-done(((bf16[4,192,384]{2,1,0:T(8,128)(2,1)}), bf16[4,192,384]{2,1,0:T(8,128)(2,1)}, u32[]{:S(2)}, u32[]{:S(2)}) %all-to-all-start.2) | async-done | bytes 589856 | tf_op jit(solution)/shard_map/all_to_all | solution.py:887
  83.0 5.8 %collective-permute-done.15.refs_6_ = bf16[4,48,1920]{2,1,0:T(8,128)(2,1)} collective-permute-done((bf16[4,48,1920]{2,1,0:T(8,128)(2,1)S(1)}, bf16[4,48,1920]{2,1,0:T(8,128)(2,1)}, u32[]{:S(2)}, u32[]{:S(2)}) %collective-permute-start.15) | collective-permute-done | bytes 737312 | tf_op jit(solution)/shard_map/ppermute | solution.py:873
  90.4 1.7 collective-permute-start.23
  93.3 8.9 %widen.1 = (f32[512,768]{1,0:T(8,128)}, bf16[512,768]{1,0:T(8,128)(2,1)}, bf16[512,3072]{1,0:T(8,128)(2,1)}, bf16[512,3072]{1,0:T(8,128)(2,1)}, bf16[4,4,48,3840]{3,2,1,0:T(8,128)(2,1)}) custom-call(bf16[512,768]{1,0:T(8,128)(2,1)} %get-tuple-element.253.refs_0_, bf16[512,768]{1,0:T(8,128)(2,1)} %get-tuple-element.254.refs_1_, ...), custom_call_target="tpu_custom_call" | custom-call | flops 99999997952 | bytes 1 | tf_op jit(solution)/shard_map/widen/pallas_call | solution.py:244
  102.3 2.2 collective-permute-done.22.refs_7_
  104.8 1.8 collective-permute-start.25
  107.1 7.3 %grad_of_down.1 = (bf16[4,4,96,768]{3,2,1,0:T(8,128)(2,1)}, bf16[4,4,96,768]{3,2,1,0:T(8,128)(2,1)}, bf16[512,768]{1,0:T(8,128)(2,1)}) custom-call(bf16[512,3072]{1,0:T(8,128)(2,1)} %get-tuple-element.263.refs_0_.refs_2_, bf16[4,128,768]{2,1,0:T(8,128)(2,1)S(1)} %copy-done.3, bf16[128,768]{1,0:T(8,128)(2,1)} %collective-permute-done.19.refs_2_, ...), custom_call_target="tpu_custom_call" | custom-call | flops 99999997952 | bytes 1 | tf_op jit(solution)/shard_map/grad_of_down/pallas_call | solution.py:244
  115.2 1.6 collective-permute-done.30.refs_13_
  116.8 9.7 %narrow0.1 = (f32[512,768]{1,0:T(8,128)}, bf16[4,4,24,3072]{3,2,1,0:T(8,128)(2,1)}, bf16[4,4,24,3072]{3,2,1,0:T(8,128)(2,1)}, f32[512,768]{1,0:T(8,128)}) custom-call(f32[512,768]{1,0:T(8,128)} %get-tuple-element.273.refs_0_, bf16[512,768]{1,0:T(8,128)(2,1)} %get-tuple-element.274.refs_1_, bf16[512,3072]{1,0:T(8,128)(2,1)} %get-tuple-element.263.refs_0_.refs_2_, ...), custom_call_target="tpu_custom_call" | custom-call | flops 99999997952 | bytes 1 | tf_op jit(solution)/shard_map/narrow0/pallas_call | solution.py:244
  127.3 1.8 collective-permute-start.31
  129.1 9.7 %narrow2.1 = (f32[512,768]{1,0:T(8,128)}, bf16[4,4,24,3072]{3,2,1,0:T(8,128)(2,1)}, bf16[4,4,24,3072]{3,2,1,0:T(8,128)(2,1)}, bf16[128,768]{1,0:T(8,128)(2,1)}, ...) custom-call(f32[512,768]{1,0:T(8,128)} %get-tuple-element.286.refs_0, ...), custom_call_target="tpu_custom_call", output_to_operand_aliasing={{1}: (15, {}), {2}: (16, {})} | custom-call | flops 99999997952 | bytes 1 | tf_op jit(solution)/shard_map/narrow2/pallas_call | solution.py:244
  138.8 4.7 %collective-permute-done.31 = bf16[8,96,768]{2,1,0:T(8,128)(2,1)S(1)} collective-permute-done((bf16[8,96,768]{2,1,0:T(8,128)(2,1)S(1)}, bf16[8,96,768]{2,1,0:T(8,128)(2,1)S(1)}, u32[]{:S(2)}, u32[]{:S(2)}) %collective-permute-start.31) | collective-permute-done | bytes 1179680 | tf_op jit(solution)/shard_map/ppermute | solution.py:873
  145.3 5.2 %turn.1 = (f32[512,768]{1,0:T(8,128)}, bf16[512,768]{1,0:T(8,128)(2,1)}, bf16[512,768]{1,0:T(8,128)(2,1)}, f32[2,768]{1,0:T(2,128)S(1)}) custom-call(f32[512,768]{1,0:T(8,128)} %get-tuple-element.273.refs_0_, f32[512,768]{1,0:T(8,128)} %get-tuple-element.301.refs_1_, bf16[512,768]{1,0:T(8,128)(2,1)} %get-tuple-element.276.refs_4_.refs_2_, ...), custom_call_target="tpu_custom_call" | custom-call | flops 99999997952 | bytes 1 | tf_op jit(solution)/shard_map/turn/pallas_call | solution.py:244
  150.5 1.9 add_convert_fusion.1
  153.7 1.8 collective-permute-start.34
  155.4 10.1 %attend_back0.1 = (bf16[512,1152]{1,0:T(8,128)(2,1)}, bf16[4,4,24,1920]{3,2,1,0:T(8,128)(2,1)}, bf16[4,4,24,1920]{3,2,1,0:T(8,128)(2,1)}) custom-call(bf16[512,768]{1,0:T(8,128)(2,1)} %get-tuple-element.311.refs_0_, bf16[512,768]{1,0:T(8,128)(2,1)} %get-tuple-element.235.refs_0_.refs_1_, bf16[512,768]{1,0:T(8,128)(2,1)} %get-tuple-element.236.refs_1_.refs_2_, ...), custom_call_target="tpu_custom_call" | custom-call | flops 99999997952 | bytes 1 | tf_op jit(solution)/shard_map/attend_back0/pallas_call | solution.py:244
  166.7 5.3 %all-to-all-start.3 = ((bf16[4,96,768]{2,1,0:T(8,128)(2,1)}), bf16[4,96,768]{2,1,0:T(8,128)(2,1)S(1)}, u32[]{:S(2)}, u32[]{:S(2)}) async-start(bf16[4,96,768]{2,1,0:T(8,128)(2,1)} %add_convert_fusion.7), calls=%async_computation.3 | async-start | bytes 1179648 | tf_op jit(solution)/shard_map/all_to_all | solution.py:887
  173.3 1.6 collective-permute-start.35
  174.9 2.6 %add_convert_fusion.4 = (bf16[2,4,24,1920]{3,2,1,0:T(8,128)(2,1)S(1)}, bf16[2,4,24,1920]{3,2,1,0:T(8,128)(2,1)}) fusion(bf16[4,4,24,1920]{3,2,1,0:T(8,128)(2,1)} %collective-permute-done.36, bf16[4,4,24,1920]{3,2,1,0:T(8,128)(2,1)S(1)} %copy-done.13), kind=kLoop, calls=%fused_computation.4 | loop fusion | flops 2949120 | bytes 4423680 | tf_op jit(solution)/shard_map/convert_element_type | solution.py:905
  177.8 9.4 %attend_back1.1 = (bf16[512,1152]{1,0:T(8,128)(2,1)}, bf16[4,4,24,1152]{3,2,1,0:T(8,128)(2,1)}, bf16[4,4,24,1152]{3,2,1,0:T(8,128)(2,1)}) custom-call(bf16[512,768]{1,0:T(8,128)(2,1)} %get-tuple-element.311.refs_0_, bf16[512,768]{1,0:T(8,128)(2,1)} %get-tuple-element.235.refs_0_.refs_1_, bf16[512,768]{1,0:T(8,128)(2,1)} %get-tuple-element.236.refs_1_.refs_2_, ...), custom_call_target="tpu_custom_call" | custom-call | flops 99999997952 | bytes 1 | tf_op jit(solution)/shard_map/attend_back1/pallas_call | solution.py:244
  188.5 2.0 collective-permute-done.37
  192.4 2.3 add_convert_fusion.6
  194.7 5.1 %all-to-all-start.4 = ((bf16[4,24,3072]{2,1,0:T(8,128)(2,1)}), bf16[4,24,3072]{2,1,0:T(8,128)(2,1)S(1)}, u32[]{:S(2)}, u32[]{:S(2)}) async-start(bf16[4,24,3072]{2,1,0:T(8,128)(2,1)} %add_convert_fusion.6), calls=%async_computation.4 | async-start | bytes 1179648 | tf_op jit(solution)/shard_map/all_to_all | solution.py:887
  199.9 1.6 collective-permute-done.41.refs_28_
  201.5 1.6 add_convert_fusion.8
  204.8 1.6 collective-permute-start.44
  206.4 7.1 %finish_tokens.1 = (bf16[128,768]{1,0:T(8,128)(2,1)}, bf16[128,768]{1,0:T(8,128)(2,1)}, bf16[128,768]{1,0:T(8,128)(2,1)}, bf16[128,768]{1,0:T(8,128)(2,1)}, f32[2,768]{1,0:T(2,128)S(1)}) custom-call(bf16[512,768]{1,0:T(8,128)(2,1)} %get-tuple-element.253.refs_0_, bf16[512,1152]{1,0:T(8,128)(2,1)} %get-tuple-element.340.refs_1_, ...), custom_call_target="tpu_custom_call" | custom-call | flops 1 | bytes 1 | tf_op jit(solution)/shard_map/finish_tokens/pallas_call | solution.py:244
  214.0 2.7 %collective-permute-start.45 = (bf16[4,24,1152]{2,1,0:T(8,128)(2,1)S(1)}, bf16[4,24,1152]{2,1,0:T(8,128)(2,1)S(1)}, u32[]{:S(2)}, u32[]{:S(2)}) collective-permute-start(bf16[4,24,1152]{2,1,0:T(8,128)(2,1)S(1)} %fusion.7), channel_id=1, source_target_pairs={{0,4},{1,3},{2,6},{3,1},{4,0},{5,7},{6,2},{7,5},{8,12},{9,11},{10,... | collective-permute-start | bytes 663560 | tf_op jit(solution)/shard_map/ppermute | solution.py:873
  217.8 2.8 %collective-permute-done.45 = bf16[4,24,1152]{2,1,0:T(8,128)(2,1)S(1)} collective-permute-done((bf16[4,24,1152]{2,1,0:T(8,128)(2,1)S(1)}, bf16[4,24,1152]{2,1,0:T(8,128)(2,1)S(1)}, u32[]{:S(2)}, u32[]{:S(2)}) %collective-permute-start.45) | collective-permute-done | bytes 221216 | tf_op jit(solution)/shard_map/ppermute | solution.py:873
  221.6 5.0 %all-to-all-start.5 = ((bf16[4,24,3072]{2,1,0:T(8,128)(2,1)}), bf16[4,24,3072]{2,1,0:T(8,128)(2,1)S(1)}, u32[]{:S(2)}, u32[]{:S(2)}) async-start(bf16[4,24,3072]{2,1,0:T(8,128)(2,1)} %pad_maximum_fusion), calls=%async_computation.5 | async-start | bytes 1179648 | tf_op jit(solution)/shard_map/all_to_all | solution.py:887
  231.7 4.2 %collective-permute-done.47.refs_31_ = bf16[128,768]{1,0:T(8,128)(2,1)S(1)} collective-permute-done((bf16[128,768]{1,0:T(8,128)(2,1)S(1)}, bf16[128,768]{1,0:T(8,128)(2,1)S(1)}, u32[]{:S(2)}, u32[]{:S(2)}) %collective-permute-start.47) | collective-permute-done | bytes 196640 | tf_op jit(solution)/shard_map/ppermute | solution.py:943
  236.0 2.4 collective-permute-done.48.refs_32_
  238.4 3.7 %all-to-all-done.5.refs_0_ = bf16[4,24,3072]{2,1,0:T(8,128)(2,1)S(1)} async-done(((bf16[4,24,3072]{2,1,0:T(8,128)(2,1)}), bf16[4,24,3072]{2,1,0:T(8,128)(2,1)S(1)}, u32[]{:S(2)}, u32[]{:S(2)}) %all-to-all-start.5) | async-done | bytes 589856 | tf_op jit(solution)/shard_map/all_to_all | solution.py:887
  243.2 10.8 %all_to_all.35.refs_3_ = bf16[32,16,128]{2,1,0:T(8,128)(2,1)S(1)} all-to-all(bf16[32,16,128]{2,1,0:T(8,128)(2,1)S(1)} %get-tuple-element.367), channel_id=1, replica_groups=mesh['dp'=8,'seq'=4] {'dp','seq'}, dimensions={0} | all-to-all | bytes 262144 | tf_op jit(solution)/shard_map/all_to_all | solution.py:926
  254.1 4.5 %update.1 = (f32[1,128]{1,0:T(1,128)}, f32[24,768]{1,0:T(8,128)}, f32[24,768]{1,0:T(8,128)}, f32[24,768]{1,0:T(8,128)}, f32[24,768]{1,0:T(8,128)}, /*index=5*/f3...) custom-call(f32[24,3072]{1,0:T(8,128)S(1)} %get-tuple-element.366.re, ...), custom_call_target="tpu_custom_call" | custom-call | flops 99999997952 | bytes 1 | tf_op jit(solution)/shard_map/update/pallas_call | solution.py:244
  (156 shorter events, 44.0 us)
Async XLA Ops:
  3.1 12.4 %collective-permute-start.5 = (bf16[96,384]{1,0:T(8,128)(2,1)S(1)}, bf16[96,384]{1,0:T(8,128)(2,1)S(1)}, u32[]{:S(2)}, u32[]{:S(2)}) collective-permute-start(bf16[96,384]{1,0:T(8,128)(2,1)S(1)} %get-tuple-element.220), channel_id=1, source_target_pairs={{0,1},{1,0},{2,3},{3,2},{4,5},{5,4},{6,7},{7,6},{8,9},{9,8},{10,11... | collective-permute-start | bytes 221192 | tf_op jit(solution)/shard_map/ppermute | solution.py:873
  4.9 20.4 %all-to-all-start = ((bf16[4,48,1280]{2,1,0:T(8,128)(2,1)}), bf16[4,48,1280]{2,1,0:T(8,128)(2,1)S(1)}, u32[]{:S(2)}, u32[]{:S(2)}) async-start(bf16[4,48,1280]{2,1,0:T(8,128)(2,1)} %broadcast_in_dim.8), calls=%async_computation | async-start | bytes 983040 | tf_op jit(solution)/shard_map/all_to_all | solution.py:887
  13.3 8.0 %collective-permute-start.2 = (bf16[128,768]{1,0:T(8,128)(2,1)}, bf16[128,768]{1,0:T(8,128)(2,1)S(1)}, u32[]{:S(2)}, u32[]{:S(2)}) collective-permute-start(bf16[128,768]{1,0:T(8,128)(2,1)} %get-tuple-element.215), channel_id=1, source_target_pairs={{0,2},{1,3},{2,0},{3,1},{4,6},{5,7},{6,4},{7,5},{8,10},{9,11},{10,... | collective-permute-start | bytes 589832 | tf_op jit(solution)/shard_map/ppermute | solution.py:943
  14.9 9.7 %collective-permute-start.3 = (bf16[128,768]{1,0:T(8,128)(2,1)}, bf16[128,768]{1,0:T(8,128)(2,1)S(1)}, u32[]{:S(2)}, u32[]{:S(2)}) collective-permute-start(bf16[128,768]{1,0:T(8,128)(2,1)} %get-tuple-element.216), channel_id=1, source_target_pairs={{0,3},{1,2},{2,1},{3,0},{4,7},{5,6},{6,5},{7,4},{8,11},{9,10},{10,... | collective-permute-start | bytes 589832 | tf_op jit(solution)/shard_map/ppermute | solution.py:943
  27.1 13.3 %collective-permute-start.6 = (bf16[4,48,1280]{2,1,0:T(8,128)(2,1)S(1)}, bf16[4,48,1280]{2,1,0:T(8,128)(2,1)S(1)}, u32[]{:S(2)}, u32[]{:S(2)}) collective-permute-start(bf16[4,48,1280]{2,1,0:T(8,128)(2,1)S(1)} %all-to-all-done.refs_4_), channel_id=1, source_target_pairs={{0,4},{1,3},{2,6},{3,1},{4,0},{5,7},{6,2},{7,5},{8,12},{9,11},{10,... | collective-permute-start | bytes 1474568 | tf_op jit(solution)/shard_map/ppermute | solution.py:873
  28.6 12.2 %collective-permute-start.7 = (bf16[4,48,1280]{2,1,0:T(8,128)(2,1)S(1)}, bf16[4,48,1280]{2,1,0:T(8,128)(2,1)S(1)}, u32[]{:S(2)}, u32[]{:S(2)}) collective-permute-start(bf16[4,48,1280]{2,1,0:T(8,128)(2,1)S(1)} %all-to-all-done.refs_4_), channel_id=1, source_target_pairs={{0,2},{1,5},{2,0},{3,7},{4,6},{5,1},{6,4},{7,3},{8,10},{9,13},{10,... | collective-permute-start | bytes 1474568 | tf_op jit(solution)/shard_map/ppermute | solution.py:873
  30.1 28.2 %all-to-all-start.1 = ((bf16[4,48,1920]{2,1,0:T(8,128)(2,1)}), bf16[4,48,1920]{2,1,0:T(8,128)(2,1)S(1)}, u32[]{:S(2)}, u32[]{:S(2)}) async-start(bf16[4,48,1920]{2,1,0:T(8,128)(2,1)} %broadcast_in_dim.9), calls=%async_computation.1 | async-start | bytes 1474560 | tf_op jit(solution)/shard_map/all_to_all | solution.py:887
  35.2 7.9 %collective-permute-start.9 = (bf16[4,48,1280]{2,1,0:T(8,128)(2,1)S(1)}, bf16[4,48,1280]{2,1,0:T(8,128)(2,1)S(1)}, u32[]{:S(2)}, u32[]{:S(2)}) collective-permute-start(bf16[4,48,1280]{2,1,0:T(8,128)(2,1)S(1)} %all-to-all-done.refs_4_), channel_id=1, source_target_pairs={{0,1},{1,0},{2,3},{3,2},{4,5},{5,4},{6,7},{7,6},{8,9},{9,8},{10,11... | collective-permute-start | bytes 1474568 | tf_op jit(solution)/shard_map/ppermute | solution.py:873
  40.8 8.8 %collective-permute-start.8 = (bf16[4,48,1280]{2,1,0:T(8,128)(2,1)S(1)}, bf16[4,48,1280]{2,1,0:T(8,128)(2,1)S(1)}, u32[]{:S(2)}, u32[]{:S(2)}) collective-permute-start(bf16[4,48,1280]{2,1,0:T(8,128)(2,1)S(1)} %collective-permute-done.6.refs_5_), channel_id=1, source_target_pairs={{0,2},{1,5},{2,0},{3,7},{4,6},{5,1},{6,4},{7,3},{8,10},{9,13},{10,... | collective-permute-start | bytes 1474568 | tf_op jit(solution)/shard_map/ppermute | solution.py:873
  42.6 7.1 %collective-permute-start.10 = (bf16[4,48,1280]{2,1,0:T(8,128)(2,1)S(1)}, bf16[4,48,1280]{2,1,0:T(8,128)(2,1)S(1)}, u32[]{:S(2)}, u32[]{:S(2)}) collective-permute-start(bf16[4,48,1280]{2,1,0:T(8,128)(2,1)S(1)} %collective-permute-done.6.refs_5_), channel_id=1, source_target_pairs={{0,1},{1,0},{2,3},{3,2},{4,5},{5,4},{6,7},{7,6},{8,9},{9,8},{10,11... | collective-permute-start | bytes 1474568 | tf_op jit(solution)/shard_map/ppermute | solution.py:873
  42.6 7.1 %collective-permute-start.11 = (bf16[4,48,1280]{2,1,0:T(8,128)(2,1)S(1)}, bf16[4,48,1280]{2,1,0:T(8,128)(2,1)S(1)}, u32[]{:S(2)}, u32[]{:S(2)}) collective-permute-start(bf16[4,48,1280]{2,1,0:T(8,128)(2,1)S(1)} %collective-permute-done.7.refs_6_), channel_id=1, source_target_pairs={{0,1},{1,0},{2,3},{3,2},{4,5},{5,4},{6,7},{7,6},{8,9},{9,8},{10,11... | collective-permute-start | bytes 1474568 | tf_op jit(solution)/shard_map/ppermute | solution.py:873
  49.7 11.6 %collective-permute-start.19 = (bf16[128,768]{1,0:T(8,128)(2,1)}, bf16[128,768]{1,0:T(8,128)(2,1)}, u32[]{:S(2)}, u32[]{:S(2)}) collective-permute-start(bf16[128,768]{1,0:T(8,128)(2,1)} %get-tuple-element.248), channel_id=1, source_target_pairs={{0,1},{1,0},{2,3},{3,2},{4,5},{5,4},{6,7},{7,6},{8,9},{9,8},{10,11... | collective-permute-start | bytes 589832 | tf_op jit(solution)/shard_map/ppermute | solution.py:943
  50.2 11.3 %collective-permute-start.20 = (bf16[128,768]{1,0:T(8,128)(2,1)}, bf16[128,768]{1,0:T(8,128)(2,1)}, u32[]{:S(2)}, u32[]{:S(2)}) collective-permute-start(bf16[128,768]{1,0:T(8,128)(2,1)} %get-tuple-element.249), channel_id=1, source_target_pairs={{0,2},{1,3},{2,0},{3,1},{4,6},{5,7},{6,4},{7,5},{8,10},{9,11},{10,... | collective-permute-start | bytes 589832 | tf_op jit(solution)/shard_map/ppermute | solution.py:943
  51.9 9.6 %collective-permute-start.21 = (bf16[128,768]{1,0:T(8,128)(2,1)}, bf16[128,768]{1,0:T(8,128)(2,1)}, u32[]{:S(2)}, u32[]{:S(2)}) collective-permute-start(bf16[128,768]{1,0:T(8,128)(2,1)} %get-tuple-element.250), channel_id=1, source_target_pairs={{0,3},{1,2},{2,1},{3,0},{4,7},{5,6},{6,5},{7,4},{8,11},{9,10},{10,... | collective-permute-start | bytes 589832 | tf_op jit(solution)/shard_map/ppermute | solution.py:943
  58.3 18.6 %collective-permute-start.13 = (bf16[4,48,1920]{2,1,0:T(8,128)(2,1)S(1)}, bf16[4,48,1920]{2,1,0:T(8,128)(2,1)S(1)}, u32[]{:S(2)}, u32[]{:S(2)}) collective-permute-start(bf16[4,48,1920]{2,1,0:T(8,128)(2,1)S(1)} %all-to-all-done.1.refs_3_), channel_id=1, source_target_pairs={{0,4},{1,3},{2,6},{3,1},{4,0},{5,7},{6,2},{7,5},{8,12},{9,11},{10,... | collective-permute-start | bytes 2211848 | tf_op jit(solution)/shard_map/ppermute | solution.py:873
  59.9 17.4 %collective-permute-start.14 = (bf16[4,48,1920]{2,1,0:T(8,128)(2,1)S(1)}, bf16[4,48,1920]{2,1,0:T(8,128)(2,1)S(1)}, u32[]{:S(2)}, u32[]{:S(2)}) collective-permute-start(bf16[4,48,1920]{2,1,0:T(8,128)(2,1)S(1)} %all-to-all-done.1.refs_3_), channel_id=1, source_target_pairs={{0,2},{1,5},{2,0},{3,7},{4,6},{5,1},{6,4},{7,3},{8,10},{9,13},{10,... | collective-permute-start | bytes 2211848 | tf_op jit(solution)/shard_map/ppermute | solution.py:873
  61.3 19.1 %collective-permute-start.16 = (bf16[4,48,1920]{2,1,0:T(8,128)(2,1)S(1)}, bf16[4,48,1920]{2,1,0:T(8,128)(2,1)}, u32[]{:S(2)}, u32[]{:S(2)}) collective-permute-start(bf16[4,48,1920]{2,1,0:T(8,128)(2,1)S(1)} %all-to-all-done.1.refs_3_), channel_id=1, source_target_pairs={{0,1},{1,0},{2,3},{3,2},{4,5},{5,4},{6,7},{7,6},{8,9},{9,8},{10,11... | collective-permute-start | bytes 2211848 | tf_op jit(solution)/shard_map/ppermute | solution.py:873
  61.5 21.5 %all-to-all-start.2 = ((bf16[4,192,384]{2,1,0:T(8,128)(2,1)}), bf16[4,192,384]{2,1,0:T(8,128)(2,1)}, u32[]{:S(2)}, u32[]{:S(2)}) async-start(bf16[4,192,384]{2,1,0:T(8,128)(2,1)} %broadcast_in_dim.10), calls=%async_computation.2 | async-start | bytes 1179648 | tf_op jit(solution)/shard_map/all_to_all | solution.py:887
  77.3 11.6 %collective-permute-start.15 = (bf16[4,48,1920]{2,1,0:T(8,128)(2,1)S(1)}, bf16[4,48,1920]{2,1,0:T(8,128)(2,1)}, u32[]{:S(2)}, u32[]{:S(2)}) collective-permute-start(bf16[4,48,1920]{2,1,0:T(8,128)(2,1)S(1)} %collective-permute-done.13.refs_4_), channel_id=1, source_target_pairs={{0,2},{1,5},{2,0},{3,7},{4,6},{5,1},{6,4},{7,3},{8,10},{9,13},{10,... | collective-permute-start | bytes 2211848 | tf_op jit(solution)/shard_map/ppermute | solution.py:873
  79.0 9.8 %collective-permute-start.17 = (bf16[4,48,1920]{2,1,0:T(8,128)(2,1)S(1)}, bf16[4,48,1920]{2,1,0:T(8,128)(2,1)}, u32[]{:S(2)}, u32[]{:S(2)}) collective-permute-start(bf16[4,48,1920]{2,1,0:T(8,128)(2,1)S(1)} %collective-permute-done.13.refs_4_), channel_id=1, source_target_pairs={{0,1},{1,0},{2,3},{3,2},{4,5},{5,4},{6,7},{7,6},{8,9},{9,8},{10,11... | collective-permute-start | bytes 2211848 | tf_op jit(solution)/shard_map/ppermute | solution.py:873
  79.2 9.7 %collective-permute-start.18 = (bf16[4,48,1920]{2,1,0:T(8,128)(2,1)S(1)}, bf16[4,48,1920]{2,1,0:T(8,128)(2,1)}, u32[]{:S(2)}, u32[]{:S(2)}) collective-permute-start(bf16[4,48,1920]{2,1,0:T(8,128)(2,1)S(1)} %collective-permute-done.14.refs_5_), channel_id=1, source_target_pairs={{0,1},{1,0},{2,3},{3,2},{4,5},{5,4},{6,7},{7,6},{8,9},{9,8},{10,11... | collective-permute-start | bytes 2211848 | tf_op jit(solution)/shard_map/ppermute | solution.py:873
  88.9 15.6 %collective-permute-start.22 = (bf16[4,192,384]{2,1,0:T(8,128)(2,1)}, bf16[4,192,384]{2,1,0:T(8,128)(2,1)S(1)}, u32[]{:S(2)}, u32[]{:S(2)}) collective-permute-start(bf16[4,192,384]{2,1,0:T(8,128)(2,1)} %all-to-all-done.2.refs_6_), channel_id=1, source_target_pairs={{0,4},{1,3},{2,6},{3,1},{4,0},{5,7},{6,2},{7,5},{8,12},{9,11},{10,... | collective-permute-start | bytes 1769480 | tf_op jit(solution)/shard_map/ppermute | solution.py:873
  90.4 14.4 %collective-permute-start.23 = (bf16[4,192,384]{2,1,0:T(8,128)(2,1)}, bf16[4,192,384]{2,1,0:T(8,128)(2,1)S(1)}, u32[]{:S(2)}, u32[]{:S(2)}) collective-permute-start(bf16[4,192,384]{2,1,0:T(8,128)(2,1)} %all-to-all-done.2.refs_6_), channel_id=1, source_target_pairs={{0,2},{1,5},{2,0},{3,7},{4,6},{5,1},{6,4},{7,3},{8,10},{9,13},{10,... | collective-permute-start | bytes 1769480 | tf_op jit(solution)/shard_map/ppermute | solution.py:873
  92.2 22.2 %collective-permute-start.26 = (bf16[4,192,384]{2,1,0:T(8,128)(2,1)}, bf16[4,192,384]{2,1,0:T(8,128)(2,1)}, u32[]{:S(2)}, u32[]{:S(2)}) collective-permute-start(bf16[4,192,384]{2,1,0:T(8,128)(2,1)} %all-to-all-done.2.refs_6_), channel_id=1, source_target_pairs={{0,1},{1,0},{2,3},{3,2},{4,5},{5,4},{6,7},{7,6},{8,9},{9,8},{10,11... | collective-permute-start | bytes 1769480 | tf_op jit(solution)/shard_map/ppermute | solution.py:873
  104.8 9.9 %collective-permute-start.25 = (bf16[4,192,384]{2,1,0:T(8,128)(2,1)S(1)}, bf16[4,192,384]{2,1,0:T(8,128)(2,1)S(1)}, u32[]{:S(2)}, u32[]{:S(2)}) collective-permute-start(bf16[4,192,384]{2,1,0:T(8,128)(2,1)S(1)} %collective-permute-done.22.refs_7_), channel_id=1, source_target_pairs={{0,2},{1,5},{2,0},{3,7},{4,6},{5,1},{6,4},{7,3},{8,10},{9,13},{10,... | collective-permute-start | bytes 1769480 | tf_op jit(solution)/shard_map/ppermute | solution.py:873
  106.6 8.1 %collective-permute-start.27 = (bf16[4,192,384]{2,1,0:T(8,128)(2,1)S(1)}, bf16[4,192,384]{2,1,0:T(8,128)(2,1)S(1)}, u32[]{:S(2)}, u32[]{:S(2)}) collective-permute-start(bf16[4,192,384]{2,1,0:T(8,128)(2,1)S(1)} %collective-permute-done.22.refs_7_), channel_id=1, source_target_pairs={{0,1},{1,0},{2,3},{3,2},{4,5},{5,4},{6,7},{7,6},{8,9},{9,8},{10,11... | collective-permute-start | bytes 1769480 | tf_op jit(solution)/shard_map/ppermute | solution.py:873
  106.6 8.1 %collective-permute-start.28 = (bf16[4,192,384]{2,1,0:T(8,128)(2,1)S(1)}, bf16[4,192,384]{2,1,0:T(8,128)(2,1)S(1)}, u32[]{:S(2)}, u32[]{:S(2)}) collective-permute-start(bf16[4,192,384]{2,1,0:T(8,128)(2,1)S(1)} %collective-permute-done.23.refs_8_), channel_id=1, source_target_pairs={{0,1},{1,0},{2,3},{3,2},{4,5},{5,4},{6,7},{7,6},{8,9},{9,8},{10,11... | collective-permute-start | bytes 1769480 | tf_op jit(solution)/shard_map/ppermute | solution.py:873
  114.7 11.9 %collective-permute-start.29 = (bf16[4,4,96,768]{3,2,1,0:T(8,128)(2,1)}, bf16[4,4,96,768]{3,2,1,0:T(8,128)(2,1)S(1)}, u32[]{:S(2)}, u32[]{:S(2)}) collective-permute-start(bf16[4,4,96,768]{3,2,1,0:T(8,128)(2,1)} %get-tuple-element.272), channel_id=1, source_target_pairs={{0,1},{1,0},{2,3},{3,2},{4,5},{5,4},{6,7},{7,6},{8,9},{9,8},{10,11... | collective-permute-start | bytes 7077896 | tf_op jit(solution)/shard_map/ppermute | solution.py:873
  127.3 16.3 %collective-permute-start.31 = (bf16[8,96,768]{2,1,0:T(8,128)(2,1)S(1)}, bf16[8,96,768]{2,1,0:T(8,128)(2,1)S(1)}, u32[]{:S(2)}, u32[]{:S(2)}) collective-permute-start(bf16[8,96,768]{2,1,0:T(8,128)(2,1)S(1)} %bitcast.50), channel_id=1, source_target_pairs={{0,2},{1,5},{2,0},{3,7},{4,6},{5,1},{6,4},{7,3},{8,10},{9,13},{10,... | collective-permute-start | bytes 3538952 | tf_op jit(solution)/shard_map/ppermute | solution.py:873
  143.7 9.9 %collective-permute-start.33 = (bf16[4,96,768]{2,1,0:T(8,128)(2,1)S(1)}, bf16[4,96,768]{2,1,0:T(8,128)(2,1)S(1)}, u32[]{:S(2)}, u32[]{:S(2)}) collective-permute-start(bf16[4,96,768]{2,1,0:T(8,128)(2,1)S(1)} %fusion.3), channel_id=1, source_target_pairs={{0,4},{1,3},{2,6},{3,1},{4,0},{5,7},{6,2},{7,5},{8,12},{9,11},{10,... | collective-permute-start | bytes 1769480 | tf_op jit(solution)/shard_map/ppermute | solution.py:873
  145.3 5.2 %collective-permute-start.32 = (bf16[4,4,24,3072]{3,2,1,0:T(8,128)(2,1)}, bf16[4,4,24,3072]{3,2,1,0:T(8,128)(2,1)S(1)}, u32[]{:S(2)}, u32[]{:S(2)}) collective-permute-start(bf16[4,4,24,3072]{3,2,1,0:T(8,128)(2,1)} %get-tuple-element.298), channel_id=1, source_target_pairs={{0,1},{1,0},{2,3},{3,2},{4,5},{5,4},{6,7},{7,6},{8,9},{9,8},{10,11... | collective-permute-start | bytes 7077896 | tf_op jit(solution)/shard_map/ppermute | solution.py:873
  153.7 18.3 %collective-permute-start.34 = (bf16[8,24,3072]{2,1,0:T(8,128)(2,1)}, bf16[8,24,3072]{2,1,0:T(8,128)(2,1)}, u32[]{:S(2)}, u32[]{:S(2)}) collective-permute-start(bf16[8,24,3072]{2,1,0:T(8,128)(2,1)} %bitcast.3), channel_id=1, source_target_pairs={{0,2},{1,5},{2,0},{3,7},{4,6},{5,1},{6,4},{7,3},{8,10},{9,13},{10,... | collective-permute-start | bytes 3538952 | tf_op jit(solution)/shard_map/ppermute | solution.py:873
  165.6 9.4 %collective-permute-start.36 = (bf16[4,4,24,1920]{3,2,1,0:T(8,128)(2,1)}, bf16[4,4,24,1920]{3,2,1,0:T(8,128)(2,1)}, u32[]{:S(2)}, u32[]{:S(2)}) collective-permute-start(bf16[4,4,24,1920]{3,2,1,0:T(8,128)(2,1)} %get-tuple-element.322), channel_id=1, source_target_pairs={{0,1},{1,0},{2,3},{3,2},{4,5},{5,4},{6,7},{7,6},{8,9},{9,8},{10,11... | collective-permute-start | bytes 4423688 | tf_op jit(solution)/shard_map/ppermute | solution.py:873
  166.7 21.8 %all-to-all-start.3 = ((bf16[4,96,768]{2,1,0:T(8,128)(2,1)}), bf16[4,96,768]{2,1,0:T(8,128)(2,1)S(1)}, u32[]{:S(2)}, u32[]{:S(2)}) async-start(bf16[4,96,768]{2,1,0:T(8,128)(2,1)} %add_convert_fusion.7), calls=%async_computation.3 | async-start | bytes 1179648 | tf_op jit(solution)/shard_map/all_to_all | solution.py:887
  173.3 15.2 %collective-permute-start.35 = (bf16[4,24,3072]{2,1,0:T(8,128)(2,1)S(1)}, bf16[4,24,3072]{2,1,0:T(8,128)(2,1)}, u32[]{:S(2)}, u32[]{:S(2)}) collective-permute-start(bf16[4,24,3072]{2,1,0:T(8,128)(2,1)S(1)} %fusion), channel_id=1, source_target_pairs={{0,4},{1,3},{2,6},{3,1},{4,0},{5,7},{6,2},{7,5},{8,12},{9,11},{10,... | collective-permute-start | bytes 1769480 | tf_op jit(solution)/shard_map/ppermute | solution.py:873
  177.5 13.0 %collective-permute-start.37 = (bf16[8,24,1920]{2,1,0:T(8,128)(2,1)}, bf16[8,24,1920]{2,1,0:T(8,128)(2,1)}, u32[]{:S(2)}, u32[]{:S(2)}) collective-permute-start(bf16[8,24,1920]{2,1,0:T(8,128)(2,1)} %bitcast.6), channel_id=1, source_target_pairs={{0,2},{1,5},{2,0},{3,7},{4,6},{5,1},{6,4},{7,3},{8,10},{9,13},{10,... | collective-permute-start | bytes 2211848 | tf_op jit(solution)/shard_map/ppermute | solution.py:873
  187.2 12.6 %collective-permute-start.38 = (bf16[4,4,24,1152]{3,2,1,0:T(8,128)(2,1)}, bf16[4,4,24,1152]{3,2,1,0:T(8,128)(2,1)}, u32[]{:S(2)}, u32[]{:S(2)}) collective-permute-start(bf16[4,4,24,1152]{3,2,1,0:T(8,128)(2,1)} %get-tuple-element.329), channel_id=1, source_target_pairs={{0,1},{1,0},{2,3},{3,2},{4,5},{5,4},{6,7},{7,6},{8,9},{9,8},{10,11... | collective-permute-start | bytes 2654216 | tf_op jit(solution)/shard_map/ppermute | solution.py:873
  190.5 9.3 %collective-permute-start.39 = (bf16[128,768]{1,0:T(8,128)(2,1)}, bf16[128,768]{1,0:T(8,128)(2,1)S(1)}, u32[]{:S(2)}, u32[]{:S(2)}) collective-permute-start(bf16[128,768]{1,0:T(8,128)(2,1)} %get-tuple-element.336), channel_id=1, source_target_pairs={{0,1},{1,0},{2,3},{3,2},{4,5},{5,4},{6,7},{7,6},{8,9},{9,8},{10,11... | collective-permute-start | bytes 589832 | tf_op jit(solution)/shard_map/ppermute | solution.py:943
  191.1 8.7 %collective-permute-start.40 = (bf16[128,768]{1,0:T(8,128)(2,1)}, bf16[128,768]{1,0:T(8,128)(2,1)S(1)}, u32[]{:S(2)}, u32[]{:S(2)}) collective-permute-start(bf16[128,768]{1,0:T(8,128)(2,1)} %get-tuple-element.337), channel_id=1, source_target_pairs={{0,2},{1,3},{2,0},{3,1},{4,6},{5,7},{6,4},{7,5},{8,10},{9,11},{10,... | collective-permute-start | bytes 589832 | tf_op jit(solution)/shard_map/ppermute | solution.py:943
  191.4 10.1 %collective-permute-start.41 = (bf16[128,768]{1,0:T(8,128)(2,1)}, bf16[128,768]{1,0:T(8,128)(2,1)}, u32[]{:S(2)}, u32[]{:S(2)}) collective-permute-start(bf16[128,768]{1,0:T(8,128)(2,1)} %get-tuple-element.338), channel_id=1, source_target_pairs={{0,3},{1,2},{2,1},{3,0},{4,7},{5,6},{6,5},{7,4},{8,11},{9,10},{10,... | collective-permute-start | bytes 589832 | tf_op jit(solution)/shard_map/ppermute | solution.py:943
  194.7 26.9 %all-to-all-start.4 = ((bf16[4,24,3072]{2,1,0:T(8,128)(2,1)}), bf16[4,24,3072]{2,1,0:T(8,128)(2,1)S(1)}, u32[]{:S(2)}, u32[]{:S(2)}) async-start(bf16[4,24,3072]{2,1,0:T(8,128)(2,1)} %add_convert_fusion.6), calls=%async_computation.4 | async-start | bytes 1179648 | tf_op jit(solution)/shard_map/all_to_all | solution.py:887
  203.1 10.8 %collective-permute-start.42 = (bf16[8,24,1152]{2,1,0:T(8,128)(2,1)S(1)}, bf16[8,24,1152]{2,1,0:T(8,128)(2,1)S(1)}, u32[]{:S(2)}, u32[]{:S(2)}) collective-permute-start(bf16[8,24,1152]{2,1,0:T(8,128)(2,1)S(1)} %bitcast.51), channel_id=1, source_target_pairs={{0,2},{1,5},{2,0},{3,7},{4,6},{5,1},{6,4},{7,3},{8,10},{9,13},{10,... | collective-permute-start | bytes 1327112 | tf_op jit(solution)/shard_map/ppermute | solution.py:873
  204.8 11.9 %collective-permute-start.44 = (bf16[4,24,1920]{2,1,0:T(8,128)(2,1)S(1)}, bf16[4,24,1920]{2,1,0:T(8,128)(2,1)S(1)}, u32[]{:S(2)}, u32[]{:S(2)}) collective-permute-start(bf16[4,24,1920]{2,1,0:T(8,128)(2,1)S(1)} %fusion.5), channel_id=1, source_target_pairs={{0,4},{1,3},{2,6},{3,1},{4,0},{5,7},{6,2},{7,5},{8,12},{9,11},{10,... | collective-permute-start | bytes 1105928 | tf_op jit(solution)/shard_map/ppermute | solution.py:873
  214.0 6.6 %collective-permute-start.45 = (bf16[4,24,1152]{2,1,0:T(8,128)(2,1)S(1)}, bf16[4,24,1152]{2,1,0:T(8,128)(2,1)S(1)}, u32[]{:S(2)}, u32[]{:S(2)}) collective-permute-start(bf16[4,24,1152]{2,1,0:T(8,128)(2,1)S(1)} %fusion.7), channel_id=1, source_target_pairs={{0,4},{1,3},{2,6},{3,1},{4,0},{5,7},{6,2},{7,5},{8,12},{9,11},{10,... | collective-permute-start | bytes 663560 | tf_op jit(solution)/shard_map/ppermute | solution.py:873
  221.6 20.5 %all-to-all-start.5 = ((bf16[4,24,3072]{2,1,0:T(8,128)(2,1)}), bf16[4,24,3072]{2,1,0:T(8,128)(2,1)S(1)}, u32[]{:S(2)}, u32[]{:S(2)}) async-start(bf16[4,24,3072]{2,1,0:T(8,128)(2,1)} %pad_maximum_fusion), calls=%async_computation.5 | async-start | bytes 1179648 | tf_op jit(solution)/shard_map/all_to_all | solution.py:887
  227.7 4.0 %collective-permute-start.46 = (bf16[128,768]{1,0:T(8,128)(2,1)S(1)}, bf16[128,768]{1,0:T(8,128)(2,1)S(1)}, u32[]{:S(2)}, u32[]{:S(2)}) collective-permute-start(bf16[128,768]{1,0:T(8,128)(2,1)S(1)} %copy-done.20), channel_id=1, source_target_pairs={{0,1},{1,0},{2,3},{3,2},{4,5},{5,4},{6,7},{7,6},{8,9},{9,8},{10,11... | collective-permute-start | bytes 589832 | tf_op jit(solution)/shard_map/ppermute | solution.py:943
  228.2 7.8 %collective-permute-start.47 = (bf16[128,768]{1,0:T(8,128)(2,1)S(1)}, bf16[128,768]{1,0:T(8,128)(2,1)S(1)}, u32[]{:S(2)}, u32[]{:S(2)}) collective-permute-start(bf16[128,768]{1,0:T(8,128)(2,1)S(1)} %copy-done.19), channel_id=1, source_target_pairs={{0,2},{1,3},{2,0},{3,1},{4,6},{5,7},{6,4},{7,5},{8,10},{9,11},{10,... | collective-permute-start | bytes 589832 | tf_op jit(solution)/shard_map/ppermute | solution.py:943
  229.0 9.4 %collective-permute-start.48 = (bf16[128,768]{1,0:T(8,128)(2,1)S(1)}, bf16[128,768]{1,0:T(8,128)(2,1)S(1)}, u32[]{:S(2)}, u32[]{:S(2)}) collective-permute-start(bf16[128,768]{1,0:T(8,128)(2,1)S(1)} %copy-done.18), channel_id=1, source_target_pairs={{0,3},{1,2},{2,1},{3,0},{4,7},{5,6},{6,5},{7,4},{8,11},{9,10},{10,... | collective-permute-start | bytes 589832 | tf_op jit(solution)/shard_map/ppermute | solution.py:943
  (31 other events, 188.4 us)
